TPU v7x, 32 devices: a whole 2x2x4 slice. The times are simulated.
32 devices in a mesh: gx: 2 (over x), gy: 4 (over y, core), gz: 4 (over z).
Axes of the slice: x: 2, y: 2, z: 4, core: 2. Of those that a mesh axis runs over, the one named last changes fastest.
Arguments:
- state: bfloat16 [32, 64, 8, 8, 128], P('gx', 'gy', 'gz'), may hold values from -6 to 6
- cotangent: bfloat16 [32, 64, 8, 8, 128], P('gx', 'gy', 'gz'), may hold values from -6 to 6
- counts: int32 [4], P('gz'), may hold values from 1 to 2, 6 in all
- edge_weights: bfloat16 [2, 2, 128, 128], replicated, may hold values from -0.5 to 0.5
- node_in: bfloat16 [2, 256, 128], replicated, may hold values from -0.375 to 0.375
- node_out: bfloat16 [2, 128, 128], replicated, may hold values from -0.5 to 0.5
- biases: float32 [2, 2, 128], replicated, may hold values from -4 to 4
Outputs:
- state_grad: bfloat16 [32, 64, 8, 8, 128], P('gx', 'gy', 'gz')
- edge_grads: float32 [2, 2, 128, 128], replicated
- node_in_grad: float32 [2, 256, 128], replicated
- node_out_grad: float32 [2, 128, 128], replicated
- bias_grads: float32 [2, 2, 128], replicated
Inputs may be any that keep to these rules, and one draw needn't show every extreme that they name: The counts sum to 6; index k of gz holds the element layers that follow those of smaller indices.
All inputs are finite; a program needn't handle non-finite values. No bound on the sum of `counts` on one device may be relied on, other than what follows from the above.
Results may differ from a plain program's by a relative error of at most 0.012.
The roundings to bfloat16 on the way count: a program that leaves them out, or rounds other values in their place, can miss the bound.
Values sent between devices are 32-bit elements; how exact they have to be, the bound alone decides.
No kernel may reach another device: no remote copies, remote signals or barrier semaphores. Data moves between devices by JAX's collectives and lax.ppermute only.
A program may use at most 128 MiB of HBM per device.

v0:
```python
import functools
import math

import jax
import jax.numpy as jnp
from jax import lax
from jax.experimental import pallas as pl
from jax.experimental.pallas import tpu as pltpu
from jax.sharding import PartitionSpec as P

f32 = jnp.float32
bf16 = jnp.bfloat16
NODES = 8
VM = pl.BlockSpec(memory_space=pltpu.VMEM)
SM = pl.BlockSpec(memory_space=pltpu.SMEM)


def dot(left, right):
    return lax.dot_general(left, right, (((1,), (0,)), ((), ())), preferred_element_type=f32)


def dot_t(left, right):
    return lax.dot_general(left, right, (((0,), (0,)), ((), ())), preferred_element_type=f32)


def silu_half(half):
    th = jnp.tanh(half)
    prod = half * th
    return half + prod, (0.5 + 0.5 * th) * ((1.0 + half) - prod)


def split_cols(value):
    high = value.astype(bf16)
    low = (value - high.astype(f32)).astype(bf16)
    return jnp.concatenate([high, low], -1)


def up(value):
    return pltpu.roll(value, NODES - 1, 1)


def down(value):
    return pltpu.roll(value, 1, 1)


def flat(value):
    return value.reshape(-1, value.shape[-1])


def node_rows(value):
    return value.reshape(-1, NODES, value.shape[-1])


def row_ids():
    return lax.broadcasted_iota(jnp.int32, (1, NODES, 128), 1)


def couple_slots(plane, filled):
    count, rows, width = plane.shape
    slots = rows // NODES
    parts = plane.reshape(count, slots, NODES, width)
    ids = row_ids()
    done = []
    for s in range(slots):
        here = parts[:, s]
        if s + 1 < slots:
            take = (ids == NODES - 1) & (s + 1 < filled)
            here = here + jnp.where(take, up(parts[:, s + 1]), 0.0)
        if s > 0:
            here = here + jnp.where(ids == 0, down(parts[:, s - 1]), 0.0)
            here = jnp.where(s < filled, here, 0.0)
        done.append(here[:, None])
    return jnp.concatenate(done, 1).reshape(plane.shape)


def elements(x_len, y_len, body):
    ey = y_len // NODES
    total = (x_len // NODES) * ey

    def step(e, carry):
        x0 = pl.multiple_of((e // ey) * NODES, NODES)
        y0 = pl.multiple_of((e % ey) * NODES, NODES)
        body(x0, y0)
        return carry

    lax.fori_loop(0, total, step, 0)


def edges_forward(h_ref, w_one, half_bias, filled, sum_ref, slope_ref):
    x_len, y_len, rows, width = h_ref.shape
    inner = row_ids() < NODES - 1

    def body(x0, y0):
        ys = pl.ds(y0, NODES)
        prev = None
        here = h_ref[x0, ys].astype(f32)
        for i in range(NODES):
            parts = []
            nxt = None
            if i < NODES - 1:
                nxt = h_ref[x0 + i + 1, ys].astype(f32)
                parts.append((nxt - here).astype(bf16))
            parts.append((here[1:] - here[:-1]).astype(bf16))
            cols = node_rows(here)
            parts.append((up(cols) - cols).reshape(here.shape).astype(bf16))
            half = dot(flat(jnp.concatenate(parts, 0)), w_one).reshape(-1, rows, width) + half_bias
            act, slope = silu_half(half)
            act = act.astype(bf16).astype(f32)
            at = 0
            total = prev
            prev = None
            if i < NODES - 1:
                prev = act[:NODES]
                total = -prev if total is None else total - prev
                slope_ref[0, x0 + i, ys] = slope[:NODES]
                at = NODES
            along_y = act[at : at + NODES - 1]
            slope_ref[1, x0 + i, pl.ds(y0, NODES - 1)] = slope[at : at + NODES - 1]
            at += NODES - 1
            along_z = jnp.where(inner, node_rows(act[at:]), 0.0)
            slope_z = jnp.where(inner, node_rows(slope[at:]), 0.0)
            slope_ref[2, x0 + i, ys] = slope_z.reshape(here.shape)
            total = total + (down(along_z) - along_z).reshape(here.shape)
            total = jnp.concatenate(
                [
                    total[:1] - along_y[:1],
                    total[1:-1] + (along_y[:-1] - along_y[1:]),
                    total[-1:] + along_y[-1:],
                ],
                0,
            )
            sum_ref[x0 + i, ys] = couple_slots(total, filled)
            here = nxt

    elements(x_len, y_len, body)


def couple_columns(sum_ref):
    x_len, y_len = sum_ref.shape[:2]
    for cut in range(NODES, x_len, NODES):
        both = sum_ref[cut - 1] + sum_ref[cut]
        sum_ref[cut - 1] = both
        sum_ref[cut] = both
    for cut in range(NODES, y_len, NODES):
        both = sum_ref[:, cut - 1] + sum_ref[:, cut]
        sum_ref[:, cut - 1] = both
        sum_ref[:, cut] = both


def pick_top(values, filled):
    top = values[0]
    for s in range(1, len(values)):
        top = jnp.where(filled == s + 1, values[s], top)
    return top


def write_faces(sc_ref, sum_ref, faces):
    x_len, y_len, rows, width = sum_ref.shape
    x_faces, (y_low, y_high, z_low, z_high) = faces[:-4], faces[-4:]
    if len(x_faces) == 1:
        x_faces[0][0] = sum_ref[sc_ref[1]]
    else:
        x_faces[0][0] = sum_ref[0]
        x_faces[1][0] = sum_ref[x_len - 1]
    y_low[...] = sum_ref[:, 0]
    y_high[...] = sum_ref[:, y_len - 1]
    z_low[...] = sum_ref[:, :, 0]
    tops = [sum_ref[:, :, s * NODES + NODES - 1] for s in range(rows // NODES)]
    z_high[...] = pick_top(tops, sc_ref[0])


def x_planes(sc_ref, received, x_len):
    if len(received) == 1:
        return [(sc_ref[1], received[0])]
    return [(0, received[0]), (x_len - 1, received[1])]


def add_halo(sc_ref, from_ref, halo, into_ref):
    x_len, y_len, rows, width = from_ref.shape
    x_recv, (y_low, y_high, z_low, z_high) = halo[:-4], halo[-4:]

    def copy(x, carry):
        into_ref[x] = from_ref[x]
        return carry

    lax.fori_loop(0, x_len, copy, 0)
    for place, ref in x_planes(sc_ref, x_recv, x_len):
        into_ref[place] += ref[0]
    into_ref[:, 0] += y_low[...]
    into_ref[:, y_len - 1] += y_high[...]
    into_ref[:, :, 0] += z_low[...]
    for s in range(rows // NODES):
        add = jnp.where(sc_ref[0] == s + 1, z_high[...], 0.0)
        into_ref[:, :, s * NODES + NODES - 1] += add


def fix_y_kernel(sc_ref, *refs):
    x_recv, (low, high, out_low, out_high) = refs[:-4], refs[-4:]
    x_len = low.shape[0]
    out_low[...] = low[...]
    out_high[...] = high[...]
    for place, ref in x_planes(sc_ref, x_recv, x_len):
        out_low[place] += ref[0, 0]
        out_high[place] += ref[0, ref.shape[1] - 1]


def fix_z_kernel(sc_ref, *refs):
    x_recv, (y_low, y_high, low, high, out_low, out_high) = refs[:-6], refs[-6:]
    x_len, y_len, width = low.shape
    slots = y_low.shape[1] // NODES
    filled = sc_ref[0]
    out_low[...] = low[...]
    out_high[...] = high[...]
    for place, ref in x_planes(sc_ref, x_recv, x_len):
        out_low[place] += ref[0, :, 0]
        out_high[place] += pick_top([ref[0, :, s * NODES + NODES - 1] for s in range(slots)], filled)
    for place, ref in ((0, y_low), (y_len - 1, y_high)):
        out_low[:, place] += ref[:, 0]
        out_high[:, place] += pick_top([ref[:, s * NODES + NODES - 1] for s in range(slots)], filled)


def node_forward(x, fx_ref, inv_ref, sum_ref, h_ref, w_two, w_in, half_bias):
    scaled = sum_ref[x] * (inv_ref[...] * fx_ref[x])
    pair = split_cols(flat(scaled))
    joined = jnp.concatenate([flat(h_ref[x]), dot(pair, w_two).astype(bf16)], -1)
    act, slope = silu_half(dot(joined, w_in) + half_bias)
    return pair[:, :128], act.astype(bf16), slope


def node_backward(x, fx_ref, inv_ref, filled, grad, feat, scaled, act, slope, w_out_t, w_in_t, sum_ref, base_ref, grads):
    out_acc, top_acc, low_acc, bias_acc = grads
    shape = sum_ref.shape[1:]
    dpn = (dot(grad, w_out_t) * slope).astype(bf16)
    out_acc[...] += dot_t(act, grad)
    both = dot_t(dpn, jnp.concatenate([feat, scaled], -1))
    top_acc[...] += both[:, :128]
    low_acc[...] += both[:, 128:]
    bias_acc[...] += jnp.sum(dpn.astype(f32).reshape(-1, NODES, 128), 0)
    dx = dot(dpn, w_in_t)
    base_ref[x] = (grad.astype(f32) + dx[:, :128]).reshape(shape)
    share = dx[:, 128:].reshape(shape) * (inv_ref[...] * fx_ref[x])
    sum_ref[x] = couple_slots(share, filled)


def edges_backward(q_ref, slope_ref, edge_ref, bias_acc):
    x_len, y_len, rows, width = q_ref.shape

    def body(x0, y0):
        ys = pl.ds(y0, NODES)
        prev = None
        here = q_ref[x0, ys]
        bias = jnp.zeros((NODES, width), f32)
        for i in range(NODES):
            total = prev
            prev = None
            nxt = None
            if i < NODES - 1:
                nxt = q_ref[x0 + i + 1, ys]
                prev = ((nxt - here) * slope_ref[0, x0 + i, ys]).astype(bf16).astype(f32)
                total = -prev if total is None else total - prev
                bias = bias + jnp.sum(node_rows(prev), 0)
            along_y = (here[1:] - here[:-1]) * slope_ref[1, x0 + i, pl.ds(y0, NODES - 1)]
            along_y = along_y.astype(bf16).astype(f32)
            cols = node_rows(here)
            along_z = (up(cols) - cols) * node_rows(slope_ref[2, x0 + i, ys])
            along_z = along_z.astype(bf16).astype(f32)
            bias = bias + jnp.sum(node_rows(along_y), 0) + jnp.sum(along_z, 0)
            total = total + (down(along_z) - along_z).reshape(here.shape)
            total = jnp.concatenate(
                [
                    total[:1] - along_y[:1],
                    total[1:-1] + (along_y[:-1] - along_y[1:]),
                    total[-1:] + along_y[-1:],
                ],
                0,
            )
            edge_ref[x0 + i, ys] = total
            here = nxt
        bias_acc[...] += bias

    elements(x_len, y_len, body)


def planes(count, body):
    def step(x, carry):
        body(x)
        return carry

    lax.fori_loop(0, count, step, 0)


def first_kernel(sc, h, w_one, edge_bias, sums, slopes, *faces):
    edges_forward(h, w_one[...], edge_bias[...], sc[0], sums, slopes)
    couple_columns(sums)
    write_faces(sc, sums, faces)


def middle_kernel(nx, sc, fx, inv, sums_in, h, w_two, w_in, node_bias, w_out, w_one, edge_bias, *refs):
    halo, refs = refs[: nx + 4], refs[nx + 4 :]
    scaled_ref, act_ref, slope_ref, next_ref, sums, slopes = refs[:6]
    faces, work = refs[6:-1], refs[-1]
    add_halo(sc, sums_in, halo, work)
    shape = h.shape[1:]

    def body(x):
        scaled, act, slope = node_forward(x, fx, inv, work, h, w_two[...], w_in[...], node_bias[...])
        scaled_ref[x] = scaled.reshape(shape)
        act_ref[x] = act.reshape(shape)
        slope_ref[x] = slope.reshape(shape)
        moved = flat(h[x]).astype(f32) + dot(act, w_out[...])
        next_ref[x] = moved.astype(bf16).reshape(shape)

    planes(h.shape[0], body)
    edges_forward(next_ref, w_one[...], edge_bias[...], sc[0], sums, slopes)
    couple_columns(sums)
    write_faces(sc, sums, faces)


def turn_kernel(nx, sc, fx, inv, sums_in, h, g_ref, w_two, w_in, node_bias, w_out_t, w_in_t, *refs):
    halo, refs = refs[: nx + 4], refs[nx + 4 :]
    base, sums, out_acc, top_acc, low_acc, bias_acc = refs[:6]
    faces, work = refs[6:-1], refs[-1]
    add_halo(sc, sums_in, halo, work)
    grads = (out_acc, top_acc, low_acc, bias_acc)
    for ref in grads:
        ref[...] = jnp.zeros_like(ref)
    slots = h.shape[2] // NODES
    live = (lax.broadcasted_iota(jnp.int32, (1, h.shape[2], 128), 1) < sc[0] * NODES).astype(f32)

    def body(x):
        scaled, act, slope = node_forward(x, fx, inv, work, h, w_two[...], w_in[...], node_bias[...])
        grad = flat((g_ref[x].astype(f32) * live).astype(bf16))
        node_backward(
            x, fx, inv, sc[0], grad, flat(h[x]), scaled, act, slope, w_out_t[...], w_in_t[...], sums, base, grads
        )

    planes(h.shape[0], body)
    couple_columns(sums)
    write_faces(sc, sums, faces)


def back_to_state(sc, sums_in, halo, h, base, slopes, w_two_t, w_one_t, work, edge_acc, bias_acc, use):
    add_halo(sc, sums_in, halo, work)
    edge_acc[...] = jnp.zeros_like(edge_acc)
    bias_acc[...] = jnp.zeros_like(bias_acc)
    shape = h.shape[1:]

    def to_q(x):
        work[x] = dot(split_cols(flat(work[x])), w_two_t[...]).reshape(shape)

    planes(h.shape[0], to_q)
    edges_backward(work, slopes, work, bias_acc)

    def body(x):
        pair = split_cols(flat(work[x]))
        both = dot_t(flat(h[x]), pair)
        edge_acc[...] += both[:, :128] + both[:, 128:]
        use(x, (flat(base[x]) + dot(pair, w_one_t[...])).astype(bf16))

    planes(h.shape[0], body)


def join_kernel(
    nx, sc, fx, inv, sums_in, h, base_in, slopes, w_two_t, w_one_t,
    h0, scaled0, act0, slope0, w_out_t, w_in_t, *refs
):
    halo, refs = refs[: nx + 4], refs[nx + 4 :]
    base, sums, edge_acc, edge_bias_acc, out_acc, top_acc, low_acc, bias_acc = refs[:8]
    faces, work = refs[8:-1], refs[-1]
    grads = (out_acc, top_acc, low_acc, bias_acc)
    for ref in grads:
        ref[...] = jnp.zeros_like(ref)

    def use(x, grad):
        node_backward(
            x, fx, inv, sc[0], grad, flat(h0[x]), flat(scaled0[x]), flat(act0[x]), flat(slope0[x]),
            w_out_t[...], w_in_t[...], sums, base, grads,
        )

    back_to_state(sc, sums_in, halo, h, base_in, slopes, w_two_t, w_one_t, work, edge_acc, edge_bias_acc, use)
    couple_columns(sums)
    write_faces(sc, sums, faces)


def last_kernel(nx, sc, sums_in, h, base_in, slopes, w_two_t, w_one_t, *refs):
    halo, refs = refs[: nx + 4], refs[nx + 4 :]
    grad_ref, edge_acc, edge_bias_acc, work = refs
    shape = h.shape[1:]

    def use(x, grad):
        grad_ref[x] = grad.reshape(shape)

    back_to_state(sc, sums_in, halo, h, base_in, slopes, w_two_t, w_one_t, work, edge_acc, edge_bias_acc, use)


def call(kernel, name, inputs, smem, outs, scratch=(), flops=0):
    total = sum(math.prod(o.shape) * o.dtype.itemsize for o in outs)
    total += sum(math.prod(i.shape) * i.dtype.itemsize for i in inputs)
    return pl.pallas_call(
        kernel,
        name=name,
        out_shape=tuple(outs),
        in_specs=[SM] * smem + [VM] * (len(inputs) - smem),
        out_specs=tuple([VM] * len(outs)),
        scratch_shapes=list(scratch),
        compiler_params=pltpu.CompilerParams(vmem_limit_bytes=40 * 1024 * 1024),
        cost_estimate=pl.CostEstimate(flops=flops, bytes_accessed=total, transcendentals=0),
    )(*inputs)


def on_device(state, cotangent, counts, edge_weights, node_in, node_out, biases):
    x_len, y_len, slots, nodes, width = state.shape
    rows = slots * nodes
    grid = (x_len, y_len, rows, width)
    size_x, size_y, size_z = (lax.axis_size(a) for a in ("gx", "gy", "gz"))
    at_x, at_y, at_z = (lax.axis_index(a) for a in ("gx", "gy", "gz"))
    filled = counts[0]
    h0 = state.reshape(grid)
    g2 = cotangent.reshape(grid)

    def inverse(length, position, size):
        ids = jnp.arange(length, dtype=jnp.int32)
        end = ids + position * length
        shared = ((ids % nodes == 0) & (end > 0)) | ((ids % nodes == nodes - 1) & (end < length * size - 1))
        return jnp.where(shared, 0.5, 1.0).astype(f32)

    fx = inverse(x_len, at_x, size_x)
    inv_y = inverse(y_len, at_y, size_y)
    ids = jnp.arange(rows, dtype=jnp.int32)
    low = (ids % nodes == 0) & ((ids >= nodes) | (at_z > 0))
    high = (ids % nodes == nodes - 1) & ((ids < (filled - 1) * nodes) | (at_z < size_z - 1))
    inv_z = jnp.where(low | high, 0.5, 1.0).astype(f32)
    inv = jnp.broadcast_to((inv_y[:, None] * inv_z[None, :])[:, :, None], (y_len, rows, width))
    single = size_x == 2
    sc = jnp.stack([filled, jnp.where(at_x == 0, x_len - 1, 0).astype(jnp.int32)])
    nx = 1 if single else 2

    def sds(shape, kind=f32):
        return jax.ShapeDtypeStruct(shape, kind)

    face_x = sds((1, y_len, rows, width))
    face_y = sds((x_len, rows, width))
    face_z = sds((x_len, y_len, width))
    face_outs = [face_x] * nx + [face_y] * 2 + [face_z] * 2
    full = sds(grid)
    full16 = sds(grid, bf16)
    full3 = sds((3,) + grid)
    square = sds((width, width))
    strip = sds((NODES, width))
    work = pltpu.VMEM(grid, f32)
    matmul = 2 * math.prod(grid) * width

    def trade(low_face, high_face, axis):
        size = lax.axis_size(axis)
        below = lax.ppermute(high_face, axis, [(i, i + 1) for i in range(size - 1)])
        above = lax.ppermute(low_face, axis, [(i + 1, i) for i in range(size - 1)])
        return below, above

    def exchange(faces):
        x_faces, (y_low, y_high, z_low, z_high) = faces[:nx], faces[nx:]
        if single:
            got_x = (lax.ppermute(x_faces[0], "gx", [(0, 1), (1, 0)]),)
        else:
            got_x = trade(x_faces[0], x_faces[1], "gx")
        y_low, y_high = call(fix_y_kernel, "fix_y", (sc, *got_x, y_low, y_high), 1, [face_y] * 2)
        got_y = trade(y_low, y_high, "gy")
        z_low, z_high = call(fix_z_kernel, "fix_z", (sc, *got_x, *got_y, z_low, z_high), 1, [face_z] * 2)
        got_z = trade(z_low, z_high, "gz")
        return (*got_x, *got_y, *got_z)

    half = jnp.bfloat16(0.5)
    w_one = [edge_weights[l, 0] * half for l in range(2)]
    w_two = [jnp.concatenate([edge_weights[l, 1]] * 2, 0) for l in range(2)]
    w_one_t = [jnp.concatenate([edge_weights[l, 0].T] * 2, 0) for l in range(2)]
    w_two_t = [jnp.concatenate([edge_weights[l, 1].T] * 2, 0) for l in range(2)]
    w_in = [node_in[l] * half for l in range(2)]
    w_in_t = [node_in[l].T for l in range(2)]
    w_out_t = [node_out[l].T for l in range(2)]
    edge_bias = [0.5 * biases[l, 0][None] for l in range(2)]
    node_bias = [0.5 * biases[l, 1][None] for l in range(2)]

    sums, slopes0, *faces = call(
        first_kernel, "edges0", (sc, h0, w_one[0], edge_bias[0]), 1, [full, full3] + face_outs, flops=3 * matmul
    )
    halo = exchange(faces)
    scaled0, act0, slope0, h1, sums, slopes1, *faces = call(
        functools.partial(middle_kernel, nx),
        "nodes0_edges1",
        (sc, fx, inv, sums, h0, w_two[0], w_in[0], node_bias[0], node_out[0], w_one[1], edge_bias[1], *halo),
        2,
        [full16, full16, full, full16, full, full3] + face_outs,
        [work],
        flops=8 * matmul,
    )
    halo = exchange(faces)
    base, sums, out1, top1, low1, nb1, *faces = call(
        functools.partial(turn_kernel, nx),
        "nodes1_back",
        (sc, fx, inv, sums, h1, g2, w_two[1], w_in[1], node_bias[1], w_out_t[1], w_in_t[1], *halo),
        2,
        [full, full, square, square, square, strip] + face_outs,
        [work],
        flops=10 * matmul,
    )
    halo = exchange(faces)
    base, sums, edge1, eb1, out0, top0, low0, nb0, *faces = call(
        functools.partial(join_kernel, nx),
        "edges1_back_nodes0_back",
        (
            sc, fx, inv, sums, h1, base, slopes1, w_two_t[1], w_one_t[1],
            h0, scaled0, act0, slope0, w_out_t[0], w_in_t[0], *halo,
        ),
        2,
        [full, full, square, strip, square, square, square, strip] + face_outs,
        [work],
        flops=12 * matmul,
    )
    halo = exchange(faces)
    grad0, edge0, eb0 = call(
        functools.partial(last_kernel, nx),
        "edges0_back",
        (sc, sums, h0, base, slopes0, w_two_t[0], w_one_t[0], *halo),
        1,
        [full16, square, strip],
        [work],
        flops=6 * matmul,
    )

    def reduce_all(value):
        for axis in ("gx", "gy", "gz"):
            size = lax.axis_size(axis)
            hop = 1
            while hop < size:
                value = value + lax.ppermute(value, axis, [(i, i ^ hop) for i in range(size)])
                hop *= 2
        return value

    summed1 = reduce_all(jnp.concatenate([out1, top1, low1, nb1], 0))
    summed0 = reduce_all(jnp.concatenate([edge1, out0, top0, low0, eb1, nb0], 0))
    last = reduce_all(jnp.concatenate([edge0, eb0], 0))
    layers_all = 3 * slots * size_z // 4
    nodes_all = x_len * size_x * y_len * size_y * layers_all * nodes
    scale = 1.0 / math.sqrt(nodes_all)

    def block(value, index):
        return value[index * width : (index + 1) * width] * scale

    def tail(value, index):
        start = value.shape[0] - (index + 1) * NODES
        return jnp.sum(value[start : start + NODES], 0) * scale

    out_grads = (block(summed0, 1), block(summed1, 0))
    tops = (block(summed0, 2).T, block(summed1, 1).T)
    lows_t = (block(summed0, 3), block(summed1, 2))
    firsts = (block(last, 0), block(summed0, 0))
    edge_biases = (tail(last, 0), tail(summed0, 1))
    node_biases = (tail(summed0, 0), tail(summed1, 0))

    def exact(left, right, dims):
        return lax.dot_general(
            left, right.astype(f32), (dims, ((), ())), precision=lax.Precision.HIGHEST, preferred_element_type=f32
        )

    edge_grads = jnp.stack(
        [jnp.stack([firsts[l], exact(lows_t[l], node_in[l, width:], ((0,), (1,)))]) for l in range(2)]
    )
    in_grads = jnp.stack(
        [
            jnp.concatenate([tops[l], exact(lows_t[l], edge_weights[l, 1], ((1,), (0,))).T], 0)
            for l in range(2)
        ]
    )
    bias_grads = jnp.stack([jnp.stack([edge_biases[l], node_biases[l]]) for l in range(2)])
    return grad0.reshape(state.shape), edge_grads, in_grads, jnp.stack(out_grads), bias_grads


def solution(mesh):
    return jax.shard_map(
        on_device,
        mesh=mesh,
        in_specs=(
            P("gx", "gy", "gz", None, None),
            P("gx", "gy", "gz", None, None),
            P("gz"),
            P(),
            P(),
            P(),
            P(),
        ),
        out_specs=(P("gx", "gy", "gz", None, None), P(), P(), P(), P()),
        check_vma=False,
    )
```

profile of v0, /device:TPU:0, one launch (start us, length us, event | category | flops | bytes accessed | tf_op | source)
XLA Modules:
  0.0 254.5 jit_solution(8439702463924046916)
XLA Ops:
  6.2 4.8 %edges0.1 = (f32[16,16,16,128]{3,2,1,0:T(8,128)S(1)}, f32[3,16,16,16,128]{4,3,2,1,0:T(8,128)S(1)}, f32[1,16,16,128]{3,2,1,0:T(8,128)S(1)}, f32[16,16,128]{2,1,0:...) custom-call(s32[2]{0:T(128)S(1)} %pad_add_fusion.sc.sc_ref, ...), custom_call_target="tpu_custom_call" | custom-call | flops 402653184 | bytes 10125832 | tf_op jit(solution)/shard_map/edges0/pallas_call | solution.py:399
  11.0 2.6 %copy-done.2 = f32[3,16,16,16,128]{4,3,2,1,0:T(8,128)} copy-done((f32[3,16,16,16,128]{4,3,2,1,0:T(8,128)}, f32[3,16,16,16,128]{4,3,2,1,0:T(8,128)S(1)}, u32[]{:S(2)}) %copy-start.2) | copy-done | bytes 6291480
  15.0 2.9 %collective-permute-start = (f32[1,16,16,128]{3,2,1,0:T(8,128)S(1)}, f32[1,16,16,128]{3,2,1,0:T(8,128)S(1)}, u32[]{:S(2)}, u32[]{:S(2)}) collective-permute-start(f32[1,16,16,128]{3,2,1,0:T(8,128)S(1)} %get-tuple-element.67), channel_id=1, source_target_pairs={{0,16},{16,0},{1,17},{17,1},{2,18},{18,2},{3,19},{19,3},{4,20},{20... | collective-permute-start | bytes 393224 | tf_op jit(solution)/shard_map/ppermute | solution.py:462
  19.6 1.8 collective-permute-done.refs_0_
  24.7 3.9 %collective-permute-done.2.refs_2_ = f32[16,16,128]{2,1,0:T(8,128)S(1)} collective-permute-done((f32[16,16,128]{2,1,0:T(8,128)S(1)}, f32[16,16,128]{2,1,0:T(8,128)S(1)}, u32[]{:S(2)}, u32[]{:S(2)}) %collective-permute-start.2) | collective-permute-done | bytes 131104 | tf_op jit(solution)/shard_map/ppermute | solution.py:456
  29.8 3.5 %collective-permute-start.3 = (f32[16,16,128]{2,1,0:T(8,128)S(1)}, f32[16,16,128]{2,1,0:T(8,128)S(1)}, u32[]{:S(2)}, u32[]{:S(2)}) collective-permute-start(f32[16,16,128]{2,1,0:T(8,128)S(1)} %get-tuple-element.74), channel_id=1, source_target_pairs={{0,1},{1,2},{2,3},{4,5},{5,6},{6,7},{8,9},{9,10},{10,11},{12,13},{... | collective-permute-start | bytes 393224 | tf_op jit(solution)/shard_map/ppermute | solution.py:455
  36.2 3.9 %collective-permute-done.4.refs_4_ = f32[16,16,128]{2,1,0:T(8,128)S(1)} collective-permute-done((f32[16,16,128]{2,1,0:T(8,128)S(1)}, f32[16,16,128]{2,1,0:T(8,128)S(1)}, u32[]{:S(2)}, u32[]{:S(2)}) %collective-permute-start.4) | collective-permute-done | bytes 131104 | tf_op jit(solution)/shard_map/ppermute | solution.py:456
  41.0 1.6 copy-done.9
  49.1 15.5 %nodes0_edges1.1 = (bf16[16,16,16,128]{3,2,1,0:T(8,128)(2,1)S(1)}, bf16[16,16,16,128]{3,2,1,0:T(8,128)(2,1)S(1)}, f32[16,16,16,128]{3,2,1,0:T(8,128)S(1)}, bf16[...) custom-call(s32[2]{0:T(128)S(1)} %pad_add_fusion.sc.sc_ref, ...), custom_call_target="tpu_custom_call" | custom-call | flops 1073741824 | bytes 18416712 | tf_op jit(solution)/shard_map/nodes0_edges1/pallas_call | solution.py:399
  68.3 1.5 collective-permute-start.5
  69.8 3.7 %collective-permute-done.5.refs_0_ = f32[1,16,16,128]{3,2,1,0:T(8,128)S(1)} collective-permute-done((f32[1,16,16,128]{3,2,1,0:T(8,128)S(1)}, f32[1,16,16,128]{3,2,1,0:T(8,128)S(1)}, u32[]{:S(2)}, u32[]{:S(2)}) %collective-permute-start.5) | collective-permute-done | bytes 131104 | tf_op jit(solution)/shard_map/ppermute | solution.py:462
  74.7 3.5 %collective-permute-start.6 = (f32[16,16,128]{2,1,0:T(8,128)}, f32[16,16,128]{2,1,0:T(8,128)}, u32[]{:S(2)}, u32[]{:S(2)}) collective-permute-start(f32[16,16,128]{2,1,0:T(8,128)} %get-tuple-element.81), channel_id=1, source_target_pairs={{0,4},{4,8},{8,12},{1,5},{5,9},{9,13},{2,6},{6,10},{10,14},{3,7},{... | collective-permute-start | bytes 393224 | tf_op jit(solution)/shard_map/ppermute | solution.py:455
  81.1 1.6 copy.25.w_two
  85.4 1.7 fix_z.5
  87.2 4.1 %collective-permute-start.8 = (f32[16,16,128]{2,1,0:T(8,128)}, f32[16,16,128]{2,1,0:T(8,128)}, u32[]{:S(2)}, u32[]{:S(2)}) collective-permute-start(f32[16,16,128]{2,1,0:T(8,128)} %get-tuple-element.85), channel_id=1, source_target_pairs={{0,1},{1,2},{2,3},{4,5},{5,6},{6,7},{8,9},{9,10},{10,11},{12,13},{... | collective-permute-start | bytes 393224 | tf_op jit(solution)/shard_map/ppermute | solution.py:455
  93.2 1.6 copy.26.w_in
  94.8 1.5 copy.39
  96.3 2.2 collective-permute-done.9.refs_4_
  98.5 1.6 copy-done.11
  103.7 12.0 %nodes1_back.1 = (f32[16,16,16,128]{3,2,1,0:T(8,128)S(1)}, f32[16,16,16,128]{3,2,1,0:T(8,128)S(1)}, f32[128,128]{1,0:T(8,128)S(1)}, f32[128,128]{1,0:T(8,128)S(1...) custom-call(s32[2]{0:T(128)S(1)} %pad_add_fusion.sc.sc_ref, ...), custom_call_target="tpu_custom_call" | custom-call | flops 1342177280 | bytes 10261064 | tf_op jit(solution)/shard_map/nodes1_back/pallas_call | solution.py:399
  118.4 1.5 collective-permute-start.10
  121.8 2.6 %collective-permute-done.10.refs_0_ = f32[1,16,16,128]{3,2,1,0:T(8,128)S(1)} collective-permute-done((f32[1,16,16,128]{3,2,1,0:T(8,128)S(1)}, f32[1,16,16,128]{3,2,1,0:T(8,128)S(1)}, u32[]{:S(2)}, u32[]{:S(2)}) %collective-permute-start.10) | collective-permute-done | bytes 131104 | tf_op jit(solution)/shard_map/ppermute | solution.py:462
  125.0 2.1 collective-permute-start.11
  129.0 1.5 collective-permute-start.30
  130.5 2.0 collective-permute-done.12.refs_2_
  134.5 3.5 %collective-permute-start.13 = (f32[16,16,128]{2,1,0:T(8,128)}, f32[16,16,128]{2,1,0:T(8,128)}, u32[]{:S(2)}, u32[]{:S(2)}) collective-permute-start(f32[16,16,128]{2,1,0:T(8,128)} %get-tuple-element.100), channel_id=1, source_target_pairs={{0,1},{1,2},{2,3},{4,5},{5,6},{6,7},{8,9},{9,10},{10,11},{12,13},{... | collective-permute-start | bytes 393224 | tf_op jit(solution)/shard_map/ppermute | solution.py:455
  142.0 3.3 %collective-permute-start.31 = (f32[392,128]{1,0:T(8,128)S(1)}, f32[392,128]{1,0:T(8,128)S(1)}, u32[]{:S(2)}, u32[]{:S(2)}) collective-permute-start(f32[392,128]{1,0:T(8,128)S(1)} %add.112), channel_id=1, source_target_pairs={{0,4},{4,0},{8,12},{12,8},{1,5},{5,1},{9,13},{13,9},{2,6},{6,2},{1... | collective-permute-start | bytes 602120 | tf_op jit(solution)/shard_map/ppermute | solution.py:534
  145.4 1.7 copy-done.5
  147.1 1.7 copy-done.7
  151.9 17.9 %edges1_back_nodes0_back.1 = (f32[16,16,16,128]{3,2,1,0:T(8,128)S(1)}, f32[16,16,16,128]{3,2,1,0:T(8,128)S(1)}, f32[128,128]{1,0:T(8,128)S(1)}, f32[8,128]{1,0:T...) custom-call(s32[2]{0:T(128)S(1)} %pad_add_fusion.sc.sc_ref, ...), custom_call_target="tpu_custom_call" | custom-call | flops 1610612736 | bytes 22913096 | tf_op jit(solution)/shard_map/edges1_back_nodes0_back/pallas_call | solution.py:399
  172.6 1.5 collective-permute-start.15
  174.7 3.3 %collective-permute-done.15.refs_0_ = f32[1,16,16,128]{3,2,1,0:T(8,128)S(1)} collective-permute-done((f32[1,16,16,128]{3,2,1,0:T(8,128)S(1)}, f32[1,16,16,128]{3,2,1,0:T(8,128)S(1)}, u32[]{:S(2)}, u32[]{:S(2)}) %collective-permute-start.15) | collective-permute-done | bytes 131104 | tf_op jit(solution)/shard_map/ppermute | solution.py:462
  178.6 3.8 %collective-permute-start.16 = (f32[16,16,128]{2,1,0:T(8,128)S(1)}, f32[16,16,128]{2,1,0:T(8,128)S(1)}, u32[]{:S(2)}, u32[]{:S(2)}) collective-permute-start(f32[16,16,128]{2,1,0:T(8,128)S(1)} %get-tuple-element.108), channel_id=1, source_target_pairs={{0,4},{4,8},{8,12},{1,5},{5,9},{9,13},{2,6},{6,10},{10,14},{3,7},{... | collective-permute-start | bytes 393224 | tf_op jit(solution)/shard_map/ppermute | solution.py:455
  183.8 3.9 %collective-permute-start.32 = (f32[392,128]{1,0:T(8,128)S(1)}, f32[392,128]{1,0:T(8,128)S(1)}, u32[]{:S(2)}, u32[]{:S(2)}) collective-permute-start(f32[392,128]{1,0:T(8,128)S(1)} %add.113), channel_id=1, source_target_pairs={{0,8},{4,12},{8,0},{12,4},{1,9},{5,13},{9,1},{13,5},{2,10},{6,14},... | collective-permute-start | bytes 602120 | tf_op jit(solution)/shard_map/ppermute | solution.py:534
  188.3 2.3 collective-permute-start.18
  190.6 1.5 collective-permute-start.19
  192.1 2.3 collective-permute-done.32
  194.9 3.2 %collective-permute-start.26 = (f32[528,128]{1,0:T(8,128)S(1)}, f32[528,128]{1,0:T(8,128)S(1)}, u32[]{:S(2)}, u32[]{:S(2)}) collective-permute-start(f32[528,128]{1,0:T(8,128)S(1)} %add.107), channel_id=1, source_target_pairs={{0,4},{4,0},{8,12},{12,8},{1,5},{5,1},{9,13},{13,9},{2,6},{6,2},{1... | collective-permute-start | bytes 811016 | tf_op jit(solution)/shard_map/ppermute | solution.py:534
  198.1 1.6 copy-done.15
  199.7 10.0 %edges0_back.1 = (bf16[16,16,16,128]{3,2,1,0:T(8,128)(2,1)}, f32[128,128]{1,0:T(8,128)S(1)}, f32[8,128]{1,0:T(8,128)S(1)}) custom-call(s32[2]{0:T(128)S(1)} %pad_add_fusion.sc.sc_ref, f32[16,16,16,128]{3,2,1,0:T(8,128)S(1)} %copy-done.15, bf16[16,16,16,128]{3,2,1,0:T(8,128)(2,1)S(1)} %bitcast.98, f32[16,16,16,128]{3,2,1,0:T(8,128)S(1)} %copy-done.13, ...), custom_call_target="tpu_custom_call" | custom-call | flops 805306368 | bytes 13438984 | tf_op jit(solution)/shard_map/edges0_back/pallas_call | solution.py:399
  209.6 1.6 collective-permute-start.20
  211.8 2.2 collective-permute-done.20
  214.0 2.7 %collective-permute-start.21 = (f32[136,128]{1,0:T(8,128)S(1)}, f32[136,128]{1,0:T(8,128)S(1)}, u32[]{:S(2)}, u32[]{:S(2)}) collective-permute-start(f32[136,128]{1,0:T(8,128)S(1)} %add.102), channel_id=1, source_target_pairs={{0,4},{4,0},{8,12},{12,8},{1,5},{5,1},{9,13},{13,9},{2,6},{6,2},{1... | collective-permute-start | bytes 208904 | tf_op jit(solution)/shard_map/ppermute | solution.py:534
  219.9 2.9 %collective-permute-done.22 = f32[136,128]{1,0:T(8,128)S(1)} collective-permute-done((f32[136,128]{1,0:T(8,128)S(1)}, f32[136,128]{1,0:T(8,128)S(1)}, u32[]{:S(2)}, u32[]{:S(2)}) %collective-permute-start.22) | collective-permute-done | bytes 69664 | tf_op jit(solution)/shard_map/ppermute | solution.py:534
  224.3 3.7 %collective-permute-done.27 = f32[528,128]{1,0:T(8,128)S(1)} collective-permute-done((f32[528,128]{1,0:T(8,128)S(1)}, f32[528,128]{1,0:T(8,128)S(1)}, u32[]{:S(2)}, u32[]{:S(2)}) %collective-permute-start.27) | collective-permute-done | bytes 270368 | tf_op jit(solution)/shard_map/ppermute | solution.py:534
  229.0 6.4 %collective-permute-done.24 = f32[136,128]{1,0:T(8,128)S(1)} collective-permute-done((f32[136,128]{1,0:T(8,128)S(1)}, f32[136,128]{1,0:T(8,128)S(1)}, u32[]{:S(2)}, u32[]{:S(2)}) %collective-permute-start.24) | collective-permute-done | bytes 69664 | tf_op jit(solution)/shard_map/ppermute | solution.py:534
  235.4 2.2 collective-permute-done.28
  238.9 12.2 %collective-permute-done.29 = f32[528,128]{1,0:T(8,128)S(1)} collective-permute-done((f32[528,128]{1,0:T(8,128)S(1)}, f32[528,128]{1,0:T(8,128)S(1)}, u32[]{:S(2)}, u32[]{:S(2)}) %collective-permute-start.29) | collective-permute-done | bytes 270368 | tf_op jit(solution)/shard_map/ppermute | solution.py:534
  (227 shorter events, 72.0 us)
Async XLA Ops:
  0.6 17.4 %copy-start.43 = (bf16[2,256,128]{2,1,0:T(8,128)(2,1)S(1)}, bf16[2,256,128]{2,1,0:T(8,128)(2,1)}, u32[]{:S(2)}) copy-start(bf16[2,256,128]{2,1,0:T(8,128)(2,1)} %param.11) | copy-start | bytes 393220
  0.6 18.2 %copy-start.51 = (bf16[2,128,128]{2,1,0:T(8,128)(2,1)S(1)}, bf16[2,128,128]{2,1,0:T(8,128)(2,1)}, u32[]{:S(2)}) copy-start(bf16[2,128,128]{2,1,0:T(8,128)(2,1)} %param.12) | copy-start | bytes 196612
  6.2 34.7 %copy-start.1 = (bf16[16,16,2,8,128]{4,3,2,1,0:T(8,128)(2,1)S(1)}, bf16[16,16,2,8,128]{4,3,2,1,0:T(8,128)(2,1)}, u32[]{:S(2)}) copy-start(bf16[16,16,2,8,128]{4,3,2,1,0:T(8,128)(2,1)} %param.7) | copy-start | bytes 3145732
  15.0 6.4 %collective-permute-start = (f32[1,16,16,128]{3,2,1,0:T(8,128)S(1)}, f32[1,16,16,128]{3,2,1,0:T(8,128)S(1)}, u32[]{:S(2)}, u32[]{:S(2)}) collective-permute-start(f32[1,16,16,128]{3,2,1,0:T(8,128)S(1)} %get-tuple-element.67), channel_id=1, source_target_pairs={{0,16},{16,0},{1,17},{17,1},{2,18},{18,2},{3,19},{19,3},{4,20},{20... | collective-permute-start | bytes 393224 | tf_op jit(solution)/shard_map/ppermute | solution.py:462
  19.6 15.0 %copy-start.45 = (bf16[1,1,128,128]{2,3,1,0:T(8,128)(2,1)}, bf16[1,1,128,128]{2,3,1,0:T(8,128)(2,1)S(1)}, u32[]{:S(2)}) copy-start(bf16[1,1,128,128]{2,3,1,0:T(8,128)(2,1)S(1)} %copy.33) | copy-start | bytes 98308
  22.0 2.7 %collective-permute-start.1 = (f32[16,16,128]{2,1,0:T(8,128)S(1)}, f32[16,16,128]{2,1,0:T(8,128)S(1)}, u32[]{:S(2)}, u32[]{:S(2)}) collective-permute-start(f32[16,16,128]{2,1,0:T(8,128)S(1)} %get-tuple-element.70), channel_id=1, source_target_pairs={{0,4},{4,8},{8,12},{1,5},{5,9},{9,13},{2,6},{6,10},{10,14},{3,7},{... | collective-permute-start | bytes 393224 | tf_op jit(solution)/shard_map/ppermute | solution.py:455
  23.3 5.2 %collective-permute-start.2 = (f32[16,16,128]{2,1,0:T(8,128)S(1)}, f32[16,16,128]{2,1,0:T(8,128)S(1)}, u32[]{:S(2)}, u32[]{:S(2)}) collective-permute-start(f32[16,16,128]{2,1,0:T(8,128)S(1)} %get-tuple-element.71), channel_id=1, source_target_pairs={{4,0},{8,4},{12,8},{5,1},{9,5},{13,9},{6,2},{10,6},{14,10},{7,3},{... | collective-permute-start | bytes 393224 | tf_op jit(solution)/shard_map/ppermute | solution.py:456
  29.8 6.4 %collective-permute-start.3 = (f32[16,16,128]{2,1,0:T(8,128)S(1)}, f32[16,16,128]{2,1,0:T(8,128)S(1)}, u32[]{:S(2)}, u32[]{:S(2)}) collective-permute-start(f32[16,16,128]{2,1,0:T(8,128)S(1)} %get-tuple-element.74), channel_id=1, source_target_pairs={{0,1},{1,2},{2,3},{4,5},{5,6},{6,7},{8,9},{9,10},{10,11},{12,13},{... | collective-permute-start | bytes 393224 | tf_op jit(solution)/shard_map/ppermute | solution.py:455
  33.3 6.9 %collective-permute-start.4 = (f32[16,16,128]{2,1,0:T(8,128)S(1)}, f32[16,16,128]{2,1,0:T(8,128)S(1)}, u32[]{:S(2)}, u32[]{:S(2)}) collective-permute-start(f32[16,16,128]{2,1,0:T(8,128)S(1)} %get-tuple-element.75), channel_id=1, source_target_pairs={{1,0},{2,1},{3,2},{5,4},{6,5},{7,6},{9,8},{10,9},{11,10},{13,12},{... | collective-permute-start | bytes 393224 | tf_op jit(solution)/shard_map/ppermute | solution.py:456
  68.3 6.5 %copy-start.37 = (f32[16,16,128]{2,1,0:T(8,128)}, f32[16,16,128]{2,1,0:T(8,128)S(1)}, u32[]{:S(2)}) copy-start(f32[16,16,128]{2,1,0:T(8,128)S(1)} %get-tuple-element.83.refs_3_) | copy-start | bytes 393220
  68.3 6.5 %copy-start.39 = (f32[16,16,128]{2,1,0:T(8,128)}, f32[16,16,128]{2,1,0:T(8,128)S(1)}, u32[]{:S(2)}) copy-start(f32[16,16,128]{2,1,0:T(8,128)S(1)} %get-tuple-element.84.refs_4_) | copy-start | bytes 393220
  68.3 5.2 %collective-permute-start.5 = (f32[1,16,16,128]{3,2,1,0:T(8,128)S(1)}, f32[1,16,16,128]{3,2,1,0:T(8,128)S(1)}, u32[]{:S(2)}, u32[]{:S(2)}) collective-permute-start(f32[1,16,16,128]{3,2,1,0:T(8,128)S(1)} %get-tuple-element.78), channel_id=1, source_target_pairs={{0,16},{16,0},{1,17},{17,1},{2,18},{18,2},{3,19},{19,3},{4,20},{20... | collective-permute-start | bytes 393224 | tf_op jit(solution)/shard_map/ppermute | solution.py:462
  74.7 8.9 %collective-permute-start.6 = (f32[16,16,128]{2,1,0:T(8,128)}, f32[16,16,128]{2,1,0:T(8,128)}, u32[]{:S(2)}, u32[]{:S(2)}) collective-permute-start(f32[16,16,128]{2,1,0:T(8,128)} %get-tuple-element.81), channel_id=1, source_target_pairs={{0,4},{4,8},{8,12},{1,5},{5,9},{9,13},{2,6},{6,10},{10,14},{3,7},{... | collective-permute-start | bytes 393224 | tf_op jit(solution)/shard_map/ppermute | solution.py:455
  78.3 5.3 %collective-permute-start.7 = (f32[16,16,128]{2,1,0:T(8,128)}, f32[16,16,128]{2,1,0:T(8,128)}, u32[]{:S(2)}, u32[]{:S(2)}) collective-permute-start(f32[16,16,128]{2,1,0:T(8,128)} %get-tuple-element.82), channel_id=1, source_target_pairs={{4,0},{8,4},{12,8},{5,1},{9,5},{13,9},{6,2},{10,6},{14,10},{7,3},{... | collective-permute-start | bytes 393224 | tf_op jit(solution)/shard_map/ppermute | solution.py:456
  87.2 9.1 %collective-permute-start.8 = (f32[16,16,128]{2,1,0:T(8,128)}, f32[16,16,128]{2,1,0:T(8,128)}, u32[]{:S(2)}, u32[]{:S(2)}) collective-permute-start(f32[16,16,128]{2,1,0:T(8,128)} %get-tuple-element.85), channel_id=1, source_target_pairs={{0,1},{1,2},{2,3},{4,5},{5,6},{6,7},{8,9},{9,10},{10,11},{12,13},{... | collective-permute-start | bytes 393224 | tf_op jit(solution)/shard_map/ppermute | solution.py:455
  91.3 7.2 %collective-permute-start.9 = (f32[16,16,128]{2,1,0:T(8,128)}, f32[16,16,128]{2,1,0:T(8,128)}, u32[]{:S(2)}, u32[]{:S(2)}) collective-permute-start(f32[16,16,128]{2,1,0:T(8,128)} %get-tuple-element.86), channel_id=1, source_target_pairs={{1,0},{2,1},{3,2},{5,4},{6,5},{7,6},{9,8},{10,9},{11,10},{13,12},{... | collective-permute-start | bytes 393224 | tf_op jit(solution)/shard_map/ppermute | solution.py:456
  118.4 6.0 %collective-permute-start.10 = (f32[1,16,16,128]{3,2,1,0:T(8,128)S(1)}, f32[1,16,16,128]{3,2,1,0:T(8,128)S(1)}, u32[]{:S(2)}, u32[]{:S(2)}) collective-permute-start(f32[1,16,16,128]{3,2,1,0:T(8,128)S(1)} %get-tuple-element.93), channel_id=1, source_target_pairs={{0,16},{16,0},{1,17},{17,1},{2,18},{18,2},{3,19},{19,3},{4,20},{20... | collective-permute-start | bytes 393224 | tf_op jit(solution)/shard_map/ppermute | solution.py:462
  125.0 5.5 %collective-permute-start.11 = (f32[16,16,128]{2,1,0:T(8,128)S(1)}, f32[16,16,128]{2,1,0:T(8,128)S(1)}, u32[]{:S(2)}, u32[]{:S(2)}) collective-permute-start(f32[16,16,128]{2,1,0:T(8,128)S(1)} %get-tuple-element.96), channel_id=1, source_target_pairs={{0,4},{4,8},{8,12},{1,5},{5,9},{9,13},{2,6},{6,10},{10,14},{3,7},{... | collective-permute-start | bytes 393224 | tf_op jit(solution)/shard_map/ppermute | solution.py:455
  127.1 5.4 %collective-permute-start.12 = (f32[16,16,128]{2,1,0:T(8,128)S(1)}, f32[16,16,128]{2,1,0:T(8,128)S(1)}, u32[]{:S(2)}, u32[]{:S(2)}) collective-permute-start(f32[16,16,128]{2,1,0:T(8,128)S(1)} %get-tuple-element.97), channel_id=1, source_target_pairs={{4,0},{8,4},{12,8},{5,1},{9,5},{13,9},{6,2},{10,6},{14,10},{7,3},{... | collective-permute-start | bytes 393224 | tf_op jit(solution)/shard_map/ppermute | solution.py:456
  129.0 12.0 %collective-permute-start.30 = (f32[392,128]{1,0:T(8,128)}, f32[392,128]{1,0:T(8,128)}, u32[]{:S(2)}, u32[]{:S(2)}) collective-permute-start(f32[392,128]{1,0:T(8,128)} %constant_dynamic-update-slice_fusion.8), channel_id=1, source_target_pairs={{0,16},{16,0},{1,17},{17,1},{2,18},{18,2},{3,19},{19,3},{4,20},{20... | collective-permute-start | bytes 602120 | tf_op jit(solution)/shard_map/ppermute | solution.py:534
  134.5 10.9 %collective-permute-start.13 = (f32[16,16,128]{2,1,0:T(8,128)}, f32[16,16,128]{2,1,0:T(8,128)}, u32[]{:S(2)}, u32[]{:S(2)}) collective-permute-start(f32[16,16,128]{2,1,0:T(8,128)} %get-tuple-element.100), channel_id=1, source_target_pairs={{0,1},{1,2},{2,3},{4,5},{5,6},{6,7},{8,9},{9,10},{10,11},{12,13},{... | collective-permute-start | bytes 393224 | tf_op jit(solution)/shard_map/ppermute | solution.py:455
  138.0 7.4 %collective-permute-start.14 = (f32[16,16,128]{2,1,0:T(8,128)}, f32[16,16,128]{2,1,0:T(8,128)}, u32[]{:S(2)}, u32[]{:S(2)}) collective-permute-start(f32[16,16,128]{2,1,0:T(8,128)} %get-tuple-element.101), channel_id=1, source_target_pairs={{1,0},{2,1},{3,2},{5,4},{6,5},{7,6},{9,8},{10,9},{11,10},{13,12},{... | collective-permute-start | bytes 393224 | tf_op jit(solution)/shard_map/ppermute | solution.py:456
  142.0 41.7 %collective-permute-start.31 = (f32[392,128]{1,0:T(8,128)S(1)}, f32[392,128]{1,0:T(8,128)S(1)}, u32[]{:S(2)}, u32[]{:S(2)}) collective-permute-start(f32[392,128]{1,0:T(8,128)S(1)} %add.112), channel_id=1, source_target_pairs={{0,4},{4,0},{8,12},{12,8},{1,5},{5,1},{9,13},{13,9},{2,6},{6,2},{1... | collective-permute-start | bytes 602120 | tf_op jit(solution)/shard_map/ppermute | solution.py:534
  145.4 52.7 %slice-start = ((s8[6291456]{0:T(1024)(128)(4,1)}), s8[4194304]{0:T(1024)(128)(4,1)S(1)}, s32[]{:S(2)}) async-start(s8[6291456]{0:T(1024)(128)(4,1)} %bitcast.99), calls=%async_computation | async-start | bytes 8388608
  151.9 46.2 %slice-start.1 = ((s8[6291456]{0:T(1024)(128)(4,1)}), s8[2097152]{0:T(1024)(128)(4,1)S(1)}, s32[]{:S(2)}) async-start(s8[6291456]{0:T(1024)(128)(4,1)} %bitcast.99), calls=%async_computation.1 | async-start | bytes 4194304
  172.6 19.5 %copy-start.46 = (bf16[1,1,128,128]{2,3,1,0:T(8,128)(2,1)S(1)}, bf16[1,1,128,128]{2,3,1,0:T(8,128)(2,1)}, u32[]{:S(2)}) copy-start(bf16[1,1,128,128]{2,3,1,0:T(8,128)(2,1)} %copy-done.45) | copy-start | bytes 98308
  172.6 19.5 %copy-start.49 = (bf16[1,1,128,128]{2,3,1,0:T(8,128)(2,1)S(1)}, bf16[1,1,128,128]{2,3,1,0:T(8,128)(2,1)}, u32[]{:S(2)}) copy-start(bf16[1,1,128,128]{2,3,1,0:T(8,128)(2,1)} %copy-done.48) | copy-start | bytes 98308
  172.6 25.5 %copy-start.13 = (f32[16,16,16,128]{3,2,1,0:T(8,128)S(1)}, f32[16,16,16,128]{3,2,1,0:T(8,128)}, u32[]{:S(2)}) copy-start(f32[16,16,16,128]{3,2,1,0:T(8,128)} %copy-done.12) | copy-start | bytes 6291460
  172.6 5.5 %collective-permute-start.15 = (f32[1,16,16,128]{3,2,1,0:T(8,128)S(1)}, f32[1,16,16,128]{3,2,1,0:T(8,128)S(1)}, u32[]{:S(2)}, u32[]{:S(2)}) collective-permute-start(f32[1,16,16,128]{3,2,1,0:T(8,128)S(1)} %get-tuple-element.105), channel_id=1, source_target_pairs={{0,16},{16,0},{1,17},{17,1},{2,18},{18,2},{3,19},{19,3},{4,20},{20... | collective-permute-start | bytes 393224 | tf_op jit(solution)/shard_map/ppermute | solution.py:462
  174.2 20.7 %collective-permute-start.25 = (f32[528,128]{1,0:T(8,128)S(1)}, f32[528,128]{1,0:T(8,128)S(1)}, u32[]{:S(2)}, u32[]{:S(2)}) collective-permute-start(f32[528,128]{1,0:T(8,128)S(1)} %constant_dynamic-update-slice_fusion.2), channel_id=1, source_target_pairs={{0,16},{16,0},{1,17},{17,1},{2,18},{18,2},{3,19},{19,3},{4,20},{20... | collective-permute-start | bytes 811016 | tf_op jit(solution)/shard_map/ppermute | solution.py:534
  178.6 9.1 %collective-permute-start.16 = (f32[16,16,128]{2,1,0:T(8,128)S(1)}, f32[16,16,128]{2,1,0:T(8,128)S(1)}, u32[]{:S(2)}, u32[]{:S(2)}) collective-permute-start(f32[16,16,128]{2,1,0:T(8,128)S(1)} %get-tuple-element.108), channel_id=1, source_target_pairs={{0,4},{4,8},{8,12},{1,5},{5,9},{9,13},{2,6},{6,10},{10,14},{3,7},{... | collective-permute-start | bytes 393224 | tf_op jit(solution)/shard_map/ppermute | solution.py:455
  182.4 5.3 %collective-permute-start.17 = (f32[16,16,128]{2,1,0:T(8,128)S(1)}, f32[16,16,128]{2,1,0:T(8,128)S(1)}, u32[]{:S(2)}, u32[]{:S(2)}) collective-permute-start(f32[16,16,128]{2,1,0:T(8,128)S(1)} %get-tuple-element.109), channel_id=1, source_target_pairs={{4,0},{8,4},{12,8},{5,1},{9,5},{13,9},{6,2},{10,6},{14,10},{7,3},{... | collective-permute-start | bytes 393224 | tf_op jit(solution)/shard_map/ppermute | solution.py:456
  183.8 10.6 %collective-permute-start.32 = (f32[392,128]{1,0:T(8,128)S(1)}, f32[392,128]{1,0:T(8,128)S(1)}, u32[]{:S(2)}, u32[]{:S(2)}) collective-permute-start(f32[392,128]{1,0:T(8,128)S(1)} %add.113), channel_id=1, source_target_pairs={{0,8},{4,12},{8,0},{12,4},{1,9},{5,13},{9,1},{13,5},{2,10},{6,14},... | collective-permute-start | bytes 602120 | tf_op jit(solution)/shard_map/ppermute | solution.py:534
  188.3 9.8 %collective-permute-start.18 = (f32[16,16,128]{2,1,0:T(8,128)S(1)}, f32[16,16,128]{2,1,0:T(8,128)S(1)}, u32[]{:S(2)}, u32[]{:S(2)}) collective-permute-start(f32[16,16,128]{2,1,0:T(8,128)S(1)} %get-tuple-element.112), channel_id=1, source_target_pairs={{0,1},{1,2},{2,3},{4,5},{5,6},{6,7},{8,9},{9,10},{10,11},{12,13},{... | collective-permute-start | bytes 393224 | tf_op jit(solution)/shard_map/ppermute | solution.py:455
  190.6 7.5 %collective-permute-start.19 = (f32[16,16,128]{2,1,0:T(8,128)S(1)}, f32[16,16,128]{2,1,0:T(8,128)S(1)}, u32[]{:S(2)}, u32[]{:S(2)}) collective-permute-start(f32[16,16,128]{2,1,0:T(8,128)S(1)} %get-tuple-element.113), channel_id=1, source_target_pairs={{1,0},{2,1},{3,2},{5,4},{6,5},{7,6},{9,8},{10,9},{11,10},{13,12},{... | collective-permute-start | bytes 393224 | tf_op jit(solution)/shard_map/ppermute | solution.py:456
  194.4 16.8 %collective-permute-start.33 = (f32[392,128]{1,0:T(8,128)S(1)}, f32[392,128]{1,0:T(8,128)S(1)}, u32[]{:S(2)}, u32[]{:S(2)}) collective-permute-start(f32[392,128]{1,0:T(8,128)S(1)} %add.114), channel_id=1, source_target_pairs={{0,1},{1,0},{2,3},{3,2},{4,5},{5,4},{6,7},{7,6},{8,9},{9,8},{10,11... | collective-permute-start | bytes 602120 | tf_op jit(solution)/shard_map/ppermute | solution.py:534
  194.9 23.6 %collective-permute-start.26 = (f32[528,128]{1,0:T(8,128)S(1)}, f32[528,128]{1,0:T(8,128)S(1)}, u32[]{:S(2)}, u32[]{:S(2)}) collective-permute-start(f32[528,128]{1,0:T(8,128)S(1)} %add.107), channel_id=1, source_target_pairs={{0,4},{4,0},{8,12},{12,8},{1,5},{5,1},{9,13},{13,9},{2,6},{6,2},{1... | collective-permute-start | bytes 811016 | tf_op jit(solution)/shard_map/ppermute | solution.py:534
  209.6 14.5 %copy-start.42 = (bf16[2,2,128,128]{3,2,1,0:T(8,128)(2,1)S(1)}, bf16[2,2,128,128]{3,2,1,0:T(8,128)(2,1)}, u32[]{:S(2)}) copy-start(bf16[2,2,128,128]{3,2,1,0:T(8,128)(2,1)} %param.10) | copy-start | bytes 393220
  209.6 18.5 %copy-start.44 = (bf16[2,256,128]{2,1,0:T(8,128)(2,1)S(1)}, bf16[2,256,128]{2,1,0:T(8,128)(2,1)}, u32[]{:S(2)}) copy-start(bf16[2,256,128]{2,1,0:T(8,128)(2,1)} %param.11) | copy-start | bytes 393220
  209.6 4.4 %collective-permute-start.20 = (f32[136,128]{1,0:T(8,128)S(1)}, f32[136,128]{1,0:T(8,128)S(1)}, u32[]{:S(2)}, u32[]{:S(2)}) collective-permute-start(f32[136,128]{1,0:T(8,128)S(1)} %constant_dynamic-update-slice_fusion), channel_id=1, source_target_pairs={{0,16},{16,0},{1,17},{17,1},{2,18},{18,2},{3,19},{19,3},{4,20},{20... | collective-permute-start | bytes 208904 | tf_op jit(solution)/shard_map/ppermute | solution.py:534
  211.2 12.8 %collective-permute-start.34 = (f32[392,128]{1,0:T(8,128)S(1)}, f32[392,128]{1,0:T(8,128)S(1)}, u32[]{:S(2)}, u32[]{:S(2)}) collective-permute-start(f32[392,128]{1,0:T(8,128)S(1)} %add.115), channel_id=1, source_target_pairs={{0,2},{1,3},{2,0},{3,1},{4,6},{5,7},{6,4},{7,5},{8,10},{9,11},{10,... | collective-permute-start | bytes 602120 | tf_op jit(solution)/shard_map/ppermute | solution.py:534
  214.0 3.7 %collective-permute-start.21 = (f32[136,128]{1,0:T(8,128)S(1)}, f32[136,128]{1,0:T(8,128)S(1)}, u32[]{:S(2)}, u32[]{:S(2)}) collective-permute-start(f32[136,128]{1,0:T(8,128)S(1)} %add.102), channel_id=1, source_target_pairs={{0,4},{4,0},{8,12},{12,8},{1,5},{5,1},{9,13},{13,9},{2,6},{6,2},{1... | collective-permute-start | bytes 208904 | tf_op jit(solution)/shard_map/ppermute | solution.py:534
  217.7 5.1 %collective-permute-start.22 = (f32[136,128]{1,0:T(8,128)S(1)}, f32[136,128]{1,0:T(8,128)S(1)}, u32[]{:S(2)}, u32[]{:S(2)}) collective-permute-start(f32[136,128]{1,0:T(8,128)S(1)} %add.103), channel_id=1, source_target_pairs={{0,8},{4,12},{8,0},{12,4},{1,9},{5,13},{9,1},{13,5},{2,10},{6,14},... | collective-permute-start | bytes 208904 | tf_op jit(solution)/shard_map/ppermute | solution.py:534
  218.5 9.5 %collective-permute-start.27 = (f32[528,128]{1,0:T(8,128)S(1)}, f32[528,128]{1,0:T(8,128)S(1)}, u32[]{:S(2)}, u32[]{:S(2)}) collective-permute-start(f32[528,128]{1,0:T(8,128)S(1)} %add.108), channel_id=1, source_target_pairs={{0,8},{4,12},{8,0},{12,4},{1,9},{5,13},{9,1},{13,5},{2,10},{6,14},... | collective-permute-start | bytes 811016 | tf_op jit(solution)/shard_map/ppermute | solution.py:534
  222.8 5.6 %collective-permute-start.23 = (f32[136,128]{1,0:T(8,128)S(1)}, f32[136,128]{1,0:T(8,128)S(1)}, u32[]{:S(2)}, u32[]{:S(2)}) collective-permute-start(f32[136,128]{1,0:T(8,128)S(1)} %add.104), channel_id=1, source_target_pairs={{0,1},{1,0},{2,3},{3,2},{4,5},{5,4},{6,7},{7,6},{8,9},{9,8},{10,11... | collective-permute-start | bytes 208904 | tf_op jit(solution)/shard_map/ppermute | solution.py:534
  228.0 9.5 %collective-permute-start.28 = (f32[528,128]{1,0:T(8,128)S(1)}, f32[528,128]{1,0:T(8,128)S(1)}, u32[]{:S(2)}, u32[]{:S(2)}) collective-permute-start(f32[528,128]{1,0:T(8,128)S(1)} %add.109), channel_id=1, source_target_pairs={{0,1},{1,0},{2,3},{3,2},{4,5},{5,4},{6,7},{7,6},{8,9},{9,8},{10,11... | collective-permute-start | bytes 811016 | tf_op jit(solution)/shard_map/ppermute | solution.py:534
  228.4 6.9 %collective-permute-start.24 = (f32[136,128]{1,0:T(8,128)S(1)}, f32[136,128]{1,0:T(8,128)S(1)}, u32[]{:S(2)}, u32[]{:S(2)}) collective-permute-start(f32[136,128]{1,0:T(8,128)S(1)} %add.105), channel_id=1, source_target_pairs={{0,2},{1,3},{2,0},{3,1},{4,6},{5,7},{6,4},{7,5},{8,10},{9,11},{10,... | collective-permute-start | bytes 208904 | tf_op jit(solution)/shard_map/ppermute | solution.py:534
  237.6 13.5 %collective-permute-start.29 = (f32[528,128]{1,0:T(8,128)S(1)}, f32[528,128]{1,0:T(8,128)S(1)}, u32[]{:S(2)}, u32[]{:S(2)}) collective-permute-start(f32[528,128]{1,0:T(8,128)S(1)} %add.110), channel_id=1, source_target_pairs={{0,2},{1,3},{2,0},{3,1},{4,6},{5,7},{6,4},{7,5},{8,10},{9,11},{10,... | collective-permute-start | bytes 811016 | tf_op jit(solution)/shard_map/ppermute | solution.py:534
  (41 other events, 50.4 us)
where the time goes:
time: 256 us; the launch traced here: 254 us
  Pallas kernels  67.4 us (26%)
  starting transfers between devices  63.9 us (25%)
  waiting for transfers between devices  57.3 us (22%)
  local copies, waits for them, and re-layouts  55.7 us (22%)
  other arithmetic  7.19 us (3%)
    pallas_call x13, Pallas kernels, call(): pl.pallas_call(kernel, name=name, out_shape=tuple(outs), in_specs=[SM] *...  67.4 us
    unnamed x126, local copies, waits for them, and re-layouts  47.5 us
    ppermute x15, waiting for transfers between devices, reduce_all(): lax.ppermute(value, axis, [(i, i ^ hop) for i in range(size)])  33.8 us
    ppermute x8, starting transfers between devices, trade(): below = lax.ppermute(high_face, axis, [(i, i + 1) for i in range(size - 1)])  24 us
    ppermute x15, starting transfers between devices, reduce_all(): lax.ppermute(value, axis, [(i, i ^ hop) for i in range(size)])  22 us
    ppermute x8, waiting for transfers between devices, trade(): above = lax.ppermute(low_face, axis, [(i + 1, i) for i in range(size - 1)])  12 us
    ppermute x4, waiting for transfers between devices, exchange(): got_x = (lax.ppermute(x_faces[0], 'gx', [(0, 1), (1, 0)]),)  11.5 us
    ppermute x8, starting transfers between devices, trade(): above = lax.ppermute(low_face, axis, [(i + 1, i) for i in range(size - 1)])  10.5 us
  transfers between devices with their start and end apart: 35, of which 17 were waited for; matrix products, arithmetic and copies ran while one was open for 7% of the time, Pallas kernels for 12%

commit v1 on v0

v1 whole, which is shorter than its diff:
```python
import functools
import math

import jax
import jax.numpy as jnp
from jax import lax
from jax.experimental import pallas as pl
from jax.experimental.pallas import tpu as pltpu
from jax.sharding import PartitionSpec as P

f32 = jnp.float32
bf16 = jnp.bfloat16
NODES = 8
VMEM_LIMIT = 12 * 1024 * 1024
VM = pl.BlockSpec(memory_space=pltpu.VMEM)
SM = pl.BlockSpec(memory_space=pltpu.SMEM)


def dot(left, right):
    return lax.dot_general(left, right, (((1,), (0,)), ((), ())), preferred_element_type=f32)


def dot_t(left, right):
    return lax.dot_general(left, right, (((0,), (0,)), ((), ())), preferred_element_type=f32)


def dot_rt(left, right):
    return lax.dot_general(left, right, (((1,), (1,)), ((), ())), preferred_element_type=f32)


def silu_half(half):
    th = jnp.tanh(half)
    prod = half * th
    return half + prod, (0.5 + 0.5 * th) * ((1.0 + half) - prod)


def split_cols(value):
    high = value.astype(bf16)
    low = (value - high.astype(f32)).astype(bf16)
    return jnp.concatenate([high, low], -1)


def up(value):
    return pltpu.roll(value, NODES - 1, 1)


def down(value):
    return pltpu.roll(value, 1, 1)


def flat(value):
    return value.reshape(-1, value.shape[-1])


def node_rows(value):
    return value.reshape(-1, NODES, value.shape[-1])


def row_ids():
    return lax.broadcasted_iota(jnp.int32, (1, NODES, 128), 1)


def couple_slots(plane, filled):
    count, rows, width = plane.shape
    slots = rows // NODES
    parts = plane.reshape(count, slots, NODES, width)
    ids = row_ids()
    done = []
    for s in range(slots):
        here = parts[:, s]
        if s + 1 < slots:
            take = (ids == NODES - 1) & (s + 1 < filled)
            here = here + jnp.where(take, up(parts[:, s + 1]), 0.0)
        if s > 0:
            here = here + jnp.where(ids == 0, down(parts[:, s - 1]), 0.0)
            here = jnp.where(s < filled, here, 0.0)
        done.append(here[:, None])
    return jnp.concatenate(done, 1).reshape(plane.shape)


def elements(x_len, y_len, body):
    ey = y_len // NODES
    total = (x_len // NODES) * ey

    def step(e, carry):
        x0 = pl.multiple_of((e // ey) * NODES, NODES)
        y0 = pl.multiple_of((e % ey) * NODES, NODES)
        body(x0, y0)
        return carry

    lax.fori_loop(0, total, step, 0)


def edges_forward(h_ref, w_one, half_bias, filled, sum_ref, slope_ref):
    x_len, y_len, rows, width = h_ref.shape
    inner = row_ids() < NODES - 1

    def body(x0, y0):
        ys = pl.ds(y0, NODES)
        prev = None
        here = h_ref[x0, ys].astype(f32)
        for i in range(NODES):
            parts = []
            nxt = None
            if i < NODES - 1:
                nxt = h_ref[x0 + i + 1, ys].astype(f32)
                parts.append((nxt - here).astype(bf16))
            parts.append((here[1:] - here[:-1]).astype(bf16))
            cols = node_rows(here)
            parts.append((up(cols) - cols).reshape(here.shape).astype(bf16))
            half = dot(flat(jnp.concatenate(parts, 0)), w_one).reshape(-1, rows, width) + half_bias
            act, slope = silu_half(half)
            act = act.astype(bf16).astype(f32)
            at = 0
            total = prev
            prev = None
            if i < NODES - 1:
                prev = act[:NODES]
                total = -prev if total is None else total - prev
                slope_ref[0, x0 + i, ys] = slope[:NODES]
                at = NODES
            along_y = act[at : at + NODES - 1]
            slope_ref[1, x0 + i, pl.ds(y0, NODES - 1)] = slope[at : at + NODES - 1]
            at += NODES - 1
            along_z = jnp.where(inner, node_rows(act[at:]), 0.0)
            slope_z = jnp.where(inner, node_rows(slope[at:]), 0.0)
            slope_ref[2, x0 + i, ys] = slope_z.reshape(here.shape)
            total = total + (down(along_z) - along_z).reshape(here.shape)
            total = jnp.concatenate(
                [
                    total[:1] - along_y[:1],
                    total[1:-1] + (along_y[:-1] - along_y[1:]),
                    total[-1:] + along_y[-1:],
                ],
                0,
            )
            sum_ref[x0 + i, ys] = couple_slots(total, filled)
            here = nxt

    elements(x_len, y_len, body)


def couple_columns(sum_ref):
    x_len, y_len = sum_ref.shape[:2]
    for cut in range(NODES, x_len, NODES):
        both = sum_ref[cut - 1] + sum_ref[cut]
        sum_ref[cut - 1] = both
        sum_ref[cut] = both
    for cut in range(NODES, y_len, NODES):
        both = sum_ref[:, cut - 1] + sum_ref[:, cut]
        sum_ref[:, cut - 1] = both
        sum_ref[:, cut] = both


def face_place(sc_ref, axis, kind, last):
    return jnp.where((sc_ref[1 + axis] + kind) % 2 == 0, last, 0)


def end_rows(values, filled, take_top):
    picked = values(0)
    slots = values.slots
    for s in range(slots):
        picked = jnp.where(take_top & (filled == s + 1), values(s * NODES + NODES - 1), picked)
    return picked


class RowReader:
    def __init__(self, slots, read):
        self.slots = slots
        self.read = read

    def __call__(self, row):
        return self.read(row)


def takes_top(sc_ref, kind):
    return (sc_ref[3] + kind) % 2 == 0


def write_faces(sc_ref, sum_ref, faces, counts):
    x_len, y_len, rows, width = sum_ref.shape
    nx, ny, nz = counts
    reader = RowReader(rows // NODES, lambda row: sum_ref[:, :, row])
    for kind in range(nx):
        faces[kind][...] = sum_ref[face_place(sc_ref, 0, kind, x_len - 1)]
    for kind in range(ny):
        faces[nx + kind][...] = sum_ref[:, face_place(sc_ref, 1, kind, y_len - 1)]
    for kind in range(nz):
        faces[nx + ny + kind][...] = end_rows(reader, sc_ref[0], takes_top(sc_ref, kind))


def add_halo(sc_ref, from_ref, halo, into_ref, counts):
    x_len, y_len, rows, width = from_ref.shape
    nx, ny, nz = counts

    def copy(x, carry):
        into_ref[x] = from_ref[x]
        return carry

    lax.fori_loop(0, x_len, copy, 0)
    for kind in range(nx):
        into_ref[face_place(sc_ref, 0, kind, x_len - 1)] += halo[kind][...]
    for kind in range(ny):
        into_ref[:, face_place(sc_ref, 1, kind, y_len - 1)] += halo[nx + kind][...]
    if nz:
        got = [halo[nx + ny + kind][...] for kind in range(nz)]
        tops = [takes_top(sc_ref, kind) for kind in range(nz)]
        from_below = sum(jnp.where(top, 0.0, value) for top, value in zip(tops, got))
        from_above = sum(jnp.where(top, value, 0.0) for top, value in zip(tops, got))
        into_ref[:, :, 0] += from_below
        for s in range(rows // NODES):
            into_ref[:, :, s * NODES + NODES - 1] += jnp.where(sc_ref[0] == s + 1, from_above, 0.0)


def fix_y_kernel(counts, sc_ref, *refs):
    nx, ny, nz = counts
    got, faces, outs = refs[:nx], refs[nx : nx + ny], refs[nx + ny :]
    x_len = faces[0].shape[0]
    for k in range(ny):
        outs[k][...] = faces[k][...]
    for kind in range(nx):
        place = face_place(sc_ref, 0, kind, x_len - 1)
        for k in range(ny):
            y_len = got[kind].shape[0]
            outs[k][place] += got[kind][face_place(sc_ref, 1, k, y_len - 1)]


def fix_z_kernel(counts, sc_ref, *refs):
    nx, ny, nz = counts
    got_x, refs = refs[:nx], refs[nx:]
    got_y, refs = refs[:ny], refs[ny:]
    faces, outs = refs[:nz], refs[nz:]
    x_len, y_len, width = faces[0].shape
    for k in range(nz):
        outs[k][...] = faces[k][...]
    for k in range(nz):
        top = takes_top(sc_ref, k)
        for kind in range(nx):
            ref = got_x[kind]
            reader = RowReader(ref.shape[1] // NODES, lambda row, ref=ref: ref[:, row])
            outs[k][face_place(sc_ref, 0, kind, x_len - 1)] += end_rows(reader, sc_ref[0], top)
        for kind in range(ny):
            ref = got_y[kind]
            reader = RowReader(ref.shape[1] // NODES, lambda row, ref=ref: ref[:, row])
            add = end_rows(reader, sc_ref[0], top)
            first = face_place(sc_ref, 1, kind, 1) == 0
            outs[k][:, 0] += jnp.where(first, add, 0.0)
            outs[k][:, y_len - 1] += jnp.where(first, 0.0, add)


def write_inverse(sc_ref, inv_ref, sizes):
    y_len, rows, width = inv_ref.shape
    filled, at_y, at_z = sc_ref[0], sc_ref[2], sc_ref[3]
    ids = lax.broadcasted_iota(jnp.int32, (rows, width), 0)
    node = ids % NODES
    low = (node == 0) & ((ids >= NODES) | (at_z > 0))
    high = (node == NODES - 1) & ((ids < (filled - 1) * NODES) | (at_z < sizes[2] - 1))
    along_z = jnp.where(low | high, 0.5, 1.0).astype(f32)
    for y in range(y_len):
        inv_ref[y] = along_z * end_factor(y, y_len, at_y, sizes[1])


def end_factor(place, length, position, size):
    whole = place + position * length
    low = (place % NODES == 0) & (whole > 0)
    high = (place % NODES == NODES - 1) & (whole < length * size - 1)
    return jnp.where(low | high, 0.5, 1.0).astype(f32)


CHUNK = 4


def scale_planes(sc_ref, inv_ref, x, block, x_len, size_x):
    inv = inv_ref[...]
    parts = [block[c] * (inv * end_factor(x + c, x_len, sc_ref[1], size_x)) for c in range(CHUNK)]
    return jnp.stack(parts, 0)


def node_forward(sc_ref, x, inv_ref, size_x, sum_ref, h_ref, weights, layer):
    edge_w, node_in, node_out, biases = weights
    at = pl.ds(x, CHUNK)
    scaled = scale_planes(sc_ref, inv_ref, x, sum_ref[at], sum_ref.shape[0], size_x)
    pair = split_cols(flat(scaled))
    w_two = edge_w[layer, 1]
    joined = jnp.concatenate([flat(h_ref[at]), dot(pair, jnp.concatenate([w_two, w_two], 0)).astype(bf16)], -1)
    half = jnp.bfloat16(0.5)
    act, slope = silu_half(dot(joined, node_in[layer] * half) + 0.5 * biases[layer, pl.ds(1, 1)])
    return pair[:, :128], act.astype(bf16), slope


def node_backward(sc_ref, x, inv_ref, size_x, grad, feat, scaled, act, slope, weights, layer, sum_ref, base_ref, grads):
    edge_w, node_in, node_out, biases = weights
    shape = (CHUNK,) + sum_ref.shape[1:]
    at = pl.ds(x, CHUNK)
    dpn = (dot_rt(grad, node_out[layer]) * slope).astype(bf16)
    grads[0, pl.ds(0, 128)] += dot_t(act, grad)
    both = dot_t(dpn, jnp.concatenate([feat, scaled], -1))
    grads[0, pl.ds(128, 128)] += both[:, :128]
    grads[0, pl.ds(256, 128)] += both[:, 128:]
    grads[0, pl.ds(384, NODES)] += jnp.sum(dpn.astype(f32).reshape(-1, NODES, 128), 0)
    dx = dot_rt(dpn, node_in[layer])
    base_ref[at] = (grad.astype(f32) + dx[:, :128]).reshape(shape)
    share = scale_planes(sc_ref, inv_ref, x, dx[:, 128:].reshape(shape), sum_ref.shape[0], size_x)
    joined = couple_slots(share.reshape((-1,) + shape[2:]), sc_ref[0])
    sum_ref[at] = joined.reshape(shape)


def edges_backward(q_ref, slope_ref, edge_ref, bias_acc):
    x_len, y_len, rows, width = q_ref.shape

    def body(x0, y0):
        ys = pl.ds(y0, NODES)
        prev = None
        here = q_ref[x0, ys]
        bias = jnp.zeros((NODES, width), f32)
        for i in range(NODES):
            total = prev
            prev = None
            nxt = None
            if i < NODES - 1:
                nxt = q_ref[x0 + i + 1, ys]
                prev = ((nxt - here) * slope_ref[0, x0 + i, ys]).astype(bf16).astype(f32)
                total = -prev if total is None else total - prev
                bias = bias + jnp.sum(node_rows(prev), 0)
            along_y = (here[1:] - here[:-1]) * slope_ref[1, x0 + i, pl.ds(y0, NODES - 1)]
            along_y = along_y.astype(bf16).astype(f32)
            cols = node_rows(here)
            along_z = (up(cols) - cols) * node_rows(slope_ref[2, x0 + i, ys])
            along_z = along_z.astype(bf16).astype(f32)
            bias = bias + jnp.sum(node_rows(along_y), 0) + jnp.sum(along_z, 0)
            total = total + (down(along_z) - along_z).reshape(here.shape)
            total = jnp.concatenate(
                [
                    total[:1] - along_y[:1],
                    total[1:-1] + (along_y[:-1] - along_y[1:]),
                    total[-1:] + along_y[-1:],
                ],
                0,
            )
            edge_ref[x0 + i, ys] = total
            here = nxt
        bias_acc[...] += bias

    elements(x_len, y_len, body)


def planes(count, body):
    def step(c, carry):
        body(pl.multiple_of(c * CHUNK, CHUNK))
        return carry

    lax.fori_loop(0, count // CHUNK, step, 0)


def half_weights(weights, layer):
    edge_w, node_in, node_out, biases = weights
    return edge_w[layer, 0] * jnp.bfloat16(0.5), 0.5 * biases[layer, pl.ds(0, 1)]


def first_kernel(counts, sizes, sc, edge_w, node_in, node_out, biases, h, *refs):
    weights = (edge_w, node_in, node_out, biases)
    sums, slopes = refs[:2]
    faces = refs[2:]
    w_one, bias = half_weights(weights, 0)
    edges_forward(h, w_one, bias, sc[0], sums, slopes)
    couple_columns(sums)
    write_faces(sc, sums, faces, counts)


def middle_kernel(counts, sizes, sc, edge_w, node_in, node_out, biases, sums_in, h, *refs):
    weights = (edge_w, node_in, node_out, biases)
    n = sum(counts)
    halo, refs = refs[:n], refs[n:]
    scaled_ref, act_ref, slope_ref, next_ref, sums, slopes = refs[:6]
    faces, (work, inv) = refs[6:-2], refs[-2:]
    add_halo(sc, sums_in, halo, work, counts)
    write_inverse(sc, inv, sizes)
    shape = (CHUNK,) + h.shape[1:]

    def body(x):
        at = pl.ds(x, CHUNK)
        scaled, act, slope = node_forward(sc, x, inv, sizes[0], work, h, weights, 0)
        scaled_ref[at] = scaled.reshape(shape)
        act_ref[at] = act.reshape(shape)
        slope_ref[at] = slope.reshape(shape)
        moved = flat(h[at]).astype(f32) + dot(act, node_out[0])
        next_ref[at] = moved.astype(bf16).reshape(shape)

    planes(h.shape[0], body)
    w_one, bias = half_weights(weights, 1)
    edges_forward(next_ref, w_one, bias, sc[0], sums, slopes)
    couple_columns(sums)
    write_faces(sc, sums, faces, counts)


def turn_kernel(counts, sizes, sc, edge_w, node_in, node_out, biases, sums_in, h, g_ref, *refs):
    weights = (edge_w, node_in, node_out, biases)
    n = sum(counts)
    halo, refs = refs[:n], refs[n:]
    base, sums, grads = refs[:3]
    faces, (work, inv) = refs[3:-2], refs[-2:]
    add_halo(sc, sums_in, halo, work, counts)
    write_inverse(sc, inv, sizes)
    grads[...] = jnp.zeros_like(grads)
    live = (lax.broadcasted_iota(jnp.int32, (1, 1, h.shape[2], 128), 2) < sc[0] * NODES).astype(f32)

    def body(x):
        at = pl.ds(x, CHUNK)
        scaled, act, slope = node_forward(sc, x, inv, sizes[0], work, h, weights, 1)
        grad = flat((g_ref[at].astype(f32) * live).astype(bf16))
        node_backward(
            sc, x, inv, sizes[0], grad, flat(h[at]), scaled, act, slope, weights, 1, sums, base, grads
        )

    planes(h.shape[0], body)
    couple_columns(sums)
    write_faces(sc, sums, faces, counts)


def back_to_state(counts, sc, weights, layer, sums_in, halo, h, base, slopes, work, grads, row, use):
    edge_w = weights[0]
    add_halo(sc, sums_in, halo, work, counts)
    shape = (CHUNK,) + h.shape[1:]
    w_two = edge_w[layer, 1]
    w_two = jnp.concatenate([w_two, w_two], 1)
    w_one = edge_w[layer, 0]
    w_one = jnp.concatenate([w_one, w_one], 1)

    def to_q(x):
        at = pl.ds(x, CHUNK)
        work[at] = dot_rt(split_cols(flat(work[at])), w_two).reshape(shape)

    planes(h.shape[0], to_q)
    edges_backward(work, slopes, work, grads.at[0, pl.ds(row + 128, NODES)])

    def body(x):
        at = pl.ds(x, CHUNK)
        pair = split_cols(flat(work[at]))
        both = dot_t(flat(h[at]), pair)
        grads[0, pl.ds(row, 128)] += both[:, :128] + both[:, 128:]
        use(x, (flat(base[at]) + dot_rt(pair, w_one)).astype(bf16))

    planes(h.shape[0], body)


def join_kernel(
    counts, sizes, sc, edge_w, node_in, node_out, biases,
    sums_in, h, base_in, slopes, h0, scaled0, act0, slope0, *refs
):
    weights = (edge_w, node_in, node_out, biases)
    n = sum(counts)
    halo, refs = refs[:n], refs[n:]
    base, sums, grads = refs[:3]
    faces, (work, inv) = refs[3:-2], refs[-2:]
    write_inverse(sc, inv, sizes)
    grads[...] = jnp.zeros_like(grads)

    def use(x, grad):
        at = pl.ds(x, CHUNK)
        node_backward(
            sc, x, inv, sizes[0], grad, flat(h0[at]), flat(scaled0[at]), flat(act0[at]), flat(slope0[at]),
            weights, 0, sums, base, grads,
        )

    back_to_state(counts, sc, weights, 1, sums_in, halo, h, base_in, slopes, work, grads, 384 + NODES, use)
    couple_columns(sums)
    write_faces(sc, sums, faces, counts)


def last_kernel(counts, sizes, sc, edge_w, node_in, node_out, biases, sums_in, h, base_in, slopes, *refs):
    weights = (edge_w, node_in, node_out, biases)
    n = sum(counts)
    halo, refs = refs[:n], refs[n:]
    grad_ref, grads, work = refs
    grads[...] = jnp.zeros_like(grads)
    shape = (CHUNK,) + h.shape[1:]

    def use(x, grad):
        grad_ref[pl.ds(x, CHUNK)] = grad.reshape(shape)

    back_to_state(counts, sc, weights, 0, sums_in, halo, h, base_in, slopes, work, grads, 0, use)


def finish_kernel(scale, edge_w, node_in, sum0, sum1, last, edge_grads, in_grads, out_grads, bias_grads):
    width = edge_w.shape[-1]

    def rows_of(ref, start, count=width):
        return ref[pl.ds(start, count)] * scale

    def bias_of(ref, start):
        return jnp.sum(rows_of(ref, start, NODES), 0, keepdims=True)

    end = 3 * width
    firsts = ((last, 0), (sum0, end + NODES))
    for layer, ref in enumerate((sum0, sum1)):
        out_grads[layer] = rows_of(ref, 0)
        in_grads[layer, pl.ds(0, width)] = rows_of(ref, width).T
        bias_grads[layer, pl.ds(1, 1)] = bias_of(ref, end)
        source, start = firsts[layer]
        edge_grads[layer, 0] = rows_of(source, start)
        bias_grads[layer, pl.ds(0, 1)] = bias_of(source, start + width)
        mixed = rows_of(ref, 2 * width).T
        high = mixed.astype(bf16)
        low = (mixed - high.astype(f32)).astype(bf16)
        lower = node_in[layer, pl.ds(width, width)]
        edge_grads[layer, 1] = dot_rt(high, lower) + dot_rt(low, lower)
        w_two = edge_w[layer, 1]
        in_grads[layer, pl.ds(width, width)] = dot_t(w_two, high) + dot_t(w_two, low)


def call(kernel, name, inputs, outs, scratch=(), flops=0):
    total = sum(math.prod(o.shape) * o.dtype.itemsize for o in outs)
    total += sum(math.prod(i.shape) * i.dtype.itemsize for i in inputs)
    return pl.pallas_call(
        kernel,
        name=name,
        out_shape=tuple(outs),
        in_specs=[SM] + [VM] * (len(inputs) - 1),
        out_specs=tuple([VM] * len(outs)),
        scratch_shapes=list(scratch),
        compiler_params=pltpu.CompilerParams(vmem_limit_bytes=VMEM_LIMIT),
        cost_estimate=pl.CostEstimate(flops=flops, bytes_accessed=total, transcendentals=0),
    )(*inputs)


def pairs(size, kind):
    return [
        pair for low in range(kind, size - 1, 2) for pair in ((low, low + 1), (low + 1, low))
    ]


def double(value, axis, hop):
    size = lax.axis_size(axis)
    return value + lax.ppermute(value, axis, [(i, i ^ hop) for i in range(size)])


def hops(size):
    found = []
    hop = 1
    while hop < size:
        found.append(hop)
        hop *= 2
    return found


def sum_steps(value):
    steps = [("gy", 1)] + [("gx", hop) for hop in hops(lax.axis_size("gx"))]
    steps += [("gy", hop) for hop in hops(lax.axis_size("gy"))[1:]]
    steps = [step for step in steps if lax.axis_size(step[0]) > 1]
    rows, width = value.shape
    unit = NODES << len(steps)
    padded = -(-rows // unit) * unit
    value = jnp.pad(value, ((0, padded - rows), (0, 0))).reshape((2,) * len(steps) + (-1, width))
    for axis, hop in steps:
        size = lax.axis_size(axis)
        bit = (lax.axis_index(axis) // hop) % 2
        keep = lax.dynamic_index_in_dim(value, bit, 0, keepdims=False)
        send = lax.dynamic_index_in_dim(value, 1 - bit, 0, keepdims=False)
        value = yield keep + lax.ppermute(send, axis, [(i, i ^ hop) for i in range(size)])
    for hop in hops(lax.axis_size("gz")):
        value = yield double(value, "gz", hop)
    for axis, hop in reversed(steps):
        size = lax.axis_size(axis)
        bit = (lax.axis_index(axis) // hop) % 2
        other = lax.ppermute(value, axis, [(i, i ^ hop) for i in range(size)])
        value = yield jnp.where(bit == 0, jnp.stack([value, other]), jnp.stack([other, value]))
    yield value.reshape(padded, width)[:rows]


class Background:
    def __init__(self):
        self.active = []

    def add(self, value):
        entry = [sum_steps(value), None, None]
        entry[2] = "ready"
        self.active.append(entry)
        return entry

    def advance(self, entry, tied):
        steps, value, state = entry
        try:
            entry[1] = next(steps) if state == "ready" else steps.send(tied)
            entry[2] = "going"
        except StopIteration:
            entry[2] = "done"

    def beside(self, anchor):
        for entry in self.active:
            if entry[2] == "going":
                anchor, tied = lax.optimization_barrier((anchor, entry[1]))
                self.advance(entry, tied)
            elif entry[2] == "ready":
                self.advance(entry, None)
        return anchor

    def finish(self, entry):
        while entry[2] != "done":
            self.advance(entry, entry[1])
        return entry[1]


def on_device(state, cotangent, counts, edge_weights, node_in, node_out, biases):
    x_len, y_len, slots, nodes, width = state.shape
    rows = slots * nodes
    grid = (x_len, y_len, rows, width)
    axes = ("gx", "gy", "gz")
    sizes = tuple(lax.axis_size(a) for a in axes)
    trades = tuple(min(size - 1, 2) for size in sizes)
    nx, ny, nz = trades
    h0 = state.reshape(grid)
    g2 = cotangent.reshape(grid)
    sc = jnp.stack([counts[0]] + [lax.axis_index(a).astype(jnp.int32) for a in axes])

    def sds(shape, kind=f32):
        return jax.ShapeDtypeStruct(shape, kind)

    face_x = sds((y_len, rows, width))
    face_y = sds((x_len, rows, width))
    face_z = sds((x_len, y_len, width))
    face_outs = [face_x] * nx + [face_y] * ny + [face_z] * nz
    full = sds(grid)
    full16 = sds(grid, bf16)
    full3 = sds((3,) + grid)
    work = pltpu.VMEM(grid, f32)
    inv = pltpu.VMEM((y_len, rows, width), f32)
    matmul = 2 * math.prod(grid) * width
    weights = (edge_weights, node_in, node_out, biases)

    def run(kernel, name, inputs, outs, scratch, flops):
        body = functools.partial(kernel, trades, sizes)
        return call(body, name, (sc, *weights, *inputs), outs, scratch, flops * matmul)

    def trade(faces, axis):
        size = lax.axis_size(axis)
        return [lax.ppermute(face, axis, pairs(size, kind)) for kind, face in enumerate(faces)]

    background = Background()

    def exchange(faces):
        got_x = trade(faces[:nx], "gx")
        fix = functools.partial(fix_y_kernel, trades)
        faces_y = call(fix, "fix_y", (sc, *got_x, *faces[nx : nx + ny]), [face_y] * ny)
        got_y = trade(background.beside(faces_y), "gy")
        fix = functools.partial(fix_z_kernel, trades)
        faces_z = call(fix, "fix_z", (sc, *got_x, *got_y, *faces[nx + ny :]), [face_z] * nz)
        faces_z = background.beside(faces_z)
        got_z = background.beside(trade(faces_z, "gz"))
        return (*got_x, *got_y, *got_z)

    sums, slopes0, *faces = run(first_kernel, "edges0", (h0,), [full, full3] + face_outs, [], 3)
    halo = exchange(faces)
    scaled0, act0, slope0, h1, sums, slopes1, *faces = run(
        middle_kernel, "nodes0_edges1", (sums, h0, *halo),
        [full16, full16, full, full16, full, full3] + face_outs, [work, inv], 8,
    )
    halo = exchange(faces)
    turn_rows = sds((1, 3 * width + NODES, width))
    base, sums, grads1, *faces = run(
        turn_kernel, "nodes1_back", (sums, h1, g2, *halo), [full, full, turn_rows] + face_outs, [work, inv], 10
    )
    sum1 = background.add(grads1[0])
    halo = exchange(faces)
    join_rows = sds((1, 4 * width + 2 * NODES, width))
    base, sums, grads0, *faces = run(
        join_kernel, "edges1_back_nodes0_back", (sums, h1, base, slopes1, h0, scaled0, act0, slope0, *halo),
        [full, full, join_rows] + face_outs, [work, inv], 12,
    )
    sum0 = background.add(grads0[0])
    halo = exchange(faces)
    last_rows = sds((1, width + NODES, width))
    grad0, last = run(last_kernel, "edges0_back", (sums, h0, base, slopes0, *halo), [full16, last_rows], [work], 6)

    last = last[0]
    for axis in ("gz", "gy", "gx"):
        for hop in reversed(hops(lax.axis_size(axis))):
            last = double(background.beside(last), axis, hop)
    summed1, summed0 = background.finish(sum1), background.finish(sum0)
    layers_all = 3 * slots * sizes[2] // 4
    nodes_all = x_len * sizes[0] * y_len * sizes[1] * layers_all * nodes
    scale = 1.0 / math.sqrt(nodes_all)

    edge_grads, in_grads, out_grads, bias_grads = pl.pallas_call(
        functools.partial(finish_kernel, scale),
        name="finish",
        out_shape=(
            sds(edge_weights.shape),
            sds(node_in.shape),
            sds(node_out.shape),
            sds(biases.shape),
        ),
        in_specs=[VM] * 5,
        out_specs=(VM, VM, VM, VM),
        compiler_params=pltpu.CompilerParams(vmem_limit_bytes=VMEM_LIMIT),
    )(edge_weights, node_in, summed0, summed1, last)
    return grad0.reshape(state.shape), edge_grads, in_grads, out_grads, bias_grads


def solution(mesh):
    return jax.shard_map(
        on_device,
        mesh=mesh,
        in_specs=(
            P("gx", "gy", "gz", None, None),
            P("gx", "gy", "gz", None, None),
            P("gz"),
            P(),
            P(),
            P(),
            P(),
        ),
        out_specs=(P("gx", "gy", "gz", None, None), P(), P(), P(), P()),
        check_vma=False,
    )
```

time: 256 us -> 200 us (0.78)
  Pallas kernels: 67.4 us -> 41 us
  local copies, waits for them, and re-layouts: 55.7 us -> 40.3 us
  waiting for transfers between devices: 57.3 us -> 43.1 us
  starting transfers between devices: 63.9 us -> 70.5 us
  other arithmetic: 7.19 us -> 2.05 us
    pallas_call x13 -> x14, Pallas kernels: 67.4 us -> 41 us  [the longest x13 39.9 us: call(): pl.pallas_call(kernel, name=name, out_shape=tuple(outs), in_specs=[SM] +...]
    ppermute x35 -> x41, waiting for transfers between devices: 57.3 us -> 43.1 us  [the longest x20 21.1 us: trade(): lax.ppermute(face, axis, pairs(size, kind))]
    unnamed x126 -> x68, local copies, waits for them, and re-layouts: 47.5 us -> 39.5 us
    ppermute x35 -> x41, starting transfers between devices: 63.9 us -> 70.5 us  [the longest x20 28.6 us: trade(): lax.ppermute(face, axis, pairs(size, kind))]
    mul x4 -> x0, local copies, waits for them, and re-layouts: 3.14 us -> none  [the longest x2 2.31 us: on_device(): w_in = [node_in[l] * half for l in range(2)]]
    slice x3 -> x2, local copies, waits for them, and re-layouts: 2.72 us -> 0.03 us  [sum_steps(): yield value.reshape(padded, width)[:rows]]
  transfers between devices with their start and end apart: 35 -> 41, of which waited for: 17 -> 19; matrix products, arithmetic and copies ran while one was open for 7% -> 1% of each run, Pallas kernels for 12% -> 8%
where the time goes in v1:
time: 200 us; the launch traced here: 199 us
  starting transfers between devices  70.5 us (35%)
  waiting for transfers between devices  43.1 us (22%)
  Pallas kernels  41 us (20%)
  local copies, waits for them, and re-layouts  40.3 us (20%)
  other arithmetic  2.05 us (1%)
    pallas_call x13, Pallas kernels, call(): pl.pallas_call(kernel, name=name, out_shape=tuple(outs), in_specs=[SM] +...  39.9 us
    unnamed x68, local copies, waits for them, and re-layouts  39.5 us
    ppermute x20, starting transfers between devices, trade(): lax.ppermute(face, axis, pairs(size, kind))  28.6 us
    ppermute x20, waiting for transfers between devices, trade(): lax.ppermute(face, axis, pairs(size, kind))  21.1 us
    ppermute x9, starting transfers between devices, double(): lax.ppermute(value, axis, [(i, i ^ hop) for i in range(size)])  18.4 us
    ppermute x9, waiting for transfers between devices, double(): lax.ppermute(value, axis, [(i, i ^ hop) for i in range(size)])  17.7 us
    ppermute x6, starting transfers between devices, sum_steps(): lax.ppermute(send, axis, [(i, i ^ hop) for i in range(size)])  16.2 us
    ppermute x6, starting transfers between devices, sum_steps(): other = lax.ppermute(value, axis, [(i, i ^ hop) for i in range(size)])  7.27 us
  transfers between devices with their start and end apart: 41, of which 19 were waited for; matrix products, arithmetic and copies ran while one was open for 1% of the time, Pallas kernels for 8%

profile of v1, /device:TPU:0, one launch (start us, length us, event | category | flops | bytes accessed | tf_op | source)
XLA Modules:
  0.0 198.8 jit_solution(7179464513400640693)
XLA Ops:
  5.9 5.1 %edges0.1 = (f32[16,16,16,128]{3,2,1,0:T(8,128)S(1)}, f32[3,16,16,16,128]{4,3,2,1,0:T(8,128)S(1)}, f32[16,16,128]{2,1,0:T(8,128)S(1)}, f32[16,16,128]{2,1,0:T(8,...) custom-call(s32[4]{0:T(128)S(1)} %pad_add_fusion.sc.sc_ref, ...), custom_call_target="tpu_custom_call" | custom-call | flops 402653184 | bytes 10422288 | tf_op jit(solution)/shard_map/edges0/pallas_call | solution.py:514
  11.0 2.6 %copy-done.2 = f32[3,16,16,16,128]{4,3,2,1,0:T(8,128)} copy-done((f32[3,16,16,16,128]{4,3,2,1,0:T(8,128)}, f32[3,16,16,16,128]{4,3,2,1,0:T(8,128)S(1)}, u32[]{:S(2)}) %copy-start.2) | copy-done | bytes 6291480
  13.6 2.9 %collective-permute-start = (f32[16,16,128]{2,1,0:T(8,128)S(1)}, f32[16,16,128]{2,1,0:T(8,128)S(1)}, u32[]{:S(2)}, u32[]{:S(2)}) collective-permute-start(f32[16,16,128]{2,1,0:T(8,128)S(1)} %get-tuple-element.100), channel_id=1, source_target_pairs={{0,16},{16,0},{1,17},{17,1},{2,18},{18,2},{3,19},{19,3},{4,20},{20... | collective-permute-start | bytes 393224 | tf_op jit(solution)/shard_map/ppermute | solution.py:636
  16.6 3.5 %collective-permute-done.refs_0_ = f32[16,16,128]{2,1,0:T(8,128)S(1)} collective-permute-done((f32[16,16,128]{2,1,0:T(8,128)S(1)}, f32[16,16,128]{2,1,0:T(8,128)S(1)}, u32[]{:S(2)}, u32[]{:S(2)}) %collective-permute-start) | collective-permute-done | bytes 131104 | tf_op jit(solution)/shard_map/ppermute | solution.py:636
  22.7 1.9 collective-permute-start.3
  25.3 2.5 %collective-permute-done.3.refs_3_ = f32[16,16,128]{2,1,0:T(8,128)S(1)} collective-permute-done((f32[16,16,128]{2,1,0:T(8,128)S(1)}, f32[16,16,128]{2,1,0:T(8,128)S(1)}, u32[]{:S(2)}, u32[]{:S(2)}) %collective-permute-start.3) | collective-permute-done | bytes 131104 | tf_op jit(solution)/shard_map/ppermute | solution.py:636
  27.8 8.8 %nodes0_edges1.1 = (bf16[16,16,16,128]{3,2,1,0:T(8,128)(2,1)S(1)}, bf16[16,16,16,128]{3,2,1,0:T(8,128)(2,1)S(1)}, f32[16,16,16,128]{3,2,1,0:T(8,128)S(1)}, bf16[...) custom-call(s32[4]{0:T(128)S(1)} %pad_add_fusion.sc.sc_ref, ...), custom_call_target="tpu_custom_call" | custom-call | flops 1073741824 | bytes 18417680 | tf_op jit(solution)/shard_map/nodes0_edges1/pallas_call | solution.py:514
  36.6 2.7 %copy-done.4 = f32[3,16,16,16,128]{4,3,2,1,0:T(8,128)} copy-done((f32[3,16,16,16,128]{4,3,2,1,0:T(8,128)}, f32[3,16,16,16,128]{4,3,2,1,0:T(8,128)S(1)}, u32[]{:S(2)}) %copy-start.4) | copy-done | bytes 6291480
  43.9 1.7 collective-permute-start.5
  45.6 3.2 %collective-permute-done.5.refs_0_ = f32[16,16,128]{2,1,0:T(8,128)S(1)} collective-permute-done((f32[16,16,128]{2,1,0:T(8,128)S(1)}, f32[16,16,128]{2,1,0:T(8,128)S(1)}, u32[]{:S(2)}, u32[]{:S(2)}) %collective-permute-start.5) | collective-permute-done | bytes 131104 | tf_op jit(solution)/shard_map/ppermute | solution.py:636
  49.4 3.6 %collective-permute-start.6 = (f32[16,16,128]{2,1,0:T(8,128)S(1)}, f32[16,16,128]{2,1,0:T(8,128)S(1)}, u32[]{:S(2)}, u32[]{:S(2)}) collective-permute-start(f32[16,16,128]{2,1,0:T(8,128)S(1)} %get-tuple-element.114), channel_id=1, source_target_pairs={{0,4},{4,0},{8,12},{12,8},{1,5},{5,1},{9,13},{13,9},{2,6},{6,2},{1... | collective-permute-start | bytes 393224 | tf_op jit(solution)/shard_map/ppermute | solution.py:636
  54.7 4.8 %collective-permute-start.8 = (f32[16,16,128]{2,1,0:T(8,128)S(1)}, f32[16,16,128]{2,1,0:T(8,128)S(1)}, u32[]{:S(2)}, u32[]{:S(2)}) collective-permute-start(f32[16,16,128]{2,1,0:T(8,128)S(1)} %get-tuple-element.118), channel_id=1, source_target_pairs={{0,1},{1,0},{2,3},{3,2},{4,5},{5,4},{6,7},{7,6},{8,9},{9,8},{10,11... | collective-permute-start | bytes 393224 | tf_op jit(solution)/shard_map/ppermute | solution.py:636
  60.2 2.3 %collective-permute-done.8.refs_3_ = f32[16,16,128]{2,1,0:T(8,128)S(1)} collective-permute-done((f32[16,16,128]{2,1,0:T(8,128)S(1)}, f32[16,16,128]{2,1,0:T(8,128)S(1)}, u32[]{:S(2)}, u32[]{:S(2)}) %collective-permute-start.8) | collective-permute-done | bytes 131104 | tf_op jit(solution)/shard_map/ppermute | solution.py:636
  62.5 1.6 copy-done.11
  65.3 6.5 %nodes1_back.1 = (f32[16,16,16,128]{3,2,1,0:T(8,128)S(1)}, f32[16,16,16,128]{3,2,1,0:T(8,128)S(1)}, f32[1,392,128]{2,1,0:T(8,128)S(1)}, f32[16,16,128]{2,1,0:T(8...) custom-call(s32[4]{0:T(128)S(1)} %pad_add_fusion.sc.sc_ref, ...), custom_call_target="tpu_custom_call" | custom-call | flops 1342177280 | bytes 10229776 | tf_op jit(solution)/shard_map/nodes1_back/pallas_call | solution.py:514
  74.4 1.5 collective-permute-start.10
  76.6 5.9 %collective-permute-start.13 = (f32[2,2,56,128]{3,2,1,0:T(8,128)}, f32[2,2,56,128]{3,2,1,0:T(8,128)}, u32[]{:S(2)}, u32[]{:S(2)}) collective-permute-start(f32[2,2,56,128]{3,2,1,0:T(8,128)} %dynamic-slice_bitcast_fusion.1), channel_id=1, source_target_pairs={{0,4},{4,0},{8,12},{12,8},{1,5},{5,1},{9,13},{13,9},{2,6},{6,2},{1... | collective-permute-start | bytes 344072 | tf_op jit(solution)/shard_map/ppermute | solution.py:559
  83.1 2.2 %collective-permute-start.11 = (f32[16,16,128]{2,1,0:T(8,128)S(1)}, f32[16,16,128]{2,1,0:T(8,128)S(1)}, u32[]{:S(2)}, u32[]{:S(2)}) collective-permute-start(f32[16,16,128]{2,1,0:T(8,128)S(1)} %get-tuple-element.129), channel_id=1, source_target_pairs={{0,4},{4,0},{8,12},{12,8},{1,5},{5,1},{9,13},{13,9},{2,6},{6,2},{1... | collective-permute-start | bytes 393224 | tf_op jit(solution)/shard_map/ppermute | solution.py:636
  88.5 1.6 collective-permute-start.16
  90.1 3.9 %collective-permute-start.14 = (f32[16,16,128]{2,1,0:T(8,128)S(1)}, f32[16,16,128]{2,1,0:T(8,128)S(1)}, u32[]{:S(2)}, u32[]{:S(2)}) collective-permute-start(f32[16,16,128]{2,1,0:T(8,128)S(1)} %get-tuple-element.136), channel_id=1, source_target_pairs={{0,1},{1,0},{2,3},{3,2},{4,5},{5,4},{6,7},{7,6},{8,9},{9,8},{10,11... | collective-permute-start | bytes 393224 | tf_op jit(solution)/shard_map/ppermute | solution.py:636
  97.0 8.0 %collective-permute-start.18 = (f32[56,128]{1,0:T(8,128)S(1)}, f32[56,128]{1,0:T(8,128)S(1)}, u32[]{:S(2)}, u32[]{:S(2)}) collective-permute-start(f32[56,128]{1,0:T(8,128)S(1)} %dynamic-slice_bitcast_fusion.5), channel_id=1, source_target_pairs={{0,8},{4,12},{8,0},{12,4},{1,9},{5,13},{9,1},{13,5},{2,10},{6,14},... | collective-permute-start | bytes 86024 | tf_op jit(solution)/shard_map/ppermute | solution.py:559
  105.0 2.8 %copy-done.5 = f32[3,16,16,16,128]{4,3,2,1,0:T(8,128)S(1)} copy-done((f32[3,16,16,16,128]{4,3,2,1,0:T(8,128)S(1)}, f32[3,16,16,16,128]{4,3,2,1,0:T(8,128)}, u32[]{:S(2)}) %copy-start.5) | copy-done | bytes 6291480
  107.7 1.6 copy-done.17
  109.3 1.6 copy-done.19
  110.9 1.6 copy-done.21
  115.0 8.1 %edges1_back_nodes0_back.1 = (f32[16,16,16,128]{3,2,1,0:T(8,128)S(1)}, f32[16,16,16,128]{3,2,1,0:T(8,128)S(1)}, f32[1,528,128]{2,1,0:T(8,128)S(1)}, f32[16,16,12...) custom-call(s32[4]{0:T(128)S(1)} %pad_add_fusion.sc.sc_ref, ...), custom_call_target="tpu_custom_call" | custom-call | flops 1610612736 | bytes 22882320 | tf_op jit(solution)/shard_map/edges1_back_nodes0_back/pallas_call | solution.py:514
  126.4 4.3 %collective-permute-done.17.refs_0_ = f32[16,16,128]{2,1,0:T(8,128)S(1)} collective-permute-done((f32[16,16,128]{2,1,0:T(8,128)S(1)}, f32[16,16,128]{2,1,0:T(8,128)S(1)}, u32[]{:S(2)}, u32[]{:S(2)}) %collective-permute-start.17) | collective-permute-done | bytes 131104 | tf_op jit(solution)/shard_map/ppermute | solution.py:636
  131.3 4.0 %collective-permute-start.21 = (f32[56,128]{1,0:T(8,128)S(1)}, f32[56,128]{1,0:T(8,128)S(1)}, u32[]{:S(2)}, u32[]{:S(2)}) collective-permute-start(f32[56,128]{1,0:T(8,128)S(1)} %bitcast_add_fusion.5), channel_id=1, source_target_pairs={{0,1},{1,0},{2,3},{3,2},{4,5},{5,4},{6,7},{7,6},{8,9},{9,8},{10,11... | collective-permute-start | bytes 86024 | tf_op jit(solution)/shard_map/ppermute | solution.py:534
  138.4 3.5 %collective-permute-start.25 = (f32[56,128]{1,0:T(8,128)S(1)}, f32[56,128]{1,0:T(8,128)S(1)}, u32[]{:S(2)}, u32[]{:S(2)}) collective-permute-start(f32[56,128]{1,0:T(8,128)S(1)} %add.116), channel_id=1, source_target_pairs={{0,2},{1,3},{2,0},{3,1},{4,6},{5,7},{6,4},{7,5},{8,10},{9,11},{10,... | collective-permute-start | bytes 86024 | tf_op jit(solution)/shard_map/ppermute | solution.py:534
  143.8 3.1 %collective-permute-done.23.refs_3_ = f32[16,16,128]{2,1,0:T(8,128)S(1)} collective-permute-done((f32[16,16,128]{2,1,0:T(8,128)S(1)}, f32[16,16,128]{2,1,0:T(8,128)S(1)}, u32[]{:S(2)}, u32[]{:S(2)}) %collective-permute-start.23) | collective-permute-done | bytes 131104 | tf_op jit(solution)/shard_map/ppermute | solution.py:636
  146.9 2.9 %collective-permute-start.27 = (f32[56,128]{1,0:T(8,128)S(1)}, f32[56,128]{1,0:T(8,128)S(1)}, u32[]{:S(2)}, u32[]{:S(2)}) collective-permute-start(f32[56,128]{1,0:T(8,128)S(1)} %add.118), channel_id=1, source_target_pairs={{0,8},{4,12},{8,0},{12,4},{1,9},{5,13},{9,1},{13,5},{2,10},{6,14},... | collective-permute-start | bytes 86024 | tf_op jit(solution)/shard_map/ppermute | solution.py:565
  149.9 2.8 %copy-done.3 = f32[3,16,16,16,128]{4,3,2,1,0:T(8,128)S(1)} copy-done((f32[3,16,16,16,128]{4,3,2,1,0:T(8,128)S(1)}, f32[3,16,16,16,128]{4,3,2,1,0:T(8,128)}, u32[]{:S(2)}) %copy-start.3) | copy-done | bytes 6291480
  152.7 1.6 copy-done.13
  154.2 1.6 copy-done.15
  155.8 6.5 %edges0_back.1 = (bf16[16,16,16,128]{3,2,1,0:T(8,128)(2,1)}, f32[1,136,128]{2,1,0:T(8,128)S(1)}) custom-call(s32[4]{0:T(128)S(1)} %pad_add_fusion.sc.sc_ref, bf16[2,2,128,128]{3,2,1,0:T(8,128)(2,1)S(1)} %copy-done.7, bf16[2,256,128]{2,1,0:T(8,128)(2,1)S(1)} %copy-done.9, bf16[2,128,128]{2,1,0:T(8,128)(2,1)S(1)} %copy-done.23, f32[2,2,128]{2,1,0:T(2,128)S(1)} %copy-done.32, ...), custom_call_target="tpu_custom_call" | custom-call | flops 805306368 | bytes 13637648 | tf_op jit(solution)/shard_map/edges0_back/pallas_call | solution.py:514
  162.4 1.6 collective-permute-start.30
  163.9 3.8 %collective-permute-start.29 = (f32[136,128]{1,0:T(8,128)S(1)}, f32[136,128]{1,0:T(8,128)S(1)}, u32[]{:S(2)}, u32[]{:S(2)}) collective-permute-start(f32[136,128]{1,0:T(8,128)S(1)} %bitcast.56), channel_id=1, source_target_pairs={{0,2},{1,3},{2,0},{3,1},{4,6},{5,7},{6,4},{7,5},{8,10},{9,11},{10,... | collective-permute-start | bytes 208904 | tf_op jit(solution)/shard_map/ppermute | solution.py:534
  167.8 2.3 %collective-permute-done.29 = f32[136,128]{1,0:T(8,128)S(1)} collective-permute-done((f32[136,128]{1,0:T(8,128)S(1)}, f32[136,128]{1,0:T(8,128)S(1)}, u32[]{:S(2)}, u32[]{:S(2)}) %collective-permute-start.29) | collective-permute-done | bytes 69664 | tf_op jit(solution)/shard_map/ppermute | solution.py:534
  170.1 3.0 %collective-permute-start.31 = (f32[72,128]{1,0:T(8,128)S(1)}, f32[72,128]{1,0:T(8,128)S(1)}, u32[]{:S(2)}, u32[]{:S(2)}) collective-permute-start(f32[72,128]{1,0:T(8,128)S(1)} %bitcast_add_fusion.4), channel_id=1, source_target_pairs={{0,1},{1,0},{2,3},{3,2},{4,5},{5,4},{6,7},{7,6},{8,9},{9,8},{10,11... | collective-permute-start | bytes 110600 | tf_op jit(solution)/shard_map/ppermute | solution.py:534
  173.2 2.1 %collective-permute-done.31 = f32[72,128]{1,0:T(8,128)S(1)} collective-permute-done((f32[72,128]{1,0:T(8,128)S(1)}, f32[72,128]{1,0:T(8,128)S(1)}, u32[]{:S(2)}, u32[]{:S(2)}) %collective-permute-start.31) | collective-permute-done | bytes 36896 | tf_op jit(solution)/shard_map/ppermute | solution.py:534
  175.3 1.9 collective-permute-start.32
  177.2 1.5 collective-permute-start.34
  178.7 3.4 %collective-permute-done.34 = f32[72,128]{1,0:T(8,128)S(1)} collective-permute-done((f32[72,128]{1,0:T(8,128)S(1)}, f32[72,128]{1,0:T(8,128)S(1)}, u32[]{:S(2)}, u32[]{:S(2)}) %collective-permute-start.34) | collective-permute-done | bytes 36896 | tf_op jit(solution)/shard_map/ppermute | solution.py:534
  182.1 2.0 %collective-permute-start.36 = (f32[72,128]{1,0:T(8,128)S(1)}, f32[72,128]{1,0:T(8,128)S(1)}, u32[]{:S(2)}, u32[]{:S(2)}) collective-permute-start(f32[72,128]{1,0:T(8,128)S(1)} %add.124), channel_id=1, source_target_pairs={{0,8},{4,12},{8,0},{12,4},{1,9},{5,13},{9,1},{13,5},{2,10},{6,14},... | collective-permute-start | bytes 110600 | tf_op jit(solution)/shard_map/ppermute | solution.py:565
  184.3 1.8 collective-permute-done.36
  186.1 2.4 %collective-permute-done.35 = f32[136,128]{1,0:T(8,128)S(1)} collective-permute-done((f32[136,128]{1,0:T(8,128)S(1)}, f32[136,128]{1,0:T(8,128)S(1)}, u32[]{:S(2)}, u32[]{:S(2)}) %collective-permute-start.35) | collective-permute-done | bytes 69664 | tf_op jit(solution)/shard_map/ppermute | solution.py:534
  190.4 2.5 %collective-permute-done.38 = f32[2,72,128]{2,1,0:T(8,128)S(1)} collective-permute-done((f32[2,72,128]{2,1,0:T(8,128)S(1)}, f32[2,72,128]{2,1,0:T(8,128)S(1)}, u32[]{:S(2)}, u32[]{:S(2)}) %collective-permute-start.38) | collective-permute-done | bytes 73760 | tf_op jit(solution)/shard_map/ppermute | solution.py:565
  193.7 4.0 %collective-permute-done.40 = f32[136,128]{1,0:T(8,128)S(1)} collective-permute-done((f32[136,128]{1,0:T(8,128)S(1)}, f32[136,128]{1,0:T(8,128)S(1)}, u32[]{:S(2)}, u32[]{:S(2)}) %collective-permute-start.40) | collective-permute-done | bytes 69664 | tf_op jit(solution)/shard_map/ppermute | solution.py:534
  (148 shorter events, 42.2 us)
Async XLA Ops:
  5.9 21.8 %copy-start.1 = (bf16[16,16,2,8,128]{4,3,2,1,0:T(8,128)(2,1)S(1)}, bf16[16,16,2,8,128]{4,3,2,1,0:T(8,128)(2,1)}, u32[]{:S(2)}) copy-start(bf16[16,16,2,8,128]{4,3,2,1,0:T(8,128)(2,1)} %param.7) | copy-start | bytes 3145732
  5.9 21.8 %copy-start.7 = (bf16[2,2,128,128]{3,2,1,0:T(8,128)(2,1)S(1)}, bf16[2,2,128,128]{3,2,1,0:T(8,128)(2,1)}, u32[]{:S(2)}) copy-start(bf16[2,2,128,128]{3,2,1,0:T(8,128)(2,1)} %edge_w.11) | copy-start | bytes 393220
  5.9 21.9 %copy-start.9 = (bf16[2,256,128]{2,1,0:T(8,128)(2,1)S(1)}, bf16[2,256,128]{2,1,0:T(8,128)(2,1)}, u32[]{:S(2)}) copy-start(bf16[2,256,128]{2,1,0:T(8,128)(2,1)} %node_in.11) | copy-start | bytes 393220
  13.6 6.4 %collective-permute-start = (f32[16,16,128]{2,1,0:T(8,128)S(1)}, f32[16,16,128]{2,1,0:T(8,128)S(1)}, u32[]{:S(2)}, u32[]{:S(2)}) collective-permute-start(f32[16,16,128]{2,1,0:T(8,128)S(1)} %get-tuple-element.100), channel_id=1, source_target_pairs={{0,16},{16,0},{1,17},{17,1},{2,18},{18,2},{3,19},{19,3},{4,20},{20... | collective-permute-start | bytes 393224 | tf_op jit(solution)/shard_map/ppermute | solution.py:636
  20.6 1.4 collective-permute-start.1
  20.7 1.3 collective-permute-start.2
  22.7 5.0 %collective-permute-start.3 = (f32[16,16,128]{2,1,0:T(8,128)S(1)}, f32[16,16,128]{2,1,0:T(8,128)S(1)}, u32[]{:S(2)}, u32[]{:S(2)}) collective-permute-start(f32[16,16,128]{2,1,0:T(8,128)S(1)} %get-tuple-element.107), channel_id=1, source_target_pairs={{0,1},{1,0},{2,3},{3,2},{4,5},{5,4},{6,7},{7,6},{8,9},{9,8},{10,11... | collective-permute-start | bytes 393224 | tf_op jit(solution)/shard_map/ppermute | solution.py:636
  24.6 3.1 %collective-permute-start.4 = (f32[16,16,128]{2,1,0:T(8,128)S(1)}, f32[16,16,128]{2,1,0:T(8,128)S(1)}, u32[]{:S(2)}, u32[]{:S(2)}) collective-permute-start(f32[16,16,128]{2,1,0:T(8,128)S(1)} %get-tuple-element.108), channel_id=1, source_target_pairs={{1,2},{2,1},{5,6},{6,5},{9,10},{10,9},{13,14},{14,13},{17,18},{18,... | collective-permute-start | bytes 393224 | tf_op jit(solution)/shard_map/ppermute | solution.py:636
  27.8 34.7 %copy-start.23 = (bf16[2,128,128]{2,1,0:T(8,128)(2,1)S(1)}, bf16[2,128,128]{2,1,0:T(8,128)(2,1)}, u32[]{:S(2)}) copy-start(bf16[2,128,128]{2,1,0:T(8,128)(2,1)} %node_out.9) | copy-start | bytes 196612
  27.8 34.7 %copy-start.32 = (f32[2,2,128]{2,1,0:T(2,128)S(1)}, f32[2,2,128]{2,1,0:T(2,128)}, u32[]{:S(2)}) copy-start(f32[2,2,128]{2,1,0:T(2,128)} %biases.9) | copy-start | bytes 6148
  43.9 5.0 %collective-permute-start.5 = (f32[16,16,128]{2,1,0:T(8,128)S(1)}, f32[16,16,128]{2,1,0:T(8,128)S(1)}, u32[]{:S(2)}, u32[]{:S(2)}) collective-permute-start(f32[16,16,128]{2,1,0:T(8,128)S(1)} %get-tuple-element.111), channel_id=1, source_target_pairs={{0,16},{16,0},{1,17},{17,1},{2,18},{18,2},{3,19},{19,3},{4,20},{20... | collective-permute-start | bytes 393224 | tf_op jit(solution)/shard_map/ppermute | solution.py:636
  49.4 4.6 %collective-permute-start.6 = (f32[16,16,128]{2,1,0:T(8,128)S(1)}, f32[16,16,128]{2,1,0:T(8,128)S(1)}, u32[]{:S(2)}, u32[]{:S(2)}) collective-permute-start(f32[16,16,128]{2,1,0:T(8,128)S(1)} %get-tuple-element.114), channel_id=1, source_target_pairs={{0,4},{4,0},{8,12},{12,8},{1,5},{5,1},{9,13},{13,9},{2,6},{6,2},{1... | collective-permute-start | bytes 393224 | tf_op jit(solution)/shard_map/ppermute | solution.py:636
  53.0 1.0 collective-permute-start.7
  54.7 7.8 %collective-permute-start.8 = (f32[16,16,128]{2,1,0:T(8,128)S(1)}, f32[16,16,128]{2,1,0:T(8,128)S(1)}, u32[]{:S(2)}, u32[]{:S(2)}) collective-permute-start(f32[16,16,128]{2,1,0:T(8,128)S(1)} %get-tuple-element.118), channel_id=1, source_target_pairs={{0,1},{1,0},{2,3},{3,2},{4,5},{5,4},{6,7},{7,6},{8,9},{9,8},{10,11... | collective-permute-start | bytes 393224 | tf_op jit(solution)/shard_map/ppermute | solution.py:636
  59.5 3.0 %collective-permute-start.9 = (f32[16,16,128]{2,1,0:T(8,128)S(1)}, f32[16,16,128]{2,1,0:T(8,128)S(1)}, u32[]{:S(2)}, u32[]{:S(2)}) collective-permute-start(f32[16,16,128]{2,1,0:T(8,128)S(1)} %get-tuple-element.119), channel_id=1, source_target_pairs={{1,2},{2,1},{5,6},{6,5},{9,10},{10,9},{13,14},{14,13},{17,18},{18,... | collective-permute-start | bytes 393224 | tf_op jit(solution)/shard_map/ppermute | solution.py:636
  74.4 8.1 %collective-permute-start.10 = (f32[16,16,128]{2,1,0:T(8,128)}, f32[16,16,128]{2,1,0:T(8,128)S(1)}, u32[]{:S(2)}, u32[]{:S(2)}) collective-permute-start(f32[16,16,128]{2,1,0:T(8,128)} %get-tuple-element.126), channel_id=1, source_target_pairs={{0,16},{16,0},{1,17},{17,1},{2,18},{18,2},{3,19},{19,3},{4,20},{20... | collective-permute-start | bytes 393224 | tf_op jit(solution)/shard_map/ppermute | solution.py:636
  76.6 9.3 %collective-permute-start.13 = (f32[2,2,56,128]{3,2,1,0:T(8,128)}, f32[2,2,56,128]{3,2,1,0:T(8,128)}, u32[]{:S(2)}, u32[]{:S(2)}) collective-permute-start(f32[2,2,56,128]{3,2,1,0:T(8,128)} %dynamic-slice_bitcast_fusion.1), channel_id=1, source_target_pairs={{0,4},{4,0},{8,12},{12,8},{1,5},{5,1},{9,13},{13,9},{2,6},{6,2},{1... | collective-permute-start | bytes 344072 | tf_op jit(solution)/shard_map/ppermute | solution.py:559
  83.1 3.8 %collective-permute-start.11 = (f32[16,16,128]{2,1,0:T(8,128)S(1)}, f32[16,16,128]{2,1,0:T(8,128)S(1)}, u32[]{:S(2)}, u32[]{:S(2)}) collective-permute-start(f32[16,16,128]{2,1,0:T(8,128)S(1)} %get-tuple-element.129), channel_id=1, source_target_pairs={{0,4},{4,0},{8,12},{12,8},{1,5},{5,1},{9,13},{13,9},{2,6},{6,2},{1... | collective-permute-start | bytes 393224 | tf_op jit(solution)/shard_map/ppermute | solution.py:636
  85.3 1.6 collective-permute-start.12
  88.5 6.3 %collective-permute-start.16 = (f32[2,56,128]{2,1,0:T(8,128)S(1)}, f32[2,56,128]{2,1,0:T(8,128)S(1)}, u32[]{:S(2)}, u32[]{:S(2)}) collective-permute-start(f32[2,56,128]{2,1,0:T(8,128)S(1)} %dynamic-slice_bitcast_fusion.3), channel_id=1, source_target_pairs={{0,16},{16,0},{1,17},{17,1},{2,18},{18,2},{3,19},{19,3},{4,20},{20... | collective-permute-start | bytes 172040 | tf_op jit(solution)/shard_map/ppermute | solution.py:559
  90.1 6.9 %collective-permute-start.14 = (f32[16,16,128]{2,1,0:T(8,128)S(1)}, f32[16,16,128]{2,1,0:T(8,128)S(1)}, u32[]{:S(2)}, u32[]{:S(2)}) collective-permute-start(f32[16,16,128]{2,1,0:T(8,128)S(1)} %get-tuple-element.136), channel_id=1, source_target_pairs={{0,1},{1,0},{2,3},{3,2},{4,5},{5,4},{6,7},{7,6},{8,9},{9,8},{10,11... | collective-permute-start | bytes 393224 | tf_op jit(solution)/shard_map/ppermute | solution.py:636
  94.0 2.9 %collective-permute-start.15 = (f32[16,16,128]{2,1,0:T(8,128)S(1)}, f32[16,16,128]{2,1,0:T(8,128)S(1)}, u32[]{:S(2)}, u32[]{:S(2)}) collective-permute-start(f32[16,16,128]{2,1,0:T(8,128)S(1)} %get-tuple-element.137), channel_id=1, source_target_pairs={{1,2},{2,1},{5,6},{6,5},{9,10},{10,9},{13,14},{14,13},{17,18},{18,... | collective-permute-start | bytes 393224 | tf_op jit(solution)/shard_map/ppermute | solution.py:636
  97.0 29.4 %collective-permute-start.18 = (f32[56,128]{1,0:T(8,128)S(1)}, f32[56,128]{1,0:T(8,128)S(1)}, u32[]{:S(2)}, u32[]{:S(2)}) collective-permute-start(f32[56,128]{1,0:T(8,128)S(1)} %dynamic-slice_bitcast_fusion.5), channel_id=1, source_target_pairs={{0,8},{4,12},{8,0},{12,4},{1,9},{5,13},{9,1},{13,5},{2,10},{6,14},... | collective-permute-start | bytes 86024 | tf_op jit(solution)/shard_map/ppermute | solution.py:559
  104.9 2.8 %copy-start.5 = (f32[3,16,16,16,128]{4,3,2,1,0:T(8,128)S(1)}, f32[3,16,16,16,128]{4,3,2,1,0:T(8,128)}, u32[]{:S(2)}) copy-start(f32[3,16,16,16,128]{4,3,2,1,0:T(8,128)} %copy-done.4) | copy-start | bytes 18874372
  125.7 5.0 %collective-permute-start.17 = (f32[16,16,128]{2,1,0:T(8,128)S(1)}, f32[16,16,128]{2,1,0:T(8,128)S(1)}, u32[]{:S(2)}, u32[]{:S(2)}) collective-permute-start(f32[16,16,128]{2,1,0:T(8,128)S(1)} %get-tuple-element.144), channel_id=1, source_target_pairs={{0,16},{16,0},{1,17},{17,1},{2,18},{18,2},{3,19},{19,3},{4,20},{20... | collective-permute-start | bytes 393224 | tf_op jit(solution)/shard_map/ppermute | solution.py:636
  126.3 9.6 %collective-permute-start.22 = (f32[2,2,72,128]{3,2,1,0:T(8,128)S(1)}, f32[2,2,72,128]{3,2,1,0:T(8,128)S(1)}, u32[]{:S(2)}, u32[]{:S(2)}) collective-permute-start(f32[2,2,72,128]{3,2,1,0:T(8,128)S(1)} %dynamic-slice_bitcast_fusion), channel_id=1, source_target_pairs={{0,4},{4,0},{8,12},{12,8},{1,5},{5,1},{9,13},{13,9},{2,6},{6,2},{1... | collective-permute-start | bytes 442376 | tf_op jit(solution)/shard_map/ppermute | solution.py:559
  131.3 5.8 %collective-permute-start.21 = (f32[56,128]{1,0:T(8,128)S(1)}, f32[56,128]{1,0:T(8,128)S(1)}, u32[]{:S(2)}, u32[]{:S(2)}) collective-permute-start(f32[56,128]{1,0:T(8,128)S(1)} %bitcast_add_fusion.5), channel_id=1, source_target_pairs={{0,1},{1,0},{2,3},{3,2},{4,5},{5,4},{6,7},{7,6},{8,9},{9,8},{10,11... | collective-permute-start | bytes 86024 | tf_op jit(solution)/shard_map/ppermute | solution.py:534
  135.2 1.9 collective-permute-start.19
  135.3 1.9 collective-permute-start.20
  137.8 5.9 %collective-permute-start.26 = (f32[2,72,128]{2,1,0:T(8,128)S(1)}, f32[2,72,128]{2,1,0:T(8,128)S(1)}, u32[]{:S(2)}, u32[]{:S(2)}) collective-permute-start(f32[2,72,128]{2,1,0:T(8,128)S(1)} %dynamic-slice_bitcast_fusion.2), channel_id=1, source_target_pairs={{0,16},{16,0},{1,17},{17,1},{2,18},{18,2},{3,19},{19,3},{4,20},{20... | collective-permute-start | bytes 221192 | tf_op jit(solution)/shard_map/ppermute | solution.py:559
  138.4 5.3 %collective-permute-start.25 = (f32[56,128]{1,0:T(8,128)S(1)}, f32[56,128]{1,0:T(8,128)S(1)}, u32[]{:S(2)}, u32[]{:S(2)}) collective-permute-start(f32[56,128]{1,0:T(8,128)S(1)} %add.116), channel_id=1, source_target_pairs={{0,2},{1,3},{2,0},{3,1},{4,6},{5,7},{6,4},{7,5},{8,10},{9,11},{10,... | collective-permute-start | bytes 86024 | tf_op jit(solution)/shard_map/ppermute | solution.py:534
  141.9 5.0 %collective-permute-start.23 = (f32[16,16,128]{2,1,0:T(8,128)S(1)}, f32[16,16,128]{2,1,0:T(8,128)S(1)}, u32[]{:S(2)}, u32[]{:S(2)}) collective-permute-start(f32[16,16,128]{2,1,0:T(8,128)S(1)} %get-tuple-element.160), channel_id=1, source_target_pairs={{0,1},{1,0},{2,3},{3,2},{4,5},{5,4},{6,7},{7,6},{8,9},{9,8},{10,11... | collective-permute-start | bytes 393224 | tf_op jit(solution)/shard_map/ppermute | solution.py:636
  141.9 5.0 %collective-permute-start.24 = (f32[16,16,128]{2,1,0:T(8,128)S(1)}, f32[16,16,128]{2,1,0:T(8,128)S(1)}, u32[]{:S(2)}, u32[]{:S(2)}) collective-permute-start(f32[16,16,128]{2,1,0:T(8,128)S(1)} %get-tuple-element.161), channel_id=1, source_target_pairs={{1,2},{2,1},{5,6},{6,5},{9,10},{10,9},{13,14},{14,13},{17,18},{18,... | collective-permute-start | bytes 393224 | tf_op jit(solution)/shard_map/ppermute | solution.py:636
  146.9 15.5 %collective-permute-start.27 = (f32[56,128]{1,0:T(8,128)S(1)}, f32[56,128]{1,0:T(8,128)S(1)}, u32[]{:S(2)}, u32[]{:S(2)}) collective-permute-start(f32[56,128]{1,0:T(8,128)S(1)} %add.118), channel_id=1, source_target_pairs={{0,8},{4,12},{8,0},{12,4},{1,9},{5,13},{9,1},{13,5},{2,10},{6,14},... | collective-permute-start | bytes 86024 | tf_op jit(solution)/shard_map/ppermute | solution.py:565
  149.8 14.1 %collective-permute-start.28 = (f32[72,128]{1,0:T(8,128)S(1)}, f32[72,128]{1,0:T(8,128)S(1)}, u32[]{:S(2)}, u32[]{:S(2)}) collective-permute-start(f32[72,128]{1,0:T(8,128)S(1)} %dynamic-slice_bitcast_fusion.4), channel_id=1, source_target_pairs={{0,8},{4,12},{8,0},{12,4},{1,9},{5,13},{9,1},{13,5},{2,10},{6,14},... | collective-permute-start | bytes 110600 | tf_op jit(solution)/shard_map/ppermute | solution.py:559
  149.9 2.8 %copy-start.3 = (f32[3,16,16,16,128]{4,3,2,1,0:T(8,128)S(1)}, f32[3,16,16,16,128]{4,3,2,1,0:T(8,128)}, u32[]{:S(2)}) copy-start(f32[3,16,16,16,128]{4,3,2,1,0:T(8,128)} %copy-done.2) | copy-start | bytes 18874372
  162.4 5.4 %collective-permute-start.30 = (f32[2,56,128]{2,1,0:T(8,128)S(1)}, f32[2,56,128]{2,1,0:T(8,128)S(1)}, u32[]{:S(2)}, u32[]{:S(2)}) collective-permute-start(f32[2,56,128]{2,1,0:T(8,128)S(1)} %maximum_select_fusion.5), channel_id=1, source_target_pairs={{0,16},{16,0},{1,17},{17,1},{2,18},{18,2},{3,19},{19,3},{4,20},{20... | collective-permute-start | bytes 172040 | tf_op jit(solution)/shard_map/ppermute | solution.py:565
  163.9 6.1 %collective-permute-start.29 = (f32[136,128]{1,0:T(8,128)S(1)}, f32[136,128]{1,0:T(8,128)S(1)}, u32[]{:S(2)}, u32[]{:S(2)}) collective-permute-start(f32[136,128]{1,0:T(8,128)S(1)} %bitcast.56), channel_id=1, source_target_pairs={{0,2},{1,3},{2,0},{3,1},{4,6},{5,7},{6,4},{7,5},{8,10},{9,11},{10,... | collective-permute-start | bytes 208904 | tf_op jit(solution)/shard_map/ppermute | solution.py:534
  170.1 12.0 %collective-permute-start.33 = (f32[2,2,56,128]{3,2,1,0:T(8,128)S(1)}, f32[2,2,56,128]{3,2,1,0:T(8,128)S(1)}, u32[]{:S(2)}, u32[]{:S(2)}) collective-permute-start(f32[2,2,56,128]{3,2,1,0:T(8,128)S(1)} %maximum_select_fusion.3), channel_id=1, source_target_pairs={{0,4},{4,0},{8,12},{12,8},{1,5},{5,1},{9,13},{13,9},{2,6},{6,2},{1... | collective-permute-start | bytes 344072 | tf_op jit(solution)/shard_map/ppermute | solution.py:565
  170.1 5.1 %collective-permute-start.31 = (f32[72,128]{1,0:T(8,128)S(1)}, f32[72,128]{1,0:T(8,128)S(1)}, u32[]{:S(2)}, u32[]{:S(2)}) collective-permute-start(f32[72,128]{1,0:T(8,128)S(1)} %bitcast_add_fusion.4), channel_id=1, source_target_pairs={{0,1},{1,0},{2,3},{3,2},{4,5},{5,4},{6,7},{7,6},{8,9},{9,8},{10,11... | collective-permute-start | bytes 110600 | tf_op jit(solution)/shard_map/ppermute | solution.py:534
  175.3 6.8 %collective-permute-start.32 = (f32[136,128]{1,0:T(8,128)S(1)}, f32[136,128]{1,0:T(8,128)S(1)}, u32[]{:S(2)}, u32[]{:S(2)}) collective-permute-start(f32[136,128]{1,0:T(8,128)S(1)} %add.121), channel_id=1, source_target_pairs={{0,1},{1,0},{2,3},{3,2},{4,5},{5,4},{6,7},{7,6},{8,9},{9,8},{10,11... | collective-permute-start | bytes 208904 | tf_op jit(solution)/shard_map/ppermute | solution.py:534
  177.2 4.9 %collective-permute-start.34 = (f32[72,128]{1,0:T(8,128)S(1)}, f32[72,128]{1,0:T(8,128)S(1)}, u32[]{:S(2)}, u32[]{:S(2)}) collective-permute-start(f32[72,128]{1,0:T(8,128)S(1)} %add.122), channel_id=1, source_target_pairs={{0,2},{1,3},{2,0},{3,1},{4,6},{5,7},{6,4},{7,5},{8,10},{9,11},{10,... | collective-permute-start | bytes 110600 | tf_op jit(solution)/shard_map/ppermute | solution.py:534
  182.1 4.0 %collective-permute-start.36 = (f32[72,128]{1,0:T(8,128)S(1)}, f32[72,128]{1,0:T(8,128)S(1)}, u32[]{:S(2)}, u32[]{:S(2)}) collective-permute-start(f32[72,128]{1,0:T(8,128)S(1)} %add.124), channel_id=1, source_target_pairs={{0,8},{4,12},{8,0},{12,4},{1,9},{5,13},{9,1},{13,5},{2,10},{6,14},... | collective-permute-start | bytes 110600 | tf_op jit(solution)/shard_map/ppermute | solution.py:565
  184.1 4.4 %collective-permute-start.35 = (f32[136,128]{1,0:T(8,128)S(1)}, f32[136,128]{1,0:T(8,128)S(1)}, u32[]{:S(2)}, u32[]{:S(2)}) collective-permute-start(f32[136,128]{1,0:T(8,128)S(1)} %add.123), channel_id=1, source_target_pairs={{0,8},{4,12},{8,0},{12,4},{1,9},{5,13},{9,1},{13,5},{2,10},{6,14},... | collective-permute-start | bytes 208904 | tf_op jit(solution)/shard_map/ppermute | solution.py:534
  188.5 4.4 %collective-permute-start.38 = (f32[2,72,128]{2,1,0:T(8,128)S(1)}, f32[2,72,128]{2,1,0:T(8,128)S(1)}, u32[]{:S(2)}, u32[]{:S(2)}) collective-permute-start(f32[2,72,128]{2,1,0:T(8,128)S(1)} %maximum_select_fusion.4), channel_id=1, source_target_pairs={{0,16},{16,0},{1,17},{17,1},{2,18},{18,2},{3,19},{19,3},{4,20},{20... | collective-permute-start | bytes 221192 | tf_op jit(solution)/shard_map/ppermute | solution.py:565
  189.2 1.3 collective-permute-start.37
  193.0 4.7 %collective-permute-start.39 = (f32[2,2,72,128]{3,2,1,0:T(8,128)S(1)}, f32[2,2,72,128]{3,2,1,0:T(8,128)S(1)}, u32[]{:S(2)}, u32[]{:S(2)}) collective-permute-start(f32[2,2,72,128]{3,2,1,0:T(8,128)S(1)} %maximum_select_fusion.2), channel_id=1, source_target_pairs={{0,4},{4,0},{8,12},{12,8},{1,5},{5,1},{9,13},{13,9},{2,6},{6,2},{1... | collective-permute-start | bytes 442376 | tf_op jit(solution)/shard_map/ppermute | solution.py:565
  193.0 4.6 %collective-permute-start.40 = (f32[136,128]{1,0:T(8,128)S(1)}, f32[136,128]{1,0:T(8,128)S(1)}, u32[]{:S(2)}, u32[]{:S(2)}) collective-permute-start(f32[136,128]{1,0:T(8,128)S(1)} %add.126), channel_id=1, source_target_pairs={{0,16},{16,0},{1,17},{17,1},{2,18},{18,2},{3,19},{19,3},{4,20},{20... | collective-permute-start | bytes 208904 | tf_op jit(solution)/shard_map/ppermute | solution.py:534
  (27 other events, 37.2 us)

commit v2 on v1

--- a/solution.py
+++ b/solution.py
@@ -293,11 +293,11 @@
     shape = (CHUNK,) + sum_ref.shape[1:]
     at = pl.ds(x, CHUNK)
     dpn = (dot_rt(grad, node_out[layer]) * slope).astype(bf16)
-    grads[0, pl.ds(0, 128)] += dot_t(act, grad)
+    grads[pl.ds(0, 128)] += dot_t(act, grad)
     both = dot_t(dpn, jnp.concatenate([feat, scaled], -1))
-    grads[0, pl.ds(128, 128)] += both[:, :128]
-    grads[0, pl.ds(256, 128)] += both[:, 128:]
-    grads[0, pl.ds(384, NODES)] += jnp.sum(dpn.astype(f32).reshape(-1, NODES, 128), 0)
+    grads[pl.ds(128, 128)] += both[:, :128]
+    grads[pl.ds(256, 128)] += both[:, 128:]
+    grads[pl.ds(384, NODES)] += jnp.sum(dpn.astype(f32).reshape(-1, NODES, 128), 0)
     dx = dot_rt(dpn, node_in[layer])
     base_ref[at] = (grad.astype(f32) + dx[:, :128]).reshape(shape)
     share = scale_planes(sc_ref, inv_ref, x, dx[:, 128:].reshape(shape), sum_ref.shape[0], size_x)
@@ -357,11 +357,18 @@
     return edge_w[layer, 0] * jnp.bfloat16(0.5), 0.5 * biases[layer, pl.ds(0, 1)]
 
 
-def first_kernel(counts, sizes, sc, edge_w, node_in, node_out, biases, h, *refs):
-    weights = (edge_w, node_in, node_out, biases)
+def first_kernel(counts, sizes, sc, edge_w_in, biases_in, h_in, *refs):
     sums, slopes = refs[:2]
-    faces = refs[2:]
-    w_one, bias = half_weights(weights, 0)
+    faces, (h, edge_w, biases, sems) = refs[2:-4], refs[-4:]
+    moves = [
+        pltpu.make_async_copy(source, target, sems.at[k])
+        for k, (source, target) in enumerate(((h_in, h), (edge_w_in, edge_w), (biases_in, biases)))
+    ]
+    for move in moves:
+        move.start()
+    for move in moves:
+        move.wait()
+    w_one, bias = half_weights((edge_w, None, None, biases), 0)
     edges_forward(h, w_one, bias, sc[0], sums, slopes)
     couple_columns(sums)
     write_faces(sc, sums, faces, counts)
@@ -397,8 +404,8 @@
     weights = (edge_w, node_in, node_out, biases)
     n = sum(counts)
     halo, refs = refs[:n], refs[n:]
-    base, sums, grads = refs[:3]
-    faces, (work, inv) = refs[3:-2], refs[-2:]
+    base, sums, keep, send = refs[:4]
+    faces, (work, inv, grads) = refs[4:-3], refs[-3:]
     add_halo(sc, sums_in, halo, work, counts)
     write_inverse(sc, inv, sizes)
     grads[...] = jnp.zeros_like(grads)
@@ -415,6 +422,7 @@
     planes(h.shape[0], body)
     couple_columns(sums)
     write_faces(sc, sums, faces, counts)
+    write_halves(sc, halving_steps(sizes)[0], grads, keep, send)
 
 
 def back_to_state(counts, sc, weights, layer, sums_in, halo, h, base, slopes, work, grads, row, use):
@@ -431,13 +439,13 @@
         work[at] = dot_rt(split_cols(flat(work[at])), w_two).reshape(shape)
 
     planes(h.shape[0], to_q)
-    edges_backward(work, slopes, work, grads.at[0, pl.ds(row + 128, NODES)])
+    edges_backward(work, slopes, work, grads.at[pl.ds(row + 128, NODES)])
 
     def body(x):
         at = pl.ds(x, CHUNK)
         pair = split_cols(flat(work[at]))
         both = dot_t(flat(h[at]), pair)
-        grads[0, pl.ds(row, 128)] += both[:, :128] + both[:, 128:]
+        grads[pl.ds(row, 128)] += both[:, :128] + both[:, 128:]
         use(x, (flat(base[at]) + dot_rt(pair, w_one)).astype(bf16))
 
     planes(h.shape[0], body)
@@ -450,8 +458,8 @@
     weights = (edge_w, node_in, node_out, biases)
     n = sum(counts)
     halo, refs = refs[:n], refs[n:]
-    base, sums, grads = refs[:3]
-    faces, (work, inv) = refs[3:-2], refs[-2:]
+    base, sums, keep, send = refs[:4]
+    faces, (work, inv, grads) = refs[4:-3], refs[-3:]
     write_inverse(sc, inv, sizes)
     grads[...] = jnp.zeros_like(grads)
 
@@ -465,6 +473,7 @@
     back_to_state(counts, sc, weights, 1, sums_in, halo, h, base_in, slopes, work, grads, 384 + NODES, use)
     couple_columns(sums)
     write_faces(sc, sums, faces, counts)
+    write_halves(sc, halving_steps(sizes)[0], grads, keep, send)
 
 
 def last_kernel(counts, sizes, sc, edge_w, node_in, node_out, biases, sums_in, h, base_in, slopes, *refs):
@@ -481,25 +490,27 @@
     back_to_state(counts, sc, weights, 0, sums_in, halo, h, base_in, slopes, work, grads, 0, use)
 
 
-def finish_kernel(scale, edge_w, node_in, sum0, sum1, last, edge_grads, in_grads, out_grads, bias_grads):
+def finish_kernel(scale, last_rows, sc, edge_w, node_in, both, sum1, edge_grads, in_grads, out_grads, bias_grads):
     width = edge_w.shape[-1]
 
-    def rows_of(ref, start, count=width):
-        return ref[pl.ds(start, count)] * scale
-
-    def bias_of(ref, start):
-        return jnp.sum(rows_of(ref, start, NODES), 0, keepdims=True)
+    def rows_of(part, start, count=width):
+        ref, offset = part
+        return ref[pl.ds(offset + start, count)] * scale
+
+    def bias_of(part, start):
+        return jnp.sum(rows_of(part, start, NODES), 0, keepdims=True)
 
     end = 3 * width
+    last, sum0 = (both, 0), (both, last_rows)
     firsts = ((last, 0), (sum0, end + NODES))
-    for layer, ref in enumerate((sum0, sum1)):
-        out_grads[layer] = rows_of(ref, 0)
-        in_grads[layer, pl.ds(0, width)] = rows_of(ref, width).T
-        bias_grads[layer, pl.ds(1, 1)] = bias_of(ref, end)
+    for layer, part in enumerate((sum0, (sum1, 0))):
+        out_grads[layer] = rows_of(part, 0)
+        in_grads[layer, pl.ds(0, width)] = rows_of(part, width).T
+        bias_grads[layer, pl.ds(1, 1)] = bias_of(part, end)
         source, start = firsts[layer]
         edge_grads[layer, 0] = rows_of(source, start)
         bias_grads[layer, pl.ds(0, 1)] = bias_of(source, start + width)
-        mixed = rows_of(ref, 2 * width).T
+        mixed = rows_of(part, 2 * width).T
         high = mixed.astype(bf16)
         low = (mixed - high.astype(f32)).astype(bf16)
         lower = node_in[layer, pl.ds(width, width)]
@@ -508,14 +519,14 @@
         in_grads[layer, pl.ds(width, width)] = dot_t(w_two, high) + dot_t(w_two, low)
 
 
-def call(kernel, name, inputs, outs, scratch=(), flops=0):
+def call(kernel, name, inputs, outs, scratch=(), flops=0, where=VM):
     total = sum(math.prod(o.shape) * o.dtype.itemsize for o in outs)
     total += sum(math.prod(i.shape) * i.dtype.itemsize for i in inputs)
     return pl.pallas_call(
         kernel,
         name=name,
         out_shape=tuple(outs),
-        in_specs=[SM] + [VM] * (len(inputs) - 1),
+        in_specs=[SM] + [where] * (len(inputs) - 1),
         out_specs=tuple([VM] * len(outs)),
         scratch_shapes=list(scratch),
         compiler_params=pltpu.CompilerParams(vmem_limit_bytes=VMEM_LIMIT),
@@ -527,11 +538,6 @@
     return [
         pair for low in range(kind, size - 1, 2) for pair in ((low, low + 1), (low + 1, low))
     ]
-
-
-def double(value, axis, hop):
-    size = lax.axis_size(axis)
-    return value + lax.ppermute(value, axis, [(i, i ^ hop) for i in range(size)])
 
 
 def hops(size):
@@ -543,60 +549,125 @@
     return found
 
 
-def sum_steps(value):
-    steps = [("gy", 1)] + [("gx", hop) for hop in hops(lax.axis_size("gx"))]
-    steps += [("gy", hop) for hop in hops(lax.axis_size("gy"))[1:]]
-    steps = [step for step in steps if lax.axis_size(step[0]) > 1]
-    rows, width = value.shape
-    unit = NODES << len(steps)
-    padded = -(-rows // unit) * unit
-    value = jnp.pad(value, ((0, padded - rows), (0, 0))).reshape((2,) * len(steps) + (-1, width))
-    for axis, hop in steps:
-        size = lax.axis_size(axis)
-        bit = (lax.axis_index(axis) // hop) % 2
-        keep = lax.dynamic_index_in_dim(value, bit, 0, keepdims=False)
-        send = lax.dynamic_index_in_dim(value, 1 - bit, 0, keepdims=False)
-        value = yield keep + lax.ppermute(send, axis, [(i, i ^ hop) for i in range(size)])
-    for hop in hops(lax.axis_size("gz")):
-        value = yield double(value, "gz", hop)
-    for axis, hop in reversed(steps):
-        size = lax.axis_size(axis)
-        bit = (lax.axis_index(axis) // hop) % 2
-        other = lax.ppermute(value, axis, [(i, i ^ hop) for i in range(size)])
-        value = yield jnp.where(bit == 0, jnp.stack([value, other]), jnp.stack([other, value]))
-    yield value.reshape(padded, width)[:rows]
+def halving_steps(sizes):
+    steps = [(1, hop) for hop in hops(sizes[1])[:1]]
+    steps += [(0, hop) for hop in hops(sizes[0])]
+    return steps + [(1, hop) for hop in hops(sizes[1])[1:]]
+
+
+def padded_rows(rows, sizes):
+    unit = NODES << len(halving_steps(sizes))
+    return -(-rows // unit) * unit
+
+
+def bit_of(sc_ref, step):
+    axis, hop = step
+    return (sc_ref[1 + axis] // hop) % 2
+
+
+def write_halves(sc_ref, step, from_ref, keep, send):
+    half = keep.shape[0]
+    bit = bit_of(sc_ref, step)
+    keep[...] = from_ref[pl.ds(pl.multiple_of(bit * half, NODES), half)]
+    send[...] = from_ref[pl.ds(pl.multiple_of((1 - bit) * half, NODES), half)]
+
+
+def halve_kernel(step, sc, keep_in, got, keep, send, total):
+    total[...] = keep_in[...] + got[...]
+    write_halves(sc, step, total, keep, send)
+
+
+def add_kernel(sc, left, right, out):
+    out[...] = left[...] + right[...]
+
+
+def join_kernel_of(step, start, sc, value, got, out):
+    half = value.shape[0] - start
+    bit = bit_of(sc, step)
+    if start:
+        out[pl.ds(0, start)] = value[pl.ds(0, start)] + got[pl.ds(0, start)]
+    out[pl.ds(pl.multiple_of(start + bit * half, NODES), half)] = value[pl.ds(start, half)]
+    out[pl.ds(pl.multiple_of(start + (1 - bit) * half, NODES), half)] = got[pl.ds(start, half)]
+
+
+def stack_kernel(sc, first, left, right, out):
+    rows = first.shape[0]
+    out[pl.ds(0, rows)] = first[...]
+    out[pl.ds(rows, left.shape[0])] = left[...] + right[...]
+
+
+def swap(value, step):
+    axis = ("gx", "gy", "gz")[step[0]]
+    return lax.ppermute(value, axis, [(i, i ^ step[1]) for i in range(lax.axis_size(axis))])
+
+
+def rows_like(rows, width=128):
+    return jax.ShapeDtypeStruct((rows, width), f32)
+
+
+def halve(sc, sizes, keep, send):
+    steps = halving_steps(sizes)
+    got = swap(send, steps[0])
+    for step in steps[1:]:
+        keep, got = yield keep, got
+        half = rows_like(keep.shape[0] // 2)
+        keep, send = call(
+            functools.partial(halve_kernel, step), "halve", (sc, keep, got), [half, half],
+            [pltpu.VMEM(keep.shape, f32)],
+        )
+        got = swap(send, step)
+    keep, got = yield keep, got
+    return keep, got
+
+
+def sum_all(sc, sizes, keep, send):
+    keep, got = yield from halve(sc, sizes, keep, send)
+    (value,) = call(add_kernel, "add", (sc, keep, got), [rows_like(keep.shape[0])])
+    for hop in hops(sizes[2]):
+        got = swap(value, (2, hop))
+        value, got = yield value, got
+        (value,) = call(add_kernel, "add", (sc, value, got), [rows_like(value.shape[0])])
+    for step in reversed(halving_steps(sizes)):
+        got = swap(value, step)
+        value, got = yield value, got
+        out = rows_like(2 * value.shape[0])
+        (value,) = call(functools.partial(join_kernel_of, step, 0), "join", (sc, value, got), [out])
+    yield value, None
 
 
 class Background:
     def __init__(self):
-        self.active = []
-
-    def add(self, value):
-        entry = [sum_steps(value), None, None]
-        entry[2] = "ready"
-        self.active.append(entry)
-        return entry
+        self.active = {}
+
+    def add(self, name, steps):
+        self.active[name] = [steps, None]
 
     def advance(self, entry, tied):
-        steps, value, state = entry
+        steps, pending = entry
         try:
-            entry[1] = next(steps) if state == "ready" else steps.send(tied)
-            entry[2] = "going"
+            entry[1] = next(steps) if pending is None else steps.send(tied)
         except StopIteration:
-            entry[2] = "done"
+            entry[0] = None
 
     def beside(self, anchor):
-        for entry in self.active:
-            if entry[2] == "going":
-                anchor, tied = lax.optimization_barrier((anchor, entry[1]))
+        for entry in self.active.values():
+            steps, pending = entry
+            if steps is None:
+                continue
+            if pending is None:
+                self.advance(entry, None)
+            elif pending[1] is not None:
+                anchor, tied = lax.optimization_barrier((anchor, pending))
                 self.advance(entry, tied)
-            elif entry[2] == "ready":
-                self.advance(entry, None)
         return anchor
 
-    def finish(self, entry):
-        while entry[2] != "done":
-            self.advance(entry, entry[1])
+    def finish(self, name):
+        entry = self.active[name]
+        while entry[0] is not None:
+            done = entry[1]
+            if done is not None and done[1] is None:
+                return done[0]
+            self.advance(entry, done)
         return entry[1]
 
 
@@ -633,66 +704,75 @@
 
     def trade(faces, axis):
         size = lax.axis_size(axis)
-        return [lax.ppermute(face, axis, pairs(size, kind)) for kind, face in enumerate(faces)]
+        got = [lax.ppermute(face, axis, pairs(size, kind)) for kind, face in reversed(list(enumerate(faces)))]
+        return got[::-1]
 
     background = Background()
 
     def exchange(faces):
-        got_x = trade(faces[:nx], "gx")
+        got_x = trade(background.beside(faces[:nx]), "gx")
         fix = functools.partial(fix_y_kernel, trades)
         faces_y = call(fix, "fix_y", (sc, *got_x, *faces[nx : nx + ny]), [face_y] * ny)
         got_y = trade(background.beside(faces_y), "gy")
         fix = functools.partial(fix_z_kernel, trades)
         faces_z = call(fix, "fix_z", (sc, *got_x, *got_y, *faces[nx + ny :]), [face_z] * nz)
-        faces_z = background.beside(faces_z)
-        got_z = background.beside(trade(faces_z, "gz"))
+        got_z = background.beside(trade(background.beside(faces_z), "gz"))
         return (*got_x, *got_y, *got_z)
 
-    sums, slopes0, *faces = run(first_kernel, "edges0", (h0,), [full, full3] + face_outs, [], 3)
+    sums, slopes0, *faces = call(
+        functools.partial(first_kernel, trades, sizes), "edges0", (sc, edge_weights, biases, h0), [full, full3] + face_outs,
+        [
+            pltpu.VMEM(grid, bf16),
+            pltpu.VMEM(edge_weights.shape, bf16),
+            pltpu.VMEM(biases.shape, f32),
+            pltpu.SemaphoreType.DMA((3,)),
+        ],
+        3 * matmul, pl.BlockSpec(memory_space=pltpu.HBM),
+    )
     halo = exchange(faces)
     scaled0, act0, slope0, h1, sums, slopes1, *faces = run(
         middle_kernel, "nodes0_edges1", (sums, h0, *halo),
         [full16, full16, full, full16, full, full3] + face_outs, [work, inv], 8,
     )
     halo = exchange(faces)
-    turn_rows = sds((1, 3 * width + NODES, width))
-    base, sums, grads1, *faces = run(
-        turn_kernel, "nodes1_back", (sums, h1, g2, *halo), [full, full, turn_rows] + face_outs, [work, inv], 10
+    def sum_rows(rows):
+        total = padded_rows(rows, sizes)
+        return [rows_like(total // 2)] * 2, pltpu.VMEM((total, width), f32)
+
+    halves, scratch = sum_rows(3 * width + NODES)
+    base, sums, keep, send, *faces = run(
+        turn_kernel, "nodes1_back", (sums, h1, g2, *halo), [full, full] + halves + face_outs, [work, inv, scratch], 10
     )
-    sum1 = background.add(grads1[0])
+    background.add("layer1", sum_all(sc, sizes, keep, send))
     halo = exchange(faces)
-    join_rows = sds((1, 4 * width + 2 * NODES, width))
-    base, sums, grads0, *faces = run(
+    halves, scratch = sum_rows(4 * width + 2 * NODES)
+    base, sums, keep, send, *faces = run(
         join_kernel, "edges1_back_nodes0_back", (sums, h1, base, slopes1, h0, scaled0, act0, slope0, *halo),
-        [full, full, join_rows] + face_outs, [work, inv], 12,
+        [full, full] + halves + face_outs, [work, inv, scratch], 12,
     )
-    sum0 = background.add(grads0[0])
+    background.add("layer0", halve(sc, sizes, keep, send))
     halo = exchange(faces)
-    last_rows = sds((1, width + NODES, width))
-    grad0, last = run(last_kernel, "edges0_back", (sums, h0, base, slopes0, *halo), [full16, last_rows], [work], 6)
-
-    last = last[0]
-    for axis in ("gz", "gy", "gx"):
-        for hop in reversed(hops(lax.axis_size(axis))):
-            last = double(background.beside(last), axis, hop)
-    summed1, summed0 = background.finish(sum1), background.finish(sum0)
+    tail_rows = width + NODES
+    grad0, last = run(
+        last_kernel, "edges0_back", (sums, h0, base, slopes0, *halo), [full16, rows_like(tail_rows)], [work], 6
+    )
+    last = background.beside(last)
+    summed1 = background.finish("layer1")
+    keep, got = background.finish("layer0")
+    (value,) = call(stack_kernel, "stack", (sc, last, keep, got), [rows_like(tail_rows + keep.shape[0])])
+    for hop in hops(sizes[2]):
+        (value,) = call(add_kernel, "add", (sc, value, swap(value, (2, hop))), [rows_like(value.shape[0])])
+    for step in reversed(halving_steps(sizes)):
+        out = rows_like(2 * value.shape[0] - tail_rows)
+        body = functools.partial(join_kernel_of, step, tail_rows)
+        (value,) = call(body, "join", (sc, value, swap(value, step)), [out])
     layers_all = 3 * slots * sizes[2] // 4
     nodes_all = x_len * sizes[0] * y_len * sizes[1] * layers_all * nodes
     scale = 1.0 / math.sqrt(nodes_all)
-
-    edge_grads, in_grads, out_grads, bias_grads = pl.pallas_call(
-        functools.partial(finish_kernel, scale),
-        name="finish",
-        out_shape=(
-            sds(edge_weights.shape),
-            sds(node_in.shape),
-            sds(node_out.shape),
-            sds(biases.shape),
-        ),
-        in_specs=[VM] * 5,
-        out_specs=(VM, VM, VM, VM),
-        compiler_params=pltpu.CompilerParams(vmem_limit_bytes=VMEM_LIMIT),
-    )(edge_weights, node_in, summed0, summed1, last)
+    edge_grads, in_grads, out_grads, bias_grads = call(
+        functools.partial(finish_kernel, scale, tail_rows), "finish", (sc, edge_weights, node_in, value, summed1),
+        [sds(edge_weights.shape), sds(node_in.shape), sds(node_out.shape), sds(biases.shape)],
+    )
     return grad0.reshape(state.shape), edge_grads, in_grads, out_grads, bias_grads
 
 

time: 200 us -> 162 us (0.81)
  local copies, waits for them, and re-layouts: 40.3 us -> 2.84 us
  Pallas kernels: 41 us -> 50.7 us
  starting transfers between devices: 70.5 us -> 61.1 us
    unnamed x68 -> x18, local copies, waits for them, and re-layouts: 39.5 us -> 2.84 us
    pallas_call x13 -> x30, Pallas kernels: 39.9 us -> 50.7 us  [call(): pl.pallas_call(kernel, name=name, out_shape=tuple(outs), in_specs=[SM] +...]
    ppermute x21 -> x16, starting transfers between devices: 41.9 us -> 31.1 us  [swap(): lax.ppermute(value, axis, [(i, i ^ step[1]) for i in range(lax.axis_size(...]
    ppermute x21 -> x16, waiting for transfers between devices: 22 us -> 28.7 us  [swap(): lax.ppermute(value, axis, [(i, i ^ step[1]) for i in range(lax.axis_size(...]
    ppermute x20, waiting for transfers between devices: 21.1 us -> 16.3 us  [trade(): lax.ppermute(face, axis, pairs(size, kind))]
  transfers between devices with their start and end apart: 41 -> 36, of which waited for: 19 -> 20; matrix products, arithmetic and copies ran while one was open for 1% -> 0% of each run, Pallas kernels for 8% -> 13%
where the time goes in v2:
time: 162 us; the launch traced here: 161 us
  starting transfers between devices  61.1 us (38%)
  Pallas kernels  50.7 us (31%)
  waiting for transfers between devices  44.9 us (28%)
  local copies, waits for them, and re-layouts  2.84 us (2%)
  between operations  1.66 us (1%)
    pallas_call x30, Pallas kernels, call(): pl.pallas_call(kernel, name=name, out_shape=tuple(outs), in_specs=[SM] +...  50.7 us
    ppermute x16, starting transfers between devices, swap(): lax.ppermute(value, axis, [(i, i ^ step[1]) for i in range(lax.axis_size(...  31.1 us
    ppermute x20, starting transfers between devices, trade(): lax.ppermute(face, axis, pairs(size, kind))  30 us
    ppermute x16, waiting for transfers between devices, swap(): lax.ppermute(value, axis, [(i, i ^ step[1]) for i in range(lax.axis_size(...  28.7 us
    ppermute x20, waiting for transfers between devices, trade(): lax.ppermute(face, axis, pairs(size, kind))  16.3 us
  transfers between devices with their start and end apart: 36, of which 20 were waited for; matrix products, arithmetic and copies ran while one was open for 0% of the time, Pallas kernels for 13%

profile of v2, /device:TPU:0, one launch (start us, length us, event | category | flops | bytes accessed | tf_op | source)
XLA Modules:
  0.0 161.4 jit_solution(669490643915181056)
XLA Ops:
  1.4 1.2 copy-done
  2.6 0.9 copy-done.2
  4.2 5.3 %edges0.1 = (f32[16,16,16,128]{3,2,1,0:T(8,128)S(1)}, f32[3,16,16,16,128]{4,3,2,1,0:T(8,128)S(1)}, f32[16,16,128]{2,1,0:T(8,128)S(1)}, f32[16,16,128]{2,1,0:T(8,...) custom-call(s32[4]{0:T(128)S(1)} %pad_add_fusion.sc.sc_ref, ...), custom_call_target="tpu_custom_call" | custom-call | flops 402653184 | bytes 10225680 | tf_op jit(solution)/shard_map/edges0/pallas_call | solution.py:525
  9.5 3.0 %collective-permute-start = (f32[16,16,128]{2,1,0:T(8,128)S(1)}, f32[16,16,128]{2,1,0:T(8,128)S(1)}, u32[]{:S(2)}, u32[]{:S(2)}) collective-permute-start(f32[16,16,128]{2,1,0:T(8,128)S(1)} %get-tuple-element.112), channel_id=1, source_target_pairs={{0,16},{16,0},{1,17},{17,1},{2,18},{18,2},{3,19},{19,3},{4,20},{20... | collective-permute-start | bytes 393224 | tf_op jit(solution)/shard_map/ppermute | solution.py:707
  12.5 3.5 %collective-permute-done.refs_0_ = f32[16,16,128]{2,1,0:T(8,128)S(1)} collective-permute-done((f32[16,16,128]{2,1,0:T(8,128)S(1)}, f32[16,16,128]{2,1,0:T(8,128)S(1)}, u32[]{:S(2)}, u32[]{:S(2)}) %collective-permute-start) | collective-permute-done | bytes 131104 | tf_op jit(solution)/shard_map/ppermute | solution.py:707
  18.0 0.7 fix_z.4
  18.7 1.9 %collective-permute-start.3 = (f32[16,16,128]{2,1,0:T(8,128)S(1)}, f32[16,16,128]{2,1,0:T(8,128)S(1)}, u32[]{:S(2)}, u32[]{:S(2)}) collective-permute-start(f32[16,16,128]{2,1,0:T(8,128)S(1)} %get-tuple-element.119), channel_id=1, source_target_pairs={{0,1},{1,0},{2,3},{3,2},{4,5},{5,4},{6,7},{7,6},{8,9},{9,8},{10,11... | collective-permute-start | bytes 393224 | tf_op jit(solution)/shard_map/ppermute | solution.py:707
  21.3 2.5 %collective-permute-done.3.refs_3_ = f32[16,16,128]{2,1,0:T(8,128)S(1)} collective-permute-done((f32[16,16,128]{2,1,0:T(8,128)S(1)}, f32[16,16,128]{2,1,0:T(8,128)S(1)}, u32[]{:S(2)}, u32[]{:S(2)}) %collective-permute-start.3) | collective-permute-done | bytes 131104 | tf_op jit(solution)/shard_map/ppermute | solution.py:707
  23.8 8.7 %nodes0_edges1.1 = (bf16[16,16,16,128]{3,2,1,0:T(8,128)(2,1)S(1)}, bf16[16,16,16,128]{3,2,1,0:T(8,128)(2,1)S(1)}, f32[16,16,16,128]{3,2,1,0:T(8,128)S(1)}, bf16[...) custom-call(s32[4]{0:T(128)S(1)} %pad_add_fusion.sc.sc_ref, ...), custom_call_target="tpu_custom_call" | custom-call | flops 1073741824 | bytes 18417680 | tf_op jit(solution)/shard_map/nodes0_edges1/pallas_call | solution.py:525
  32.5 1.8 %collective-permute-start.5 = (f32[16,16,128]{2,1,0:T(8,128)S(1)}, f32[16,16,128]{2,1,0:T(8,128)S(1)}, u32[]{:S(2)}, u32[]{:S(2)}) collective-permute-start(f32[16,16,128]{2,1,0:T(8,128)S(1)} %get-tuple-element.123), channel_id=1, source_target_pairs={{0,16},{16,0},{1,17},{17,1},{2,18},{18,2},{3,19},{19,3},{4,20},{20... | collective-permute-start | bytes 393224 | tf_op jit(solution)/shard_map/ppermute | solution.py:707
  34.3 3.2 %collective-permute-done.5.refs_0_ = f32[16,16,128]{2,1,0:T(8,128)S(1)} collective-permute-done((f32[16,16,128]{2,1,0:T(8,128)S(1)}, f32[16,16,128]{2,1,0:T(8,128)S(1)}, u32[]{:S(2)}, u32[]{:S(2)}) %collective-permute-start.5) | collective-permute-done | bytes 131104 | tf_op jit(solution)/shard_map/ppermute | solution.py:707
  38.1 3.6 %collective-permute-start.6 = (f32[16,16,128]{2,1,0:T(8,128)S(1)}, f32[16,16,128]{2,1,0:T(8,128)S(1)}, u32[]{:S(2)}, u32[]{:S(2)}) collective-permute-start(f32[16,16,128]{2,1,0:T(8,128)S(1)} %get-tuple-element.126), channel_id=1, source_target_pairs={{0,4},{4,0},{8,12},{12,8},{1,5},{5,1},{9,13},{13,9},{2,6},{6,2},{1... | collective-permute-start | bytes 393224 | tf_op jit(solution)/shard_map/ppermute | solution.py:707
  42.7 0.7 fix_z.5
  43.4 4.8 %collective-permute-start.8 = (f32[16,16,128]{2,1,0:T(8,128)S(1)}, f32[16,16,128]{2,1,0:T(8,128)S(1)}, u32[]{:S(2)}, u32[]{:S(2)}) collective-permute-start(f32[16,16,128]{2,1,0:T(8,128)S(1)} %get-tuple-element.130), channel_id=1, source_target_pairs={{0,1},{1,0},{2,3},{3,2},{4,5},{5,4},{6,7},{7,6},{8,9},{9,8},{10,11... | collective-permute-start | bytes 393224 | tf_op jit(solution)/shard_map/ppermute | solution.py:707
  48.9 2.3 %collective-permute-done.8.refs_3_ = f32[16,16,128]{2,1,0:T(8,128)S(1)} collective-permute-done((f32[16,16,128]{2,1,0:T(8,128)S(1)}, f32[16,16,128]{2,1,0:T(8,128)S(1)}, u32[]{:S(2)}, u32[]{:S(2)}) %collective-permute-start.8) | collective-permute-done | bytes 131104 | tf_op jit(solution)/shard_map/ppermute | solution.py:707
  51.1 6.4 %nodes1_back.1 = (f32[16,16,16,128]{3,2,1,0:T(8,128)S(1)}, f32[16,16,16,128]{3,2,1,0:T(8,128)S(1)}, f32[224,128]{1,0:T(8,128)S(1)}, f32[224,128]{1,0:T(8,128)S(1...) custom-call(s32[4]{0:T(128)S(1)} %pad_add_fusion.sc.sc_ref, ...), custom_call_target="tpu_custom_call" | custom-call | flops 1342177280 | bytes 10258448 | tf_op jit(solution)/shard_map/nodes1_back/pallas_call | solution.py:525
  57.5 1.6 collective-permute-start.10
  59.1 5.9 %collective-permute-start.11 = (f32[224,128]{1,0:T(8,128)S(1)}, f32[224,128]{1,0:T(8,128)S(1)}, u32[]{:S(2)}, u32[]{:S(2)}) collective-permute-start(f32[224,128]{1,0:T(8,128)S(1)} %get-tuple-element.144), channel_id=1, source_target_pairs={{0,4},{4,0},{8,12},{12,8},{1,5},{5,1},{9,13},{13,9},{2,6},{6,2},{1... | collective-permute-start | bytes 344072 | tf_op jit(solution)/shard_map/ppermute | solution.py:601
  65.9 2.3 %collective-permute-start.12 = (f32[16,16,128]{2,1,0:T(8,128)S(1)}, f32[16,16,128]{2,1,0:T(8,128)S(1)}, u32[]{:S(2)}, u32[]{:S(2)}) collective-permute-start(f32[16,16,128]{2,1,0:T(8,128)S(1)} %get-tuple-element.145), channel_id=1, source_target_pairs={{0,4},{4,0},{8,12},{12,8},{1,5},{5,1},{9,13},{13,9},{2,6},{6,2},{1... | collective-permute-start | bytes 393224 | tf_op jit(solution)/shard_map/ppermute | solution.py:707
  69.5 1.6 collective-permute-start.14
  71.0 0.7 fix_z.6
  71.7 2.0 %collective-permute-done.14.got = f32[112,128]{1,0:T(8,128)S(1)} collective-permute-done((f32[112,128]{1,0:T(8,128)S(1)}, f32[112,128]{1,0:T(8,128)S(1)}, u32[]{:S(2)}, u32[]{:S(2)}) %collective-permute-start.14) | collective-permute-done | bytes 57376 | tf_op jit(solution)/shard_map/ppermute | solution.py:601
  73.7 3.9 %collective-permute-start.15 = (f32[16,16,128]{2,1,0:T(8,128)S(1)}, f32[16,16,128]{2,1,0:T(8,128)S(1)}, u32[]{:S(2)}, u32[]{:S(2)}) collective-permute-start(f32[16,16,128]{2,1,0:T(8,128)S(1)} %get-tuple-element.155), channel_id=1, source_target_pairs={{0,1},{1,0},{2,3},{3,2},{4,5},{5,4},{6,7},{7,6},{8,9},{9,8},{10,11... | collective-permute-start | bytes 393224 | tf_op jit(solution)/shard_map/ppermute | solution.py:707
  77.6 0.8 collective-permute-start.16
  79.0 5.0 %collective-permute-start.17 = (f32[56,128]{1,0:T(8,128)S(1)}, f32[56,128]{1,0:T(8,128)S(1)}, u32[]{:S(2)}, u32[]{:S(2)}) collective-permute-start(f32[56,128]{1,0:T(8,128)S(1)} %get-tuple-element.160), channel_id=1, source_target_pairs={{0,8},{4,12},{8,0},{12,4},{1,9},{5,13},{9,1},{13,5},{2,10},{6,14},... | collective-permute-start | bytes 86024 | tf_op jit(solution)/shard_map/ppermute | solution.py:601
  84.0 1.9 %collective-permute-done.17.right = f32[56,128]{1,0:T(8,128)S(1)} collective-permute-done((f32[56,128]{1,0:T(8,128)S(1)}, f32[56,128]{1,0:T(8,128)S(1)}, u32[]{:S(2)}, u32[]{:S(2)}) %collective-permute-start.17) | collective-permute-done | bytes 28704 | tf_op jit(solution)/shard_map/ppermute | solution.py:601
  86.5 3.3 %collective-permute-start.18 = (f32[56,128]{1,0:T(8,128)S(1)}, f32[56,128]{1,0:T(8,128)S(1)}, u32[]{:S(2)}, u32[]{:S(2)}) collective-permute-start(f32[56,128]{1,0:T(8,128)S(1)} %add.11.left), channel_id=1, source_target_pairs={{0,1},{1,0},{2,3},{3,2},{4,5},{5,4},{6,7},{7,6},{8,9},{9,8},{10,11... | collective-permute-start | bytes 86024 | tf_op jit(solution)/shard_map/ppermute | solution.py:601
  89.8 8.2 %edges1_back_nodes0_back.1 = (f32[16,16,16,128]{3,2,1,0:T(8,128)S(1)}, f32[16,16,16,128]{3,2,1,0:T(8,128)S(1)}, f32[288,128]{1,0:T(8,128)S(1)}, f32[288,128]{1,0...) custom-call(s32[4]{0:T(128)S(1)} %pad_add_fusion.sc.sc_ref, ...), custom_call_target="tpu_custom_call" | custom-call | flops 1610612736 | bytes 22906896 | tf_op jit(solution)/shard_map/edges1_back_nodes0_back/pallas_call | solution.py:525
  98.0 1.6 collective-permute-start.19
  100.4 3.5 %collective-permute-done.19.refs_0_ = f32[16,16,128]{2,1,0:T(8,128)S(1)} collective-permute-done((f32[16,16,128]{2,1,0:T(8,128)S(1)}, f32[16,16,128]{2,1,0:T(8,128)S(1)}, u32[]{:S(2)}, u32[]{:S(2)}) %collective-permute-start.19) | collective-permute-done | bytes 131104 | tf_op jit(solution)/shard_map/ppermute | solution.py:707
  106.2 1.2 collective-permute-start.25
  108.0 3.4 %collective-permute-start.24 = (f32[56,128]{1,0:T(8,128)S(1)}, f32[56,128]{1,0:T(8,128)S(1)}, u32[]{:S(2)}, u32[]{:S(2)}) collective-permute-start(f32[56,128]{1,0:T(8,128)S(1)} %add.13.value), channel_id=1, source_target_pairs={{0,8},{4,12},{8,0},{12,4},{1,9},{5,13},{9,1},{13,5},{2,10},{6,14},... | collective-permute-start | bytes 86024 | tf_op jit(solution)/shard_map/ppermute | solution.py:601
  111.4 0.7 fix_z.7
  112.1 1.2 collective-permute-done.24.got
  114.5 1.0 collective-permute-start.28
  115.5 3.5 %collective-permute-done.28.got = f32[112,128]{1,0:T(8,128)S(1)} collective-permute-done((f32[112,128]{1,0:T(8,128)S(1)}, f32[112,128]{1,0:T(8,128)S(1)}, u32[]{:S(2)}, u32[]{:S(2)}) %collective-permute-start.28) | collective-permute-done | bytes 57376 | tf_op jit(solution)/shard_map/ppermute | solution.py:601
  120.5 1.6 collective-permute-start.29
  122.1 2.4 %collective-permute-done.29.right = f32[72,128]{1,0:T(8,128)S(1)} collective-permute-done((f32[72,128]{1,0:T(8,128)S(1)}, f32[72,128]{1,0:T(8,128)S(1)}, u32[]{:S(2)}, u32[]{:S(2)}) %collective-permute-start.29) | collective-permute-done | bytes 36896 | tf_op jit(solution)/shard_map/ppermute | solution.py:601
  124.5 6.5 %edges0_back.1 = (bf16[16,16,16,128]{3,2,1,0:T(8,128)(2,1)}, f32[136,128]{1,0:T(8,128)S(1)}) custom-call(s32[4]{0:T(128)S(1)} %pad_add_fusion.sc.sc_ref, bf16[2,2,128,128]{3,2,1,0:T(8,128)(2,1)S(1)} %copy-done.3, bf16[2,256,128]{2,1,0:T(8,128)(2,1)S(1)} %copy-done.4, bf16[2,128,128]{2,1,0:T(8,128)(2,1)S(1)} %copy-done.5, f32[2,2,128]{2,1,0:T(2,128)S(1)} %copy-done.8, ...), custom_call_target="tpu_custom_call" | custom-call | flops 805306368 | bytes 13637648 | tf_op jit(solution)/shard_map/edges0_back/pallas_call | solution.py:525
  131.6 3.7 %collective-permute-start.31 = (f32[208,128]{1,0:T(8,128)S(1)}, f32[208,128]{1,0:T(8,128)S(1)}, u32[]{:S(2)}, u32[]{:S(2)}) collective-permute-start(f32[208,128]{1,0:T(8,128)S(1)} %stack.17.left), channel_id=1, source_target_pairs={{0,1},{1,0},{2,3},{3,2},{4,5},{5,4},{6,7},{7,6},{8,9},{9,8},{10,11... | collective-permute-start | bytes 319496 | tf_op jit(solution)/shard_map/ppermute | solution.py:601
  135.3 2.7 %collective-permute-done.31.right = f32[208,128]{1,0:T(8,128)S(1)} collective-permute-done((f32[208,128]{1,0:T(8,128)S(1)}, f32[208,128]{1,0:T(8,128)S(1)}, u32[]{:S(2)}, u32[]{:S(2)}) %collective-permute-start.31) | collective-permute-done | bytes 106528 | tf_op jit(solution)/shard_map/ppermute | solution.py:601
  138.5 2.9 %collective-permute-start.32 = (f32[208,128]{1,0:T(8,128)S(1)}, f32[208,128]{1,0:T(8,128)S(1)}, u32[]{:S(2)}, u32[]{:S(2)}) collective-permute-start(f32[208,128]{1,0:T(8,128)S(1)} %add.14.left), channel_id=1, source_target_pairs={{0,2},{1,3},{2,0},{3,1},{4,6},{5,7},{6,4},{7,5},{8,10},{9,11},{10,... | collective-permute-start | bytes 319496 | tf_op jit(solution)/shard_map/ppermute | solution.py:601
  141.5 4.5 %collective-permute-done.32.right = f32[208,128]{1,0:T(8,128)S(1)} collective-permute-done((f32[208,128]{1,0:T(8,128)S(1)}, f32[208,128]{1,0:T(8,128)S(1)}, u32[]{:S(2)}, u32[]{:S(2)}) %collective-permute-start.32) | collective-permute-done | bytes 106528 | tf_op jit(solution)/shard_map/ppermute | solution.py:601
  146.6 4.7 %collective-permute-done.33.got = f32[208,128]{1,0:T(8,128)S(1)} collective-permute-done((f32[208,128]{1,0:T(8,128)S(1)}, f32[208,128]{1,0:T(8,128)S(1)}, u32[]{:S(2)}, u32[]{:S(2)}) %collective-permute-start.33) | collective-permute-done | bytes 106528 | tf_op jit(solution)/shard_map/ppermute | solution.py:601
  151.9 1.0 collective-permute-start.34
  152.8 4.2 %collective-permute-done.34.got = f32[280,128]{1,0:T(8,128)S(1)} collective-permute-done((f32[280,128]{1,0:T(8,128)S(1)}, f32[280,128]{1,0:T(8,128)S(1)}, u32[]{:S(2)}, u32[]{:S(2)}) %collective-permute-start.34) | collective-permute-done | bytes 143392 | tf_op jit(solution)/shard_map/ppermute | solution.py:601
  158.2 0.9 collective-permute-done.35.got
  159.7 1.7 %finish.1 = (f32[2,2,128,128]{3,2,1,0:T(8,128)}, f32[2,256,128]{2,1,0:T(8,128)}, f32[2,128,128]{2,1,0:T(8,128)}, f32[2,2,128]{2,1,0:T(2,128)}) custom-call(s32[4]{0:T(128)S(1)} %pad_add_fusion.sc.sc_ref, bf16[2,2,128,128]{3,2,1,0:T(8,128)(2,1)S(1)} %copy-done.3, bf16[2,256,128]{2,1,0:T(8,128)(2,1)S(1)} %copy-done.4, f32[712,128]{1,0:T(8,128)S(1)} %join.10.both, ...), custom_call_target="tpu_custom_call" | custom-call | bytes 1513488 | tf_op jit(solution)/shard_map/finish/pallas_call | solution.py:525
  (73 shorter events, 19.4 us)
Async XLA Ops:
  0.6 23.1 %copy-start.8 = (f32[2,2,128]{2,1,0:T(2,128)S(1)}, f32[2,2,128]{2,1,0:T(2,128)}, u32[]{:S(2)}) copy-start(f32[2,2,128]{2,1,0:T(2,128)} %biases.7) | copy-start | bytes 6148
  1.4 1.2 copy-start
  2.6 0.9 copy-start.2
  3.5 0.7 copy-start.7
  4.2 19.6 %copy-start.1 = (bf16[16,16,2,8,128]{4,3,2,1,0:T(8,128)(2,1)S(1)}, bf16[16,16,2,8,128]{4,3,2,1,0:T(8,128)(2,1)}, u32[]{:S(2)}) copy-start(bf16[16,16,2,8,128]{4,3,2,1,0:T(8,128)(2,1)} %param.7) | copy-start | bytes 3145732
  4.2 19.6 %copy-start.3 = (bf16[2,2,128,128]{3,2,1,0:T(8,128)(2,1)S(1)}, bf16[2,2,128,128]{3,2,1,0:T(8,128)(2,1)}, u32[]{:S(2)}) copy-start(bf16[2,2,128,128]{3,2,1,0:T(8,128)(2,1)} %edge_w.9) | copy-start | bytes 393220
  4.2 19.6 %copy-start.4 = (bf16[2,256,128]{2,1,0:T(8,128)(2,1)S(1)}, bf16[2,256,128]{2,1,0:T(8,128)(2,1)}, u32[]{:S(2)}) copy-start(bf16[2,256,128]{2,1,0:T(8,128)(2,1)} %node_in.9) | copy-start | bytes 393220
  4.2 19.6 %copy-start.5 = (bf16[2,128,128]{2,1,0:T(8,128)(2,1)S(1)}, bf16[2,128,128]{2,1,0:T(8,128)(2,1)}, u32[]{:S(2)}) copy-start(bf16[2,128,128]{2,1,0:T(8,128)(2,1)} %node_out.7) | copy-start | bytes 196612
  9.5 6.5 %collective-permute-start = (f32[16,16,128]{2,1,0:T(8,128)S(1)}, f32[16,16,128]{2,1,0:T(8,128)S(1)}, u32[]{:S(2)}, u32[]{:S(2)}) collective-permute-start(f32[16,16,128]{2,1,0:T(8,128)S(1)} %get-tuple-element.112), channel_id=1, source_target_pairs={{0,16},{16,0},{1,17},{17,1},{2,18},{18,2},{3,19},{19,3},{4,20},{20... | collective-permute-start | bytes 393224 | tf_op jit(solution)/shard_map/ppermute | solution.py:707
  16.6 1.4 collective-permute-start.1
  16.7 1.3 collective-permute-start.2
  18.7 5.0 %collective-permute-start.3 = (f32[16,16,128]{2,1,0:T(8,128)S(1)}, f32[16,16,128]{2,1,0:T(8,128)S(1)}, u32[]{:S(2)}, u32[]{:S(2)}) collective-permute-start(f32[16,16,128]{2,1,0:T(8,128)S(1)} %get-tuple-element.119), channel_id=1, source_target_pairs={{0,1},{1,0},{2,3},{3,2},{4,5},{5,4},{6,7},{7,6},{8,9},{9,8},{10,11... | collective-permute-start | bytes 393224 | tf_op jit(solution)/shard_map/ppermute | solution.py:707
  20.6 3.1 %collective-permute-start.4 = (f32[16,16,128]{2,1,0:T(8,128)S(1)}, f32[16,16,128]{2,1,0:T(8,128)S(1)}, u32[]{:S(2)}, u32[]{:S(2)}) collective-permute-start(f32[16,16,128]{2,1,0:T(8,128)S(1)} %get-tuple-element.120), channel_id=1, source_target_pairs={{1,2},{2,1},{5,6},{6,5},{9,10},{10,9},{13,14},{14,13},{17,18},{18,... | collective-permute-start | bytes 393224 | tf_op jit(solution)/shard_map/ppermute | solution.py:707
  23.8 27.4 %copy-start.6 = (bf16[16,16,2,8,128]{4,3,2,1,0:T(8,128)(2,1)S(1)}, bf16[16,16,2,8,128]{4,3,2,1,0:T(8,128)(2,1)}, u32[]{:S(2)}) copy-start(bf16[16,16,2,8,128]{4,3,2,1,0:T(8,128)(2,1)} %param.8) | copy-start | bytes 3145732
  32.5 5.0 %collective-permute-start.5 = (f32[16,16,128]{2,1,0:T(8,128)S(1)}, f32[16,16,128]{2,1,0:T(8,128)S(1)}, u32[]{:S(2)}, u32[]{:S(2)}) collective-permute-start(f32[16,16,128]{2,1,0:T(8,128)S(1)} %get-tuple-element.123), channel_id=1, source_target_pairs={{0,16},{16,0},{1,17},{17,1},{2,18},{18,2},{3,19},{19,3},{4,20},{20... | collective-permute-start | bytes 393224 | tf_op jit(solution)/shard_map/ppermute | solution.py:707
  38.1 4.6 %collective-permute-start.6 = (f32[16,16,128]{2,1,0:T(8,128)S(1)}, f32[16,16,128]{2,1,0:T(8,128)S(1)}, u32[]{:S(2)}, u32[]{:S(2)}) collective-permute-start(f32[16,16,128]{2,1,0:T(8,128)S(1)} %get-tuple-element.126), channel_id=1, source_target_pairs={{0,4},{4,0},{8,12},{12,8},{1,5},{5,1},{9,13},{13,9},{2,6},{6,2},{1... | collective-permute-start | bytes 393224 | tf_op jit(solution)/shard_map/ppermute | solution.py:707
  41.7 1.0 collective-permute-start.7
  43.4 7.8 %collective-permute-start.8 = (f32[16,16,128]{2,1,0:T(8,128)S(1)}, f32[16,16,128]{2,1,0:T(8,128)S(1)}, u32[]{:S(2)}, u32[]{:S(2)}) collective-permute-start(f32[16,16,128]{2,1,0:T(8,128)S(1)} %get-tuple-element.130), channel_id=1, source_target_pairs={{0,1},{1,0},{2,3},{3,2},{4,5},{5,4},{6,7},{7,6},{8,9},{9,8},{10,11... | collective-permute-start | bytes 393224 | tf_op jit(solution)/shard_map/ppermute | solution.py:707
  48.2 3.0 %collective-permute-start.9 = (f32[16,16,128]{2,1,0:T(8,128)S(1)}, f32[16,16,128]{2,1,0:T(8,128)S(1)}, u32[]{:S(2)}, u32[]{:S(2)}) collective-permute-start(f32[16,16,128]{2,1,0:T(8,128)S(1)} %get-tuple-element.131), channel_id=1, source_target_pairs={{1,2},{2,1},{5,6},{6,5},{9,10},{10,9},{13,14},{14,13},{17,18},{18,... | collective-permute-start | bytes 393224 | tf_op jit(solution)/shard_map/ppermute | solution.py:707
  57.5 7.4 %collective-permute-start.10 = (f32[16,16,128]{2,1,0:T(8,128)S(1)}, f32[16,16,128]{2,1,0:T(8,128)S(1)}, u32[]{:S(2)}, u32[]{:S(2)}) collective-permute-start(f32[16,16,128]{2,1,0:T(8,128)S(1)} %get-tuple-element.138), channel_id=1, source_target_pairs={{0,16},{16,0},{1,17},{17,1},{2,18},{18,2},{3,19},{19,3},{4,20},{20... | collective-permute-start | bytes 393224 | tf_op jit(solution)/shard_map/ppermute | solution.py:707
  59.1 6.8 %collective-permute-start.11 = (f32[224,128]{1,0:T(8,128)S(1)}, f32[224,128]{1,0:T(8,128)S(1)}, u32[]{:S(2)}, u32[]{:S(2)}) collective-permute-start(f32[224,128]{1,0:T(8,128)S(1)} %get-tuple-element.144), channel_id=1, source_target_pairs={{0,4},{4,0},{8,12},{12,8},{1,5},{5,1},{9,13},{13,9},{2,6},{6,2},{1... | collective-permute-start | bytes 344072 | tf_op jit(solution)/shard_map/ppermute | solution.py:601
  65.9 5.1 %collective-permute-start.12 = (f32[16,16,128]{2,1,0:T(8,128)S(1)}, f32[16,16,128]{2,1,0:T(8,128)S(1)}, u32[]{:S(2)}, u32[]{:S(2)}) collective-permute-start(f32[16,16,128]{2,1,0:T(8,128)S(1)} %get-tuple-element.145), channel_id=1, source_target_pairs={{0,4},{4,0},{8,12},{12,8},{1,5},{5,1},{9,13},{13,9},{2,6},{6,2},{1... | collective-permute-start | bytes 393224 | tf_op jit(solution)/shard_map/ppermute | solution.py:707
  68.2 2.8 %collective-permute-start.13 = (f32[16,16,128]{2,1,0:T(8,128)S(1)}, f32[16,16,128]{2,1,0:T(8,128)S(1)}, u32[]{:S(2)}, u32[]{:S(2)}) collective-permute-start(f32[16,16,128]{2,1,0:T(8,128)S(1)} %get-tuple-element.146), channel_id=1, source_target_pairs={{4,8},{8,4},{5,9},{9,5},{6,10},{10,6},{7,11},{11,7},{20,24},{24,20... | collective-permute-start | bytes 393224 | tf_op jit(solution)/shard_map/ppermute | solution.py:707
  69.5 4.2 %collective-permute-start.14 = (f32[112,128]{1,0:T(8,128)S(1)}, f32[112,128]{1,0:T(8,128)S(1)}, u32[]{:S(2)}, u32[]{:S(2)}) collective-permute-start(f32[112,128]{1,0:T(8,128)S(1)} %get-tuple-element.154), channel_id=1, source_target_pairs={{0,16},{16,0},{1,17},{17,1},{2,18},{18,2},{3,19},{19,3},{4,20},{20... | collective-permute-start | bytes 172040 | tf_op jit(solution)/shard_map/ppermute | solution.py:601
  73.7 12.2 %collective-permute-start.15 = (f32[16,16,128]{2,1,0:T(8,128)S(1)}, f32[16,16,128]{2,1,0:T(8,128)S(1)}, u32[]{:S(2)}, u32[]{:S(2)}) collective-permute-start(f32[16,16,128]{2,1,0:T(8,128)S(1)} %get-tuple-element.155), channel_id=1, source_target_pairs={{0,1},{1,0},{2,3},{3,2},{4,5},{5,4},{6,7},{7,6},{8,9},{9,8},{10,11... | collective-permute-start | bytes 393224 | tf_op jit(solution)/shard_map/ppermute | solution.py:707
  77.6 8.3 %collective-permute-start.16 = (f32[16,16,128]{2,1,0:T(8,128)S(1)}, f32[16,16,128]{2,1,0:T(8,128)S(1)}, u32[]{:S(2)}, u32[]{:S(2)}) collective-permute-start(f32[16,16,128]{2,1,0:T(8,128)S(1)} %get-tuple-element.156), channel_id=1, source_target_pairs={{1,2},{2,1},{5,6},{6,5},{9,10},{10,9},{13,14},{14,13},{17,18},{18,... | collective-permute-start | bytes 393224 | tf_op jit(solution)/shard_map/ppermute | solution.py:707
  79.0 6.9 %collective-permute-start.17 = (f32[56,128]{1,0:T(8,128)S(1)}, f32[56,128]{1,0:T(8,128)S(1)}, u32[]{:S(2)}, u32[]{:S(2)}) collective-permute-start(f32[56,128]{1,0:T(8,128)S(1)} %get-tuple-element.160), channel_id=1, source_target_pairs={{0,8},{4,12},{8,0},{12,4},{1,9},{5,13},{9,1},{13,5},{2,10},{6,14},... | collective-permute-start | bytes 86024 | tf_op jit(solution)/shard_map/ppermute | solution.py:601
  86.5 11.6 %collective-permute-start.18 = (f32[56,128]{1,0:T(8,128)S(1)}, f32[56,128]{1,0:T(8,128)S(1)}, u32[]{:S(2)}, u32[]{:S(2)}) collective-permute-start(f32[56,128]{1,0:T(8,128)S(1)} %add.11.left), channel_id=1, source_target_pairs={{0,1},{1,0},{2,3},{3,2},{4,5},{5,4},{6,7},{7,6},{8,9},{9,8},{10,11... | collective-permute-start | bytes 86024 | tf_op jit(solution)/shard_map/ppermute | solution.py:601
  98.0 7.0 %collective-permute-start.21 = (f32[288,128]{1,0:T(8,128)S(1)}, f32[288,128]{1,0:T(8,128)S(1)}, u32[]{:S(2)}, u32[]{:S(2)}) collective-permute-start(f32[288,128]{1,0:T(8,128)S(1)} %get-tuple-element.179), channel_id=1, source_target_pairs={{0,4},{4,0},{8,12},{12,8},{1,5},{5,1},{9,13},{13,9},{2,6},{6,2},{1... | collective-permute-start | bytes 442376 | tf_op jit(solution)/shard_map/ppermute | solution.py:601
  98.0 5.9 %collective-permute-start.19 = (f32[16,16,128]{2,1,0:T(8,128)S(1)}, f32[16,16,128]{2,1,0:T(8,128)S(1)}, u32[]{:S(2)}, u32[]{:S(2)}) collective-permute-start(f32[16,16,128]{2,1,0:T(8,128)S(1)} %get-tuple-element.169), channel_id=1, source_target_pairs={{0,16},{16,0},{1,17},{17,1},{2,18},{18,2},{3,19},{19,3},{4,20},{20... | collective-permute-start | bytes 393224 | tf_op jit(solution)/shard_map/ppermute | solution.py:707
  100.2 4.8 %collective-permute-start.20 = (f32[56,128]{1,0:T(8,128)S(1)}, f32[56,128]{1,0:T(8,128)S(1)}, u32[]{:S(2)}, u32[]{:S(2)}) collective-permute-start(f32[56,128]{1,0:T(8,128)S(1)} %add.12.left), channel_id=1, source_target_pairs={{0,2},{1,3},{2,0},{3,1},{4,6},{5,7},{6,4},{7,5},{8,10},{9,11},{10,... | collective-permute-start | bytes 86024 | tf_op jit(solution)/shard_map/ppermute | solution.py:601
  105.0 6.4 %collective-permute-start.22 = (f32[16,16,128]{2,1,0:T(8,128)S(1)}, f32[16,16,128]{2,1,0:T(8,128)S(1)}, u32[]{:S(2)}, u32[]{:S(2)}) collective-permute-start(f32[16,16,128]{2,1,0:T(8,128)S(1)} %get-tuple-element.180), channel_id=1, source_target_pairs={{0,4},{4,0},{8,12},{12,8},{1,5},{5,1},{9,13},{13,9},{2,6},{6,2},{1... | collective-permute-start | bytes 393224 | tf_op jit(solution)/shard_map/ppermute | solution.py:707
  105.0 6.4 %collective-permute-start.23 = (f32[16,16,128]{2,1,0:T(8,128)S(1)}, f32[16,16,128]{2,1,0:T(8,128)S(1)}, u32[]{:S(2)}, u32[]{:S(2)}) collective-permute-start(f32[16,16,128]{2,1,0:T(8,128)S(1)} %get-tuple-element.181), channel_id=1, source_target_pairs={{4,8},{8,4},{5,9},{9,5},{6,10},{10,6},{7,11},{11,7},{20,24},{24,20... | collective-permute-start | bytes 393224 | tf_op jit(solution)/shard_map/ppermute | solution.py:707
  106.2 7.0 %collective-permute-start.25 = (f32[144,128]{1,0:T(8,128)S(1)}, f32[144,128]{1,0:T(8,128)S(1)}, u32[]{:S(2)}, u32[]{:S(2)}) collective-permute-start(f32[144,128]{1,0:T(8,128)S(1)} %get-tuple-element.193), channel_id=1, source_target_pairs={{0,16},{16,0},{1,17},{17,1},{2,18},{18,2},{3,19},{19,3},{4,20},{20... | collective-permute-start | bytes 221192 | tf_op jit(solution)/shard_map/ppermute | solution.py:601
  108.0 5.3 %collective-permute-start.24 = (f32[56,128]{1,0:T(8,128)S(1)}, f32[56,128]{1,0:T(8,128)S(1)}, u32[]{:S(2)}, u32[]{:S(2)}) collective-permute-start(f32[56,128]{1,0:T(8,128)S(1)} %add.13.value), channel_id=1, source_target_pairs={{0,8},{4,12},{8,0},{12,4},{1,9},{5,13},{9,1},{13,5},{2,10},{6,14},... | collective-permute-start | bytes 86024 | tf_op jit(solution)/shard_map/ppermute | solution.py:601
  113.3 6.0 %collective-permute-start.26 = (f32[16,16,128]{2,1,0:T(8,128)S(1)}, f32[16,16,128]{2,1,0:T(8,128)S(1)}, u32[]{:S(2)}, u32[]{:S(2)}) collective-permute-start(f32[16,16,128]{2,1,0:T(8,128)S(1)} %get-tuple-element.194), channel_id=1, source_target_pairs={{0,1},{1,0},{2,3},{3,2},{4,5},{5,4},{6,7},{7,6},{8,9},{9,8},{10,11... | collective-permute-start | bytes 393224 | tf_op jit(solution)/shard_map/ppermute | solution.py:707
  113.3 6.0 %collective-permute-start.27 = (f32[16,16,128]{2,1,0:T(8,128)S(1)}, f32[16,16,128]{2,1,0:T(8,128)S(1)}, u32[]{:S(2)}, u32[]{:S(2)}) collective-permute-start(f32[16,16,128]{2,1,0:T(8,128)S(1)} %get-tuple-element.195), channel_id=1, source_target_pairs={{1,2},{2,1},{5,6},{6,5},{9,10},{10,9},{13,14},{14,13},{17,18},{18,... | collective-permute-start | bytes 393224 | tf_op jit(solution)/shard_map/ppermute | solution.py:707
  114.5 4.5 %collective-permute-start.28 = (f32[112,128]{1,0:T(8,128)S(1)}, f32[112,128]{1,0:T(8,128)S(1)}, u32[]{:S(2)}, u32[]{:S(2)}) collective-permute-start(f32[112,128]{1,0:T(8,128)S(1)} %join.6.value), channel_id=1, source_target_pairs={{0,16},{16,0},{1,17},{17,1},{2,18},{18,2},{3,19},{19,3},{4,20},{20... | collective-permute-start | bytes 172040 | tf_op jit(solution)/shard_map/ppermute | solution.py:601
  119.8 11.2 %collective-permute-start.30 = (f32[224,128]{1,0:T(8,128)S(1)}, f32[224,128]{1,0:T(8,128)S(1)}, u32[]{:S(2)}, u32[]{:S(2)}) collective-permute-start(f32[224,128]{1,0:T(8,128)S(1)} %join.7.value), channel_id=1, source_target_pairs={{0,4},{4,0},{8,12},{12,8},{1,5},{5,1},{9,13},{13,9},{2,6},{6,2},{1... | collective-permute-start | bytes 344072 | tf_op jit(solution)/shard_map/ppermute | solution.py:601
  120.5 4.0 %collective-permute-start.29 = (f32[72,128]{1,0:T(8,128)S(1)}, f32[72,128]{1,0:T(8,128)S(1)}, u32[]{:S(2)}, u32[]{:S(2)}) collective-permute-start(f32[72,128]{1,0:T(8,128)S(1)} %get-tuple-element.203), channel_id=1, source_target_pairs={{0,8},{4,12},{8,0},{12,4},{1,9},{5,13},{9,1},{13,5},{2,10},{6,14},... | collective-permute-start | bytes 110600 | tf_op jit(solution)/shard_map/ppermute | solution.py:601
  131.6 6.4 %collective-permute-start.31 = (f32[208,128]{1,0:T(8,128)S(1)}, f32[208,128]{1,0:T(8,128)S(1)}, u32[]{:S(2)}, u32[]{:S(2)}) collective-permute-start(f32[208,128]{1,0:T(8,128)S(1)} %stack.17.left), channel_id=1, source_target_pairs={{0,1},{1,0},{2,3},{3,2},{4,5},{5,4},{6,7},{7,6},{8,9},{9,8},{10,11... | collective-permute-start | bytes 319496 | tf_op jit(solution)/shard_map/ppermute | solution.py:601
  138.5 7.4 %collective-permute-start.32 = (f32[208,128]{1,0:T(8,128)S(1)}, f32[208,128]{1,0:T(8,128)S(1)}, u32[]{:S(2)}, u32[]{:S(2)}) collective-permute-start(f32[208,128]{1,0:T(8,128)S(1)} %add.14.left), channel_id=1, source_target_pairs={{0,2},{1,3},{2,0},{3,1},{4,6},{5,7},{6,4},{7,5},{8,10},{9,11},{10,... | collective-permute-start | bytes 319496 | tf_op jit(solution)/shard_map/ppermute | solution.py:601
  146.5 4.8 %collective-permute-start.33 = (f32[208,128]{1,0:T(8,128)S(1)}, f32[208,128]{1,0:T(8,128)S(1)}, u32[]{:S(2)}, u32[]{:S(2)}) collective-permute-start(f32[208,128]{1,0:T(8,128)S(1)} %add.15.value), channel_id=1, source_target_pairs={{0,8},{4,12},{8,0},{12,4},{1,9},{5,13},{9,1},{13,5},{2,10},{6,14},... | collective-permute-start | bytes 319496 | tf_op jit(solution)/shard_map/ppermute | solution.py:601
  151.9 5.2 %collective-permute-start.34 = (f32[280,128]{1,0:T(8,128)S(1)}, f32[280,128]{1,0:T(8,128)S(1)}, u32[]{:S(2)}, u32[]{:S(2)}) collective-permute-start(f32[280,128]{1,0:T(8,128)S(1)} %join.8.value), channel_id=1, source_target_pairs={{0,16},{16,0},{1,17},{17,1},{2,18},{18,2},{3,19},{19,3},{4,20},{20... | collective-permute-start | bytes 430088 | tf_op jit(solution)/shard_map/ppermute | solution.py:601
  157.6 1.5 collective-permute-start.35

commit v3 on v2

--- a/solution.py
+++ b/solution.py
@@ -181,12 +181,10 @@
     x_len, y_len, rows, width = sum_ref.shape
     nx, ny, nz = counts
     reader = RowReader(rows // NODES, lambda row: sum_ref[:, :, row])
-    for kind in range(nx):
-        faces[kind][...] = sum_ref[face_place(sc_ref, 0, kind, x_len - 1)]
     for kind in range(ny):
-        faces[nx + kind][...] = sum_ref[:, face_place(sc_ref, 1, kind, y_len - 1)]
+        faces[kind][...] = sum_ref[:, face_place(sc_ref, 1, kind, y_len - 1)]
     for kind in range(nz):
-        faces[nx + ny + kind][...] = end_rows(reader, sc_ref[0], takes_top(sc_ref, kind))
+        faces[ny + kind][...] = end_rows(reader, sc_ref[0], takes_top(sc_ref, kind))
 
 
 def add_halo(sc_ref, from_ref, halo, into_ref, counts):
@@ -272,37 +270,115 @@
 
 def scale_planes(sc_ref, inv_ref, x, block, x_len, size_x):
     inv = inv_ref[...]
-    parts = [block[c] * (inv * end_factor(x + c, x_len, sc_ref[1], size_x)) for c in range(CHUNK)]
+    parts = [block[c] * (inv * end_factor(x + c, x_len, sc_ref[1], size_x)) for c in range(block.shape[0])]
     return jnp.stack(parts, 0)
 
 
-def node_forward(sc_ref, x, inv_ref, size_x, sum_ref, h_ref, weights, layer):
+def node_forward(scaled, feat, weights, layer):
     edge_w, node_in, node_out, biases = weights
-    at = pl.ds(x, CHUNK)
-    scaled = scale_planes(sc_ref, inv_ref, x, sum_ref[at], sum_ref.shape[0], size_x)
-    pair = split_cols(flat(scaled))
+    pair = split_cols(scaled)
     w_two = edge_w[layer, 1]
-    joined = jnp.concatenate([flat(h_ref[at]), dot(pair, jnp.concatenate([w_two, w_two], 0)).astype(bf16)], -1)
+    joined = jnp.concatenate([feat, dot(pair, jnp.concatenate([w_two, w_two], 0)).astype(bf16)], -1)
     half = jnp.bfloat16(0.5)
     act, slope = silu_half(dot(joined, node_in[layer] * half) + 0.5 * biases[layer, pl.ds(1, 1)])
     return pair[:, :128], act.astype(bf16), slope
 
 
+def node_slopes(grad, slope, weights, layer):
+    return (dot_rt(grad, weights[2][layer]) * slope).astype(bf16)
+
+
 def node_backward(sc_ref, x, inv_ref, size_x, grad, feat, scaled, act, slope, weights, layer, sum_ref, base_ref, grads):
-    edge_w, node_in, node_out, biases = weights
     shape = (CHUNK,) + sum_ref.shape[1:]
     at = pl.ds(x, CHUNK)
-    dpn = (dot_rt(grad, node_out[layer]) * slope).astype(bf16)
+    dpn = node_slopes(grad, slope, weights, layer)
     grads[pl.ds(0, 128)] += dot_t(act, grad)
     both = dot_t(dpn, jnp.concatenate([feat, scaled], -1))
     grads[pl.ds(128, 128)] += both[:, :128]
     grads[pl.ds(256, 128)] += both[:, 128:]
     grads[pl.ds(384, NODES)] += jnp.sum(dpn.astype(f32).reshape(-1, NODES, 128), 0)
-    dx = dot_rt(dpn, node_in[layer])
+    dx = dot_rt(dpn, weights[1][layer])
     base_ref[at] = (grad.astype(f32) + dx[:, :128]).reshape(shape)
     share = scale_planes(sc_ref, inv_ref, x, dx[:, 128:].reshape(shape), sum_ref.shape[0], size_x)
     joined = couple_slots(share.reshape((-1,) + shape[2:]), sc_ref[0])
     sum_ref[at] = joined.reshape(shape)
+
+
+def couple_plane(plane):
+    y_len = plane.shape[0]
+    parts = [plane[y] for y in range(y_len)]
+    for cut in range(NODES, y_len, NODES):
+        both = parts[cut - 1] + parts[cut]
+        parts[cut - 1] = parts[cut] = both
+    return jnp.stack(parts, 0)
+
+
+def along_y(plane, combine):
+    return [
+        combine(plane[y : y + NODES - 1], plane[y + 1 : y + NODES], y) for y in range(0, plane.shape[0], NODES)
+    ]
+
+
+def spread_plane(sign, edge_x, edges_y, edge_z):
+    total = sign * edge_x + (down(edge_z) - edge_z).reshape(edge_x.shape)
+    parts = []
+    for k, edge in enumerate(edges_y):
+        here = total[k * NODES : (k + 1) * NODES]
+        parts += [here[:1] - edge[:1], here[1:-1] + (edge[:-1] - edge[1:]), here[-1:] + edge[-1:]]
+    return jnp.concatenate(parts, 0)
+
+
+def plane_forward(low, high, at_high, w_one, half_bias, filled):
+    y_len, rows, width = low.shape
+    here = jnp.where(at_high, high, low)
+    cols = node_rows(here)
+    parts = [(high - low).astype(bf16)]
+    parts += along_y(here, lambda lower, upper, y: (upper - lower).astype(bf16))
+    parts.append((up(cols) - cols).reshape(here.shape).astype(bf16))
+    half = dot(flat(jnp.concatenate(parts, 0)), w_one).reshape(-1, rows, width) + half_bias
+    act = silu_half(half)[0].astype(bf16).astype(f32)
+    at = y_len
+    edges_y = []
+    for _ in range(y_len // NODES):
+        edges_y.append(act[at : at + NODES - 1])
+        at += NODES - 1
+    edge_z = jnp.where(row_ids() < NODES - 1, node_rows(act[at:]), 0.0)
+    total = spread_plane(jnp.where(at_high, 1.0, -1.0), act[:y_len], edges_y, edge_z)
+    return couple_plane(couple_slots(total, filled))
+
+
+def plane_backward(low, high, at_high, slope_x, slope_y, slope_z):
+    here = jnp.where(at_high, high, low)
+    cols = node_rows(here)
+    edge_x = ((high - low) * slope_x).astype(bf16).astype(f32)
+    edges_y = along_y(
+        here, lambda lower, upper, y: ((upper - lower) * slope_y[y : y + NODES - 1]).astype(bf16).astype(f32)
+    )
+    edge_z = ((up(cols) - cols) * node_rows(slope_z)).astype(bf16).astype(f32)
+    return spread_plane(jnp.where(at_high, 1.0, -1.0), edge_x, edges_y, edge_z)
+
+
+def face_planes(sc_ref, kind, x_len):
+    place = face_place(sc_ref, 0, kind, x_len - 1)
+    at_high = place > 0
+    return place, jnp.where(at_high, x_len - 2, 0), at_high
+
+
+def halo_planes(sc_ref, from_ref, halo, kind, start, into_ref, counts):
+    x_len, y_len, rows, width = from_ref.shape
+    nx, ny, nz = counts
+    for c in range(2):
+        into_ref[c] = from_ref[start + c]
+    into_ref[face_place(sc_ref, 0, kind, x_len - 1) - start] += halo[kind][...]
+    for c in range(2):
+        for k in range(ny):
+            into_ref[c, face_place(sc_ref, 1, k, y_len - 1)] += halo[nx + k][start + c]
+        for k in range(nz):
+            got = halo[nx + ny + k][start + c]
+            top = takes_top(sc_ref, k)
+            into_ref[c, :, 0] += jnp.where(top, 0.0, got)
+            for s in range(rows // NODES):
+                into_ref[c, :, s * NODES + NODES - 1] += jnp.where(top & (sc_ref[0] == s + 1), got, 0.0)
 
 
 def edges_backward(q_ref, slope_ref, edge_ref, bias_acc):
@@ -357,21 +433,81 @@
     return edge_w[layer, 0] * jnp.bfloat16(0.5), 0.5 * biases[layer, pl.ds(0, 1)]
 
 
-def first_kernel(counts, sizes, sc, edge_w_in, biases_in, h_in, *refs):
-    sums, slopes = refs[:2]
-    faces, (h, edge_w, biases, sems) = refs[2:-4], refs[-4:]
-    moves = [
-        pltpu.make_async_copy(source, target, sems.at[k])
-        for k, (source, target) in enumerate(((h_in, h), (edge_w_in, edge_w), (biases_in, biases)))
-    ]
-    for move in moves:
-        move.start()
-    for move in moves:
-        move.wait()
+def first_kernel(counts, sizes, sc, edge_w, biases, h, sums, slopes, *faces):
     w_one, bias = half_weights((edge_w, None, None, biases), 0)
     edges_forward(h, w_one, bias, sc[0], sums, slopes)
     couple_columns(sums)
     write_faces(sc, sums, faces, counts)
+
+
+def first_face_kernel(counts, sizes, sc, edge_w, biases, h, *faces):
+    w_one, bias = half_weights((edge_w, None, None, biases), 0)
+    for kind, face in enumerate(faces):
+        place, start, at_high = face_planes(sc, kind, h.shape[0])
+        face[...] = plane_forward(
+            h[start].astype(f32), h[start + 1].astype(f32), at_high, w_one, bias, sc[0]
+        )
+
+
+def middle_face_kernel(counts, sizes, sc, edge_w, node_in, node_out, biases, sums_in, h, *refs):
+    weights = (edge_w, node_in, node_out, biases)
+    n = sum(counts)
+    halo, faces, (pair, inv) = refs[:n], refs[n:-2], refs[-2:]
+    write_inverse(sc, inv, sizes)
+    w_one, bias = half_weights(weights, 1)
+    x_len = h.shape[0]
+    for kind, face in enumerate(faces):
+        place, start, at_high = face_planes(sc, kind, x_len)
+        halo_planes(sc, sums_in, halo, kind, start, pair, counts)
+        sums_at = flat(scale_planes(sc, inv, start, pair[...], x_len, sizes[0]))
+        feat = flat(h[pl.ds(start, 2)])
+        scaled, act, slope = node_forward(sums_at, feat, weights, 0)
+        moved = (feat.astype(f32) + dot(act, node_out[0])).astype(bf16).astype(f32).reshape(pair.shape)
+        face[...] = plane_forward(moved[0], moved[1], at_high, w_one, bias, sc[0])
+
+
+def face_share(sc, sizes, inv, place, x_len, grad, slope, weights, layer, shape):
+    dpn = node_slopes(grad, slope, weights, layer)
+    dx = dot_rt(dpn, weights[1][layer, pl.ds(128, 128)]).reshape((1,) + shape)
+    share = scale_planes(sc, inv, place, dx, x_len, sizes[0])
+    return couple_plane(couple_slots(share[0], sc[0]))
+
+
+def turn_face_kernel(counts, sizes, sc, edge_w, node_in, node_out, biases, sums_in, h, g_ref, *refs):
+    weights = (edge_w, node_in, node_out, biases)
+    n = sum(counts)
+    halo, faces, (pair, inv) = refs[:n], refs[n:-2], refs[-2:]
+    write_inverse(sc, inv, sizes)
+    x_len, shape = h.shape[0], h.shape[1:]
+    live = (lax.broadcasted_iota(jnp.int32, (1, h.shape[2], 128), 1) < sc[0] * NODES).astype(f32)
+    for kind, face in enumerate(faces):
+        place, start, at_high = face_planes(sc, kind, x_len)
+        halo_planes(sc, sums_in, halo, kind, start, pair, counts)
+        plane = pair[place - start][None]
+        sums_at = flat(scale_planes(sc, inv, place, plane, x_len, sizes[0]))
+        scaled, act, slope = node_forward(sums_at, flat(h[place]), weights, 1)
+        grad = flat((g_ref[place].astype(f32) * live).astype(bf16))
+        face[...] = face_share(sc, sizes, inv, place, x_len, grad, slope, weights, 1, shape)
+
+
+def join_face_kernel(counts, sizes, sc, edge_w, node_in, node_out, biases, sums_in, base_in, slopes, slope0, *refs):
+    weights = (edge_w, node_in, node_out, biases)
+    n = sum(counts)
+    halo, faces, (pair, inv) = refs[:n], refs[n:-2], refs[-2:]
+    write_inverse(sc, inv, sizes)
+    x_len, shape = base_in.shape[0], base_in.shape[1:]
+    w_two, w_one = twice(edge_w[1, 1]), twice(edge_w[1, 0])
+    for kind, face in enumerate(faces):
+        place, start, at_high = face_planes(sc, kind, x_len)
+        halo_planes(sc, sums_in, halo, kind, start, pair, counts)
+        q = dot_rt(split_cols(flat(pair[...])), w_two).reshape(pair.shape)
+        edge = plane_backward(q[0], q[1], at_high, slopes[0, start], slopes[1, place], slopes[2, place])
+        grad = (flat(base_in[place]) + dot_rt(split_cols(flat(edge)), w_one)).astype(bf16)
+        face[...] = face_share(sc, sizes, inv, place, x_len, grad, flat(slope0[place]), weights, 0, shape)
+
+
+def twice(weight):
+    return jnp.concatenate([weight, weight], 1)
 
 
 def middle_kernel(counts, sizes, sc, edge_w, node_in, node_out, biases, sums_in, h, *refs):
@@ -386,7 +522,8 @@
 
     def body(x):
         at = pl.ds(x, CHUNK)
-        scaled, act, slope = node_forward(sc, x, inv, sizes[0], work, h, weights, 0)
+        sums_at = flat(scale_planes(sc, inv, x, work[at], h.shape[0], sizes[0]))
+        scaled, act, slope = node_forward(sums_at, flat(h[at]), weights, 0)
         scaled_ref[at] = scaled.reshape(shape)
         act_ref[at] = act.reshape(shape)
         slope_ref[at] = slope.reshape(shape)
@@ -404,8 +541,8 @@
     weights = (edge_w, node_in, node_out, biases)
     n = sum(counts)
     halo, refs = refs[:n], refs[n:]
-    base, sums, keep, send = refs[:4]
-    faces, (work, inv, grads) = refs[4:-3], refs[-3:]
+    base, sums, grads = refs[:3]
+    faces, (work, inv) = refs[3:-2], refs[-2:]
     add_halo(sc, sums_in, halo, work, counts)
     write_inverse(sc, inv, sizes)
     grads[...] = jnp.zeros_like(grads)
@@ -413,7 +550,8 @@
 
     def body(x):
         at = pl.ds(x, CHUNK)
-        scaled, act, slope = node_forward(sc, x, inv, sizes[0], work, h, weights, 1)
+        sums_at = flat(scale_planes(sc, inv, x, work[at], h.shape[0], sizes[0]))
+        scaled, act, slope = node_forward(sums_at, flat(h[at]), weights, 1)
         grad = flat((g_ref[at].astype(f32) * live).astype(bf16))
         node_backward(
             sc, x, inv, sizes[0], grad, flat(h[at]), scaled, act, slope, weights, 1, sums, base, grads
@@ -422,17 +560,12 @@
     planes(h.shape[0], body)
     couple_columns(sums)
     write_faces(sc, sums, faces, counts)
-    write_halves(sc, halving_steps(sizes)[0], grads, keep, send)
-
-
-def back_to_state(counts, sc, weights, layer, sums_in, halo, h, base, slopes, work, grads, row, use):
-    edge_w = weights[0]
+
+
+def edge_parts(counts, sc, weights, layer, sums_in, halo, h, slopes, work, grads, row):
     add_halo(sc, sums_in, halo, work, counts)
     shape = (CHUNK,) + h.shape[1:]
-    w_two = edge_w[layer, 1]
-    w_two = jnp.concatenate([w_two, w_two], 1)
-    w_one = edge_w[layer, 0]
-    w_one = jnp.concatenate([w_one, w_one], 1)
+    w_two = twice(weights[0][layer, 1])
 
     def to_q(x):
         at = pl.ds(x, CHUNK)
@@ -441,19 +574,15 @@
     planes(h.shape[0], to_q)
     edges_backward(work, slopes, work, grads.at[pl.ds(row + 128, NODES)])
 
-    def body(x):
-        at = pl.ds(x, CHUNK)
-        pair = split_cols(flat(work[at]))
-        both = dot_t(flat(h[at]), pair)
-        grads[pl.ds(row, 128)] += both[:, :128] + both[:, 128:]
-        use(x, (flat(base[at]) + dot_rt(pair, w_one)).astype(bf16))
-
-    planes(h.shape[0], body)
+
+def edge_product(h, x, pair, grads, row):
+    both = dot_t(flat(h[pl.ds(x, CHUNK)]), pair)
+    grads[pl.ds(row, 128)] += both[:, :128] + both[:, 128:]
 
 
 def join_kernel(
     counts, sizes, sc, edge_w, node_in, node_out, biases,
-    sums_in, h, base_in, slopes, h0, scaled0, act0, slope0, *refs
+    sums_in, h, base_in, slopes, h0, scaled0, act0, slope0, grads1, *refs
 ):
     weights = (edge_w, node_in, node_out, biases)
     n = sum(counts)
@@ -462,35 +591,53 @@
     faces, (work, inv, grads) = refs[4:-3], refs[-3:]
     write_inverse(sc, inv, sizes)
     grads[...] = jnp.zeros_like(grads)
-
-    def use(x, grad):
+    grads[pl.ds(512 + 2 * NODES, grads1.shape[0])] = grads1[...]
+
+    row = 384 + NODES
+    edge_parts(counts, sc, weights, 1, sums_in, halo, h, slopes, work, grads, row)
+    w_one = twice(edge_w[1, 0])
+
+    def body(x):
         at = pl.ds(x, CHUNK)
+        pair = split_cols(flat(work[at]))
+        edge_product(h, x, pair, grads, row)
+        grad = (flat(base_in[at]) + dot_rt(pair, w_one)).astype(bf16)
         node_backward(
             sc, x, inv, sizes[0], grad, flat(h0[at]), flat(scaled0[at]), flat(act0[at]), flat(slope0[at]),
             weights, 0, sums, base, grads,
         )
 
-    back_to_state(counts, sc, weights, 1, sums_in, halo, h, base_in, slopes, work, grads, 384 + NODES, use)
+    planes(h.shape[0], body)
     couple_columns(sums)
     write_faces(sc, sums, faces, counts)
     write_halves(sc, halving_steps(sizes)[0], grads, keep, send)
 
 
-def last_kernel(counts, sizes, sc, edge_w, node_in, node_out, biases, sums_in, h, base_in, slopes, *refs):
-    weights = (edge_w, node_in, node_out, biases)
+def last_kernel(counts, sizes, sc, edge_w, node_in, node_out, biases, sums_in, h, slopes, *refs):
     n = sum(counts)
-    halo, refs = refs[:n], refs[n:]
-    grad_ref, grads, work = refs
+    halo, (edges, grads) = refs[:n], refs[n:]
     grads[...] = jnp.zeros_like(grads)
-    shape = (CHUNK,) + h.shape[1:]
-
-    def use(x, grad):
-        grad_ref[pl.ds(x, CHUNK)] = grad.reshape(shape)
-
-    back_to_state(counts, sc, weights, 0, sums_in, halo, h, base_in, slopes, work, grads, 0, use)
-
-
-def finish_kernel(scale, last_rows, sc, edge_w, node_in, both, sum1, edge_grads, in_grads, out_grads, bias_grads):
+    edge_parts(counts, sc, (edge_w,), 0, sums_in, halo, h, slopes, edges, grads, 0)
+
+    def body(x):
+        edge_product(h, x, split_cols(flat(edges[pl.ds(x, CHUNK)])), grads, 0)
+
+    planes(h.shape[0], body)
+
+
+def state_kernel(sc, edge_w, base_in, edges, grad_ref):
+    shape = (CHUNK,) + edges.shape[1:]
+    w_one = twice(edge_w[0, 0])
+
+    def body(x):
+        at = pl.ds(x, CHUNK)
+        pair = split_cols(flat(edges[at]))
+        grad_ref[at] = (flat(base_in[at]) + dot_rt(pair, w_one)).astype(bf16).reshape(shape)
+
+    planes(edges.shape[0], body)
+
+
+def finish_kernel(scale, last_rows, sc, edge_w, node_in, both, edge_grads, in_grads, out_grads, bias_grads):
     width = edge_w.shape[-1]
 
     def rows_of(part, start, count=width):
@@ -502,8 +649,9 @@
 
     end = 3 * width
     last, sum0 = (both, 0), (both, last_rows)
+    sum1 = (both, last_rows + 512 + 2 * NODES)
     firsts = ((last, 0), (sum0, end + NODES))
-    for layer, part in enumerate((sum0, (sum1, 0))):
+    for layer, part in enumerate((sum0, sum1)):
         out_grads[layer] = rows_of(part, 0)
         in_grads[layer, pl.ds(0, width)] = rows_of(part, width).T
         bias_grads[layer, pl.ds(1, 1)] = bias_of(part, end)
@@ -519,14 +667,14 @@
         in_grads[layer, pl.ds(width, width)] = dot_t(w_two, high) + dot_t(w_two, low)
 
 
-def call(kernel, name, inputs, outs, scratch=(), flops=0, where=VM):
+def call(kernel, name, inputs, outs, scratch=(), flops=0):
     total = sum(math.prod(o.shape) * o.dtype.itemsize for o in outs)
     total += sum(math.prod(i.shape) * i.dtype.itemsize for i in inputs)
     return pl.pallas_call(
         kernel,
         name=name,
         out_shape=tuple(outs),
-        in_specs=[SM] + [where] * (len(inputs) - 1),
+        in_specs=[SM] + [VM] * (len(inputs) - 1),
         out_specs=tuple([VM] * len(outs)),
         scratch_shapes=list(scratch),
         compiler_params=pltpu.CompilerParams(vmem_limit_bytes=VMEM_LIMIT),
@@ -620,21 +768,6 @@
     return keep, got
 
 
-def sum_all(sc, sizes, keep, send):
-    keep, got = yield from halve(sc, sizes, keep, send)
-    (value,) = call(add_kernel, "add", (sc, keep, got), [rows_like(keep.shape[0])])
-    for hop in hops(sizes[2]):
-        got = swap(value, (2, hop))
-        value, got = yield value, got
-        (value,) = call(add_kernel, "add", (sc, value, got), [rows_like(value.shape[0])])
-    for step in reversed(halving_steps(sizes)):
-        got = swap(value, step)
-        value, got = yield value, got
-        out = rows_like(2 * value.shape[0])
-        (value,) = call(functools.partial(join_kernel_of, step, 0), "join", (sc, value, got), [out])
-    yield value, None
-
-
 class Background:
     def __init__(self):
         self.active = {}
@@ -689,7 +822,7 @@
     face_x = sds((y_len, rows, width))
     face_y = sds((x_len, rows, width))
     face_z = sds((x_len, y_len, width))
-    face_outs = [face_x] * nx + [face_y] * ny + [face_z] * nz
+    face_outs = [face_y] * ny + [face_z] * nz
     full = sds(grid)
     full16 = sds(grid, bf16)
     full3 = sds((3,) + grid)
@@ -709,56 +842,56 @@
 
     background = Background()
 
-    def exchange(faces):
-        got_x = trade(background.beside(faces[:nx]), "gx")
+    pair = pltpu.VMEM((2,) + grid[1:], f32)
+
+    def first_trade(kernel, name, inputs, scratch, flops):
+        faces = call(functools.partial(kernel, trades, sizes), name, (sc, *inputs), [face_x] * nx, scratch, flops)
+        return trade(faces, "gx")
+
+    def exchange(got_x, faces):
         fix = functools.partial(fix_y_kernel, trades)
-        faces_y = call(fix, "fix_y", (sc, *got_x, *faces[nx : nx + ny]), [face_y] * ny)
+        faces_y = call(fix, "fix_y", (sc, *got_x, *faces[:ny]), [face_y] * ny)
         got_y = trade(background.beside(faces_y), "gy")
         fix = functools.partial(fix_z_kernel, trades)
-        faces_z = call(fix, "fix_z", (sc, *got_x, *got_y, *faces[nx + ny :]), [face_z] * nz)
+        faces_z = call(fix, "fix_z", (sc, *got_x, *got_y, *faces[ny:]), [face_z] * nz)
         got_z = background.beside(trade(background.beside(faces_z), "gz"))
         return (*got_x, *got_y, *got_z)
 
+    got_x = first_trade(first_face_kernel, "face0", (edge_weights, biases, h0), [], matmul // 8)
     sums, slopes0, *faces = call(
-        functools.partial(first_kernel, trades, sizes), "edges0", (sc, edge_weights, biases, h0), [full, full3] + face_outs,
-        [
-            pltpu.VMEM(grid, bf16),
-            pltpu.VMEM(edge_weights.shape, bf16),
-            pltpu.VMEM(biases.shape, f32),
-            pltpu.SemaphoreType.DMA((3,)),
-        ],
-        3 * matmul, pl.BlockSpec(memory_space=pltpu.HBM),
+        functools.partial(first_kernel, trades, sizes), "edges0", (sc, edge_weights, biases, h0),
+        [full, full3] + face_outs, [], 3 * matmul,
     )
-    halo = exchange(faces)
+    halo = exchange(got_x, faces)
+    inputs = (*weights, sums, h0, *halo)
+    got_x = first_trade(middle_face_kernel, "face1", inputs, [pair, inv], matmul // 4)
     scaled0, act0, slope0, h1, sums, slopes1, *faces = run(
         middle_kernel, "nodes0_edges1", (sums, h0, *halo),
         [full16, full16, full, full16, full, full3] + face_outs, [work, inv], 8,
     )
-    halo = exchange(faces)
-    def sum_rows(rows):
-        total = padded_rows(rows, sizes)
-        return [rows_like(total // 2)] * 2, pltpu.VMEM((total, width), f32)
-
-    halves, scratch = sum_rows(3 * width + NODES)
+    halo = exchange(got_x, faces)
+    inputs = (*weights, sums, h1, g2, *halo)
+    got_x = first_trade(turn_face_kernel, "face2", inputs, [pair, inv], matmul // 4)
+    base, sums, grads1, *faces = run(
+        turn_kernel, "nodes1_back", (sums, h1, g2, *halo), [full, full, rows_like(3 * width + NODES)] + face_outs,
+        [work, inv], 10,
+    )
+    halo = exchange(got_x, faces)
+    inputs = (*weights, sums, base, slopes1, slope0, *halo)
+    got_x = first_trade(join_face_kernel, "face3", inputs, [pair, inv], matmul // 4)
+    grad_rows = padded_rows(7 * width + 3 * NODES, sizes)
+    half = rows_like(grad_rows // 2)
     base, sums, keep, send, *faces = run(
-        turn_kernel, "nodes1_back", (sums, h1, g2, *halo), [full, full] + halves + face_outs, [work, inv, scratch], 10
+        join_kernel, "edges1_back_nodes0_back",
+        (sums, h1, base, slopes1, h0, scaled0, act0, slope0, grads1, *halo),
+        [full, full, half, half] + face_outs, [work, inv, pltpu.VMEM((grad_rows, width), f32)], 12,
     )
-    background.add("layer1", sum_all(sc, sizes, keep, send))
-    halo = exchange(faces)
-    halves, scratch = sum_rows(4 * width + 2 * NODES)
-    base, sums, keep, send, *faces = run(
-        join_kernel, "edges1_back_nodes0_back", (sums, h1, base, slopes1, h0, scaled0, act0, slope0, *halo),
-        [full, full] + halves + face_outs, [work, inv, scratch], 12,
-    )
-    background.add("layer0", halve(sc, sizes, keep, send))
-    halo = exchange(faces)
+    background.add("sums", halve(sc, sizes, keep, send))
+    halo = exchange(got_x, faces)
     tail_rows = width + NODES
-    grad0, last = run(
-        last_kernel, "edges0_back", (sums, h0, base, slopes0, *halo), [full16, rows_like(tail_rows)], [work], 6
-    )
-    last = background.beside(last)
-    summed1 = background.finish("layer1")
-    keep, got = background.finish("layer0")
+    edges, last = run(last_kernel, "edges0_back", (sums, h0, slopes0, *halo), [full, rows_like(tail_rows)], [], 6)
+    (grad0,) = call(state_kernel, "state_grad", (sc, edge_weights, base, edges), [full16], [], 2 * matmul)
+    keep, got = background.finish("sums")
     (value,) = call(stack_kernel, "stack", (sc, last, keep, got), [rows_like(tail_rows + keep.shape[0])])
     for hop in hops(sizes[2]):
         (value,) = call(add_kernel, "add", (sc, value, swap(value, (2, hop))), [rows_like(value.shape[0])])
@@ -770,7 +903,7 @@
     nodes_all = x_len * sizes[0] * y_len * sizes[1] * layers_all * nodes
     scale = 1.0 / math.sqrt(nodes_all)
     edge_grads, in_grads, out_grads, bias_grads = call(
-        functools.partial(finish_kernel, scale, tail_rows), "finish", (sc, edge_weights, node_in, value, summed1),
+        functools.partial(finish_kernel, scale, tail_rows), "finish", (sc, edge_weights, node_in, value),
         [sds(edge_weights.shape), sds(node_in.shape), sds(node_out.shape), sds(biases.shape)],
     )
     return grad0.reshape(state.shape), edge_grads, in_grads, out_grads, bias_grads

time: 162 us -> 143 us (0.88)
  waiting for transfers between devices: 44.9 us -> 30 us
  starting transfers between devices: 61.1 us -> 56 us
    ppermute x16 -> x8, starting transfers between devices: 31.1 us -> 20.4 us  [swap(): lax.ppermute(value, axis, [(i, i ^ step[1]) for i in range(lax.axis_size(...]
    ppermute x16 -> x8, waiting for transfers between devices: 28.7 us -> 20.9 us  [swap(): lax.ppermute(value, axis, [(i, i ^ step[1]) for i in range(lax.axis_size(...]
    ppermute x20, waiting for transfers between devices: 16.3 us -> 9.11 us  [trade(): lax.ppermute(face, axis, pairs(size, kind))]
    ppermute x20, starting transfers between devices: 30 us -> 35.6 us  [trade(): lax.ppermute(face, axis, pairs(size, kind))]
    pallas_call x30 -> x27, Pallas kernels: 50.7 us -> 52 us  [call(): pl.pallas_call(kernel, name=name, out_shape=tuple(outs), in_specs=[SM] +...]
  transfers between devices with their start and end apart: 36 -> 28, of which waited for: 20 -> 12; matrix products, arithmetic and copies ran while one was open for 0% -> 0% of each run, Pallas kernels for 13% -> 27%
where the time goes in v3:
time: 143 us
  starting transfers between devices  56 us (39%)
  Pallas kernels  52 us (36%)
  waiting for transfers between devices  30 us (21%)
  local copies, waits for them, and re-layouts  2.83 us (2%)
  between operations  1.61 us (1%)
    pallas_call x27, Pallas kernels, call(): pl.pallas_call(kernel, name=name, out_shape=tuple(outs), in_specs=[SM] +...  52 us
    ppermute x20, starting transfers between devices, trade(): lax.ppermute(face, axis, pairs(size, kind))  35.6 us
    ppermute x8, waiting for transfers between devices, swap(): lax.ppermute(value, axis, [(i, i ^ step[1]) for i in range(lax.axis_size(...  20.9 us
    ppermute x8, starting transfers between devices, swap(): lax.ppermute(value, axis, [(i, i ^ step[1]) for i in range(lax.axis_size(...  20.4 us
    ppermute x20, waiting for transfers between devices, trade(): lax.ppermute(face, axis, pairs(size, kind))  9.11 us
  transfers between devices with their start and end apart: 28, of which 12 were waited for; matrix products, arithmetic and copies ran while one was open for 0% of the time, Pallas kernels for 27%

profile of v3, /device:TPU:0, one launch (start us, length us, event | category | flops | bytes accessed | tf_op | source)
XLA Modules:
  0.0 142.5 jit_solution(8452840107667863315)
XLA Ops:
  1.4 1.2 copy-done
  2.6 0.9 copy-done.2
  3.5 0.7 copy-done.7
  4.2 0.8 face0.1
  5.0 3.0 %collective-permute-start = (f32[16,16,128]{2,1,0:T(8,128)S(1)}, f32[16,16,128]{2,1,0:T(8,128)S(1)}, u32[]{:S(2)}, u32[]{:S(2)}) collective-permute-start(f32[16,16,128]{2,1,0:T(8,128)S(1)} %face0.1), channel_id=1, source_target_pairs={{0,16},{16,0},{1,17},{17,1},{2,18},{18,2},{3,19},{19,3},{4,20},{20... | collective-permute-start | bytes 393224 | tf_op jit(solution)/shard_map/ppermute | solution.py:840
  8.0 5.1 %edges0.1 = (f32[16,16,16,128]{3,2,1,0:T(8,128)S(1)}, f32[3,16,16,16,128]{4,3,2,1,0:T(8,128)S(1)}, f32[16,16,128]{2,1,0:T(8,128)S(1)}, f32[16,16,128]{2,1,0:T(8,...) custom-call(s32[4]{0:T(128)S(1)} %pad_add_fusion.sc.sc_ref, bf16[2,2,128,128]{3,2,1,0:T(8,128)(2,1)S(1)} %copy-done.2, ...), custom_call_target="tpu_custom_call" | custom-call | flops 402653184 | bytes 10094608 | tf_op jit(solution)/shard_map/edges0/pallas_call | solution.py:673
  13.8 0.7 collective-permute-start.2
  14.4 0.7 collective-permute-done.1.refs_1_
  15.1 0.7 fix_z.4
  15.8 1.6 %collective-permute-start.3 = (f32[16,16,128]{2,1,0:T(8,128)S(1)}, f32[16,16,128]{2,1,0:T(8,128)S(1)}, u32[]{:S(2)}, u32[]{:S(2)}) collective-permute-start(f32[16,16,128]{2,1,0:T(8,128)S(1)} %get-tuple-element.77), channel_id=1, source_target_pairs={{0,1},{1,0},{2,3},{3,2},{4,5},{5,4},{6,7},{7,6},{8,9},{9,8},{10,11... | collective-permute-start | bytes 393224 | tf_op jit(solution)/shard_map/ppermute | solution.py:840
  17.4 0.7 collective-permute-start.4
  18.1 2.7 %collective-permute-done.3.refs_3_ = f32[16,16,128]{2,1,0:T(8,128)S(1)} collective-permute-done((f32[16,16,128]{2,1,0:T(8,128)S(1)}, f32[16,16,128]{2,1,0:T(8,128)S(1)}, u32[]{:S(2)}, u32[]{:S(2)}) %collective-permute-start.3) | collective-permute-done | bytes 131104 | tf_op jit(solution)/shard_map/ppermute | solution.py:840
  20.8 1.4 face1.1
  22.5 8.7 %nodes0_edges1.1 = (bf16[16,16,16,128]{3,2,1,0:T(8,128)(2,1)S(1)}, bf16[16,16,16,128]{3,2,1,0:T(8,128)(2,1)S(1)}, f32[16,16,16,128]{3,2,1,0:T(8,128)S(1)}, bf16[...) custom-call(s32[4]{0:T(128)S(1)} %pad_add_fusion.sc.sc_ref, ...), custom_call_target="tpu_custom_call" | custom-call | flops 1073741824 | bytes 18286608 | tf_op jit(solution)/shard_map/nodes0_edges1/pallas_call | solution.py:673
  31.8 4.6 %collective-permute-start.6 = (f32[16,16,128]{2,1,0:T(8,128)S(1)}, f32[16,16,128]{2,1,0:T(8,128)S(1)}, u32[]{:S(2)}, u32[]{:S(2)}) collective-permute-start(f32[16,16,128]{2,1,0:T(8,128)S(1)} %get-tuple-element.83), channel_id=1, source_target_pairs={{0,4},{4,0},{8,12},{12,8},{1,5},{5,1},{9,13},{13,9},{2,6},{6,2},{1... | collective-permute-start | bytes 393224 | tf_op jit(solution)/shard_map/ppermute | solution.py:840
  36.3 0.7 collective-permute-start.7
  37.3 0.7 fix_z.5
  38.0 4.8 %collective-permute-start.8 = (f32[16,16,128]{2,1,0:T(8,128)S(1)}, f32[16,16,128]{2,1,0:T(8,128)S(1)}, u32[]{:S(2)}, u32[]{:S(2)}) collective-permute-start(f32[16,16,128]{2,1,0:T(8,128)S(1)} %get-tuple-element.87), channel_id=1, source_target_pairs={{0,1},{1,0},{2,3},{3,2},{4,5},{5,4},{6,7},{7,6},{8,9},{9,8},{10,11... | collective-permute-start | bytes 393224 | tf_op jit(solution)/shard_map/ppermute | solution.py:840
  42.8 0.7 collective-permute-start.9
  43.5 2.3 %collective-permute-done.8.refs_3_ = f32[16,16,128]{2,1,0:T(8,128)S(1)} collective-permute-done((f32[16,16,128]{2,1,0:T(8,128)S(1)}, f32[16,16,128]{2,1,0:T(8,128)S(1)}, u32[]{:S(2)}, u32[]{:S(2)}) %collective-permute-start.8) | collective-permute-done | bytes 131104 | tf_op jit(solution)/shard_map/ppermute | solution.py:840
  45.8 1.2 face2.1
  47.0 1.6 %collective-permute-start.10 = (f32[16,16,128]{2,1,0:T(8,128)S(1)}, f32[16,16,128]{2,1,0:T(8,128)S(1)}, u32[]{:S(2)}, u32[]{:S(2)}) collective-permute-start(f32[16,16,128]{2,1,0:T(8,128)S(1)} %face2.1), channel_id=1, source_target_pairs={{0,16},{16,0},{1,17},{17,1},{2,18},{18,2},{3,19},{19,3},{4,20},{20... | collective-permute-start | bytes 393224 | tf_op jit(solution)/shard_map/ppermute | solution.py:840
  48.5 6.3 %nodes1_back.1 = (f32[16,16,16,128]{3,2,1,0:T(8,128)S(1)}, f32[16,16,16,128]{3,2,1,0:T(8,128)S(1)}, f32[392,128]{1,0:T(8,128)S(1)}, f32[16,16,128]{2,1,0:T(8,128...) custom-call(s32[4]{0:T(128)S(1)} %pad_add_fusion.sc.sc_ref, ...), custom_call_target="tpu_custom_call" | custom-call | flops 1342177280 | bytes 10098704 | tf_op jit(solution)/shard_map/nodes1_back/pallas_call | solution.py:673
  55.4 5.1 %collective-permute-start.11 = (f32[16,16,128]{2,1,0:T(8,128)S(1)}, f32[16,16,128]{2,1,0:T(8,128)S(1)}, u32[]{:S(2)}, u32[]{:S(2)}) collective-permute-start(f32[16,16,128]{2,1,0:T(8,128)S(1)} %get-tuple-element.98), channel_id=1, source_target_pairs={{0,4},{4,0},{8,12},{12,8},{1,5},{5,1},{9,13},{13,9},{2,6},{6,2},{1... | collective-permute-start | bytes 393224 | tf_op jit(solution)/shard_map/ppermute | solution.py:840
  61.4 0.7 fix_z.6
  62.1 4.3 %collective-permute-start.13 = (f32[16,16,128]{2,1,0:T(8,128)S(1)}, f32[16,16,128]{2,1,0:T(8,128)S(1)}, u32[]{:S(2)}, u32[]{:S(2)}) collective-permute-start(f32[16,16,128]{2,1,0:T(8,128)S(1)} %get-tuple-element.102), channel_id=1, source_target_pairs={{0,1},{1,0},{2,3},{3,2},{4,5},{5,4},{6,7},{7,6},{8,9},{9,8},{10,11... | collective-permute-start | bytes 393224 | tf_op jit(solution)/shard_map/ppermute | solution.py:840
  66.4 0.8 collective-permute-start.14
  67.3 2.1 %collective-permute-done.13.refs_3_ = f32[16,16,128]{2,1,0:T(8,128)S(1)} collective-permute-done((f32[16,16,128]{2,1,0:T(8,128)S(1)}, f32[16,16,128]{2,1,0:T(8,128)S(1)}, u32[]{:S(2)}, u32[]{:S(2)}) %collective-permute-start.13) | collective-permute-done | bytes 131104 | tf_op jit(solution)/shard_map/ppermute | solution.py:840
  69.4 1.3 face3.1
  71.3 8.1 %edges1_back_nodes0_back.1 = (f32[16,16,16,128]{3,2,1,0:T(8,128)S(1)}, f32[16,16,16,128]{3,2,1,0:T(8,128)S(1)}, f32[480,128]{1,0:T(8,128)S(1)}, f32[480,128]{1,0...) custom-call(s32[4]{0:T(128)S(1)} %pad_add_fusion.sc.sc_ref, ...), custom_call_target="tpu_custom_call" | custom-call | flops 1610612736 | bytes 23173136 | tf_op jit(solution)/shard_map/edges1_back_nodes0_back/pallas_call | solution.py:673
  79.4 5.1 %collective-permute-start.18 = (f32[480,128]{1,0:T(8,128)S(1)}, f32[480,128]{1,0:T(8,128)S(1)}, u32[]{:S(2)}, u32[]{:S(2)}) collective-permute-start(f32[480,128]{1,0:T(8,128)S(1)} %get-tuple-element.116), channel_id=1, source_target_pairs={{0,4},{4,0},{8,12},{12,8},{1,5},{5,1},{9,13},{13,9},{2,6},{6,2},{1... | collective-permute-start | bytes 737288 | tf_op jit(solution)/shard_map/ppermute | solution.py:749
  85.2 0.7 collective-permute-start.17
  85.9 0.7 collective-permute-done.16.refs_1_
  86.5 0.7 fix_z.7
  87.2 4.3 %collective-permute-start.19 = (f32[16,16,128]{2,1,0:T(8,128)S(1)}, f32[16,16,128]{2,1,0:T(8,128)S(1)}, u32[]{:S(2)}, u32[]{:S(2)}) collective-permute-start(f32[16,16,128]{2,1,0:T(8,128)S(1)} %get-tuple-element.117), channel_id=1, source_target_pairs={{0,1},{1,0},{2,3},{3,2},{4,5},{5,4},{6,7},{7,6},{8,9},{9,8},{10,11... | collective-permute-start | bytes 393224 | tf_op jit(solution)/shard_map/ppermute | solution.py:840
  92.8 1.5 %collective-permute-start.21 = (f32[240,128]{1,0:T(8,128)S(1)}, f32[240,128]{1,0:T(8,128)S(1)}, u32[]{:S(2)}, u32[]{:S(2)}) collective-permute-start(f32[240,128]{1,0:T(8,128)S(1)} %get-tuple-element.122), channel_id=1, source_target_pairs={{0,16},{16,0},{1,17},{17,1},{2,18},{18,2},{3,19},{19,3},{4,20},{20... | collective-permute-start | bytes 368648 | tf_op jit(solution)/shard_map/ppermute | solution.py:749
  94.3 3.4 %collective-permute-done.21.got = f32[240,128]{1,0:T(8,128)S(1)} collective-permute-done((f32[240,128]{1,0:T(8,128)S(1)}, f32[240,128]{1,0:T(8,128)S(1)}, u32[]{:S(2)}, u32[]{:S(2)}) %collective-permute-start.21) | collective-permute-done | bytes 122912 | tf_op jit(solution)/shard_map/ppermute | solution.py:749
  98.3 7.7 %collective-permute-start.22 = (f32[120,128]{1,0:T(8,128)S(1)}, f32[120,128]{1,0:T(8,128)S(1)}, u32[]{:S(2)}, u32[]{:S(2)}) collective-permute-start(f32[120,128]{1,0:T(8,128)S(1)} %get-tuple-element.130), channel_id=1, source_target_pairs={{0,8},{4,12},{8,0},{12,4},{1,9},{5,13},{9,1},{13,5},{2,10},{6,14},... | collective-permute-start | bytes 184328 | tf_op jit(solution)/shard_map/ppermute | solution.py:749
  106.0 5.1 %edges0_back.1 = (f32[16,16,16,128]{3,2,1,0:T(8,128)S(1)}, f32[136,128]{1,0:T(8,128)S(1)}) custom-call(s32[4]{0:T(128)S(1)} %pad_add_fusion.sc.sc_ref, bf16[2,2,128,128]{3,2,1,0:T(8,128)(2,1)S(1)} %copy-done.3, bf16[2,256,128]{2,1,0:T(8,128)(2,1)S(1)} %copy-done.4, bf16[2,128,128]{2,1,0:T(8,128)(2,1)S(1)} %copy-done.6, f32[2,2,128]{2,1,0:T(2,128)S(1)} %copy-done.7, ...), custom_call_target="tpu_custom_call" | custom-call | flops 805306368 | bytes 12589072 | tf_op jit(solution)/shard_map/edges0_back/pallas_call | solution.py:673
  111.6 3.3 %collective-permute-start.23 = (f32[256,128]{1,0:T(8,128)S(1)}, f32[256,128]{1,0:T(8,128)S(1)}, u32[]{:S(2)}, u32[]{:S(2)}) collective-permute-start(f32[256,128]{1,0:T(8,128)S(1)} %stack.17.left), channel_id=1, source_target_pairs={{0,1},{1,0},{2,3},{3,2},{4,5},{5,4},{6,7},{7,6},{8,9},{9,8},{10,11... | collective-permute-start | bytes 393224 | tf_op jit(solution)/shard_map/ppermute | solution.py:749
  115.0 3.5 %collective-permute-done.23.right = f32[256,128]{1,0:T(8,128)S(1)} collective-permute-done((f32[256,128]{1,0:T(8,128)S(1)}, f32[256,128]{1,0:T(8,128)S(1)}, u32[]{:S(2)}, u32[]{:S(2)}) %collective-permute-start.23) | collective-permute-done | bytes 131104 | tf_op jit(solution)/shard_map/ppermute | solution.py:749
  119.0 1.0 collective-permute-start.24
  120.0 4.9 %collective-permute-done.24.right = f32[256,128]{1,0:T(8,128)S(1)} collective-permute-done((f32[256,128]{1,0:T(8,128)S(1)}, f32[256,128]{1,0:T(8,128)S(1)}, u32[]{:S(2)}, u32[]{:S(2)}) %collective-permute-start.24) | collective-permute-done | bytes 131104 | tf_op jit(solution)/shard_map/ppermute | solution.py:749
  125.6 5.0 %collective-permute-done.25.got = f32[256,128]{1,0:T(8,128)S(1)} collective-permute-done((f32[256,128]{1,0:T(8,128)S(1)}, f32[256,128]{1,0:T(8,128)S(1)}, u32[]{:S(2)}, u32[]{:S(2)}) %collective-permute-start.25) | collective-permute-done | bytes 131104 | tf_op jit(solution)/shard_map/ppermute | solution.py:749
  131.1 1.6 %collective-permute-start.26 = (f32[376,128]{1,0:T(8,128)S(1)}, f32[376,128]{1,0:T(8,128)S(1)}, u32[]{:S(2)}, u32[]{:S(2)}) collective-permute-start(f32[376,128]{1,0:T(8,128)S(1)} %join.3.value), channel_id=1, source_target_pairs={{0,16},{16,0},{1,17},{17,1},{2,18},{18,2},{3,19},{19,3},{4,20},{20... | collective-permute-start | bytes 577544 | tf_op jit(solution)/shard_map/ppermute | solution.py:749
  132.7 4.1 %collective-permute-done.26.got = f32[376,128]{1,0:T(8,128)S(1)} collective-permute-done((f32[376,128]{1,0:T(8,128)S(1)}, f32[376,128]{1,0:T(8,128)S(1)}, u32[]{:S(2)}, u32[]{:S(2)}) %collective-permute-start.26) | collective-permute-done | bytes 192544 | tf_op jit(solution)/shard_map/ppermute | solution.py:749
  137.5 2.8 %state_grad.1 = bf16[16,16,16,128]{3,2,1,0:T(8,128)(2,1)} custom-call(s32[4]{0:T(128)S(1)} %pad_add_fusion.sc.sc_ref, bf16[2,2,128,128]{3,2,1,0:T(8,128)(2,1)S(1)} %copy-done.3, f32[16,16,16,128]{3,2,1,0:T(8,128)S(1)} %get-tuple-element.104.base_in, f32[16,16,16,128]{3,2,1,0:T(8,128)S(1)} %get-tuple-element.125.edges), custom_call_target="tpu_custom_call" | custom-call | flops 268435456 | bytes 5373968 | tf_op jit(solution)/shard_map/state_grad/pallas_call | solution.py:673
  140.8 1.7 %finish.1 = (f32[2,2,128,128]{3,2,1,0:T(8,128)}, f32[2,256,128]{2,1,0:T(8,128)}, f32[2,128,128]{2,1,0:T(8,128)}, f32[2,2,128]{2,1,0:T(2,128)}) custom-call(s32[4]{0:T(128)S(1)} %pad_add_fusion.sc.sc_ref, bf16[2,2,128,128]{3,2,1,0:T(8,128)(2,1)S(1)} %copy-done.3, bf16[2,256,128]{2,1,0:T(8,128)(2,1)S(1)} %copy-done.4, f32[1096,128]{1,0:T(8,128)S(1)} %join.5.both), custom_call_target="tpu_custom_call" | custom-call | bytes 1480720 | tf_op jit(solution)/shard_map/finish/pallas_call | solution.py:673
  (52 shorter events, 10.0 us)
Async XLA Ops:
  1.4 1.2 copy-start
  2.6 0.9 copy-start.2
  3.5 0.7 copy-start.7
  4.2 16.6 %copy-start.1 = (bf16[16,16,2,8,128]{4,3,2,1,0:T(8,128)(2,1)S(1)}, bf16[16,16,2,8,128]{4,3,2,1,0:T(8,128)(2,1)}, u32[]{:S(2)}) copy-start(bf16[16,16,2,8,128]{4,3,2,1,0:T(8,128)(2,1)} %param.7) | copy-start | bytes 3145732
  4.2 16.6 %copy-start.3 = (bf16[2,2,128,128]{3,2,1,0:T(8,128)(2,1)S(1)}, bf16[2,2,128,128]{3,2,1,0:T(8,128)(2,1)}, u32[]{:S(2)}) copy-start(bf16[2,2,128,128]{3,2,1,0:T(8,128)(2,1)} %edge_w.21) | copy-start | bytes 393220
  4.2 16.7 %copy-start.4 = (bf16[2,256,128]{2,1,0:T(8,128)(2,1)S(1)}, bf16[2,256,128]{2,1,0:T(8,128)(2,1)}, u32[]{:S(2)}) copy-start(bf16[2,256,128]{2,1,0:T(8,128)(2,1)} %node_in.15) | copy-start | bytes 393220
  4.2 16.7 %copy-start.6 = (bf16[2,128,128]{2,1,0:T(8,128)(2,1)S(1)}, bf16[2,128,128]{2,1,0:T(8,128)(2,1)}, u32[]{:S(2)}) copy-start(bf16[2,128,128]{2,1,0:T(8,128)(2,1)} %node_out.13) | copy-start | bytes 196612
  5.0 8.1 %collective-permute-start = (f32[16,16,128]{2,1,0:T(8,128)S(1)}, f32[16,16,128]{2,1,0:T(8,128)S(1)}, u32[]{:S(2)}, u32[]{:S(2)}) collective-permute-start(f32[16,16,128]{2,1,0:T(8,128)S(1)} %face0.1), channel_id=1, source_target_pairs={{0,16},{16,0},{1,17},{17,1},{2,18},{18,2},{3,19},{19,3},{4,20},{20... | collective-permute-start | bytes 393224 | tf_op jit(solution)/shard_map/ppermute | solution.py:840
  13.7 1.4 collective-permute-start.1
  13.8 1.3 collective-permute-start.2
  15.8 5.0 %collective-permute-start.3 = (f32[16,16,128]{2,1,0:T(8,128)S(1)}, f32[16,16,128]{2,1,0:T(8,128)S(1)}, u32[]{:S(2)}, u32[]{:S(2)}) collective-permute-start(f32[16,16,128]{2,1,0:T(8,128)S(1)} %get-tuple-element.77), channel_id=1, source_target_pairs={{0,1},{1,0},{2,3},{3,2},{4,5},{5,4},{6,7},{7,6},{8,9},{9,8},{10,11... | collective-permute-start | bytes 393224 | tf_op jit(solution)/shard_map/ppermute | solution.py:840
  17.4 3.4 %collective-permute-start.4 = (f32[16,16,128]{2,1,0:T(8,128)S(1)}, f32[16,16,128]{2,1,0:T(8,128)S(1)}, u32[]{:S(2)}, u32[]{:S(2)}) collective-permute-start(f32[16,16,128]{2,1,0:T(8,128)S(1)} %get-tuple-element.78), channel_id=1, source_target_pairs={{1,2},{2,1},{5,6},{6,5},{9,10},{10,9},{13,14},{14,13},{17,18},{18,... | collective-permute-start | bytes 393224 | tf_op jit(solution)/shard_map/ppermute | solution.py:840
  22.3 23.5 %copy-start.5 = (bf16[16,16,2,8,128]{4,3,2,1,0:T(8,128)(2,1)S(1)}, bf16[16,16,2,8,128]{4,3,2,1,0:T(8,128)(2,1)}, u32[]{:S(2)}) copy-start(bf16[16,16,2,8,128]{4,3,2,1,0:T(8,128)(2,1)} %param.8) | copy-start | bytes 3145732
  22.3 8.9 %collective-permute-start.5 = (f32[16,16,128]{2,1,0:T(8,128)S(1)}, f32[16,16,128]{2,1,0:T(8,128)S(1)}, u32[]{:S(2)}, u32[]{:S(2)}) collective-permute-start(f32[16,16,128]{2,1,0:T(8,128)S(1)} %face1.1), channel_id=1, source_target_pairs={{0,16},{16,0},{1,17},{17,1},{2,18},{18,2},{3,19},{19,3},{4,20},{20... | collective-permute-start | bytes 393224 | tf_op jit(solution)/shard_map/ppermute | solution.py:840
  31.8 5.6 %collective-permute-start.6 = (f32[16,16,128]{2,1,0:T(8,128)S(1)}, f32[16,16,128]{2,1,0:T(8,128)S(1)}, u32[]{:S(2)}, u32[]{:S(2)}) collective-permute-start(f32[16,16,128]{2,1,0:T(8,128)S(1)} %get-tuple-element.83), channel_id=1, source_target_pairs={{0,4},{4,0},{8,12},{12,8},{1,5},{5,1},{9,13},{13,9},{2,6},{6,2},{1... | collective-permute-start | bytes 393224 | tf_op jit(solution)/shard_map/ppermute | solution.py:840
  36.3 1.0 collective-permute-start.7
  38.0 7.8 %collective-permute-start.8 = (f32[16,16,128]{2,1,0:T(8,128)S(1)}, f32[16,16,128]{2,1,0:T(8,128)S(1)}, u32[]{:S(2)}, u32[]{:S(2)}) collective-permute-start(f32[16,16,128]{2,1,0:T(8,128)S(1)} %get-tuple-element.87), channel_id=1, source_target_pairs={{0,1},{1,0},{2,3},{3,2},{4,5},{5,4},{6,7},{7,6},{8,9},{9,8},{10,11... | collective-permute-start | bytes 393224 | tf_op jit(solution)/shard_map/ppermute | solution.py:840
  42.8 3.0 %collective-permute-start.9 = (f32[16,16,128]{2,1,0:T(8,128)S(1)}, f32[16,16,128]{2,1,0:T(8,128)S(1)}, u32[]{:S(2)}, u32[]{:S(2)}) collective-permute-start(f32[16,16,128]{2,1,0:T(8,128)S(1)} %get-tuple-element.88), channel_id=1, source_target_pairs={{1,2},{2,1},{5,6},{6,5},{9,10},{10,9},{13,14},{14,13},{17,18},{18,... | collective-permute-start | bytes 393224 | tf_op jit(solution)/shard_map/ppermute | solution.py:840
  47.0 7.8 %collective-permute-start.10 = (f32[16,16,128]{2,1,0:T(8,128)S(1)}, f32[16,16,128]{2,1,0:T(8,128)S(1)}, u32[]{:S(2)}, u32[]{:S(2)}) collective-permute-start(f32[16,16,128]{2,1,0:T(8,128)S(1)} %face2.1), channel_id=1, source_target_pairs={{0,16},{16,0},{1,17},{17,1},{2,18},{18,2},{3,19},{19,3},{4,20},{20... | collective-permute-start | bytes 393224 | tf_op jit(solution)/shard_map/ppermute | solution.py:840
  55.4 6.0 %collective-permute-start.11 = (f32[16,16,128]{2,1,0:T(8,128)S(1)}, f32[16,16,128]{2,1,0:T(8,128)S(1)}, u32[]{:S(2)}, u32[]{:S(2)}) collective-permute-start(f32[16,16,128]{2,1,0:T(8,128)S(1)} %get-tuple-element.98), channel_id=1, source_target_pairs={{0,4},{4,0},{8,12},{12,8},{1,5},{5,1},{9,13},{13,9},{2,6},{6,2},{1... | collective-permute-start | bytes 393224 | tf_op jit(solution)/shard_map/ppermute | solution.py:840
  60.5 1.0 collective-permute-start.12
  62.1 7.2 %collective-permute-start.13 = (f32[16,16,128]{2,1,0:T(8,128)S(1)}, f32[16,16,128]{2,1,0:T(8,128)S(1)}, u32[]{:S(2)}, u32[]{:S(2)}) collective-permute-start(f32[16,16,128]{2,1,0:T(8,128)S(1)} %get-tuple-element.102), channel_id=1, source_target_pairs={{0,1},{1,0},{2,3},{3,2},{4,5},{5,4},{6,7},{7,6},{8,9},{9,8},{10,11... | collective-permute-start | bytes 393224 | tf_op jit(solution)/shard_map/ppermute | solution.py:840
  66.4 3.0 %collective-permute-start.14 = (f32[16,16,128]{2,1,0:T(8,128)S(1)}, f32[16,16,128]{2,1,0:T(8,128)S(1)}, u32[]{:S(2)}, u32[]{:S(2)}) collective-permute-start(f32[16,16,128]{2,1,0:T(8,128)S(1)} %get-tuple-element.103), channel_id=1, source_target_pairs={{1,2},{2,1},{5,6},{6,5},{9,10},{10,9},{13,14},{14,13},{17,18},{18,... | collective-permute-start | bytes 393224 | tf_op jit(solution)/shard_map/ppermute | solution.py:840
  70.7 13.8 %collective-permute-start.15 = (f32[16,16,128]{2,1,0:T(8,128)S(1)}, f32[16,16,128]{2,1,0:T(8,128)S(1)}, u32[]{:S(2)}, u32[]{:S(2)}) collective-permute-start(f32[16,16,128]{2,1,0:T(8,128)S(1)} %face3.1), channel_id=1, source_target_pairs={{0,16},{16,0},{1,17},{17,1},{2,18},{18,2},{3,19},{19,3},{4,20},{20... | collective-permute-start | bytes 393224 | tf_op jit(solution)/shard_map/ppermute | solution.py:840
  79.4 7.8 %collective-permute-start.18 = (f32[480,128]{1,0:T(8,128)S(1)}, f32[480,128]{1,0:T(8,128)S(1)}, u32[]{:S(2)}, u32[]{:S(2)}) collective-permute-start(f32[480,128]{1,0:T(8,128)S(1)} %get-tuple-element.116), channel_id=1, source_target_pairs={{0,4},{4,0},{8,12},{12,8},{1,5},{5,1},{9,13},{13,9},{2,6},{6,2},{1... | collective-permute-start | bytes 737288 | tf_op jit(solution)/shard_map/ppermute | solution.py:749
  85.1 1.4 collective-permute-start.16
  85.2 1.3 collective-permute-start.17
  87.2 10.5 %collective-permute-start.19 = (f32[16,16,128]{2,1,0:T(8,128)S(1)}, f32[16,16,128]{2,1,0:T(8,128)S(1)}, u32[]{:S(2)}, u32[]{:S(2)}) collective-permute-start(f32[16,16,128]{2,1,0:T(8,128)S(1)} %get-tuple-element.117), channel_id=1, source_target_pairs={{0,1},{1,0},{2,3},{3,2},{4,5},{5,4},{6,7},{7,6},{8,9},{9,8},{10,11... | collective-permute-start | bytes 393224 | tf_op jit(solution)/shard_map/ppermute | solution.py:840
  91.5 6.2 %collective-permute-start.20 = (f32[16,16,128]{2,1,0:T(8,128)S(1)}, f32[16,16,128]{2,1,0:T(8,128)S(1)}, u32[]{:S(2)}, u32[]{:S(2)}) collective-permute-start(f32[16,16,128]{2,1,0:T(8,128)S(1)} %get-tuple-element.118), channel_id=1, source_target_pairs={{1,2},{2,1},{5,6},{6,5},{9,10},{10,9},{13,14},{14,13},{17,18},{18,... | collective-permute-start | bytes 393224 | tf_op jit(solution)/shard_map/ppermute | solution.py:840
  92.8 4.9 %collective-permute-start.21 = (f32[240,128]{1,0:T(8,128)S(1)}, f32[240,128]{1,0:T(8,128)S(1)}, u32[]{:S(2)}, u32[]{:S(2)}) collective-permute-start(f32[240,128]{1,0:T(8,128)S(1)} %get-tuple-element.122), channel_id=1, source_target_pairs={{0,16},{16,0},{1,17},{17,1},{2,18},{18,2},{3,19},{19,3},{4,20},{20... | collective-permute-start | bytes 368648 | tf_op jit(solution)/shard_map/ppermute | solution.py:749
  98.3 12.8 %collective-permute-start.22 = (f32[120,128]{1,0:T(8,128)S(1)}, f32[120,128]{1,0:T(8,128)S(1)}, u32[]{:S(2)}, u32[]{:S(2)}) collective-permute-start(f32[120,128]{1,0:T(8,128)S(1)} %get-tuple-element.130), channel_id=1, source_target_pairs={{0,8},{4,12},{8,0},{12,4},{1,9},{5,13},{9,1},{13,5},{2,10},{6,14},... | collective-permute-start | bytes 184328 | tf_op jit(solution)/shard_map/ppermute | solution.py:749
  111.6 6.8 %collective-permute-start.23 = (f32[256,128]{1,0:T(8,128)S(1)}, f32[256,128]{1,0:T(8,128)S(1)}, u32[]{:S(2)}, u32[]{:S(2)}) collective-permute-start(f32[256,128]{1,0:T(8,128)S(1)} %stack.17.left), channel_id=1, source_target_pairs={{0,1},{1,0},{2,3},{3,2},{4,5},{5,4},{6,7},{7,6},{8,9},{9,8},{10,11... | collective-permute-start | bytes 393224 | tf_op jit(solution)/shard_map/ppermute | solution.py:749
  119.0 5.9 %collective-permute-start.24 = (f32[256,128]{1,0:T(8,128)S(1)}, f32[256,128]{1,0:T(8,128)S(1)}, u32[]{:S(2)}, u32[]{:S(2)}) collective-permute-start(f32[256,128]{1,0:T(8,128)S(1)} %add.8.left), channel_id=1, source_target_pairs={{0,2},{1,3},{2,0},{3,1},{4,6},{5,7},{6,4},{7,5},{8,10},{9,11},{10,... | collective-permute-start | bytes 393224 | tf_op jit(solution)/shard_map/ppermute | solution.py:749
  125.5 5.0 %collective-permute-start.25 = (f32[256,128]{1,0:T(8,128)S(1)}, f32[256,128]{1,0:T(8,128)S(1)}, u32[]{:S(2)}, u32[]{:S(2)}) collective-permute-start(f32[256,128]{1,0:T(8,128)S(1)} %add.9.value), channel_id=1, source_target_pairs={{0,8},{4,12},{8,0},{12,4},{1,9},{5,13},{9,1},{13,5},{2,10},{6,14},... | collective-permute-start | bytes 393224 | tf_op jit(solution)/shard_map/ppermute | solution.py:749
  131.1 5.7 %collective-permute-start.26 = (f32[376,128]{1,0:T(8,128)S(1)}, f32[376,128]{1,0:T(8,128)S(1)}, u32[]{:S(2)}, u32[]{:S(2)}) collective-permute-start(f32[376,128]{1,0:T(8,128)S(1)} %join.3.value), channel_id=1, source_target_pairs={{0,16},{16,0},{1,17},{17,1},{2,18},{18,2},{3,19},{19,3},{4,20},{20... | collective-permute-start | bytes 577544 | tf_op jit(solution)/shard_map/ppermute | solution.py:749
  137.4 2.9 %collective-permute-start.27 = (f32[616,128]{1,0:T(8,128)S(1)}, f32[616,128]{1,0:T(8,128)S(1)}, u32[]{:S(2)}, u32[]{:S(2)}) collective-permute-start(f32[616,128]{1,0:T(8,128)S(1)} %join.4.value), channel_id=1, source_target_pairs={{0,4},{4,0},{8,12},{12,8},{1,5},{5,1},{9,13},{13,9},{2,6},{6,2},{1... | collective-permute-start | bytes 946184 | tf_op jit(solution)/shard_map/ppermute | solution.py:749

commit v4 on v3

--- a/solution.py
+++ b/solution.py
@@ -91,7 +91,7 @@
     lax.fori_loop(0, total, step, 0)
 
 
-def edges_forward(h_ref, w_one, half_bias, filled, sum_ref, slope_ref):
+def edges_forward(h_ref, w_one, half_bias, filled, sum_ref, half_ref):
     x_len, y_len, rows, width = h_ref.shape
     inner = row_ids() < NODES - 1
 
@@ -109,22 +109,20 @@
             cols = node_rows(here)
             parts.append((up(cols) - cols).reshape(here.shape).astype(bf16))
             half = dot(flat(jnp.concatenate(parts, 0)), w_one).reshape(-1, rows, width) + half_bias
-            act, slope = silu_half(half)
-            act = act.astype(bf16).astype(f32)
+            act = (half + half * jnp.tanh(half)).astype(bf16).astype(f32)
             at = 0
             total = prev
             prev = None
             if i < NODES - 1:
                 prev = act[:NODES]
                 total = -prev if total is None else total - prev
-                slope_ref[0, x0 + i, ys] = slope[:NODES]
+                half_ref[0, x0 + i, ys] = half[:NODES]
                 at = NODES
             along_y = act[at : at + NODES - 1]
-            slope_ref[1, x0 + i, pl.ds(y0, NODES - 1)] = slope[at : at + NODES - 1]
+            half_ref[1, x0 + i, pl.ds(y0, NODES - 1)] = half[at : at + NODES - 1]
             at += NODES - 1
             along_z = jnp.where(inner, node_rows(act[at:]), 0.0)
-            slope_z = jnp.where(inner, node_rows(slope[at:]), 0.0)
-            slope_ref[2, x0 + i, ys] = slope_z.reshape(here.shape)
+            half_ref[2, x0 + i, ys] = half[at:]
             total = total + (down(along_z) - along_z).reshape(here.shape)
             total = jnp.concatenate(
                 [
@@ -138,6 +136,20 @@
             here = nxt
 
     elements(x_len, y_len, body)
+
+
+def slope_kernel(sc, half_in, slope_out):
+    inner = row_ids() < NODES - 1
+
+    def step(x, carry):
+        for k in range(3):
+            slope = silu_half(half_in[k, x])[1]
+            if k == 2:
+                slope = jnp.where(inner, node_rows(slope), 0.0).reshape(slope.shape)
+            slope_out[k, x] = slope
+        return carry
+
+    lax.fori_loop(0, half_in.shape[1], step, 0)
 
 
 def couple_columns(sum_ref):
@@ -288,20 +300,20 @@
     return (dot_rt(grad, weights[2][layer]) * slope).astype(bf16)
 
 
-def node_backward(sc_ref, x, inv_ref, size_x, grad, feat, scaled, act, slope, weights, layer, sum_ref, base_ref, grads):
+def node_share(sc_ref, x, inv_ref, size_x, dpn, weights, layer, sum_ref):
     shape = (CHUNK,) + sum_ref.shape[1:]
-    at = pl.ds(x, CHUNK)
-    dpn = node_slopes(grad, slope, weights, layer)
+    dx = dot_rt(dpn, weights[1][layer, pl.ds(128, 128)]).reshape(shape)
+    share = scale_planes(sc_ref, inv_ref, x, dx, sum_ref.shape[0], size_x)
+    joined = couple_slots(share.reshape((-1,) + shape[2:]), sc_ref[0])
+    sum_ref[pl.ds(x, CHUNK)] = joined.reshape(shape)
+
+
+def node_products(grad, feat, scaled, act, dpn, grads):
     grads[pl.ds(0, 128)] += dot_t(act, grad)
     both = dot_t(dpn, jnp.concatenate([feat, scaled], -1))
     grads[pl.ds(128, 128)] += both[:, :128]
     grads[pl.ds(256, 128)] += both[:, 128:]
     grads[pl.ds(384, NODES)] += jnp.sum(dpn.astype(f32).reshape(-1, NODES, 128), 0)
-    dx = dot_rt(dpn, weights[1][layer])
-    base_ref[at] = (grad.astype(f32) + dx[:, :128]).reshape(shape)
-    share = scale_planes(sc_ref, inv_ref, x, dx[:, 128:].reshape(shape), sum_ref.shape[0], size_x)
-    joined = couple_slots(share.reshape((-1,) + shape[2:]), sc_ref[0])
-    sum_ref[at] = joined.reshape(shape)
 
 
 def couple_plane(plane):
@@ -541,25 +553,45 @@
     weights = (edge_w, node_in, node_out, biases)
     n = sum(counts)
     halo, refs = refs[:n], refs[n:]
-    base, sums, grads = refs[:3]
-    faces, (work, inv) = refs[3:-2], refs[-2:]
+    scaled_ref, act_ref, dpn_ref, sums = refs[:4]
+    faces, (work, inv) = refs[4:-2], refs[-2:]
     add_halo(sc, sums_in, halo, work, counts)
     write_inverse(sc, inv, sizes)
-    grads[...] = jnp.zeros_like(grads)
-    live = (lax.broadcasted_iota(jnp.int32, (1, 1, h.shape[2], 128), 2) < sc[0] * NODES).astype(f32)
+    shape = (CHUNK,) + h.shape[1:]
+    live = live_rows(sc, h)
 
     def body(x):
         at = pl.ds(x, CHUNK)
         sums_at = flat(scale_planes(sc, inv, x, work[at], h.shape[0], sizes[0]))
         scaled, act, slope = node_forward(sums_at, flat(h[at]), weights, 1)
+        scaled_ref[at] = scaled.reshape(shape)
+        act_ref[at] = act.reshape(shape)
         grad = flat((g_ref[at].astype(f32) * live).astype(bf16))
-        node_backward(
-            sc, x, inv, sizes[0], grad, flat(h[at]), scaled, act, slope, weights, 1, sums, base, grads
-        )
+        dpn = node_slopes(grad, slope, weights, 1)
+        dpn_ref[at] = dpn.reshape(shape)
+        node_share(sc, x, inv, sizes[0], dpn, weights, 1, sums)
 
     planes(h.shape[0], body)
     couple_columns(sums)
     write_faces(sc, sums, faces, counts)
+
+
+def live_rows(sc, h):
+    return (lax.broadcasted_iota(jnp.int32, (1, 1, h.shape[2], 128), 2) < sc[0] * NODES).astype(f32)
+
+
+def products_kernel(sc, node_in, h, g_ref, scaled, act, dpn, base, grads):
+    grads[...] = jnp.zeros_like(grads)
+    live = live_rows(sc, h)
+
+    def body(x):
+        at = pl.ds(x, CHUNK)
+        grad = (g_ref[at].astype(f32) * live).astype(bf16)
+        node_products(flat(grad), flat(h[at]), flat(scaled[at]), flat(act[at]), flat(dpn[at]), grads)
+        dx = dot_rt(flat(dpn[at]), node_in[1, pl.ds(0, 128)])
+        base[at] = grad.astype(f32) + dx.reshape(grad.shape)
+
+    planes(h.shape[0], body)
 
 
 def edge_parts(counts, sc, weights, layer, sums_in, halo, h, slopes, work, grads, row):
@@ -587,13 +619,14 @@
     weights = (edge_w, node_in, node_out, biases)
     n = sum(counts)
     halo, refs = refs[:n], refs[n:]
-    base, sums, keep, send = refs[:4]
-    faces, (work, inv, grads) = refs[4:-3], refs[-3:]
+    grad_ref, dpn_ref, sums, keep, send = refs[:5]
+    faces, (work, inv, grads) = refs[5:-3], refs[-3:]
     write_inverse(sc, inv, sizes)
     grads[...] = jnp.zeros_like(grads)
     grads[pl.ds(512 + 2 * NODES, grads1.shape[0])] = grads1[...]
 
     row = 384 + NODES
+    shape = (CHUNK,) + h.shape[1:]
     edge_parts(counts, sc, weights, 1, sums_in, halo, h, slopes, work, grads, row)
     w_one = twice(edge_w[1, 0])
 
@@ -602,10 +635,11 @@
         pair = split_cols(flat(work[at]))
         edge_product(h, x, pair, grads, row)
         grad = (flat(base_in[at]) + dot_rt(pair, w_one)).astype(bf16)
-        node_backward(
-            sc, x, inv, sizes[0], grad, flat(h0[at]), flat(scaled0[at]), flat(act0[at]), flat(slope0[at]),
-            weights, 0, sums, base, grads,
-        )
+        dpn = node_slopes(grad, flat(slope0[at]), weights, 0)
+        node_products(grad, flat(h0[at]), flat(scaled0[at]), flat(act0[at]), dpn, grads)
+        grad_ref[at] = grad.reshape(shape)
+        dpn_ref[at] = dpn.reshape(shape)
+        node_share(sc, x, inv, sizes[0], dpn, weights, 0, sums)
 
     planes(h.shape[0], body)
     couple_columns(sums)
@@ -625,20 +659,22 @@
     planes(h.shape[0], body)
 
 
-def state_kernel(sc, edge_w, base_in, edges, grad_ref):
+def state_kernel(sc, edge_w, node_in, grad_in, dpn, edges, grad_ref):
     shape = (CHUNK,) + edges.shape[1:]
-    w_one = twice(edge_w[0, 0])
+    weight = jnp.concatenate([twice(edge_w[0, 0]), node_in[0, pl.ds(0, 128)]], 1)
 
     def body(x):
         at = pl.ds(x, CHUNK)
-        pair = split_cols(flat(edges[at]))
-        grad_ref[at] = (flat(base_in[at]) + dot_rt(pair, w_one)).astype(bf16).reshape(shape)
+        parts = jnp.concatenate([split_cols(flat(edges[at])), flat(dpn[at])], -1)
+        grad_ref[at] = (flat(grad_in[at]).astype(f32) + dot_rt(parts, weight)).astype(bf16).reshape(shape)
 
     planes(edges.shape[0], body)
 
 
-def finish_kernel(scale, last_rows, sc, edge_w, node_in, both, edge_grads, in_grads, out_grads, bias_grads):
+def finish_kernel(scale, last_rows, step, sc, edge_w, node_in, value, got, *refs):
+    edge_grads, in_grads, out_grads, bias_grads, both = refs
     width = edge_w.shape[-1]
+    join_kernel_of(step, last_rows, sc, value, got, both)
 
     def rows_of(part, start, count=width):
         ref, offset = part
@@ -667,7 +703,7 @@
         in_grads[layer, pl.ds(width, width)] = dot_t(w_two, high) + dot_t(w_two, low)
 
 
-def call(kernel, name, inputs, outs, scratch=(), flops=0):
+def call(kernel, name, inputs, outs, scratch=(), flops=0, aliases=None):
     total = sum(math.prod(o.shape) * o.dtype.itemsize for o in outs)
     total += sum(math.prod(i.shape) * i.dtype.itemsize for i in inputs)
     return pl.pallas_call(
@@ -677,6 +713,7 @@
         in_specs=[SM] + [VM] * (len(inputs) - 1),
         out_specs=tuple([VM] * len(outs)),
         scratch_shapes=list(scratch),
+        input_output_aliases=aliases or {},
         compiler_params=pltpu.CompilerParams(vmem_limit_bytes=VMEM_LIMIT),
         cost_estimate=pl.CostEstimate(flops=flops, bytes_accessed=total, transcendentals=0),
     )(*inputs)
@@ -848,54 +885,72 @@
         faces = call(functools.partial(kernel, trades, sizes), name, (sc, *inputs), [face_x] * nx, scratch, flops)
         return trade(faces, "gx")
 
-    def exchange(got_x, faces):
+    def exchange(got_x, faces, work=None, held=()):
         fix = functools.partial(fix_y_kernel, trades)
         faces_y = call(fix, "fix_y", (sc, *got_x, *faces[:ny]), [face_y] * ny)
         got_y = trade(background.beside(faces_y), "gy")
         fix = functools.partial(fix_z_kernel, trades)
         faces_z = call(fix, "fix_z", (sc, *got_x, *got_y, *faces[ny:]), [face_z] * nz)
-        got_z = background.beside(trade(background.beside(faces_z), "gz"))
-        return (*got_x, *got_y, *got_z)
+        faces_z = background.beside(faces_z)
+        done = None
+        if work is not None:
+            faces_z, held = lax.optimization_barrier((faces_z, held))
+            done = work(*held)
+        got_z = background.beside(trade(faces_z, "gz"))
+        got_z, done = lax.optimization_barrier((got_z, done))
+        return (*got_x, *got_y, *got_z), done
+
+    def to_slopes(half):
+        return call(slope_kernel, "slopes", (sc, half), [full3], [], matmul, {1: 0})[0]
+
+    def products(*held):
+        return call(
+            products_kernel, "nodes1_products", (sc, node_in, *held), [full, rows_like(3 * width + NODES)], [], 6 * matmul
+        )
 
     got_x = first_trade(first_face_kernel, "face0", (edge_weights, biases, h0), [], matmul // 8)
     sums, slopes0, *faces = call(
         functools.partial(first_kernel, trades, sizes), "edges0", (sc, edge_weights, biases, h0),
         [full, full3] + face_outs, [], 3 * matmul,
     )
-    halo = exchange(got_x, faces)
+    halo, slopes0 = exchange(got_x, faces, to_slopes, (slopes0,))
     inputs = (*weights, sums, h0, *halo)
     got_x = first_trade(middle_face_kernel, "face1", inputs, [pair, inv], matmul // 4)
     scaled0, act0, slope0, h1, sums, slopes1, *faces = run(
         middle_kernel, "nodes0_edges1", (sums, h0, *halo),
         [full16, full16, full, full16, full, full3] + face_outs, [work, inv], 8,
     )
-    halo = exchange(got_x, faces)
+    halo, slopes1 = exchange(got_x, faces, to_slopes, (slopes1,))
     inputs = (*weights, sums, h1, g2, *halo)
     got_x = first_trade(turn_face_kernel, "face2", inputs, [pair, inv], matmul // 4)
-    base, sums, grads1, *faces = run(
-        turn_kernel, "nodes1_back", (sums, h1, g2, *halo), [full, full, rows_like(3 * width + NODES)] + face_outs,
-        [work, inv], 10,
+    scaled1, act1, dpn1, sums, *faces = run(
+        turn_kernel, "nodes1_back", (sums, h1, g2, *halo), [full16] * 3 + [full] + face_outs, [work, inv], 7
     )
-    halo = exchange(got_x, faces)
+    halo, (base, grads1) = exchange(got_x, faces, products, (h1, g2, scaled1, act1, dpn1))
     inputs = (*weights, sums, base, slopes1, slope0, *halo)
     got_x = first_trade(join_face_kernel, "face3", inputs, [pair, inv], matmul // 4)
     grad_rows = padded_rows(7 * width + 3 * NODES, sizes)
     half = rows_like(grad_rows // 2)
-    base, sums, keep, send, *faces = run(
+    grad_in, dpn0, sums, keep, send, *faces = run(
         join_kernel, "edges1_back_nodes0_back",
         (sums, h1, base, slopes1, h0, scaled0, act0, slope0, grads1, *halo),
-        [full, full, half, half] + face_outs, [work, inv, pltpu.VMEM((grad_rows, width), f32)], 12,
+        [full16, full16, full, half, half] + face_outs, [work, inv, pltpu.VMEM((grad_rows, width), f32)], 12,
     )
     background.add("sums", halve(sc, sizes, keep, send))
-    halo = exchange(got_x, faces)
+    halo, _ = exchange(got_x, faces)
     tail_rows = width + NODES
     edges, last = run(last_kernel, "edges0_back", (sums, h0, slopes0, *halo), [full, rows_like(tail_rows)], [], 6)
-    (grad0,) = call(state_kernel, "state_grad", (sc, edge_weights, base, edges), [full16], [], 2 * matmul)
     keep, got = background.finish("sums")
     (value,) = call(stack_kernel, "stack", (sc, last, keep, got), [rows_like(tail_rows + keep.shape[0])])
-    for hop in hops(sizes[2]):
+    value, grad_in, dpn0, edges = lax.optimization_barrier((value, grad_in, dpn0, edges))
+    (grad0,) = call(
+        state_kernel, "state_grad", (sc, edge_weights, node_in, grad_in, dpn0, edges), [full16], [], 4 * matmul
+    )
+    for hop in reversed(hops(sizes[2])):
         (value,) = call(add_kernel, "add", (sc, value, swap(value, (2, hop))), [rows_like(value.shape[0])])
-    for step in reversed(halving_steps(sizes)):
+        value, grad0 = lax.optimization_barrier((value, grad0))
+    first, *rest = halving_steps(sizes)
+    for step in reversed(rest):
         out = rows_like(2 * value.shape[0] - tail_rows)
         body = functools.partial(join_kernel_of, step, tail_rows)
         (value,) = call(body, "join", (sc, value, swap(value, step)), [out])
@@ -903,8 +958,10 @@
     nodes_all = x_len * sizes[0] * y_len * sizes[1] * layers_all * nodes
     scale = 1.0 / math.sqrt(nodes_all)
     edge_grads, in_grads, out_grads, bias_grads = call(
-        functools.partial(finish_kernel, scale, tail_rows), "finish", (sc, edge_weights, node_in, value),
+        functools.partial(finish_kernel, scale, tail_rows, first), "finish",
+        (sc, edge_weights, node_in, value, swap(value, first)),
         [sds(edge_weights.shape), sds(node_in.shape), sds(node_out.shape), sds(biases.shape)],
+        [pltpu.VMEM((2 * value.shape[0] - tail_rows, width), f32)],
     )
     return grad0.reshape(state.shape), edge_grads, in_grads, out_grads, bias_grads
 

time: 143 us -> 138 us (0.965)
  waiting for transfers between devices: 30 us -> 21.1 us
  Pallas kernels: 52 us -> 55 us
    ppermute x20, waiting for transfers between devices: 9.11 us -> 2.14 us  [trade(): lax.ppermute(face, axis, pairs(size, kind))]
    pallas_call x27 -> x29, Pallas kernels: 52 us -> 55 us  [call(): pl.pallas_call(kernel, name=name, out_shape=tuple(outs), in_specs=[SM] +...]
    ppermute x8, waiting for transfers between devices: 20.9 us -> 19 us  [swap(): lax.ppermute(value, axis, [(i, i ^ step[1]) for i in range(lax.axis_size(...]
    ppermute x8, starting transfers between devices: 20.4 us -> 21.9 us  [swap(): lax.ppermute(value, axis, [(i, i ^ step[1]) for i in range(lax.axis_size(...]
  transfers between devices with their start and end apart: 28 -> 28, of which waited for: 12 -> 11; matrix products, arithmetic and copies ran while one was open for 0% -> 0% of each run, Pallas kernels for 27% -> 30%
where the time goes in v4:
time: 138 us
  starting transfers between devices  57.1 us (41%)
  Pallas kernels  55 us (40%)
  waiting for transfers between devices  21.1 us (15%)
  local copies, waits for them, and re-layouts  2.84 us (2%)
  between operations  1.7 us (1%)
    pallas_call x29, Pallas kernels, call(): pl.pallas_call(kernel, name=name, out_shape=tuple(outs), in_specs=[SM] +...  55 us
    ppermute x20, starting transfers between devices, trade(): lax.ppermute(face, axis, pairs(size, kind))  35.2 us
    ppermute x8, starting transfers between devices, swap(): lax.ppermute(value, axis, [(i, i ^ step[1]) for i in range(lax.axis_size(...  21.9 us
    ppermute x8, waiting for transfers between devices, swap(): lax.ppermute(value, axis, [(i, i ^ step[1]) for i in range(lax.axis_size(...  19 us
    unnamed x16, local copies, waits for them, and re-layouts  2.84 us
  transfers between devices with their start and end apart: 28, of which 11 were waited for; matrix products, arithmetic and copies ran while one was open for 0% of the time, Pallas kernels for 30%

profile of v4, /device:TPU:0, one launch (start us, length us, event | category | flops | bytes accessed | tf_op | source)
XLA Modules:
  0.0 137.8 jit_solution(7640241407956559501)
XLA Ops:
  1.4 1.2 copy-done
  2.6 0.9 copy-done.2
  3.5 0.7 copy-done.7
  4.2 0.8 face0.1
  5.0 3.0 %collective-permute-start = (f32[16,16,128]{2,1,0:T(8,128)S(1)}, f32[16,16,128]{2,1,0:T(8,128)S(1)}, u32[]{:S(2)}, u32[]{:S(2)}) collective-permute-start(f32[16,16,128]{2,1,0:T(8,128)S(1)} %face0.1), channel_id=1, source_target_pairs={{0,16},{16,0},{1,17},{17,1},{2,18},{18,2},{3,19},{19,3},{4,20},{20... | collective-permute-start | bytes 393224 | tf_op jit(solution)/shard_map/ppermute | solution.py:877
  8.0 4.0 %edges0.1 = (f32[16,16,16,128]{3,2,1,0:T(8,128)S(1)}, f32[3,16,16,16,128]{4,3,2,1,0:T(8,128)S(1)}, f32[16,16,128]{2,1,0:T(8,128)S(1)}, f32[16,16,128]{2,1,0:T(8,...) custom-call(s32[4]{0:T(128)S(1)} %pad_add_fusion.sc.sc_ref, bf16[2,2,128,128]{3,2,1,0:T(8,128)(2,1)S(1)} %copy-done.2, ...), custom_call_target="tpu_custom_call" | custom-call | flops 402653184 | bytes 10094608 | tf_op jit(solution)/shard_map/edges0/pallas_call | solution.py:709
  12.6 0.7 collective-permute-start.2
  13.3 0.7 collective-permute-done.1.refs_1_
  14.0 0.7 fix_z.4
  14.7 1.6 %collective-permute-start.3 = (f32[16,16,128]{2,1,0:T(8,128)S(1)}, f32[16,16,128]{2,1,0:T(8,128)S(1)}, u32[]{:S(2)}, u32[]{:S(2)}) collective-permute-start(f32[16,16,128]{2,1,0:T(8,128)S(1)} %get-tuple-element.117), channel_id=1, source_target_pairs={{0,1},{1,0},{2,3},{3,2},{4,5},{5,4},{6,7},{7,6},{8,9},{9,8},{10,11... | collective-permute-start | bytes 393224 | tf_op jit(solution)/shard_map/ppermute | solution.py:877
  16.3 0.7 collective-permute-start.4
  17.0 2.6 %slopes.2 = f32[3,16,16,16,128]{4,3,2,1,0:T(8,128)S(1)} custom-call(s32[4]{0:T(128)S(1)} %pad_add_fusion.sc.sc_ref, f32[3,16,16,16,128]{4,3,2,1,0:T(8,128)S(1)} %get-tuple-element.119.half_in), custom_call_target="tpu_custom_call", output_to_operand_aliasing={{}: (1, {})} | custom-call | flops 134217728 | bytes 12582928 | tf_op jit(solution)/shard_map/slopes/pallas_call | solution.py:709
  19.8 1.4 %face1.1 = f32[16,16,128]{2,1,0:T(8,128)S(1)} custom-call(s32[4]{0:T(128)S(1)} %pad_add_fusion.sc.sc_ref, bf16[2,2,128,128]{3,2,1,0:T(8,128)(2,1)S(1)} %copy-done.3, bf16[2,256,128]{2,1,0:T(8,128)(2,1)S(1)} %copy-done.4, bf16[2,128,128]{2,1,0:T(8,128)(2,1)S(1)} %copy-done.6, f32[2,2,128]{2,1,0:T(2,128)S(1)} %copy-done.7, ...), custom_call_target="tpu_custom_call" | custom-call | flops 33554432 | bytes 4261904 | tf_op jit(solution)/shard_map/face1/pallas_call | solution.py:709
  21.2 1.3 collective-permute-start.5
  22.5 7.6 %nodes0_edges1.1 = (bf16[16,16,16,128]{3,2,1,0:T(8,128)(2,1)S(1)}, bf16[16,16,16,128]{3,2,1,0:T(8,128)(2,1)S(1)}, f32[16,16,16,128]{3,2,1,0:T(8,128)S(1)}, bf16[...) custom-call(s32[4]{0:T(128)S(1)} %pad_add_fusion.sc.sc_ref, ...), custom_call_target="tpu_custom_call" | custom-call | flops 1073741824 | bytes 18286608 | tf_op jit(solution)/shard_map/nodes0_edges1/pallas_call | solution.py:709
  30.6 5.1 %collective-permute-start.6 = (f32[16,16,128]{2,1,0:T(8,128)S(1)}, f32[16,16,128]{2,1,0:T(8,128)S(1)}, u32[]{:S(2)}, u32[]{:S(2)}) collective-permute-start(f32[16,16,128]{2,1,0:T(8,128)S(1)} %get-tuple-element.126), channel_id=1, source_target_pairs={{0,4},{4,0},{8,12},{12,8},{1,5},{5,1},{9,13},{13,9},{2,6},{6,2},{1... | collective-permute-start | bytes 393224 | tf_op jit(solution)/shard_map/ppermute | solution.py:877
  36.8 0.7 fix_z.5
  37.5 4.2 %collective-permute-start.8 = (f32[16,16,128]{2,1,0:T(8,128)S(1)}, f32[16,16,128]{2,1,0:T(8,128)S(1)}, u32[]{:S(2)}, u32[]{:S(2)}) collective-permute-start(f32[16,16,128]{2,1,0:T(8,128)S(1)} %get-tuple-element.133), channel_id=1, source_target_pairs={{0,1},{1,0},{2,3},{3,2},{4,5},{5,4},{6,7},{7,6},{8,9},{9,8},{10,11... | collective-permute-start | bytes 393224 | tf_op jit(solution)/shard_map/ppermute | solution.py:877
  42.3 2.6 %slopes.3 = f32[3,16,16,16,128]{4,3,2,1,0:T(8,128)S(1)} custom-call(s32[4]{0:T(128)S(1)} %pad_add_fusion.sc.sc_ref, f32[3,16,16,16,128]{4,3,2,1,0:T(8,128)S(1)} %get-tuple-element.135.half_in), custom_call_target="tpu_custom_call", output_to_operand_aliasing={{}: (1, {})} | custom-call | flops 134217728 | bytes 12582928 | tf_op jit(solution)/shard_map/slopes/pallas_call | solution.py:709
  44.9 1.2 face2.1
  46.1 0.8 collective-permute-start.10
  46.9 4.8 %nodes1_back.1 = (bf16[16,16,16,128]{3,2,1,0:T(8,128)(2,1)S(1)}, bf16[16,16,16,128]{3,2,1,0:T(8,128)(2,1)S(1)}, bf16[16,16,16,128]{3,2,1,0:T(8,128)(2,1)S(1)}, f...) custom-call(s32[4]{0:T(128)S(1)} %pad_add_fusion.sc.sc_ref, ...), custom_call_target="tpu_custom_call" | custom-call | flops 939524096 | bytes 10946576 | tf_op jit(solution)/shard_map/nodes1_back/pallas_call | solution.py:709
  52.3 5.4 %collective-permute-start.11 = (f32[16,16,128]{2,1,0:T(8,128)S(1)}, f32[16,16,128]{2,1,0:T(8,128)S(1)}, u32[]{:S(2)}, u32[]{:S(2)}) collective-permute-start(f32[16,16,128]{2,1,0:T(8,128)S(1)} %get-tuple-element.141), channel_id=1, source_target_pairs={{0,4},{4,0},{8,12},{12,8},{1,5},{5,1},{9,13},{13,9},{2,6},{6,2},{1... | collective-permute-start | bytes 393224 | tf_op jit(solution)/shard_map/ppermute | solution.py:877
  58.6 0.7 fix_z.6
  59.3 3.2 %collective-permute-start.13 = (f32[16,16,128]{2,1,0:T(8,128)S(1)}, f32[16,16,128]{2,1,0:T(8,128)S(1)}, u32[]{:S(2)}, u32[]{:S(2)}) collective-permute-start(f32[16,16,128]{2,1,0:T(8,128)S(1)} %get-tuple-element.150), channel_id=1, source_target_pairs={{0,1},{1,0},{2,3},{3,2},{4,5},{5,4},{6,7},{7,6},{8,9},{9,8},{10,11... | collective-permute-start | bytes 393224 | tf_op jit(solution)/shard_map/ppermute | solution.py:877
  62.5 0.8 collective-permute-start.14
  63.4 2.2 %nodes1_products.1 = (f32[16,16,16,128]{3,2,1,0:T(8,128)S(1)}, f32[392,128]{1,0:T(8,128)S(1)}) custom-call(s32[4]{0:T(128)S(1)} %pad_add_fusion.sc.sc_ref, bf16[2,256,128]{2,1,0:T(8,128)(2,1)S(1)} %copy-done.4, bf16[16,16,16,128]{3,2,1,0:T(8,128)(2,1)S(1)} %get-tuple-element.152.h, bf16[16,16,16,128]{3,2,1,0:T(8,128)(2,1)S(1)} %bitcast.14, ...), custom_call_target="tpu_custom_call" | custom-call | flops 805306368 | bytes 7671824 | tf_op jit(solution)/shard_map/nodes1_products/pallas_call | solution.py:709
  65.6 1.3 face3.1
  67.0 1.3 collective-permute-start.15
  68.3 7.8 %edges1_back_nodes0_back.1 = (bf16[16,16,16,128]{3,2,1,0:T(8,128)(2,1)S(1)}, bf16[16,16,16,128]{3,2,1,0:T(8,128)(2,1)S(1)}, f32[16,16,16,128]{3,2,1,0:T(8,128)S(...) custom-call(s32[4]{0:T(128)S(1)} %pad_add_fusion.sc.sc_ref, ...), custom_call_target="tpu_custom_call" | custom-call | flops 1610612736 | bytes 23173136 | tf_op jit(solution)/shard_map/edges1_back_nodes0_back/pallas_call | solution.py:709
  76.1 6.0 %collective-permute-start.18 = (f32[480,128]{1,0:T(8,128)S(1)}, f32[480,128]{1,0:T(8,128)S(1)}, u32[]{:S(2)}, u32[]{:S(2)}) collective-permute-start(f32[480,128]{1,0:T(8,128)S(1)} %get-tuple-element.178), channel_id=1, source_target_pairs={{0,4},{4,0},{8,12},{12,8},{1,5},{5,1},{9,13},{13,9},{2,6},{6,2},{1... | collective-permute-start | bytes 737288 | tf_op jit(solution)/shard_map/ppermute | solution.py:786
  82.7 0.7 collective-permute-start.17
  83.4 0.7 collective-permute-done.16.refs_1_
  84.1 0.7 fix_z.7
  84.8 3.5 %collective-permute-start.19 = (f32[16,16,128]{2,1,0:T(8,128)S(1)}, f32[16,16,128]{2,1,0:T(8,128)S(1)}, u32[]{:S(2)}, u32[]{:S(2)}) collective-permute-start(f32[16,16,128]{2,1,0:T(8,128)S(1)} %get-tuple-element.179), channel_id=1, source_target_pairs={{0,1},{1,0},{2,3},{3,2},{4,5},{5,4},{6,7},{7,6},{8,9},{9,8},{10,11... | collective-permute-start | bytes 393224 | tf_op jit(solution)/shard_map/ppermute | solution.py:877
  89.6 0.8 collective-permute-start.21
  90.4 4.1 %collective-permute-done.21.got = f32[240,128]{1,0:T(8,128)S(1)} collective-permute-done((f32[240,128]{1,0:T(8,128)S(1)}, f32[240,128]{1,0:T(8,128)S(1)}, u32[]{:S(2)}, u32[]{:S(2)}) %collective-permute-start.21) | collective-permute-done | bytes 122912 | tf_op jit(solution)/shard_map/ppermute | solution.py:786
  95.1 7.7 %collective-permute-start.22 = (f32[120,128]{1,0:T(8,128)S(1)}, f32[120,128]{1,0:T(8,128)S(1)}, u32[]{:S(2)}, u32[]{:S(2)}) collective-permute-start(f32[120,128]{1,0:T(8,128)S(1)} %get-tuple-element.193), channel_id=1, source_target_pairs={{0,8},{4,12},{8,0},{12,4},{1,9},{5,13},{9,1},{13,5},{2,10},{6,14},... | collective-permute-start | bytes 184328 | tf_op jit(solution)/shard_map/ppermute | solution.py:786
  102.8 5.1 %edges0_back.1 = (f32[16,16,16,128]{3,2,1,0:T(8,128)S(1)}, f32[136,128]{1,0:T(8,128)S(1)}) custom-call(s32[4]{0:T(128)S(1)} %pad_add_fusion.sc.sc_ref, bf16[2,2,128,128]{3,2,1,0:T(8,128)(2,1)S(1)} %copy-done.3, bf16[2,256,128]{2,1,0:T(8,128)(2,1)S(1)} %copy-done.4, bf16[2,128,128]{2,1,0:T(8,128)(2,1)S(1)} %copy-done.6, f32[2,2,128]{2,1,0:T(2,128)S(1)} %copy-done.7, ...), custom_call_target="tpu_custom_call" | custom-call | flops 805306368 | bytes 12589072 | tf_op jit(solution)/shard_map/edges0_back/pallas_call | solution.py:709
  108.4 2.8 %collective-permute-start.23 = (f32[256,128]{1,0:T(8,128)S(1)}, f32[256,128]{1,0:T(8,128)S(1)}, u32[]{:S(2)}, u32[]{:S(2)}) collective-permute-start(f32[256,128]{1,0:T(8,128)S(1)} %stack.17.left), channel_id=1, source_target_pairs={{0,2},{1,3},{2,0},{3,1},{4,6},{5,7},{6,4},{7,5},{8,10},{9,11},{10,... | collective-permute-start | bytes 393224 | tf_op jit(solution)/shard_map/ppermute | solution.py:786
  111.2 3.0 %state_grad.1 = bf16[16,16,16,128]{3,2,1,0:T(8,128)(2,1)} custom-call(s32[4]{0:T(128)S(1)} %pad_add_fusion.sc.sc_ref, bf16[2,2,128,128]{3,2,1,0:T(8,128)(2,1)S(1)} %copy-done.3, bf16[2,256,128]{2,1,0:T(8,128)(2,1)S(1)} %copy-done.4, bf16[16,16,16,128]{3,2,1,0:T(8,128)(2,1)S(1)} %get-tuple-element.198.grad_in, ...), custom_call_target="tpu_custom_call" | custom-call | flops 536870912 | bytes 5505040 | tf_op jit(solution)/shard_map/state_grad/pallas_call | solution.py:709
  115.3 3.7 %collective-permute-start.24 = (f32[256,128]{1,0:T(8,128)S(1)}, f32[256,128]{1,0:T(8,128)S(1)}, u32[]{:S(2)}, u32[]{:S(2)}) collective-permute-start(f32[256,128]{1,0:T(8,128)S(1)} %add.8.left), channel_id=1, source_target_pairs={{0,1},{1,0},{2,3},{3,2},{4,5},{5,4},{6,7},{7,6},{8,9},{9,8},{10,11... | collective-permute-start | bytes 393224 | tf_op jit(solution)/shard_map/ppermute | solution.py:786
  119.0 2.9 %collective-permute-done.24.right = f32[256,128]{1,0:T(8,128)S(1)} collective-permute-done((f32[256,128]{1,0:T(8,128)S(1)}, f32[256,128]{1,0:T(8,128)S(1)}, u32[]{:S(2)}, u32[]{:S(2)}) %collective-permute-start.24) | collective-permute-done | bytes 131104 | tf_op jit(solution)/shard_map/ppermute | solution.py:786
  122.6 5.0 %collective-permute-done.25.got = f32[256,128]{1,0:T(8,128)S(1)} collective-permute-done((f32[256,128]{1,0:T(8,128)S(1)}, f32[256,128]{1,0:T(8,128)S(1)}, u32[]{:S(2)}, u32[]{:S(2)}) %collective-permute-start.25) | collective-permute-done | bytes 131104 | tf_op jit(solution)/shard_map/ppermute | solution.py:786
  128.1 0.8 collective-permute-start.26
  129.0 4.9 %collective-permute-done.26.got = f32[376,128]{1,0:T(8,128)S(1)} collective-permute-done((f32[376,128]{1,0:T(8,128)S(1)}, f32[376,128]{1,0:T(8,128)S(1)}, u32[]{:S(2)}, u32[]{:S(2)}) %collective-permute-start.26) | collective-permute-done | bytes 192544 | tf_op jit(solution)/shard_map/ppermute | solution.py:786
  134.5 1.6 %collective-permute-done.27.got = f32[616,128]{1,0:T(8,128)S(1)} collective-permute-done((f32[616,128]{1,0:T(8,128)S(1)}, f32[616,128]{1,0:T(8,128)S(1)}, u32[]{:S(2)}, u32[]{:S(2)}) %collective-permute-start.27) | collective-permute-done | bytes 315424 | tf_op jit(solution)/shard_map/ppermute | solution.py:786
  136.1 1.7 %finish.1 = (f32[2,2,128,128]{3,2,1,0:T(8,128)}, f32[2,256,128]{2,1,0:T(8,128)}, f32[2,128,128]{2,1,0:T(8,128)}, f32[2,2,128]{2,1,0:T(2,128)}) custom-call(s32[4]{0:T(128)S(1)} %pad_add_fusion.sc.sc_ref, bf16[2,2,128,128]{3,2,1,0:T(8,128)(2,1)S(1)} %copy-done.3, bf16[2,256,128]{2,1,0:T(8,128)(2,1)S(1)} %copy-done.4, f32[616,128]{1,0:T(8,128)S(1)} %join.3.value, ...), custom_call_target="tpu_custom_call" | custom-call | bytes 1550352 | tf_op jit(solution)/shard_map/finish/pallas_call | solution.py:709
  (54 shorter events, 10.6 us)
Async XLA Ops:
  1.4 1.2 copy-start
  2.6 0.9 copy-start.2
  3.5 0.7 copy-start.7
  5.0 7.0 %collective-permute-start = (f32[16,16,128]{2,1,0:T(8,128)S(1)}, f32[16,16,128]{2,1,0:T(8,128)S(1)}, u32[]{:S(2)}, u32[]{:S(2)}) collective-permute-start(f32[16,16,128]{2,1,0:T(8,128)S(1)} %face0.1), channel_id=1, source_target_pairs={{0,16},{16,0},{1,17},{17,1},{2,18},{18,2},{3,19},{19,3},{4,20},{20... | collective-permute-start | bytes 393224 | tf_op jit(solution)/shard_map/ppermute | solution.py:877
  12.5 1.4 %collective-permute-start.1 = (f32[16,16,128]{2,1,0:T(8,128)S(1)}, f32[16,16,128]{2,1,0:T(8,128)S(1)}, u32[]{:S(2)}, u32[]{:S(2)}) collective-permute-start(f32[16,16,128]{2,1,0:T(8,128)S(1)} %get-tuple-element.110), channel_id=1, source_target_pairs={{0,4},{4,0},{8,12},{12,8},{1,5},{5,1},{9,13},{13,9},{2,6},{6,2},{1... | collective-permute-start | bytes 393224 | tf_op jit(solution)/shard_map/ppermute | solution.py:877
  12.6 1.3 collective-permute-start.2
  14.6 5.1 %copy-start.1 = (bf16[16,16,2,8,128]{4,3,2,1,0:T(8,128)(2,1)S(1)}, bf16[16,16,2,8,128]{4,3,2,1,0:T(8,128)(2,1)}, u32[]{:S(2)}) copy-start(bf16[16,16,2,8,128]{4,3,2,1,0:T(8,128)(2,1)} %param.7) | copy-start | bytes 3145732
  14.7 5.1 %copy-start.3 = (bf16[2,2,128,128]{3,2,1,0:T(8,128)(2,1)S(1)}, bf16[2,2,128,128]{3,2,1,0:T(8,128)(2,1)}, u32[]{:S(2)}) copy-start(bf16[2,2,128,128]{3,2,1,0:T(8,128)(2,1)} %edge_w.21) | copy-start | bytes 393220
  14.7 5.1 %copy-start.4 = (bf16[2,256,128]{2,1,0:T(8,128)(2,1)S(1)}, bf16[2,256,128]{2,1,0:T(8,128)(2,1)}, u32[]{:S(2)}) copy-start(bf16[2,256,128]{2,1,0:T(8,128)(2,1)} %node_in.19) | copy-start | bytes 393220
  14.7 5.1 %copy-start.6 = (bf16[2,128,128]{2,1,0:T(8,128)(2,1)S(1)}, bf16[2,128,128]{2,1,0:T(8,128)(2,1)}, u32[]{:S(2)}) copy-start(bf16[2,128,128]{2,1,0:T(8,128)(2,1)} %node_out.13) | copy-start | bytes 196612
  14.7 5.0 %collective-permute-start.3 = (f32[16,16,128]{2,1,0:T(8,128)S(1)}, f32[16,16,128]{2,1,0:T(8,128)S(1)}, u32[]{:S(2)}, u32[]{:S(2)}) collective-permute-start(f32[16,16,128]{2,1,0:T(8,128)S(1)} %get-tuple-element.117), channel_id=1, source_target_pairs={{0,1},{1,0},{2,3},{3,2},{4,5},{5,4},{6,7},{7,6},{8,9},{9,8},{10,11... | collective-permute-start | bytes 393224 | tf_op jit(solution)/shard_map/ppermute | solution.py:877
  16.3 3.4 %collective-permute-start.4 = (f32[16,16,128]{2,1,0:T(8,128)S(1)}, f32[16,16,128]{2,1,0:T(8,128)S(1)}, u32[]{:S(2)}, u32[]{:S(2)}) collective-permute-start(f32[16,16,128]{2,1,0:T(8,128)S(1)} %get-tuple-element.118), channel_id=1, source_target_pairs={{1,2},{2,1},{5,6},{6,5},{9,10},{10,9},{13,14},{14,13},{17,18},{18,... | collective-permute-start | bytes 393224 | tf_op jit(solution)/shard_map/ppermute | solution.py:877
  21.2 8.9 %collective-permute-start.5 = (f32[16,16,128]{2,1,0:T(8,128)S(1)}, f32[16,16,128]{2,1,0:T(8,128)S(1)}, u32[]{:S(2)}, u32[]{:S(2)}) collective-permute-start(f32[16,16,128]{2,1,0:T(8,128)S(1)} %face1.1), channel_id=1, source_target_pairs={{0,16},{16,0},{1,17},{17,1},{2,18},{18,2},{3,19},{19,3},{4,20},{20... | collective-permute-start | bytes 393224 | tf_op jit(solution)/shard_map/ppermute | solution.py:877
  30.6 6.1 %collective-permute-start.6 = (f32[16,16,128]{2,1,0:T(8,128)S(1)}, f32[16,16,128]{2,1,0:T(8,128)S(1)}, u32[]{:S(2)}, u32[]{:S(2)}) collective-permute-start(f32[16,16,128]{2,1,0:T(8,128)S(1)} %get-tuple-element.126), channel_id=1, source_target_pairs={{0,4},{4,0},{8,12},{12,8},{1,5},{5,1},{9,13},{13,9},{2,6},{6,2},{1... | collective-permute-start | bytes 393224 | tf_op jit(solution)/shard_map/ppermute | solution.py:877
  35.8 1.0 collective-permute-start.7
  37.4 7.5 %copy-start.5 = (bf16[16,16,2,8,128]{4,3,2,1,0:T(8,128)(2,1)S(1)}, bf16[16,16,2,8,128]{4,3,2,1,0:T(8,128)(2,1)}, u32[]{:S(2)}) copy-start(bf16[16,16,2,8,128]{4,3,2,1,0:T(8,128)(2,1)} %param.8) | copy-start | bytes 3145732
  37.5 7.4 %collective-permute-start.8 = (f32[16,16,128]{2,1,0:T(8,128)S(1)}, f32[16,16,128]{2,1,0:T(8,128)S(1)}, u32[]{:S(2)}, u32[]{:S(2)}) collective-permute-start(f32[16,16,128]{2,1,0:T(8,128)S(1)} %get-tuple-element.133), channel_id=1, source_target_pairs={{0,1},{1,0},{2,3},{3,2},{4,5},{5,4},{6,7},{7,6},{8,9},{9,8},{10,11... | collective-permute-start | bytes 393224 | tf_op jit(solution)/shard_map/ppermute | solution.py:877
  41.6 3.3 %collective-permute-start.9 = (f32[16,16,128]{2,1,0:T(8,128)S(1)}, f32[16,16,128]{2,1,0:T(8,128)S(1)}, u32[]{:S(2)}, u32[]{:S(2)}) collective-permute-start(f32[16,16,128]{2,1,0:T(8,128)S(1)} %get-tuple-element.134), channel_id=1, source_target_pairs={{1,2},{2,1},{5,6},{6,5},{9,10},{10,9},{13,14},{14,13},{17,18},{18,... | collective-permute-start | bytes 393224 | tf_op jit(solution)/shard_map/ppermute | solution.py:877
  46.1 5.6 %collective-permute-start.10 = (f32[16,16,128]{2,1,0:T(8,128)S(1)}, f32[16,16,128]{2,1,0:T(8,128)S(1)}, u32[]{:S(2)}, u32[]{:S(2)}) collective-permute-start(f32[16,16,128]{2,1,0:T(8,128)S(1)} %face2.1), channel_id=1, source_target_pairs={{0,16},{16,0},{1,17},{17,1},{2,18},{18,2},{3,19},{19,3},{4,20},{20... | collective-permute-start | bytes 393224 | tf_op jit(solution)/shard_map/ppermute | solution.py:877
  52.3 6.3 %collective-permute-start.11 = (f32[16,16,128]{2,1,0:T(8,128)S(1)}, f32[16,16,128]{2,1,0:T(8,128)S(1)}, u32[]{:S(2)}, u32[]{:S(2)}) collective-permute-start(f32[16,16,128]{2,1,0:T(8,128)S(1)} %get-tuple-element.141), channel_id=1, source_target_pairs={{0,4},{4,0},{8,12},{12,8},{1,5},{5,1},{9,13},{13,9},{2,6},{6,2},{1... | collective-permute-start | bytes 393224 | tf_op jit(solution)/shard_map/ppermute | solution.py:877
  57.6 1.0 collective-permute-start.12
  59.3 6.3 %collective-permute-start.13 = (f32[16,16,128]{2,1,0:T(8,128)S(1)}, f32[16,16,128]{2,1,0:T(8,128)S(1)}, u32[]{:S(2)}, u32[]{:S(2)}) collective-permute-start(f32[16,16,128]{2,1,0:T(8,128)S(1)} %get-tuple-element.150), channel_id=1, source_target_pairs={{0,1},{1,0},{2,3},{3,2},{4,5},{5,4},{6,7},{7,6},{8,9},{9,8},{10,11... | collective-permute-start | bytes 393224 | tf_op jit(solution)/shard_map/ppermute | solution.py:877
  62.5 3.1 %collective-permute-start.14 = (f32[16,16,128]{2,1,0:T(8,128)S(1)}, f32[16,16,128]{2,1,0:T(8,128)S(1)}, u32[]{:S(2)}, u32[]{:S(2)}) collective-permute-start(f32[16,16,128]{2,1,0:T(8,128)S(1)} %get-tuple-element.151), channel_id=1, source_target_pairs={{1,2},{2,1},{5,6},{6,5},{9,10},{10,9},{13,14},{14,13},{17,18},{18,... | collective-permute-start | bytes 393224 | tf_op jit(solution)/shard_map/ppermute | solution.py:877
  67.0 15.1 %collective-permute-start.15 = (f32[16,16,128]{2,1,0:T(8,128)S(1)}, f32[16,16,128]{2,1,0:T(8,128)S(1)}, u32[]{:S(2)}, u32[]{:S(2)}) collective-permute-start(f32[16,16,128]{2,1,0:T(8,128)S(1)} %face3.1), channel_id=1, source_target_pairs={{0,16},{16,0},{1,17},{17,1},{2,18},{18,2},{3,19},{19,3},{4,20},{20... | collective-permute-start | bytes 393224 | tf_op jit(solution)/shard_map/ppermute | solution.py:877
  76.1 8.7 %collective-permute-start.18 = (f32[480,128]{1,0:T(8,128)S(1)}, f32[480,128]{1,0:T(8,128)S(1)}, u32[]{:S(2)}, u32[]{:S(2)}) collective-permute-start(f32[480,128]{1,0:T(8,128)S(1)} %get-tuple-element.178), channel_id=1, source_target_pairs={{0,4},{4,0},{8,12},{12,8},{1,5},{5,1},{9,13},{13,9},{2,6},{6,2},{1... | collective-permute-start | bytes 737288 | tf_op jit(solution)/shard_map/ppermute | solution.py:786
  82.7 1.4 %collective-permute-start.16 = (f32[16,16,128]{2,1,0:T(8,128)S(1)}, f32[16,16,128]{2,1,0:T(8,128)S(1)}, u32[]{:S(2)}, u32[]{:S(2)}) collective-permute-start(f32[16,16,128]{2,1,0:T(8,128)S(1)} %get-tuple-element.171), channel_id=1, source_target_pairs={{0,4},{4,0},{8,12},{12,8},{1,5},{5,1},{9,13},{13,9},{2,6},{6,2},{1... | collective-permute-start | bytes 393224 | tf_op jit(solution)/shard_map/ppermute | solution.py:877
  82.7 1.3 collective-permute-start.17
  84.8 9.7 %collective-permute-start.19 = (f32[16,16,128]{2,1,0:T(8,128)S(1)}, f32[16,16,128]{2,1,0:T(8,128)S(1)}, u32[]{:S(2)}, u32[]{:S(2)}) collective-permute-start(f32[16,16,128]{2,1,0:T(8,128)S(1)} %get-tuple-element.179), channel_id=1, source_target_pairs={{0,1},{1,0},{2,3},{3,2},{4,5},{5,4},{6,7},{7,6},{8,9},{9,8},{10,11... | collective-permute-start | bytes 393224 | tf_op jit(solution)/shard_map/ppermute | solution.py:877
  88.3 6.2 %collective-permute-start.20 = (f32[16,16,128]{2,1,0:T(8,128)S(1)}, f32[16,16,128]{2,1,0:T(8,128)S(1)}, u32[]{:S(2)}, u32[]{:S(2)}) collective-permute-start(f32[16,16,128]{2,1,0:T(8,128)S(1)} %get-tuple-element.180), channel_id=1, source_target_pairs={{1,2},{2,1},{5,6},{6,5},{9,10},{10,9},{13,14},{14,13},{17,18},{18,... | collective-permute-start | bytes 393224 | tf_op jit(solution)/shard_map/ppermute | solution.py:877
  89.6 4.9 %collective-permute-start.21 = (f32[240,128]{1,0:T(8,128)S(1)}, f32[240,128]{1,0:T(8,128)S(1)}, u32[]{:S(2)}, u32[]{:S(2)}) collective-permute-start(f32[240,128]{1,0:T(8,128)S(1)} %get-tuple-element.184), channel_id=1, source_target_pairs={{0,16},{16,0},{1,17},{17,1},{2,18},{18,2},{3,19},{19,3},{4,20},{20... | collective-permute-start | bytes 368648 | tf_op jit(solution)/shard_map/ppermute | solution.py:786
  95.1 12.8 %collective-permute-start.22 = (f32[120,128]{1,0:T(8,128)S(1)}, f32[120,128]{1,0:T(8,128)S(1)}, u32[]{:S(2)}, u32[]{:S(2)}) collective-permute-start(f32[120,128]{1,0:T(8,128)S(1)} %get-tuple-element.193), channel_id=1, source_target_pairs={{0,8},{4,12},{8,0},{12,4},{1,9},{5,13},{9,1},{13,5},{2,10},{6,14},... | collective-permute-start | bytes 184328 | tf_op jit(solution)/shard_map/ppermute | solution.py:786
  108.4 6.3 %collective-permute-start.23 = (f32[256,128]{1,0:T(8,128)S(1)}, f32[256,128]{1,0:T(8,128)S(1)}, u32[]{:S(2)}, u32[]{:S(2)}) collective-permute-start(f32[256,128]{1,0:T(8,128)S(1)} %stack.17.left), channel_id=1, source_target_pairs={{0,2},{1,3},{2,0},{3,1},{4,6},{5,7},{6,4},{7,5},{8,10},{9,11},{10,... | collective-permute-start | bytes 393224 | tf_op jit(solution)/shard_map/ppermute | solution.py:786
  115.3 6.6 %collective-permute-start.24 = (f32[256,128]{1,0:T(8,128)S(1)}, f32[256,128]{1,0:T(8,128)S(1)}, u32[]{:S(2)}, u32[]{:S(2)}) collective-permute-start(f32[256,128]{1,0:T(8,128)S(1)} %add.8.left), channel_id=1, source_target_pairs={{0,1},{1,0},{2,3},{3,2},{4,5},{5,4},{6,7},{7,6},{8,9},{9,8},{10,11... | collective-permute-start | bytes 393224 | tf_op jit(solution)/shard_map/ppermute | solution.py:786
  122.5 5.0 %collective-permute-start.25 = (f32[256,128]{1,0:T(8,128)S(1)}, f32[256,128]{1,0:T(8,128)S(1)}, u32[]{:S(2)}, u32[]{:S(2)}) collective-permute-start(f32[256,128]{1,0:T(8,128)S(1)} %add.9.value), channel_id=1, source_target_pairs={{0,8},{4,12},{8,0},{12,4},{1,9},{5,13},{9,1},{13,5},{2,10},{6,14},... | collective-permute-start | bytes 393224 | tf_op jit(solution)/shard_map/ppermute | solution.py:786
  128.1 5.7 %collective-permute-start.26 = (f32[376,128]{1,0:T(8,128)S(1)}, f32[376,128]{1,0:T(8,128)S(1)}, u32[]{:S(2)}, u32[]{:S(2)}) collective-permute-start(f32[376,128]{1,0:T(8,128)S(1)} %join.2.value), channel_id=1, source_target_pairs={{0,16},{16,0},{1,17},{17,1},{2,18},{18,2},{3,19},{19,3},{4,20},{20... | collective-permute-start | bytes 577544 | tf_op jit(solution)/shard_map/ppermute | solution.py:786
  134.4 1.7 %collective-permute-start.27 = (f32[616,128]{1,0:T(8,128)S(1)}, f32[616,128]{1,0:T(8,128)S(1)}, u32[]{:S(2)}, u32[]{:S(2)}) collective-permute-start(f32[616,128]{1,0:T(8,128)S(1)} %join.3.value), channel_id=1, source_target_pairs={{0,4},{4,0},{8,12},{12,8},{1,5},{5,1},{9,13},{13,9},{2,6},{6,2},{1... | collective-permute-start | bytes 946184 | tf_op jit(solution)/shard_map/ppermute | solution.py:786

commit v5 on v4

--- a/solution.py
+++ b/solution.py
@@ -238,7 +238,7 @@
 def fix_z_kernel(counts, sc_ref, *refs):
     nx, ny, nz = counts
     got_x, refs = refs[:nx], refs[nx:]
-    got_y, refs = refs[:ny], refs[ny:]
+    got_y, refs = refs[:ny][::-1], refs[ny:]
     faces, outs = refs[:nz], refs[nz:]
     x_len, y_len, width = faces[0].shape
     for k in range(nz):
@@ -277,7 +277,7 @@
     return jnp.where(low | high, 0.5, 1.0).astype(f32)
 
 
-CHUNK = 4
+CHUNK = 8
 
 
 def scale_planes(sc_ref, inv_ref, x, block, x_len, size_x):
@@ -890,7 +890,7 @@
         faces_y = call(fix, "fix_y", (sc, *got_x, *faces[:ny]), [face_y] * ny)
         got_y = trade(background.beside(faces_y), "gy")
         fix = functools.partial(fix_z_kernel, trades)
-        faces_z = call(fix, "fix_z", (sc, *got_x, *got_y, *faces[ny:]), [face_z] * nz)
+        faces_z = call(fix, "fix_z", (sc, *got_x, *got_y[::-1], *faces[ny:]), [face_z] * nz)
         faces_z = background.beside(faces_z)
         done = None
         if work is not None:

time: 138 us -> 135 us (0.978)
  Pallas kernels: 55 us -> 51.2 us
  waiting for transfers between devices: 21.1 us -> 22.6 us
    ppermute x8, starting transfers between devices: 21.9 us -> 17.1 us  [swap(): lax.ppermute(value, axis, [(i, i ^ step[1]) for i in range(lax.axis_size(...]
    ppermute x20, starting transfers between devices: 35.2 us -> 39.5 us  [trade(): lax.ppermute(face, axis, pairs(size, kind))]
    pallas_call x29, Pallas kernels: 55 us -> 51.2 us  [call(): pl.pallas_call(kernel, name=name, out_shape=tuple(outs), in_specs=[SM] +...]
    ppermute x20, waiting for transfers between devices: 2.14 us -> 3.53 us  [trade(): lax.ppermute(face, axis, pairs(size, kind))]
  transfers between devices with their start and end apart: 28 -> 28, of which waited for: 11 -> 12; matrix products, arithmetic and copies ran while one was open for 0% -> 0% of each run, Pallas kernels for 30% -> 28%
where the time goes in v5:
time: 135 us
  starting transfers between devices  56.7 us (42%)
  Pallas kernels  51.2 us (38%)
  waiting for transfers between devices  22.6 us (17%)
  local copies, waits for them, and re-layouts  2.84 us (2%)
  between operations  1.68 us (1%)
    pallas_call x29, Pallas kernels, call(): pl.pallas_call(kernel, name=name, out_shape=tuple(outs), in_specs=[SM] +...  51.2 us
    ppermute x20, starting transfers between devices, trade(): lax.ppermute(face, axis, pairs(size, kind))  39.5 us
    ppermute x8, waiting for transfers between devices, swap(): lax.ppermute(value, axis, [(i, i ^ step[1]) for i in range(lax.axis_size(...  19.1 us
    ppermute x8, starting transfers between devices, swap(): lax.ppermute(value, axis, [(i, i ^ step[1]) for i in range(lax.axis_size(...  17.1 us
    ppermute x20, waiting for transfers between devices, trade(): lax.ppermute(face, axis, pairs(size, kind))  3.53 us
    unnamed x16, local copies, waits for them, and re-layouts  2.84 us
  transfers between devices with their start and end apart: 28, of which 12 were waited for; matrix products, arithmetic and copies ran while one was open for 0% of the time, Pallas kernels for 28%

profile of v5, /device:TPU:0, one launch (start us, length us, event | category | flops | bytes accessed | tf_op | source)
XLA Modules:
  0.0 135.1 jit_solution(14004856804066338251)
XLA Ops:
  1.4 1.2 copy-done
  2.6 0.9 copy-done.2
  3.5 0.7 copy-done.7
  4.2 0.8 face0.1
  5.0 3.0 %collective-permute-start = (f32[16,16,128]{2,1,0:T(8,128)S(1)}, f32[16,16,128]{2,1,0:T(8,128)S(1)}, u32[]{:S(2)}, u32[]{:S(2)}) collective-permute-start(f32[16,16,128]{2,1,0:T(8,128)S(1)} %face0.1), channel_id=1, source_target_pairs={{0,16},{16,0},{1,17},{17,1},{2,18},{18,2},{3,19},{19,3},{4,20},{20... | collective-permute-start | bytes 393224 | tf_op jit(solution)/shard_map/ppermute | solution.py:877
  8.0 4.0 %edges0.1 = (f32[16,16,16,128]{3,2,1,0:T(8,128)S(1)}, f32[3,16,16,16,128]{4,3,2,1,0:T(8,128)S(1)}, f32[16,16,128]{2,1,0:T(8,128)S(1)}, f32[16,16,128]{2,1,0:T(8,...) custom-call(s32[4]{0:T(128)S(1)} %pad_add_fusion.sc.sc_ref, bf16[2,2,128,128]{3,2,1,0:T(8,128)(2,1)S(1)} %copy-done.2, ...), custom_call_target="tpu_custom_call" | custom-call | flops 402653184 | bytes 10094608 | tf_op jit(solution)/shard_map/edges0/pallas_call | solution.py:709
  12.6 0.7 collective-permute-start.2
  13.3 0.7 collective-permute-done.1.refs_2_.refs_1_
  14.0 0.7 fix_z.4
  14.7 1.6 %collective-permute-start.3 = (f32[16,16,128]{2,1,0:T(8,128)S(1)}, f32[16,16,128]{2,1,0:T(8,128)S(1)}, u32[]{:S(2)}, u32[]{:S(2)}) collective-permute-start(f32[16,16,128]{2,1,0:T(8,128)S(1)} %get-tuple-element.117), channel_id=1, source_target_pairs={{0,1},{1,0},{2,3},{3,2},{4,5},{5,4},{6,7},{7,6},{8,9},{9,8},{10,11... | collective-permute-start | bytes 393224 | tf_op jit(solution)/shard_map/ppermute | solution.py:877
  16.3 0.7 collective-permute-start.4
  17.0 2.6 %slopes.2 = f32[3,16,16,16,128]{4,3,2,1,0:T(8,128)S(1)} custom-call(s32[4]{0:T(128)S(1)} %pad_add_fusion.sc.sc_ref, f32[3,16,16,16,128]{4,3,2,1,0:T(8,128)S(1)} %get-tuple-element.119.half_in), custom_call_target="tpu_custom_call", output_to_operand_aliasing={{}: (1, {})} | custom-call | flops 134217728 | bytes 12582928 | tf_op jit(solution)/shard_map/slopes/pallas_call | solution.py:709
  19.8 1.4 %face1.1 = f32[16,16,128]{2,1,0:T(8,128)S(1)} custom-call(s32[4]{0:T(128)S(1)} %pad_add_fusion.sc.sc_ref, bf16[2,2,128,128]{3,2,1,0:T(8,128)(2,1)S(1)} %copy-done.3, bf16[2,256,128]{2,1,0:T(8,128)(2,1)S(1)} %copy-done.4, bf16[2,128,128]{2,1,0:T(8,128)(2,1)S(1)} %copy-done.6, f32[2,2,128]{2,1,0:T(2,128)S(1)} %copy-done.7, ...), custom_call_target="tpu_custom_call" | custom-call | flops 33554432 | bytes 4261904 | tf_op jit(solution)/shard_map/face1/pallas_call | solution.py:709
  21.2 1.3 collective-permute-start.5
  22.5 6.8 %nodes0_edges1.1 = (bf16[16,16,16,128]{3,2,1,0:T(8,128)(2,1)S(1)}, bf16[16,16,16,128]{3,2,1,0:T(8,128)(2,1)S(1)}, f32[16,16,16,128]{3,2,1,0:T(8,128)S(1)}, bf16[...) custom-call(s32[4]{0:T(128)S(1)} %pad_add_fusion.sc.sc_ref, ...), custom_call_target="tpu_custom_call" | custom-call | flops 1073741824 | bytes 18286608 | tf_op jit(solution)/shard_map/nodes0_edges1/pallas_call | solution.py:709
  29.8 5.1 %collective-permute-start.6 = (f32[16,16,128]{2,1,0:T(8,128)S(1)}, f32[16,16,128]{2,1,0:T(8,128)S(1)}, u32[]{:S(2)}, u32[]{:S(2)}) collective-permute-start(f32[16,16,128]{2,1,0:T(8,128)S(1)} %get-tuple-element.126), channel_id=1, source_target_pairs={{0,4},{4,0},{8,12},{12,8},{1,5},{5,1},{9,13},{13,9},{2,6},{6,2},{1... | collective-permute-start | bytes 393224 | tf_op jit(solution)/shard_map/ppermute | solution.py:877
  35.9 0.7 fix_z.5
  36.6 4.2 %collective-permute-start.8 = (f32[16,16,128]{2,1,0:T(8,128)S(1)}, f32[16,16,128]{2,1,0:T(8,128)S(1)}, u32[]{:S(2)}, u32[]{:S(2)}) collective-permute-start(f32[16,16,128]{2,1,0:T(8,128)S(1)} %get-tuple-element.133), channel_id=1, source_target_pairs={{0,1},{1,0},{2,3},{3,2},{4,5},{5,4},{6,7},{7,6},{8,9},{9,8},{10,11... | collective-permute-start | bytes 393224 | tf_op jit(solution)/shard_map/ppermute | solution.py:877
  41.5 2.6 %slopes.3 = f32[3,16,16,16,128]{4,3,2,1,0:T(8,128)S(1)} custom-call(s32[4]{0:T(128)S(1)} %pad_add_fusion.sc.sc_ref, f32[3,16,16,16,128]{4,3,2,1,0:T(8,128)S(1)} %get-tuple-element.135.half_in), custom_call_target="tpu_custom_call", output_to_operand_aliasing={{}: (1, {})} | custom-call | flops 134217728 | bytes 12582928 | tf_op jit(solution)/shard_map/slopes/pallas_call | solution.py:709
  44.1 1.2 face2.1
  45.3 0.8 collective-permute-start.10
  46.1 4.2 %nodes1_back.1 = (bf16[16,16,16,128]{3,2,1,0:T(8,128)(2,1)S(1)}, bf16[16,16,16,128]{3,2,1,0:T(8,128)(2,1)S(1)}, bf16[16,16,16,128]{3,2,1,0:T(8,128)(2,1)S(1)}, f...) custom-call(s32[4]{0:T(128)S(1)} %pad_add_fusion.sc.sc_ref, ...), custom_call_target="tpu_custom_call" | custom-call | flops 939524096 | bytes 10946576 | tf_op jit(solution)/shard_map/nodes1_back/pallas_call | solution.py:709
  50.9 0.7 collective-permute-start.11
  51.6 8.6 %collective-permute-start.12 = (f32[16,16,128]{2,1,0:T(8,128)S(1)}, f32[16,16,128]{2,1,0:T(8,128)S(1)}, u32[]{:S(2)}, u32[]{:S(2)}) collective-permute-start(f32[16,16,128]{2,1,0:T(8,128)S(1)} %get-tuple-element.142), channel_id=1, source_target_pairs={{0,4},{4,0},{8,12},{12,8},{1,5},{5,1},{9,13},{13,9},{2,6},{6,2},{1... | collective-permute-start | bytes 393224 | tf_op jit(solution)/shard_map/ppermute | solution.py:877
  60.2 1.0 collective-permute-done.12.refs_2_.refs_1_
  61.2 0.7 fix_z.6
  61.9 3.8 %collective-permute-start.13 = (f32[16,16,128]{2,1,0:T(8,128)S(1)}, f32[16,16,128]{2,1,0:T(8,128)S(1)}, u32[]{:S(2)}, u32[]{:S(2)}) collective-permute-start(f32[16,16,128]{2,1,0:T(8,128)S(1)} %get-tuple-element.150), channel_id=1, source_target_pairs={{0,1},{1,0},{2,3},{3,2},{4,5},{5,4},{6,7},{7,6},{8,9},{9,8},{10,11... | collective-permute-start | bytes 393224 | tf_op jit(solution)/shard_map/ppermute | solution.py:877
  65.7 0.8 collective-permute-start.14
  66.5 1.8 %nodes1_products.1 = (f32[16,16,16,128]{3,2,1,0:T(8,128)S(1)}, f32[392,128]{1,0:T(8,128)S(1)}) custom-call(s32[4]{0:T(128)S(1)} %pad_add_fusion.sc.sc_ref, bf16[2,256,128]{2,1,0:T(8,128)(2,1)S(1)} %copy-done.4, bf16[16,16,16,128]{3,2,1,0:T(8,128)(2,1)S(1)} %get-tuple-element.152.h, bf16[16,16,16,128]{3,2,1,0:T(8,128)(2,1)S(1)} %bitcast.14, ...), custom_call_target="tpu_custom_call" | custom-call | flops 805306368 | bytes 7671824 | tf_op jit(solution)/shard_map/nodes1_products/pallas_call | solution.py:709
  68.4 0.8 collective-permute-done.13.refs_3_
  69.2 1.3 face3.1
  70.5 1.3 collective-permute-start.15
  71.8 6.9 %edges1_back_nodes0_back.1 = (bf16[16,16,16,128]{3,2,1,0:T(8,128)(2,1)S(1)}, bf16[16,16,16,128]{3,2,1,0:T(8,128)(2,1)S(1)}, f32[16,16,16,128]{3,2,1,0:T(8,128)S(...) custom-call(s32[4]{0:T(128)S(1)} %pad_add_fusion.sc.sc_ref, ...), custom_call_target="tpu_custom_call" | custom-call | flops 1610612736 | bytes 23173136 | tf_op jit(solution)/shard_map/edges1_back_nodes0_back/pallas_call | solution.py:709
  81.2 0.7 fix_z.7
  81.9 4.0 %collective-permute-start.19 = (f32[16,16,128]{2,1,0:T(8,128)S(1)}, f32[16,16,128]{2,1,0:T(8,128)S(1)}, u32[]{:S(2)}, u32[]{:S(2)}) collective-permute-start(f32[16,16,128]{2,1,0:T(8,128)S(1)} %get-tuple-element.179), channel_id=1, source_target_pairs={{0,1},{1,0},{2,3},{3,2},{4,5},{5,4},{6,7},{7,6},{8,9},{9,8},{10,11... | collective-permute-start | bytes 393224 | tf_op jit(solution)/shard_map/ppermute | solution.py:877
  87.2 0.8 collective-permute-start.21
  88.0 4.1 %collective-permute-done.21.got = f32[240,128]{1,0:T(8,128)S(1)} collective-permute-done((f32[240,128]{1,0:T(8,128)S(1)}, f32[240,128]{1,0:T(8,128)S(1)}, u32[]{:S(2)}, u32[]{:S(2)}) %collective-permute-start.21) | collective-permute-done | bytes 122912 | tf_op jit(solution)/shard_map/ppermute | solution.py:786
  92.7 7.8 %collective-permute-start.22 = (f32[120,128]{1,0:T(8,128)S(1)}, f32[120,128]{1,0:T(8,128)S(1)}, u32[]{:S(2)}, u32[]{:S(2)}) collective-permute-start(f32[120,128]{1,0:T(8,128)S(1)} %get-tuple-element.193), channel_id=1, source_target_pairs={{0,8},{4,12},{8,0},{12,4},{1,9},{5,13},{9,1},{13,5},{2,10},{6,14},... | collective-permute-start | bytes 184328 | tf_op jit(solution)/shard_map/ppermute | solution.py:786
  100.4 4.3 %edges0_back.1 = (f32[16,16,16,128]{3,2,1,0:T(8,128)S(1)}, f32[136,128]{1,0:T(8,128)S(1)}) custom-call(s32[4]{0:T(128)S(1)} %pad_add_fusion.sc.sc_ref, bf16[2,2,128,128]{3,2,1,0:T(8,128)(2,1)S(1)} %copy-done.3, bf16[2,256,128]{2,1,0:T(8,128)(2,1)S(1)} %copy-done.4, bf16[2,128,128]{2,1,0:T(8,128)(2,1)S(1)} %copy-done.6, f32[2,2,128]{2,1,0:T(2,128)S(1)} %copy-done.7, ...), custom_call_target="tpu_custom_call" | custom-call | flops 805306368 | bytes 12589072 | tf_op jit(solution)/shard_map/edges0_back/pallas_call | solution.py:709
  105.4 2.8 %collective-permute-start.23 = (f32[256,128]{1,0:T(8,128)S(1)}, f32[256,128]{1,0:T(8,128)S(1)}, u32[]{:S(2)}, u32[]{:S(2)}) collective-permute-start(f32[256,128]{1,0:T(8,128)S(1)} %stack.17.left), channel_id=1, source_target_pairs={{0,2},{1,3},{2,0},{3,1},{4,6},{5,7},{6,4},{7,5},{8,10},{9,11},{10,... | collective-permute-start | bytes 393224 | tf_op jit(solution)/shard_map/ppermute | solution.py:786
  108.2 2.7 %state_grad.1 = bf16[16,16,16,128]{3,2,1,0:T(8,128)(2,1)} custom-call(s32[4]{0:T(128)S(1)} %pad_add_fusion.sc.sc_ref, bf16[2,2,128,128]{3,2,1,0:T(8,128)(2,1)S(1)} %copy-done.3, bf16[2,256,128]{2,1,0:T(8,128)(2,1)S(1)} %copy-done.4, bf16[16,16,16,128]{3,2,1,0:T(8,128)(2,1)S(1)} %get-tuple-element.198.grad_in, ...), custom_call_target="tpu_custom_call" | custom-call | flops 536870912 | bytes 5505040 | tf_op jit(solution)/shard_map/state_grad/pallas_call | solution.py:709
  112.0 4.3 %collective-permute-start.24 = (f32[256,128]{1,0:T(8,128)S(1)}, f32[256,128]{1,0:T(8,128)S(1)}, u32[]{:S(2)}, u32[]{:S(2)}) collective-permute-start(f32[256,128]{1,0:T(8,128)S(1)} %add.8.left), channel_id=1, source_target_pairs={{0,1},{1,0},{2,3},{3,2},{4,5},{5,4},{6,7},{7,6},{8,9},{9,8},{10,11... | collective-permute-start | bytes 393224 | tf_op jit(solution)/shard_map/ppermute | solution.py:786
  116.3 2.9 %collective-permute-done.24.right = f32[256,128]{1,0:T(8,128)S(1)} collective-permute-done((f32[256,128]{1,0:T(8,128)S(1)}, f32[256,128]{1,0:T(8,128)S(1)}, u32[]{:S(2)}, u32[]{:S(2)}) %collective-permute-start.24) | collective-permute-done | bytes 131104 | tf_op jit(solution)/shard_map/ppermute | solution.py:786
  119.9 5.0 %collective-permute-done.25.got = f32[256,128]{1,0:T(8,128)S(1)} collective-permute-done((f32[256,128]{1,0:T(8,128)S(1)}, f32[256,128]{1,0:T(8,128)S(1)}, u32[]{:S(2)}, u32[]{:S(2)}) %collective-permute-start.25) | collective-permute-done | bytes 131104 | tf_op jit(solution)/shard_map/ppermute | solution.py:786
  125.4 0.8 collective-permute-start.26
  126.2 4.9 %collective-permute-done.26.got = f32[376,128]{1,0:T(8,128)S(1)} collective-permute-done((f32[376,128]{1,0:T(8,128)S(1)}, f32[376,128]{1,0:T(8,128)S(1)}, u32[]{:S(2)}, u32[]{:S(2)}) %collective-permute-start.26) | collective-permute-done | bytes 192544 | tf_op jit(solution)/shard_map/ppermute | solution.py:786
  131.7 1.6 %collective-permute-done.27.got = f32[616,128]{1,0:T(8,128)S(1)} collective-permute-done((f32[616,128]{1,0:T(8,128)S(1)}, f32[616,128]{1,0:T(8,128)S(1)}, u32[]{:S(2)}, u32[]{:S(2)}) %collective-permute-start.27) | collective-permute-done | bytes 315424 | tf_op jit(solution)/shard_map/ppermute | solution.py:786
  133.3 1.7 %finish.1 = (f32[2,2,128,128]{3,2,1,0:T(8,128)}, f32[2,256,128]{2,1,0:T(8,128)}, f32[2,128,128]{2,1,0:T(8,128)}, f32[2,2,128]{2,1,0:T(2,128)}) custom-call(s32[4]{0:T(128)S(1)} %pad_add_fusion.sc.sc_ref, bf16[2,2,128,128]{3,2,1,0:T(8,128)(2,1)S(1)} %copy-done.3, bf16[2,256,128]{2,1,0:T(8,128)(2,1)S(1)} %copy-done.4, f32[616,128]{1,0:T(8,128)S(1)} %join.3.value, ...), custom_call_target="tpu_custom_call" | custom-call | bytes 1550352 | tf_op jit(solution)/shard_map/finish/pallas_call | solution.py:709
  (54 shorter events, 11.5 us)
Async XLA Ops:
  1.4 1.2 copy-start
  2.6 0.9 copy-start.2
  3.5 0.7 copy-start.7
  5.0 7.0 %collective-permute-start = (f32[16,16,128]{2,1,0:T(8,128)S(1)}, f32[16,16,128]{2,1,0:T(8,128)S(1)}, u32[]{:S(2)}, u32[]{:S(2)}) collective-permute-start(f32[16,16,128]{2,1,0:T(8,128)S(1)} %face0.1), channel_id=1, source_target_pairs={{0,16},{16,0},{1,17},{17,1},{2,18},{18,2},{3,19},{19,3},{4,20},{20... | collective-permute-start | bytes 393224 | tf_op jit(solution)/shard_map/ppermute | solution.py:877
  12.5 1.4 %collective-permute-start.1 = (f32[16,16,128]{2,1,0:T(8,128)S(1)}, f32[16,16,128]{2,1,0:T(8,128)S(1)}, u32[]{:S(2)}, u32[]{:S(2)}) collective-permute-start(f32[16,16,128]{2,1,0:T(8,128)S(1)} %get-tuple-element.110), channel_id=1, source_target_pairs={{0,4},{4,0},{8,12},{12,8},{1,5},{5,1},{9,13},{13,9},{2,6},{6,2},{1... | collective-permute-start | bytes 393224 | tf_op jit(solution)/shard_map/ppermute | solution.py:877
  12.6 1.3 collective-permute-start.2
  14.6 5.1 %copy-start.1 = (bf16[16,16,2,8,128]{4,3,2,1,0:T(8,128)(2,1)S(1)}, bf16[16,16,2,8,128]{4,3,2,1,0:T(8,128)(2,1)}, u32[]{:S(2)}) copy-start(bf16[16,16,2,8,128]{4,3,2,1,0:T(8,128)(2,1)} %param.7) | copy-start | bytes 3145732
  14.7 5.1 %copy-start.3 = (bf16[2,2,128,128]{3,2,1,0:T(8,128)(2,1)S(1)}, bf16[2,2,128,128]{3,2,1,0:T(8,128)(2,1)}, u32[]{:S(2)}) copy-start(bf16[2,2,128,128]{3,2,1,0:T(8,128)(2,1)} %edge_w.21) | copy-start | bytes 393220
  14.7 5.1 %copy-start.4 = (bf16[2,256,128]{2,1,0:T(8,128)(2,1)S(1)}, bf16[2,256,128]{2,1,0:T(8,128)(2,1)}, u32[]{:S(2)}) copy-start(bf16[2,256,128]{2,1,0:T(8,128)(2,1)} %node_in.19) | copy-start | bytes 393220
  14.7 5.1 %copy-start.6 = (bf16[2,128,128]{2,1,0:T(8,128)(2,1)S(1)}, bf16[2,128,128]{2,1,0:T(8,128)(2,1)}, u32[]{:S(2)}) copy-start(bf16[2,128,128]{2,1,0:T(8,128)(2,1)} %node_out.13) | copy-start | bytes 196612
  14.7 5.0 %collective-permute-start.3 = (f32[16,16,128]{2,1,0:T(8,128)S(1)}, f32[16,16,128]{2,1,0:T(8,128)S(1)}, u32[]{:S(2)}, u32[]{:S(2)}) collective-permute-start(f32[16,16,128]{2,1,0:T(8,128)S(1)} %get-tuple-element.117), channel_id=1, source_target_pairs={{0,1},{1,0},{2,3},{3,2},{4,5},{5,4},{6,7},{7,6},{8,9},{9,8},{10,11... | collective-permute-start | bytes 393224 | tf_op jit(solution)/shard_map/ppermute | solution.py:877
  16.3 3.4 %collective-permute-start.4 = (f32[16,16,128]{2,1,0:T(8,128)S(1)}, f32[16,16,128]{2,1,0:T(8,128)S(1)}, u32[]{:S(2)}, u32[]{:S(2)}) collective-permute-start(f32[16,16,128]{2,1,0:T(8,128)S(1)} %get-tuple-element.118), channel_id=1, source_target_pairs={{1,2},{2,1},{5,6},{6,5},{9,10},{10,9},{13,14},{14,13},{17,18},{18,... | collective-permute-start | bytes 393224 | tf_op jit(solution)/shard_map/ppermute | solution.py:877
  21.2 8.1 %collective-permute-start.5 = (f32[16,16,128]{2,1,0:T(8,128)S(1)}, f32[16,16,128]{2,1,0:T(8,128)S(1)}, u32[]{:S(2)}, u32[]{:S(2)}) collective-permute-start(f32[16,16,128]{2,1,0:T(8,128)S(1)} %face1.1), channel_id=1, source_target_pairs={{0,16},{16,0},{1,17},{17,1},{2,18},{18,2},{3,19},{19,3},{4,20},{20... | collective-permute-start | bytes 393224 | tf_op jit(solution)/shard_map/ppermute | solution.py:877
  29.8 6.1 %collective-permute-start.6 = (f32[16,16,128]{2,1,0:T(8,128)S(1)}, f32[16,16,128]{2,1,0:T(8,128)S(1)}, u32[]{:S(2)}, u32[]{:S(2)}) collective-permute-start(f32[16,16,128]{2,1,0:T(8,128)S(1)} %get-tuple-element.126), channel_id=1, source_target_pairs={{0,4},{4,0},{8,12},{12,8},{1,5},{5,1},{9,13},{13,9},{2,6},{6,2},{1... | collective-permute-start | bytes 393224 | tf_op jit(solution)/shard_map/ppermute | solution.py:877
  35.0 1.0 collective-permute-start.7
  36.6 7.5 %copy-start.5 = (bf16[16,16,2,8,128]{4,3,2,1,0:T(8,128)(2,1)S(1)}, bf16[16,16,2,8,128]{4,3,2,1,0:T(8,128)(2,1)}, u32[]{:S(2)}) copy-start(bf16[16,16,2,8,128]{4,3,2,1,0:T(8,128)(2,1)} %param.8) | copy-start | bytes 3145732
  36.6 7.4 %collective-permute-start.8 = (f32[16,16,128]{2,1,0:T(8,128)S(1)}, f32[16,16,128]{2,1,0:T(8,128)S(1)}, u32[]{:S(2)}, u32[]{:S(2)}) collective-permute-start(f32[16,16,128]{2,1,0:T(8,128)S(1)} %get-tuple-element.133), channel_id=1, source_target_pairs={{0,1},{1,0},{2,3},{3,2},{4,5},{5,4},{6,7},{7,6},{8,9},{9,8},{10,11... | collective-permute-start | bytes 393224 | tf_op jit(solution)/shard_map/ppermute | solution.py:877
  40.8 3.3 %collective-permute-start.9 = (f32[16,16,128]{2,1,0:T(8,128)S(1)}, f32[16,16,128]{2,1,0:T(8,128)S(1)}, u32[]{:S(2)}, u32[]{:S(2)}) collective-permute-start(f32[16,16,128]{2,1,0:T(8,128)S(1)} %get-tuple-element.134), channel_id=1, source_target_pairs={{1,2},{2,1},{5,6},{6,5},{9,10},{10,9},{13,14},{14,13},{17,18},{18,... | collective-permute-start | bytes 393224 | tf_op jit(solution)/shard_map/ppermute | solution.py:877
  45.3 5.1 %collective-permute-start.10 = (f32[16,16,128]{2,1,0:T(8,128)S(1)}, f32[16,16,128]{2,1,0:T(8,128)S(1)}, u32[]{:S(2)}, u32[]{:S(2)}) collective-permute-start(f32[16,16,128]{2,1,0:T(8,128)S(1)} %face2.1), channel_id=1, source_target_pairs={{0,16},{16,0},{1,17},{17,1},{2,18},{18,2},{3,19},{19,3},{4,20},{20... | collective-permute-start | bytes 393224 | tf_op jit(solution)/shard_map/ppermute | solution.py:877
  50.9 9.3 %collective-permute-start.11 = (f32[16,16,128]{2,1,0:T(8,128)S(1)}, f32[16,16,128]{2,1,0:T(8,128)S(1)}, u32[]{:S(2)}, u32[]{:S(2)}) collective-permute-start(f32[16,16,128]{2,1,0:T(8,128)S(1)} %get-tuple-element.141), channel_id=1, source_target_pairs={{4,8},{8,4},{5,9},{9,5},{6,10},{10,6},{7,11},{11,7},{20,24},{24,20... | collective-permute-start | bytes 393224 | tf_op jit(solution)/shard_map/ppermute | solution.py:877
  51.6 9.6 %collective-permute-start.12 = (f32[16,16,128]{2,1,0:T(8,128)S(1)}, f32[16,16,128]{2,1,0:T(8,128)S(1)}, u32[]{:S(2)}, u32[]{:S(2)}) collective-permute-start(f32[16,16,128]{2,1,0:T(8,128)S(1)} %get-tuple-element.142), channel_id=1, source_target_pairs={{0,4},{4,0},{8,12},{12,8},{1,5},{5,1},{9,13},{13,9},{2,6},{6,2},{1... | collective-permute-start | bytes 393224 | tf_op jit(solution)/shard_map/ppermute | solution.py:877
  61.9 7.3 %collective-permute-start.13 = (f32[16,16,128]{2,1,0:T(8,128)S(1)}, f32[16,16,128]{2,1,0:T(8,128)S(1)}, u32[]{:S(2)}, u32[]{:S(2)}) collective-permute-start(f32[16,16,128]{2,1,0:T(8,128)S(1)} %get-tuple-element.150), channel_id=1, source_target_pairs={{0,1},{1,0},{2,3},{3,2},{4,5},{5,4},{6,7},{7,6},{8,9},{9,8},{10,11... | collective-permute-start | bytes 393224 | tf_op jit(solution)/shard_map/ppermute | solution.py:877
  65.7 3.5 %collective-permute-start.14 = (f32[16,16,128]{2,1,0:T(8,128)S(1)}, f32[16,16,128]{2,1,0:T(8,128)S(1)}, u32[]{:S(2)}, u32[]{:S(2)}) collective-permute-start(f32[16,16,128]{2,1,0:T(8,128)S(1)} %get-tuple-element.151), channel_id=1, source_target_pairs={{1,2},{2,1},{5,6},{6,5},{9,10},{10,9},{13,14},{14,13},{17,18},{18,... | collective-permute-start | bytes 393224 | tf_op jit(solution)/shard_map/ppermute | solution.py:877
  70.5 8.7 %collective-permute-start.15 = (f32[16,16,128]{2,1,0:T(8,128)S(1)}, f32[16,16,128]{2,1,0:T(8,128)S(1)}, u32[]{:S(2)}, u32[]{:S(2)}) collective-permute-start(f32[16,16,128]{2,1,0:T(8,128)S(1)} %face3.1), channel_id=1, source_target_pairs={{0,16},{16,0},{1,17},{17,1},{2,18},{18,2},{3,19},{19,3},{4,20},{20... | collective-permute-start | bytes 393224 | tf_op jit(solution)/shard_map/ppermute | solution.py:877
  78.7 3.2 %collective-permute-start.18 = (f32[480,128]{1,0:T(8,128)S(1)}, f32[480,128]{1,0:T(8,128)S(1)}, u32[]{:S(2)}, u32[]{:S(2)}) collective-permute-start(f32[480,128]{1,0:T(8,128)S(1)} %get-tuple-element.178), channel_id=1, source_target_pairs={{0,4},{4,0},{8,12},{12,8},{1,5},{5,1},{9,13},{13,9},{2,6},{6,2},{1... | collective-permute-start | bytes 737288 | tf_op jit(solution)/shard_map/ppermute | solution.py:786
  79.8 1.4 %collective-permute-start.16 = (f32[16,16,128]{2,1,0:T(8,128)S(1)}, f32[16,16,128]{2,1,0:T(8,128)S(1)}, u32[]{:S(2)}, u32[]{:S(2)}) collective-permute-start(f32[16,16,128]{2,1,0:T(8,128)S(1)} %get-tuple-element.171), channel_id=1, source_target_pairs={{0,4},{4,0},{8,12},{12,8},{1,5},{5,1},{9,13},{13,9},{2,6},{6,2},{1... | collective-permute-start | bytes 393224 | tf_op jit(solution)/shard_map/ppermute | solution.py:877
  79.9 1.3 collective-permute-start.17
  81.9 10.2 %collective-permute-start.19 = (f32[16,16,128]{2,1,0:T(8,128)S(1)}, f32[16,16,128]{2,1,0:T(8,128)S(1)}, u32[]{:S(2)}, u32[]{:S(2)}) collective-permute-start(f32[16,16,128]{2,1,0:T(8,128)S(1)} %get-tuple-element.179), channel_id=1, source_target_pairs={{0,1},{1,0},{2,3},{3,2},{4,5},{5,4},{6,7},{7,6},{8,9},{9,8},{10,11... | collective-permute-start | bytes 393224 | tf_op jit(solution)/shard_map/ppermute | solution.py:877
  85.9 6.2 %collective-permute-start.20 = (f32[16,16,128]{2,1,0:T(8,128)S(1)}, f32[16,16,128]{2,1,0:T(8,128)S(1)}, u32[]{:S(2)}, u32[]{:S(2)}) collective-permute-start(f32[16,16,128]{2,1,0:T(8,128)S(1)} %get-tuple-element.180), channel_id=1, source_target_pairs={{1,2},{2,1},{5,6},{6,5},{9,10},{10,9},{13,14},{14,13},{17,18},{18,... | collective-permute-start | bytes 393224 | tf_op jit(solution)/shard_map/ppermute | solution.py:877
  87.2 4.9 %collective-permute-start.21 = (f32[240,128]{1,0:T(8,128)S(1)}, f32[240,128]{1,0:T(8,128)S(1)}, u32[]{:S(2)}, u32[]{:S(2)}) collective-permute-start(f32[240,128]{1,0:T(8,128)S(1)} %get-tuple-element.184), channel_id=1, source_target_pairs={{0,16},{16,0},{1,17},{17,1},{2,18},{18,2},{3,19},{19,3},{4,20},{20... | collective-permute-start | bytes 368648 | tf_op jit(solution)/shard_map/ppermute | solution.py:786
  92.7 12.1 %collective-permute-start.22 = (f32[120,128]{1,0:T(8,128)S(1)}, f32[120,128]{1,0:T(8,128)S(1)}, u32[]{:S(2)}, u32[]{:S(2)}) collective-permute-start(f32[120,128]{1,0:T(8,128)S(1)} %get-tuple-element.193), channel_id=1, source_target_pairs={{0,8},{4,12},{8,0},{12,4},{1,9},{5,13},{9,1},{13,5},{2,10},{6,14},... | collective-permute-start | bytes 184328 | tf_op jit(solution)/shard_map/ppermute | solution.py:786
  105.4 6.1 %collective-permute-start.23 = (f32[256,128]{1,0:T(8,128)S(1)}, f32[256,128]{1,0:T(8,128)S(1)}, u32[]{:S(2)}, u32[]{:S(2)}) collective-permute-start(f32[256,128]{1,0:T(8,128)S(1)} %stack.17.left), channel_id=1, source_target_pairs={{0,2},{1,3},{2,0},{3,1},{4,6},{5,7},{6,4},{7,5},{8,10},{9,11},{10,... | collective-permute-start | bytes 393224 | tf_op jit(solution)/shard_map/ppermute | solution.py:786
  112.0 7.2 %collective-permute-start.24 = (f32[256,128]{1,0:T(8,128)S(1)}, f32[256,128]{1,0:T(8,128)S(1)}, u32[]{:S(2)}, u32[]{:S(2)}) collective-permute-start(f32[256,128]{1,0:T(8,128)S(1)} %add.8.left), channel_id=1, source_target_pairs={{0,1},{1,0},{2,3},{3,2},{4,5},{5,4},{6,7},{7,6},{8,9},{9,8},{10,11... | collective-permute-start | bytes 393224 | tf_op jit(solution)/shard_map/ppermute | solution.py:786
  119.8 5.0 %collective-permute-start.25 = (f32[256,128]{1,0:T(8,128)S(1)}, f32[256,128]{1,0:T(8,128)S(1)}, u32[]{:S(2)}, u32[]{:S(2)}) collective-permute-start(f32[256,128]{1,0:T(8,128)S(1)} %add.9.value), channel_id=1, source_target_pairs={{0,8},{4,12},{8,0},{12,4},{1,9},{5,13},{9,1},{13,5},{2,10},{6,14},... | collective-permute-start | bytes 393224 | tf_op jit(solution)/shard_map/ppermute | solution.py:786
  125.4 5.7 %collective-permute-start.26 = (f32[376,128]{1,0:T(8,128)S(1)}, f32[376,128]{1,0:T(8,128)S(1)}, u32[]{:S(2)}, u32[]{:S(2)}) collective-permute-start(f32[376,128]{1,0:T(8,128)S(1)} %join.2.value), channel_id=1, source_target_pairs={{0,16},{16,0},{1,17},{17,1},{2,18},{18,2},{3,19},{19,3},{4,20},{20... | collective-permute-start | bytes 577544 | tf_op jit(solution)/shard_map/ppermute | solution.py:786
  131.7 1.7 %collective-permute-start.27 = (f32[616,128]{1,0:T(8,128)S(1)}, f32[616,128]{1,0:T(8,128)S(1)}, u32[]{:S(2)}, u32[]{:S(2)}) collective-permute-start(f32[616,128]{1,0:T(8,128)S(1)} %join.3.value), channel_id=1, source_target_pairs={{0,4},{4,0},{8,12},{12,8},{1,5},{5,1},{9,13},{13,9},{2,6},{6,2},{1... | collective-permute-start | bytes 946184 | tf_op jit(solution)/shard_map/ppermute | solution.py:786

commit v6 on v5

--- a/solution.py
+++ b/solution.py
@@ -1,4 +1,5 @@
 import functools
+import itertools
 import math
 
 import jax
@@ -277,7 +278,8 @@
     return jnp.where(low | high, 0.5, 1.0).astype(f32)
 
 
-CHUNK = 8
+def chunk_of(x_len):
+    return 2 * NODES if x_len % (2 * NODES) == 0 else NODES
 
 
 def scale_planes(sc_ref, inv_ref, x, block, x_len, size_x):
@@ -301,11 +303,11 @@
 
 
 def node_share(sc_ref, x, inv_ref, size_x, dpn, weights, layer, sum_ref):
-    shape = (CHUNK,) + sum_ref.shape[1:]
+    shape = (chunk_of(sum_ref.shape[0]),) + sum_ref.shape[1:]
     dx = dot_rt(dpn, weights[1][layer, pl.ds(128, 128)]).reshape(shape)
     share = scale_planes(sc_ref, inv_ref, x, dx, sum_ref.shape[0], size_x)
     joined = couple_slots(share.reshape((-1,) + shape[2:]), sc_ref[0])
-    sum_ref[pl.ds(x, CHUNK)] = joined.reshape(shape)
+    sum_ref[pl.ds(x, shape[0])] = joined.reshape(shape)
 
 
 def node_products(grad, feat, scaled, act, dpn, grads):
@@ -433,11 +435,13 @@
 
 
 def planes(count, body):
+    chunk = chunk_of(count)
+
     def step(c, carry):
-        body(pl.multiple_of(c * CHUNK, CHUNK))
+        body(pl.multiple_of(c * chunk, chunk))
         return carry
 
-    lax.fori_loop(0, count // CHUNK, step, 0)
+    lax.fori_loop(0, count // chunk, step, 0)
 
 
 def half_weights(weights, layer):
@@ -530,10 +534,10 @@
     faces, (work, inv) = refs[6:-2], refs[-2:]
     add_halo(sc, sums_in, halo, work, counts)
     write_inverse(sc, inv, sizes)
-    shape = (CHUNK,) + h.shape[1:]
+    shape = (chunk_of(h.shape[0]),) + h.shape[1:]
 
     def body(x):
-        at = pl.ds(x, CHUNK)
+        at = pl.ds(x, chunk_of(h.shape[0]))
         sums_at = flat(scale_planes(sc, inv, x, work[at], h.shape[0], sizes[0]))
         scaled, act, slope = node_forward(sums_at, flat(h[at]), weights, 0)
         scaled_ref[at] = scaled.reshape(shape)
@@ -557,11 +561,11 @@
     faces, (work, inv) = refs[4:-2], refs[-2:]
     add_halo(sc, sums_in, halo, work, counts)
     write_inverse(sc, inv, sizes)
-    shape = (CHUNK,) + h.shape[1:]
+    shape = (chunk_of(h.shape[0]),) + h.shape[1:]
     live = live_rows(sc, h)
 
     def body(x):
-        at = pl.ds(x, CHUNK)
+        at = pl.ds(x, chunk_of(h.shape[0]))
         sums_at = flat(scale_planes(sc, inv, x, work[at], h.shape[0], sizes[0]))
         scaled, act, slope = node_forward(sums_at, flat(h[at]), weights, 1)
         scaled_ref[at] = scaled.reshape(shape)
@@ -585,7 +589,7 @@
     live = live_rows(sc, h)
 
     def body(x):
-        at = pl.ds(x, CHUNK)
+        at = pl.ds(x, chunk_of(h.shape[0]))
         grad = (g_ref[at].astype(f32) * live).astype(bf16)
         node_products(flat(grad), flat(h[at]), flat(scaled[at]), flat(act[at]), flat(dpn[at]), grads)
         dx = dot_rt(flat(dpn[at]), node_in[1, pl.ds(0, 128)])
@@ -596,11 +600,11 @@
 
 def edge_parts(counts, sc, weights, layer, sums_in, halo, h, slopes, work, grads, row):
     add_halo(sc, sums_in, halo, work, counts)
-    shape = (CHUNK,) + h.shape[1:]
+    shape = (chunk_of(h.shape[0]),) + h.shape[1:]
     w_two = twice(weights[0][layer, 1])
 
     def to_q(x):
-        at = pl.ds(x, CHUNK)
+        at = pl.ds(x, chunk_of(h.shape[0]))
         work[at] = dot_rt(split_cols(flat(work[at])), w_two).reshape(shape)
 
     planes(h.shape[0], to_q)
@@ -608,7 +612,7 @@
 
 
 def edge_product(h, x, pair, grads, row):
-    both = dot_t(flat(h[pl.ds(x, CHUNK)]), pair)
+    both = dot_t(flat(h[pl.ds(x, chunk_of(h.shape[0]))]), pair)
     grads[pl.ds(row, 128)] += both[:, :128] + both[:, 128:]
 
 
@@ -626,12 +630,12 @@
     grads[pl.ds(512 + 2 * NODES, grads1.shape[0])] = grads1[...]
 
     row = 384 + NODES
-    shape = (CHUNK,) + h.shape[1:]
+    shape = (chunk_of(h.shape[0]),) + h.shape[1:]
     edge_parts(counts, sc, weights, 1, sums_in, halo, h, slopes, work, grads, row)
     w_one = twice(edge_w[1, 0])
 
     def body(x):
-        at = pl.ds(x, CHUNK)
+        at = pl.ds(x, chunk_of(h.shape[0]))
         pair = split_cols(flat(work[at]))
         edge_product(h, x, pair, grads, row)
         grad = (flat(base_in[at]) + dot_rt(pair, w_one)).astype(bf16)
@@ -654,17 +658,17 @@
     edge_parts(counts, sc, (edge_w,), 0, sums_in, halo, h, slopes, edges, grads, 0)
 
     def body(x):
-        edge_product(h, x, split_cols(flat(edges[pl.ds(x, CHUNK)])), grads, 0)
+        edge_product(h, x, split_cols(flat(edges[pl.ds(x, chunk_of(edges.shape[0]))])), grads, 0)
 
     planes(h.shape[0], body)
 
 
 def state_kernel(sc, edge_w, node_in, grad_in, dpn, edges, grad_ref):
-    shape = (CHUNK,) + edges.shape[1:]
+    shape = (chunk_of(edges.shape[0]),) + edges.shape[1:]
     weight = jnp.concatenate([twice(edge_w[0, 0]), node_in[0, pl.ds(0, 128)]], 1)
 
     def body(x):
-        at = pl.ds(x, CHUNK)
+        at = pl.ds(x, chunk_of(edges.shape[0]))
         parts = jnp.concatenate([split_cols(flat(edges[at])), flat(dpn[at])], -1)
         grad_ref[at] = (flat(grad_in[at]).astype(f32) + dot_rt(parts, weight)).astype(bf16).reshape(shape)
 
@@ -735,9 +739,13 @@
 
 
 def halving_steps(sizes):
-    steps = [(1, hop) for hop in hops(sizes[1])[:1]]
-    steps += [(0, hop) for hop in hops(sizes[0])]
-    return steps + [(1, hop) for hop in hops(sizes[1])[1:]]
+    return [(1, hop) for hop in hops(sizes[1])[:1]] + [(0, hop) for hop in hops(sizes[0])]
+
+
+def whole_steps(sizes):
+    along_z = hops(sizes[2])
+    steps = [(2, along_z[k : k + 2]) for k in range(0, len(along_z), 2)]
+    return steps + [(1, [hop]) for hop in hops(sizes[1])[1:]]
 
 
 def padded_rows(rows, sizes):
@@ -762,8 +770,11 @@
     write_halves(sc, step, total, keep, send)
 
 
-def add_kernel(sc, left, right, out):
-    out[...] = left[...] + right[...]
+def add_kernel(sc, *refs):
+    total = refs[0][...] + refs[1][...]
+    for ref in refs[2:-1]:
+        total = total + ref[...]
+    refs[-1][...] = total
 
 
 def join_kernel_of(step, start, sc, value, got, out):
@@ -896,7 +907,7 @@
         if work is not None:
             faces_z, held = lax.optimization_barrier((faces_z, held))
             done = work(*held)
-        got_z = background.beside(trade(faces_z, "gz"))
+        got_z = trade(faces_z, "gz")
         got_z, done = lax.optimization_barrier((got_z, done))
         return (*got_x, *got_y, *got_z), done
 
@@ -946,8 +957,10 @@
     (grad0,) = call(
         state_kernel, "state_grad", (sc, edge_weights, node_in, grad_in, dpn0, edges), [full16], [], 4 * matmul
     )
-    for hop in reversed(hops(sizes[2])):
-        (value,) = call(add_kernel, "add", (sc, value, swap(value, (2, hop))), [rows_like(value.shape[0])])
+    for axis, together in whole_steps(sizes):
+        partners = [sum(c) for n in range(1, len(together) + 1) for c in itertools.combinations(together, n)]
+        got = [swap(value, (axis, partner)) for partner in partners]
+        (value,) = call(add_kernel, "add", (sc, value, *got), [rows_like(value.shape[0])])
         value, grad0 = lax.optimization_barrier((value, grad0))
     first, *rest = halving_steps(sizes)
     for step in reversed(rest):

time: 135 us -> 134 us (level)
  Pallas kernels: 51.2 us -> 48.4 us
  waiting for transfers between devices: 22.6 us -> 24.3 us
    pallas_call x29 -> x27, Pallas kernels: 51.2 us -> 48.4 us  [call(): pl.pallas_call(kernel, name=name, out_shape=tuple(outs), in_specs=[SM] +...]
  transfers between devices with their start and end apart: 28 -> 28, of which waited for: 12 -> 13; matrix products, arithmetic and copies ran while one was open for 0% -> 0% of each run, Pallas kernels for 28% -> 27%
where the time goes in v6:
time: 134 us; the launch traced here: 133 us
  starting transfers between devices  55.7 us (42%)
  Pallas kernels  48.4 us (36%)
  waiting for transfers between devices  24.3 us (18%)
  local copies, waits for them, and re-layouts  2.84 us (2%)
  between operations  1.65 us (1%)
    pallas_call x27, Pallas kernels, call(): pl.pallas_call(kernel, name=name, out_shape=tuple(outs), in_specs=[SM] +...  48.4 us
    ppermute x20, starting transfers between devices, trade(): lax.ppermute(face, axis, pairs(size, kind))  39.1 us
    ppermute x8, waiting for transfers between devices, swap(): lax.ppermute(value, axis, [(i, i ^ step[1]) for i in range(lax.axis_size(...  19.7 us
    ppermute x8, starting transfers between devices, swap(): lax.ppermute(value, axis, [(i, i ^ step[1]) for i in range(lax.axis_size(...  16.6 us
    ppermute x20, waiting for transfers between devices, trade(): lax.ppermute(face, axis, pairs(size, kind))  4.58 us
    unnamed x16, local copies, waits for them, and re-layouts  2.84 us
  transfers between devices with their start and end apart: 28, of which 13 were waited for; matrix products, arithmetic and copies ran while one was open for 0% of the time, Pallas kernels for 27%

profile of v6, /device:TPU:0, one launch (start us, length us, event | category | flops | bytes accessed | tf_op | source)
XLA Modules:
  0.0 133.0 jit_solution(15691839303479191887)
XLA Ops:
  1.4 1.2 copy-done
  2.6 0.9 copy-done.2
  3.5 0.7 copy-done.7
  4.2 0.8 face0.1
  5.0 3.0 %collective-permute-start = (f32[16,16,128]{2,1,0:T(8,128)S(1)}, f32[16,16,128]{2,1,0:T(8,128)S(1)}, u32[]{:S(2)}, u32[]{:S(2)}) collective-permute-start(f32[16,16,128]{2,1,0:T(8,128)S(1)} %face0.1), channel_id=1, source_target_pairs={{0,16},{16,0},{1,17},{17,1},{2,18},{18,2},{3,19},{19,3},{4,20},{20... | collective-permute-start | bytes 393224 | tf_op jit(solution)/shard_map/ppermute | solution.py:888
  8.0 4.0 %edges0.1 = (f32[16,16,16,128]{3,2,1,0:T(8,128)S(1)}, f32[3,16,16,16,128]{4,3,2,1,0:T(8,128)S(1)}, f32[16,16,128]{2,1,0:T(8,128)S(1)}, f32[16,16,128]{2,1,0:T(8,...) custom-call(s32[4]{0:T(128)S(1)} %pad_add_fusion.sc.sc_ref, bf16[2,2,128,128]{3,2,1,0:T(8,128)(2,1)S(1)} %copy-done.2, ...), custom_call_target="tpu_custom_call" | custom-call | flops 402653184 | bytes 10094608 | tf_op jit(solution)/shard_map/edges0/pallas_call | solution.py:713
  12.6 0.7 collective-permute-start.2
  13.3 0.7 collective-permute-done.1.refs_2_.refs_1_
  14.0 0.7 fix_z.4
  14.7 1.6 %collective-permute-start.3 = (f32[16,16,128]{2,1,0:T(8,128)S(1)}, f32[16,16,128]{2,1,0:T(8,128)S(1)}, u32[]{:S(2)}, u32[]{:S(2)}) collective-permute-start(f32[16,16,128]{2,1,0:T(8,128)S(1)} %get-tuple-element.111), channel_id=1, source_target_pairs={{0,1},{1,0},{2,3},{3,2},{4,5},{5,4},{6,7},{7,6},{8,9},{9,8},{10,11... | collective-permute-start | bytes 393224 | tf_op jit(solution)/shard_map/ppermute | solution.py:888
  17.0 2.6 %slopes.2 = f32[3,16,16,16,128]{4,3,2,1,0:T(8,128)S(1)} custom-call(s32[4]{0:T(128)S(1)} %pad_add_fusion.sc.sc_ref, f32[3,16,16,16,128]{4,3,2,1,0:T(8,128)S(1)} %get-tuple-element.113.half_in), custom_call_target="tpu_custom_call", output_to_operand_aliasing={{}: (1, {})} | custom-call | flops 134217728 | bytes 12582928 | tf_op jit(solution)/shard_map/slopes/pallas_call | solution.py:713
  19.8 1.4 %face1.1 = f32[16,16,128]{2,1,0:T(8,128)S(1)} custom-call(s32[4]{0:T(128)S(1)} %pad_add_fusion.sc.sc_ref, bf16[2,2,128,128]{3,2,1,0:T(8,128)(2,1)S(1)} %copy-done.3, bf16[2,256,128]{2,1,0:T(8,128)(2,1)S(1)} %copy-done.4, bf16[2,128,128]{2,1,0:T(8,128)(2,1)S(1)} %copy-done.6, f32[2,2,128]{2,1,0:T(2,128)S(1)} %copy-done.7, ...), custom_call_target="tpu_custom_call" | custom-call | flops 33554432 | bytes 4261904 | tf_op jit(solution)/shard_map/face1/pallas_call | solution.py:713
  21.2 1.3 collective-permute-start.5
  22.5 6.5 %nodes0_edges1.1 = (bf16[16,16,16,128]{3,2,1,0:T(8,128)(2,1)S(1)}, bf16[16,16,16,128]{3,2,1,0:T(8,128)(2,1)S(1)}, f32[16,16,16,128]{3,2,1,0:T(8,128)S(1)}, bf16[...) custom-call(s32[4]{0:T(128)S(1)} %pad_add_fusion.sc.sc_ref, ...), custom_call_target="tpu_custom_call" | custom-call | flops 1073741824 | bytes 18286608 | tf_op jit(solution)/shard_map/nodes0_edges1/pallas_call | solution.py:713
  29.6 5.1 %collective-permute-start.6 = (f32[16,16,128]{2,1,0:T(8,128)S(1)}, f32[16,16,128]{2,1,0:T(8,128)S(1)}, u32[]{:S(2)}, u32[]{:S(2)}) collective-permute-start(f32[16,16,128]{2,1,0:T(8,128)S(1)} %get-tuple-element.120), channel_id=1, source_target_pairs={{0,4},{4,0},{8,12},{12,8},{1,5},{5,1},{9,13},{13,9},{2,6},{6,2},{1... | collective-permute-start | bytes 393224 | tf_op jit(solution)/shard_map/ppermute | solution.py:888
  35.6 0.7 fix_z.5
  36.3 4.2 %collective-permute-start.8 = (f32[16,16,128]{2,1,0:T(8,128)S(1)}, f32[16,16,128]{2,1,0:T(8,128)S(1)}, u32[]{:S(2)}, u32[]{:S(2)}) collective-permute-start(f32[16,16,128]{2,1,0:T(8,128)S(1)} %get-tuple-element.127), channel_id=1, source_target_pairs={{0,1},{1,0},{2,3},{3,2},{4,5},{5,4},{6,7},{7,6},{8,9},{9,8},{10,11... | collective-permute-start | bytes 393224 | tf_op jit(solution)/shard_map/ppermute | solution.py:888
  41.2 2.6 %slopes.3 = f32[3,16,16,16,128]{4,3,2,1,0:T(8,128)S(1)} custom-call(s32[4]{0:T(128)S(1)} %pad_add_fusion.sc.sc_ref, f32[3,16,16,16,128]{4,3,2,1,0:T(8,128)S(1)} %get-tuple-element.129.half_in), custom_call_target="tpu_custom_call", output_to_operand_aliasing={{}: (1, {})} | custom-call | flops 134217728 | bytes 12582928 | tf_op jit(solution)/shard_map/slopes/pallas_call | solution.py:713
  43.8 1.2 face2.1
  45.0 0.8 collective-permute-start.10
  45.8 3.8 %nodes1_back.1 = (bf16[16,16,16,128]{3,2,1,0:T(8,128)(2,1)S(1)}, bf16[16,16,16,128]{3,2,1,0:T(8,128)(2,1)S(1)}, bf16[16,16,16,128]{3,2,1,0:T(8,128)(2,1)S(1)}, f...) custom-call(s32[4]{0:T(128)S(1)} %pad_add_fusion.sc.sc_ref, ...), custom_call_target="tpu_custom_call" | custom-call | flops 939524096 | bytes 10946576 | tf_op jit(solution)/shard_map/nodes1_back/pallas_call | solution.py:713
  50.6 0.7 collective-permute-start.11
  51.3 8.6 %collective-permute-start.12 = (f32[16,16,128]{2,1,0:T(8,128)S(1)}, f32[16,16,128]{2,1,0:T(8,128)S(1)}, u32[]{:S(2)}, u32[]{:S(2)}) collective-permute-start(f32[16,16,128]{2,1,0:T(8,128)S(1)} %get-tuple-element.136), channel_id=1, source_target_pairs={{0,4},{4,0},{8,12},{12,8},{1,5},{5,1},{9,13},{13,9},{2,6},{6,2},{1... | collective-permute-start | bytes 393224 | tf_op jit(solution)/shard_map/ppermute | solution.py:888
  59.9 1.0 collective-permute-done.12.refs_2_.refs_1_
  60.9 0.7 fix_z.6
  61.6 3.8 %collective-permute-start.13 = (f32[16,16,128]{2,1,0:T(8,128)S(1)}, f32[16,16,128]{2,1,0:T(8,128)S(1)}, u32[]{:S(2)}, u32[]{:S(2)}) collective-permute-start(f32[16,16,128]{2,1,0:T(8,128)S(1)} %get-tuple-element.144), channel_id=1, source_target_pairs={{0,1},{1,0},{2,3},{3,2},{4,5},{5,4},{6,7},{7,6},{8,9},{9,8},{10,11... | collective-permute-start | bytes 393224 | tf_op jit(solution)/shard_map/ppermute | solution.py:888
  65.4 0.8 collective-permute-start.14
  66.2 1.6 %nodes1_products.1 = (f32[16,16,16,128]{3,2,1,0:T(8,128)S(1)}, f32[392,128]{1,0:T(8,128)S(1)}) custom-call(s32[4]{0:T(128)S(1)} %pad_add_fusion.sc.sc_ref, bf16[2,256,128]{2,1,0:T(8,128)(2,1)S(1)} %copy-done.4, bf16[16,16,16,128]{3,2,1,0:T(8,128)(2,1)S(1)} %get-tuple-element.146.h, bf16[16,16,16,128]{3,2,1,0:T(8,128)(2,1)S(1)} %bitcast.14, ...), custom_call_target="tpu_custom_call" | custom-call | flops 805306368 | bytes 7671824 | tf_op jit(solution)/shard_map/nodes1_products/pallas_call | solution.py:713
  67.8 1.0 collective-permute-done.13.refs_3_
  68.8 1.3 face3.1
  70.1 0.9 collective-permute-start.15
  71.0 6.7 %edges1_back_nodes0_back.1 = (bf16[16,16,16,128]{3,2,1,0:T(8,128)(2,1)S(1)}, bf16[16,16,16,128]{3,2,1,0:T(8,128)(2,1)S(1)}, f32[16,16,16,128]{3,2,1,0:T(8,128)S(...) custom-call(s32[4]{0:T(128)S(1)} %pad_add_fusion.sc.sc_ref, ...), custom_call_target="tpu_custom_call" | custom-call | flops 1610612736 | bytes 23156752 | tf_op jit(solution)/shard_map/edges1_back_nodes0_back/pallas_call | solution.py:713
  80.2 0.7 fix_z.7
  80.9 4.0 %collective-permute-start.19 = (f32[16,16,128]{2,1,0:T(8,128)S(1)}, f32[16,16,128]{2,1,0:T(8,128)S(1)}, u32[]{:S(2)}, u32[]{:S(2)}) collective-permute-start(f32[16,16,128]{2,1,0:T(8,128)S(1)} %get-tuple-element.173), channel_id=1, source_target_pairs={{0,1},{1,0},{2,3},{3,2},{4,5},{5,4},{6,7},{7,6},{8,9},{9,8},{10,11... | collective-permute-start | bytes 393224 | tf_op jit(solution)/shard_map/ppermute | solution.py:888
  86.1 1.3 collective-permute-start.21
  87.8 4.0 %edges0_back.1 = (f32[16,16,16,128]{3,2,1,0:T(8,128)S(1)}, f32[136,128]{1,0:T(8,128)S(1)}) custom-call(s32[4]{0:T(128)S(1)} %pad_add_fusion.sc.sc_ref, bf16[2,2,128,128]{3,2,1,0:T(8,128)(2,1)S(1)} %copy-done.3, bf16[2,256,128]{2,1,0:T(8,128)(2,1)S(1)} %copy-done.4, bf16[2,128,128]{2,1,0:T(8,128)(2,1)S(1)} %copy-done.6, f32[2,2,128]{2,1,0:T(2,128)S(1)} %copy-done.7, ...), custom_call_target="tpu_custom_call" | custom-call | flops 805306368 | bytes 12589072 | tf_op jit(solution)/shard_map/edges0_back/pallas_call | solution.py:713
  92.4 4.1 %collective-permute-start.22 = (f32[368,128]{1,0:T(8,128)S(1)}, f32[368,128]{1,0:T(8,128)S(1)}, u32[]{:S(2)}, u32[]{:S(2)}) collective-permute-start(f32[368,128]{1,0:T(8,128)S(1)} %stack.17.refs_0_), channel_id=1, source_target_pairs={{0,1},{1,0},{2,3},{3,2},{4,5},{5,4},{6,7},{7,6},{8,9},{9,8},{10,11... | collective-permute-start | bytes 565256 | tf_op jit(solution)/shard_map/ppermute | solution.py:797
  96.5 1.5 %collective-permute-start.23 = (f32[368,128]{1,0:T(8,128)S(1)}, f32[368,128]{1,0:T(8,128)S(1)}, u32[]{:S(2)}, u32[]{:S(2)}) collective-permute-start(f32[368,128]{1,0:T(8,128)S(1)} %stack.17.refs_0_), channel_id=1, source_target_pairs={{0,2},{1,3},{2,0},{3,1},{4,6},{5,7},{6,4},{7,5},{8,10},{9,11},{10,... | collective-permute-start | bytes 565256 | tf_op jit(solution)/shard_map/ppermute | solution.py:797
  98.0 1.4 %collective-permute-start.24 = (f32[368,128]{1,0:T(8,128)S(1)}, f32[368,128]{1,0:T(8,128)S(1)}, u32[]{:S(2)}, u32[]{:S(2)}) collective-permute-start(f32[368,128]{1,0:T(8,128)S(1)} %stack.17.refs_0_), channel_id=1, source_target_pairs={{0,3},{1,2},{2,1},{3,0},{4,7},{5,6},{6,5},{7,4},{8,11},{9,10},{10,... | collective-permute-start | bytes 565256 | tf_op jit(solution)/shard_map/ppermute | solution.py:797
  99.4 2.5 %state_grad.1 = bf16[16,16,16,128]{3,2,1,0:T(8,128)(2,1)} custom-call(s32[4]{0:T(128)S(1)} %pad_add_fusion.sc.sc_ref, bf16[2,2,128,128]{3,2,1,0:T(8,128)(2,1)S(1)} %copy-done.3, bf16[2,256,128]{2,1,0:T(8,128)(2,1)S(1)} %copy-done.4, bf16[16,16,16,128]{3,2,1,0:T(8,128)(2,1)S(1)} %get-tuple-element.186.grad_in, ...), custom_call_target="tpu_custom_call" | custom-call | flops 536870912 | bytes 5505040 | tf_op jit(solution)/shard_map/state_grad/pallas_call | solution.py:713
  102.0 1.1 collective-permute-done.23.refs_2_
  103.0 6.2 %collective-permute-done.24.refs_3_ = f32[368,128]{1,0:T(8,128)S(1)} collective-permute-done((f32[368,128]{1,0:T(8,128)S(1)}, f32[368,128]{1,0:T(8,128)S(1)}, u32[]{:S(2)}, u32[]{:S(2)}) %collective-permute-start.24) | collective-permute-done | bytes 188448 | tf_op jit(solution)/shard_map/ppermute | solution.py:797
  109.8 6.6 %collective-permute-start.25 = (f32[368,128]{1,0:T(8,128)S(1)}, f32[368,128]{1,0:T(8,128)S(1)}, u32[]{:S(2)}, u32[]{:S(2)}) collective-permute-start(f32[368,128]{1,0:T(8,128)S(1)} %add.8.refs_0_), channel_id=1, source_target_pairs={{0,8},{4,12},{8,0},{12,4},{1,9},{5,13},{9,1},{13,5},{2,10},{6,14},... | collective-permute-start | bytes 565256 | tf_op jit(solution)/shard_map/ppermute | solution.py:797
  116.3 5.3 %collective-permute-done.25.refs_1_ = f32[368,128]{1,0:T(8,128)S(1)} collective-permute-done((f32[368,128]{1,0:T(8,128)S(1)}, f32[368,128]{1,0:T(8,128)S(1)}, u32[]{:S(2)}, u32[]{:S(2)}) %collective-permute-start.25) | collective-permute-done | bytes 188448 | tf_op jit(solution)/shard_map/ppermute | solution.py:797
  122.2 1.3 collective-permute-start.26
  123.5 5.6 %collective-permute-done.26.got = f32[368,128]{1,0:T(8,128)S(1)} collective-permute-done((f32[368,128]{1,0:T(8,128)S(1)}, f32[368,128]{1,0:T(8,128)S(1)}, u32[]{:S(2)}, u32[]{:S(2)}) %collective-permute-start.26) | collective-permute-done | bytes 188448 | tf_op jit(solution)/shard_map/ppermute | solution.py:797
  129.7 1.6 %collective-permute-done.27.got = f32[600,128]{1,0:T(8,128)S(1)} collective-permute-done((f32[600,128]{1,0:T(8,128)S(1)}, f32[600,128]{1,0:T(8,128)S(1)}, u32[]{:S(2)}, u32[]{:S(2)}) %collective-permute-start.27) | collective-permute-done | bytes 307232 | tf_op jit(solution)/shard_map/ppermute | solution.py:797
  131.3 1.7 %finish.1 = (f32[2,2,128,128]{3,2,1,0:T(8,128)}, f32[2,256,128]{2,1,0:T(8,128)}, f32[2,128,128]{2,1,0:T(8,128)}, f32[2,2,128]{2,1,0:T(2,128)}) custom-call(s32[4]{0:T(128)S(1)} %pad_add_fusion.sc.sc_ref, bf16[2,2,128,128]{3,2,1,0:T(8,128)(2,1)S(1)} %copy-done.3, bf16[2,256,128]{2,1,0:T(8,128)(2,1)S(1)} %copy-done.4, f32[600,128]{1,0:T(8,128)S(1)} %join.1.value, ...), custom_call_target="tpu_custom_call" | custom-call | bytes 1533968 | tf_op jit(solution)/shard_map/finish/pallas_call | solution.py:713
  (52 shorter events, 11.3 us)
Async XLA Ops:
  1.4 1.2 copy-start
  2.6 0.9 copy-start.2
  3.5 0.7 copy-start.7
  5.0 7.0 %collective-permute-start = (f32[16,16,128]{2,1,0:T(8,128)S(1)}, f32[16,16,128]{2,1,0:T(8,128)S(1)}, u32[]{:S(2)}, u32[]{:S(2)}) collective-permute-start(f32[16,16,128]{2,1,0:T(8,128)S(1)} %face0.1), channel_id=1, source_target_pairs={{0,16},{16,0},{1,17},{17,1},{2,18},{18,2},{3,19},{19,3},{4,20},{20... | collective-permute-start | bytes 393224 | tf_op jit(solution)/shard_map/ppermute | solution.py:888
  12.5 1.4 %collective-permute-start.1 = (f32[16,16,128]{2,1,0:T(8,128)S(1)}, f32[16,16,128]{2,1,0:T(8,128)S(1)}, u32[]{:S(2)}, u32[]{:S(2)}) collective-permute-start(f32[16,16,128]{2,1,0:T(8,128)S(1)} %get-tuple-element.104), channel_id=1, source_target_pairs={{0,4},{4,0},{8,12},{12,8},{1,5},{5,1},{9,13},{13,9},{2,6},{6,2},{1... | collective-permute-start | bytes 393224 | tf_op jit(solution)/shard_map/ppermute | solution.py:888
  12.6 1.3 %collective-permute-start.2 = (f32[16,16,128]{2,1,0:T(8,128)S(1)}, f32[16,16,128]{2,1,0:T(8,128)S(1)}, u32[]{:S(2)}, u32[]{:S(2)}) collective-permute-start(f32[16,16,128]{2,1,0:T(8,128)S(1)} %get-tuple-element.105), channel_id=1, source_target_pairs={{4,8},{8,4},{5,9},{9,5},{6,10},{10,6},{7,11},{11,7},{20,24},{24,20... | collective-permute-start | bytes 393224 | tf_op jit(solution)/shard_map/ppermute | solution.py:888
  14.6 5.1 %copy-start.1 = (bf16[16,16,2,8,128]{4,3,2,1,0:T(8,128)(2,1)S(1)}, bf16[16,16,2,8,128]{4,3,2,1,0:T(8,128)(2,1)}, u32[]{:S(2)}) copy-start(bf16[16,16,2,8,128]{4,3,2,1,0:T(8,128)(2,1)} %param.7) | copy-start | bytes 3145732
  14.7 5.1 %copy-start.3 = (bf16[2,2,128,128]{3,2,1,0:T(8,128)(2,1)S(1)}, bf16[2,2,128,128]{3,2,1,0:T(8,128)(2,1)}, u32[]{:S(2)}) copy-start(bf16[2,2,128,128]{3,2,1,0:T(8,128)(2,1)} %edge_w.21) | copy-start | bytes 393220
  14.7 5.1 %copy-start.4 = (bf16[2,256,128]{2,1,0:T(8,128)(2,1)S(1)}, bf16[2,256,128]{2,1,0:T(8,128)(2,1)}, u32[]{:S(2)}) copy-start(bf16[2,256,128]{2,1,0:T(8,128)(2,1)} %node_in.19) | copy-start | bytes 393220
  14.7 5.1 %copy-start.6 = (bf16[2,128,128]{2,1,0:T(8,128)(2,1)S(1)}, bf16[2,128,128]{2,1,0:T(8,128)(2,1)}, u32[]{:S(2)}) copy-start(bf16[2,128,128]{2,1,0:T(8,128)(2,1)} %node_out.13) | copy-start | bytes 196612
  14.7 5.0 %collective-permute-start.3 = (f32[16,16,128]{2,1,0:T(8,128)S(1)}, f32[16,16,128]{2,1,0:T(8,128)S(1)}, u32[]{:S(2)}, u32[]{:S(2)}) collective-permute-start(f32[16,16,128]{2,1,0:T(8,128)S(1)} %get-tuple-element.111), channel_id=1, source_target_pairs={{0,1},{1,0},{2,3},{3,2},{4,5},{5,4},{6,7},{7,6},{8,9},{9,8},{10,11... | collective-permute-start | bytes 393224 | tf_op jit(solution)/shard_map/ppermute | solution.py:888
  16.3 3.4 %collective-permute-start.4 = (f32[16,16,128]{2,1,0:T(8,128)S(1)}, f32[16,16,128]{2,1,0:T(8,128)S(1)}, u32[]{:S(2)}, u32[]{:S(2)}) collective-permute-start(f32[16,16,128]{2,1,0:T(8,128)S(1)} %get-tuple-element.112), channel_id=1, source_target_pairs={{1,2},{2,1},{5,6},{6,5},{9,10},{10,9},{13,14},{14,13},{17,18},{18,... | collective-permute-start | bytes 393224 | tf_op jit(solution)/shard_map/ppermute | solution.py:888
  21.2 7.8 %collective-permute-start.5 = (f32[16,16,128]{2,1,0:T(8,128)S(1)}, f32[16,16,128]{2,1,0:T(8,128)S(1)}, u32[]{:S(2)}, u32[]{:S(2)}) collective-permute-start(f32[16,16,128]{2,1,0:T(8,128)S(1)} %face1.1), channel_id=1, source_target_pairs={{0,16},{16,0},{1,17},{17,1},{2,18},{18,2},{3,19},{19,3},{4,20},{20... | collective-permute-start | bytes 393224 | tf_op jit(solution)/shard_map/ppermute | solution.py:888
  29.6 6.1 %collective-permute-start.6 = (f32[16,16,128]{2,1,0:T(8,128)S(1)}, f32[16,16,128]{2,1,0:T(8,128)S(1)}, u32[]{:S(2)}, u32[]{:S(2)}) collective-permute-start(f32[16,16,128]{2,1,0:T(8,128)S(1)} %get-tuple-element.120), channel_id=1, source_target_pairs={{0,4},{4,0},{8,12},{12,8},{1,5},{5,1},{9,13},{13,9},{2,6},{6,2},{1... | collective-permute-start | bytes 393224 | tf_op jit(solution)/shard_map/ppermute | solution.py:888
  34.7 1.0 collective-permute-start.7
  36.3 7.5 %copy-start.5 = (bf16[16,16,2,8,128]{4,3,2,1,0:T(8,128)(2,1)S(1)}, bf16[16,16,2,8,128]{4,3,2,1,0:T(8,128)(2,1)}, u32[]{:S(2)}) copy-start(bf16[16,16,2,8,128]{4,3,2,1,0:T(8,128)(2,1)} %param.8) | copy-start | bytes 3145732
  36.3 7.4 %collective-permute-start.8 = (f32[16,16,128]{2,1,0:T(8,128)S(1)}, f32[16,16,128]{2,1,0:T(8,128)S(1)}, u32[]{:S(2)}, u32[]{:S(2)}) collective-permute-start(f32[16,16,128]{2,1,0:T(8,128)S(1)} %get-tuple-element.127), channel_id=1, source_target_pairs={{0,1},{1,0},{2,3},{3,2},{4,5},{5,4},{6,7},{7,6},{8,9},{9,8},{10,11... | collective-permute-start | bytes 393224 | tf_op jit(solution)/shard_map/ppermute | solution.py:888
  40.5 3.3 %collective-permute-start.9 = (f32[16,16,128]{2,1,0:T(8,128)S(1)}, f32[16,16,128]{2,1,0:T(8,128)S(1)}, u32[]{:S(2)}, u32[]{:S(2)}) collective-permute-start(f32[16,16,128]{2,1,0:T(8,128)S(1)} %get-tuple-element.128), channel_id=1, source_target_pairs={{1,2},{2,1},{5,6},{6,5},{9,10},{10,9},{13,14},{14,13},{17,18},{18,... | collective-permute-start | bytes 393224 | tf_op jit(solution)/shard_map/ppermute | solution.py:888
  45.0 5.0 %collective-permute-start.10 = (f32[16,16,128]{2,1,0:T(8,128)S(1)}, f32[16,16,128]{2,1,0:T(8,128)S(1)}, u32[]{:S(2)}, u32[]{:S(2)}) collective-permute-start(f32[16,16,128]{2,1,0:T(8,128)S(1)} %face2.1), channel_id=1, source_target_pairs={{0,16},{16,0},{1,17},{17,1},{2,18},{18,2},{3,19},{19,3},{4,20},{20... | collective-permute-start | bytes 393224 | tf_op jit(solution)/shard_map/ppermute | solution.py:888
  50.6 9.3 %collective-permute-start.11 = (f32[16,16,128]{2,1,0:T(8,128)S(1)}, f32[16,16,128]{2,1,0:T(8,128)S(1)}, u32[]{:S(2)}, u32[]{:S(2)}) collective-permute-start(f32[16,16,128]{2,1,0:T(8,128)S(1)} %get-tuple-element.135), channel_id=1, source_target_pairs={{4,8},{8,4},{5,9},{9,5},{6,10},{10,6},{7,11},{11,7},{20,24},{24,20... | collective-permute-start | bytes 393224 | tf_op jit(solution)/shard_map/ppermute | solution.py:888
  51.3 9.6 %collective-permute-start.12 = (f32[16,16,128]{2,1,0:T(8,128)S(1)}, f32[16,16,128]{2,1,0:T(8,128)S(1)}, u32[]{:S(2)}, u32[]{:S(2)}) collective-permute-start(f32[16,16,128]{2,1,0:T(8,128)S(1)} %get-tuple-element.136), channel_id=1, source_target_pairs={{0,4},{4,0},{8,12},{12,8},{1,5},{5,1},{9,13},{13,9},{2,6},{6,2},{1... | collective-permute-start | bytes 393224 | tf_op jit(solution)/shard_map/ppermute | solution.py:888
  61.6 7.3 %collective-permute-start.13 = (f32[16,16,128]{2,1,0:T(8,128)S(1)}, f32[16,16,128]{2,1,0:T(8,128)S(1)}, u32[]{:S(2)}, u32[]{:S(2)}) collective-permute-start(f32[16,16,128]{2,1,0:T(8,128)S(1)} %get-tuple-element.144), channel_id=1, source_target_pairs={{0,1},{1,0},{2,3},{3,2},{4,5},{5,4},{6,7},{7,6},{8,9},{9,8},{10,11... | collective-permute-start | bytes 393224 | tf_op jit(solution)/shard_map/ppermute | solution.py:888
  65.4 3.5 %collective-permute-start.14 = (f32[16,16,128]{2,1,0:T(8,128)S(1)}, f32[16,16,128]{2,1,0:T(8,128)S(1)}, u32[]{:S(2)}, u32[]{:S(2)}) collective-permute-start(f32[16,16,128]{2,1,0:T(8,128)S(1)} %get-tuple-element.145), channel_id=1, source_target_pairs={{1,2},{2,1},{5,6},{6,5},{9,10},{10,9},{13,14},{14,13},{17,18},{18,... | collective-permute-start | bytes 393224 | tf_op jit(solution)/shard_map/ppermute | solution.py:888
  70.1 8.0 %collective-permute-start.15 = (f32[16,16,128]{2,1,0:T(8,128)S(1)}, f32[16,16,128]{2,1,0:T(8,128)S(1)}, u32[]{:S(2)}, u32[]{:S(2)}) collective-permute-start(f32[16,16,128]{2,1,0:T(8,128)S(1)} %face3.1), channel_id=1, source_target_pairs={{0,16},{16,0},{1,17},{17,1},{2,18},{18,2},{3,19},{19,3},{4,20},{20... | collective-permute-start | bytes 393224 | tf_op jit(solution)/shard_map/ppermute | solution.py:888
  77.7 3.2 %collective-permute-start.18 = (f32[464,128]{1,0:T(8,128)S(1)}, f32[464,128]{1,0:T(8,128)S(1)}, u32[]{:S(2)}, u32[]{:S(2)}) collective-permute-start(f32[464,128]{1,0:T(8,128)S(1)} %get-tuple-element.172), channel_id=1, source_target_pairs={{0,4},{4,0},{8,12},{12,8},{1,5},{5,1},{9,13},{13,9},{2,6},{6,2},{1... | collective-permute-start | bytes 712712 | tf_op jit(solution)/shard_map/ppermute | solution.py:797
  78.7 1.4 %collective-permute-start.16 = (f32[16,16,128]{2,1,0:T(8,128)S(1)}, f32[16,16,128]{2,1,0:T(8,128)S(1)}, u32[]{:S(2)}, u32[]{:S(2)}) collective-permute-start(f32[16,16,128]{2,1,0:T(8,128)S(1)} %get-tuple-element.165), channel_id=1, source_target_pairs={{0,4},{4,0},{8,12},{12,8},{1,5},{5,1},{9,13},{13,9},{2,6},{6,2},{1... | collective-permute-start | bytes 393224 | tf_op jit(solution)/shard_map/ppermute | solution.py:888
  78.9 1.2 collective-permute-start.17
  80.9 6.9 %collective-permute-start.19 = (f32[16,16,128]{2,1,0:T(8,128)S(1)}, f32[16,16,128]{2,1,0:T(8,128)S(1)}, u32[]{:S(2)}, u32[]{:S(2)}) collective-permute-start(f32[16,16,128]{2,1,0:T(8,128)S(1)} %get-tuple-element.173), channel_id=1, source_target_pairs={{0,1},{1,0},{2,3},{3,2},{4,5},{5,4},{6,7},{7,6},{8,9},{9,8},{10,11... | collective-permute-start | bytes 393224 | tf_op jit(solution)/shard_map/ppermute | solution.py:888
  84.9 3.0 %collective-permute-start.20 = (f32[16,16,128]{2,1,0:T(8,128)S(1)}, f32[16,16,128]{2,1,0:T(8,128)S(1)}, u32[]{:S(2)}, u32[]{:S(2)}) collective-permute-start(f32[16,16,128]{2,1,0:T(8,128)S(1)} %get-tuple-element.174), channel_id=1, source_target_pairs={{1,2},{2,1},{5,6},{6,5},{9,10},{10,9},{13,14},{14,13},{17,18},{18,... | collective-permute-start | bytes 393224 | tf_op jit(solution)/shard_map/ppermute | solution.py:888
  86.1 5.7 %collective-permute-start.21 = (f32[232,128]{1,0:T(8,128)S(1)}, f32[232,128]{1,0:T(8,128)S(1)}, u32[]{:S(2)}, u32[]{:S(2)}) collective-permute-start(f32[232,128]{1,0:T(8,128)S(1)} %get-tuple-element.181), channel_id=1, source_target_pairs={{0,16},{16,0},{1,17},{17,1},{2,18},{18,2},{3,19},{19,3},{4,20},{20... | collective-permute-start | bytes 356360 | tf_op jit(solution)/shard_map/ppermute | solution.py:797
  92.4 9.5 %collective-permute-start.22 = (f32[368,128]{1,0:T(8,128)S(1)}, f32[368,128]{1,0:T(8,128)S(1)}, u32[]{:S(2)}, u32[]{:S(2)}) collective-permute-start(f32[368,128]{1,0:T(8,128)S(1)} %stack.17.refs_0_), channel_id=1, source_target_pairs={{0,1},{1,0},{2,3},{3,2},{4,5},{5,4},{6,7},{7,6},{8,9},{9,8},{10,11... | collective-permute-start | bytes 565256 | tf_op jit(solution)/shard_map/ppermute | solution.py:797
  96.5 6.5 %collective-permute-start.23 = (f32[368,128]{1,0:T(8,128)S(1)}, f32[368,128]{1,0:T(8,128)S(1)}, u32[]{:S(2)}, u32[]{:S(2)}) collective-permute-start(f32[368,128]{1,0:T(8,128)S(1)} %stack.17.refs_0_), channel_id=1, source_target_pairs={{0,2},{1,3},{2,0},{3,1},{4,6},{5,7},{6,4},{7,5},{8,10},{9,11},{10,... | collective-permute-start | bytes 565256 | tf_op jit(solution)/shard_map/ppermute | solution.py:797
  98.0 11.2 %collective-permute-start.24 = (f32[368,128]{1,0:T(8,128)S(1)}, f32[368,128]{1,0:T(8,128)S(1)}, u32[]{:S(2)}, u32[]{:S(2)}) collective-permute-start(f32[368,128]{1,0:T(8,128)S(1)} %stack.17.refs_0_), channel_id=1, source_target_pairs={{0,3},{1,2},{2,1},{3,0},{4,7},{5,6},{6,5},{7,4},{8,11},{9,10},{10,... | collective-permute-start | bytes 565256 | tf_op jit(solution)/shard_map/ppermute | solution.py:797
  109.8 11.8 %collective-permute-start.25 = (f32[368,128]{1,0:T(8,128)S(1)}, f32[368,128]{1,0:T(8,128)S(1)}, u32[]{:S(2)}, u32[]{:S(2)}) collective-permute-start(f32[368,128]{1,0:T(8,128)S(1)} %add.8.refs_0_), channel_id=1, source_target_pairs={{0,8},{4,12},{8,0},{12,4},{1,9},{5,13},{9,1},{13,5},{2,10},{6,14},... | collective-permute-start | bytes 565256 | tf_op jit(solution)/shard_map/ppermute | solution.py:797
  122.2 6.8 %collective-permute-start.26 = (f32[368,128]{1,0:T(8,128)S(1)}, f32[368,128]{1,0:T(8,128)S(1)}, u32[]{:S(2)}, u32[]{:S(2)}) collective-permute-start(f32[368,128]{1,0:T(8,128)S(1)} %add.9.value), channel_id=1, source_target_pairs={{0,16},{16,0},{1,17},{17,1},{2,18},{18,2},{3,19},{19,3},{4,20},{20... | collective-permute-start | bytes 565256 | tf_op jit(solution)/shard_map/ppermute | solution.py:797
  129.6 1.7 %collective-permute-start.27 = (f32[600,128]{1,0:T(8,128)S(1)}, f32[600,128]{1,0:T(8,128)S(1)}, u32[]{:S(2)}, u32[]{:S(2)}) collective-permute-start(f32[600,128]{1,0:T(8,128)S(1)} %join.1.value), channel_id=1, source_target_pairs={{0,4},{4,0},{8,12},{12,8},{1,5},{5,1},{9,13},{13,9},{2,6},{6,2},{1... | collective-permute-start | bytes 921608 | tf_op jit(solution)/shard_map/ppermute | solution.py:797

commit v7 on v6

--- a/solution.py
+++ b/solution.py
@@ -169,6 +169,19 @@
     return jnp.where((sc_ref[1 + axis] + kind) % 2 == 0, last, 0)
 
 
+class Trades(tuple):
+    sizes = ()
+
+
+def from_partner(sc_ref, counts, axis, kind, value):
+    size = counts.sizes[axis]
+    if kind == 0 and size % 2 == 0:
+        return value
+    at = sc_ref[1 + axis]
+    partner = at + jnp.where((at + kind) % 2 == 0, 1, -1)
+    return jnp.where((partner >= 0) & (partner < size), value, 0.0)
+
+
 def end_rows(values, filled, take_top):
     picked = values(0)
     slots = values.slots
@@ -210,11 +223,13 @@
 
     lax.fori_loop(0, x_len, copy, 0)
     for kind in range(nx):
-        into_ref[face_place(sc_ref, 0, kind, x_len - 1)] += halo[kind][...]
+        got = from_partner(sc_ref, counts, 0, kind, halo[kind][...])
+        into_ref[face_place(sc_ref, 0, kind, x_len - 1)] += got
     for kind in range(ny):
-        into_ref[:, face_place(sc_ref, 1, kind, y_len - 1)] += halo[nx + kind][...]
+        got = from_partner(sc_ref, counts, 1, kind, halo[nx + kind][...])
+        into_ref[:, face_place(sc_ref, 1, kind, y_len - 1)] += got
     if nz:
-        got = [halo[nx + ny + kind][...] for kind in range(nz)]
+        got = [from_partner(sc_ref, counts, 2, kind, halo[nx + ny + kind][...]) for kind in range(nz)]
         tops = [takes_top(sc_ref, kind) for kind in range(nz)]
         from_below = sum(jnp.where(top, 0.0, value) for top, value in zip(tops, got))
         from_above = sum(jnp.where(top, value, 0.0) for top, value in zip(tops, got))
@@ -233,7 +248,8 @@
         place = face_place(sc_ref, 0, kind, x_len - 1)
         for k in range(ny):
             y_len = got[kind].shape[0]
-            outs[k][place] += got[kind][face_place(sc_ref, 1, k, y_len - 1)]
+            line = got[kind][face_place(sc_ref, 1, k, y_len - 1)]
+            outs[k][place] += from_partner(sc_ref, counts, 0, kind, line)
 
 
 def fix_z_kernel(counts, sc_ref, *refs):
@@ -249,11 +265,12 @@
         for kind in range(nx):
             ref = got_x[kind]
             reader = RowReader(ref.shape[1] // NODES, lambda row, ref=ref: ref[:, row])
-            outs[k][face_place(sc_ref, 0, kind, x_len - 1)] += end_rows(reader, sc_ref[0], top)
+            line = from_partner(sc_ref, counts, 0, kind, end_rows(reader, sc_ref[0], top))
+            outs[k][face_place(sc_ref, 0, kind, x_len - 1)] += line
         for kind in range(ny):
             ref = got_y[kind]
             reader = RowReader(ref.shape[1] // NODES, lambda row, ref=ref: ref[:, row])
-            add = end_rows(reader, sc_ref[0], top)
+            add = from_partner(sc_ref, counts, 1, kind, end_rows(reader, sc_ref[0], top))
             first = face_place(sc_ref, 1, kind, 1) == 0
             outs[k][:, 0] += jnp.where(first, add, 0.0)
             outs[k][:, y_len - 1] += jnp.where(first, 0.0, add)
@@ -383,12 +400,13 @@
     nx, ny, nz = counts
     for c in range(2):
         into_ref[c] = from_ref[start + c]
-    into_ref[face_place(sc_ref, 0, kind, x_len - 1) - start] += halo[kind][...]
+    into_ref[face_place(sc_ref, 0, kind, x_len - 1) - start] += from_partner(sc_ref, counts, 0, kind, halo[kind][...])
     for c in range(2):
         for k in range(ny):
-            into_ref[c, face_place(sc_ref, 1, k, y_len - 1)] += halo[nx + k][start + c]
+            got = from_partner(sc_ref, counts, 1, k, halo[nx + k][start + c])
+            into_ref[c, face_place(sc_ref, 1, k, y_len - 1)] += got
         for k in range(nz):
-            got = halo[nx + ny + k][start + c]
+            got = from_partner(sc_ref, counts, 2, k, halo[nx + ny + k][start + c])
             top = takes_top(sc_ref, k)
             into_ref[c, :, 0] += jnp.where(top, 0.0, got)
             for s in range(rows // NODES):
@@ -724,9 +742,9 @@
 
 
 def pairs(size, kind):
-    return [
-        pair for low in range(kind, size - 1, 2) for pair in ((low, low + 1), (low + 1, low))
-    ]
+    matched = [pair for low in range(kind, size - 1, 2) for pair in ((low, low + 1), (low + 1, low))]
+    alone = set(range(size)) - {source for source, target in matched}
+    return matched + [(i, i) for i in sorted(alone)]
 
 
 def hops(size):
@@ -739,13 +757,12 @@
 
 
 def halving_steps(sizes):
-    return [(1, hop) for hop in hops(sizes[1])[:1]] + [(0, hop) for hop in hops(sizes[0])]
+    return [(1, hop) for hop in hops(sizes[1])] + [(0, hop) for hop in hops(sizes[0])]
 
 
 def whole_steps(sizes):
     along_z = hops(sizes[2])
-    steps = [(2, along_z[k : k + 2]) for k in range(0, len(along_z), 2)]
-    return steps + [(1, [hop]) for hop in hops(sizes[1])[1:]]
+    return [(2, along_z[k : k + 2]) for k in range(0, len(along_z), 2)]
 
 
 def padded_rows(rows, sizes):
@@ -858,7 +875,8 @@
     grid = (x_len, y_len, rows, width)
     axes = ("gx", "gy", "gz")
     sizes = tuple(lax.axis_size(a) for a in axes)
-    trades = tuple(min(size - 1, 2) for size in sizes)
+    trades = Trades(min(size - 1, 2) for size in sizes)
+    trades.sizes = sizes
     nx, ny, nz = trades
     h0 = state.reshape(grid)
     g2 = cotangent.reshape(grid)

time: 134 us -> 135 us (level)
    ppermute x8 -> x9, waiting for transfers between devices: 19.7 us -> 21.5 us  [swap(): lax.ppermute(value, axis, [(i, i ^ step[1]) for i in range(lax.axis_size(...]
    pallas_call x27 -> x28, Pallas kernels: 48.4 us -> 49.1 us  [call(): pl.pallas_call(kernel, name=name, out_shape=tuple(outs), in_specs=[SM] +...]
    ppermute x8 -> x9, starting transfers between devices: 16.6 us -> 16.3 us  [swap(): lax.ppermute(value, axis, [(i, i ^ step[1]) for i in range(lax.axis_size(...]
  transfers between devices with their start and end apart: 28 -> 29, of which waited for: 13 -> 12; matrix products, arithmetic and copies ran while one was open for 0% -> 0% of each run, Pallas kernels for 27% -> 27%
where the time goes in v7:
time: 135 us
  starting transfers between devices  55.4 us (41%)
  Pallas kernels  49.1 us (36%)
  waiting for transfers between devices  25.6 us (19%)
  local copies, waits for them, and re-layouts  2.84 us (2%)
  between operations  1.66 us (1%)
    pallas_call x28, Pallas kernels, call(): pl.pallas_call(kernel, name=name, out_shape=tuple(outs), in_specs=[SM] +...  49.1 us
    ppermute x20, starting transfers between devices, trade(): lax.ppermute(face, axis, pairs(size, kind))  39.1 us
    ppermute x9, waiting for transfers between devices, swap(): lax.ppermute(value, axis, [(i, i ^ step[1]) for i in range(lax.axis_size(...  21.5 us
    ppermute x9, starting transfers between devices, swap(): lax.ppermute(value, axis, [(i, i ^ step[1]) for i in range(lax.axis_size(...  16.3 us
    ppermute x20, waiting for transfers between devices, trade(): lax.ppermute(face, axis, pairs(size, kind))  4.14 us
    unnamed x16, local copies, waits for them, and re-layouts  2.84 us
  transfers between devices with their start and end apart: 29, of which 12 were waited for; matrix products, arithmetic and copies ran while one was open for 0% of the time, Pallas kernels for 27%

profile of v7, /device:TPU:0, one launch (start us, length us, event | category | flops | bytes accessed | tf_op | source)
XLA Modules:
  0.0 134.7 jit_solution(1209161076284915355)
XLA Ops:
  1.4 1.2 copy-done
  2.6 0.9 copy-done.2
  3.5 0.7 copy-done.7
  4.2 0.8 face0.1
  5.0 3.0 %collective-permute-start = (f32[16,16,128]{2,1,0:T(8,128)S(1)}, f32[16,16,128]{2,1,0:T(8,128)S(1)}, u32[]{:S(2)}, u32[]{:S(2)}) collective-permute-start(f32[16,16,128]{2,1,0:T(8,128)S(1)} %face0.1), channel_id=1, source_target_pairs={{0,16},{16,0},{1,17},{17,1},{2,18},{18,2},{3,19},{19,3},{4,20},{20... | collective-permute-start | bytes 393224 | tf_op jit(solution)/shard_map/ppermute | solution.py:906
  8.0 4.0 %edges0.1 = (f32[16,16,16,128]{3,2,1,0:T(8,128)S(1)}, f32[3,16,16,16,128]{4,3,2,1,0:T(8,128)S(1)}, f32[16,16,128]{2,1,0:T(8,128)S(1)}, f32[16,16,128]{2,1,0:T(8,...) custom-call(s32[4]{0:T(128)S(1)} %pad_add_fusion.sc.sc_ref, bf16[2,2,128,128]{3,2,1,0:T(8,128)(2,1)S(1)} %copy-done.2, ...), custom_call_target="tpu_custom_call" | custom-call | flops 402653184 | bytes 10094608 | tf_op jit(solution)/shard_map/edges0/pallas_call | solution.py:731
  12.6 0.7 collective-permute-start.2
  13.3 0.7 collective-permute-done.1.refs_2_.refs_1_
  14.0 0.7 fix_z.4
  14.7 1.6 %collective-permute-start.3 = (f32[16,16,128]{2,1,0:T(8,128)S(1)}, f32[16,16,128]{2,1,0:T(8,128)S(1)}, u32[]{:S(2)}, u32[]{:S(2)}) collective-permute-start(f32[16,16,128]{2,1,0:T(8,128)S(1)} %get-tuple-element.111), channel_id=1, source_target_pairs={{0,1},{1,0},{2,3},{3,2},{4,5},{5,4},{6,7},{7,6},{8,9},{9,8},{10,11... | collective-permute-start | bytes 393224 | tf_op jit(solution)/shard_map/ppermute | solution.py:906
  16.3 0.7 collective-permute-start.4
  17.0 2.6 %slopes.2 = f32[3,16,16,16,128]{4,3,2,1,0:T(8,128)S(1)} custom-call(s32[4]{0:T(128)S(1)} %pad_add_fusion.sc.sc_ref, f32[3,16,16,16,128]{4,3,2,1,0:T(8,128)S(1)} %get-tuple-element.113.half_in), custom_call_target="tpu_custom_call", output_to_operand_aliasing={{}: (1, {})} | custom-call | flops 134217728 | bytes 12582928 | tf_op jit(solution)/shard_map/slopes/pallas_call | solution.py:731
  19.8 1.4 %face1.1 = f32[16,16,128]{2,1,0:T(8,128)S(1)} custom-call(s32[4]{0:T(128)S(1)} %pad_add_fusion.sc.sc_ref, bf16[2,2,128,128]{3,2,1,0:T(8,128)(2,1)S(1)} %copy-done.3, bf16[2,256,128]{2,1,0:T(8,128)(2,1)S(1)} %copy-done.4, bf16[2,128,128]{2,1,0:T(8,128)(2,1)S(1)} %copy-done.6, f32[2,2,128]{2,1,0:T(2,128)S(1)} %copy-done.7, ...), custom_call_target="tpu_custom_call" | custom-call | flops 33554432 | bytes 4261904 | tf_op jit(solution)/shard_map/face1/pallas_call | solution.py:731
  21.2 1.3 collective-permute-start.5
  22.5 6.4 %nodes0_edges1.1 = (bf16[16,16,16,128]{3,2,1,0:T(8,128)(2,1)S(1)}, bf16[16,16,16,128]{3,2,1,0:T(8,128)(2,1)S(1)}, f32[16,16,16,128]{3,2,1,0:T(8,128)S(1)}, bf16[...) custom-call(s32[4]{0:T(128)S(1)} %pad_add_fusion.sc.sc_ref, ...), custom_call_target="tpu_custom_call" | custom-call | flops 1073741824 | bytes 18286608 | tf_op jit(solution)/shard_map/nodes0_edges1/pallas_call | solution.py:731
  29.6 5.1 %collective-permute-start.6 = (f32[16,16,128]{2,1,0:T(8,128)S(1)}, f32[16,16,128]{2,1,0:T(8,128)S(1)}, u32[]{:S(2)}, u32[]{:S(2)}) collective-permute-start(f32[16,16,128]{2,1,0:T(8,128)S(1)} %get-tuple-element.120), channel_id=1, source_target_pairs={{0,4},{4,0},{8,12},{12,8},{1,5},{5,1},{9,13},{13,9},{2,6},{6,2},{1... | collective-permute-start | bytes 393224 | tf_op jit(solution)/shard_map/ppermute | solution.py:906
  35.7 0.7 fix_z.5
  36.4 4.2 %collective-permute-start.8 = (f32[16,16,128]{2,1,0:T(8,128)S(1)}, f32[16,16,128]{2,1,0:T(8,128)S(1)}, u32[]{:S(2)}, u32[]{:S(2)}) collective-permute-start(f32[16,16,128]{2,1,0:T(8,128)S(1)} %get-tuple-element.127), channel_id=1, source_target_pairs={{0,1},{1,0},{2,3},{3,2},{4,5},{5,4},{6,7},{7,6},{8,9},{9,8},{10,11... | collective-permute-start | bytes 393224 | tf_op jit(solution)/shard_map/ppermute | solution.py:906
  41.2 2.6 %slopes.3 = f32[3,16,16,16,128]{4,3,2,1,0:T(8,128)S(1)} custom-call(s32[4]{0:T(128)S(1)} %pad_add_fusion.sc.sc_ref, f32[3,16,16,16,128]{4,3,2,1,0:T(8,128)S(1)} %get-tuple-element.129.half_in), custom_call_target="tpu_custom_call", output_to_operand_aliasing={{}: (1, {})} | custom-call | flops 134217728 | bytes 12582928 | tf_op jit(solution)/shard_map/slopes/pallas_call | solution.py:731
  43.8 1.2 face2.1
  45.0 0.8 collective-permute-start.10
  45.8 3.8 %nodes1_back.1 = (bf16[16,16,16,128]{3,2,1,0:T(8,128)(2,1)S(1)}, bf16[16,16,16,128]{3,2,1,0:T(8,128)(2,1)S(1)}, bf16[16,16,16,128]{3,2,1,0:T(8,128)(2,1)S(1)}, f...) custom-call(s32[4]{0:T(128)S(1)} %pad_add_fusion.sc.sc_ref, ...), custom_call_target="tpu_custom_call" | custom-call | flops 939524096 | bytes 10946576 | tf_op jit(solution)/shard_map/nodes1_back/pallas_call | solution.py:731
  50.6 0.7 collective-permute-start.11
  51.3 8.6 %collective-permute-start.12 = (f32[16,16,128]{2,1,0:T(8,128)S(1)}, f32[16,16,128]{2,1,0:T(8,128)S(1)}, u32[]{:S(2)}, u32[]{:S(2)}) collective-permute-start(f32[16,16,128]{2,1,0:T(8,128)S(1)} %get-tuple-element.136), channel_id=1, source_target_pairs={{0,4},{4,0},{8,12},{12,8},{1,5},{5,1},{9,13},{13,9},{2,6},{6,2},{1... | collective-permute-start | bytes 393224 | tf_op jit(solution)/shard_map/ppermute | solution.py:906
  59.9 1.0 collective-permute-done.12.refs_2_.refs_1_
  60.9 0.7 fix_z.6
  61.6 3.8 %collective-permute-start.13 = (f32[16,16,128]{2,1,0:T(8,128)S(1)}, f32[16,16,128]{2,1,0:T(8,128)S(1)}, u32[]{:S(2)}, u32[]{:S(2)}) collective-permute-start(f32[16,16,128]{2,1,0:T(8,128)S(1)} %get-tuple-element.144), channel_id=1, source_target_pairs={{0,1},{1,0},{2,3},{3,2},{4,5},{5,4},{6,7},{7,6},{8,9},{9,8},{10,11... | collective-permute-start | bytes 393224 | tf_op jit(solution)/shard_map/ppermute | solution.py:906
  65.4 0.8 collective-permute-start.14
  66.2 1.6 %nodes1_products.1 = (f32[16,16,16,128]{3,2,1,0:T(8,128)S(1)}, f32[392,128]{1,0:T(8,128)S(1)}) custom-call(s32[4]{0:T(128)S(1)} %pad_add_fusion.sc.sc_ref, bf16[2,256,128]{2,1,0:T(8,128)(2,1)S(1)} %copy-done.4, bf16[16,16,16,128]{3,2,1,0:T(8,128)(2,1)S(1)} %get-tuple-element.146.h, bf16[16,16,16,128]{3,2,1,0:T(8,128)(2,1)S(1)} %bitcast.14, ...), custom_call_target="tpu_custom_call" | custom-call | flops 805306368 | bytes 7671824 | tf_op jit(solution)/shard_map/nodes1_products/pallas_call | solution.py:731
  67.9 1.0 collective-permute-done.13.refs_3_
  68.9 1.3 face3.1
  70.2 0.9 collective-permute-start.15
  71.1 6.7 %edges1_back_nodes0_back.1 = (bf16[16,16,16,128]{3,2,1,0:T(8,128)(2,1)S(1)}, bf16[16,16,16,128]{3,2,1,0:T(8,128)(2,1)S(1)}, f32[16,16,16,128]{3,2,1,0:T(8,128)S(...) custom-call(s32[4]{0:T(128)S(1)} %pad_add_fusion.sc.sc_ref, ...), custom_call_target="tpu_custom_call" | custom-call | flops 1610612736 | bytes 23173136 | tf_op jit(solution)/shard_map/edges1_back_nodes0_back/pallas_call | solution.py:731
  80.2 0.7 fix_z.7
  80.9 4.0 %collective-permute-start.19 = (f32[16,16,128]{2,1,0:T(8,128)S(1)}, f32[16,16,128]{2,1,0:T(8,128)S(1)}, u32[]{:S(2)}, u32[]{:S(2)}) collective-permute-start(f32[16,16,128]{2,1,0:T(8,128)S(1)} %get-tuple-element.173), channel_id=1, source_target_pairs={{0,1},{1,0},{2,3},{3,2},{4,5},{5,4},{6,7},{7,6},{8,9},{9,8},{10,11... | collective-permute-start | bytes 393224 | tf_op jit(solution)/shard_map/ppermute | solution.py:906
  86.2 7.8 %collective-permute-start.21 = (f32[240,128]{1,0:T(8,128)S(1)}, f32[240,128]{1,0:T(8,128)S(1)}, u32[]{:S(2)}, u32[]{:S(2)}) collective-permute-start(f32[240,128]{1,0:T(8,128)S(1)} %get-tuple-element.181), channel_id=1, source_target_pairs={{0,8},{4,12},{8,0},{12,4},{1,9},{5,13},{9,1},{13,5},{2,10},{6,14},... | collective-permute-start | bytes 368648 | tf_op jit(solution)/shard_map/ppermute | solution.py:814
  94.0 3.3 %collective-permute-done.21.got = f32[240,128]{1,0:T(8,128)S(1)} collective-permute-done((f32[240,128]{1,0:T(8,128)S(1)}, f32[240,128]{1,0:T(8,128)S(1)}, u32[]{:S(2)}, u32[]{:S(2)}) %collective-permute-start.21) | collective-permute-done | bytes 122912 | tf_op jit(solution)/shard_map/ppermute | solution.py:814
  97.9 1.2 collective-permute-start.22
  99.1 4.1 %edges0_back.1 = (f32[16,16,16,128]{3,2,1,0:T(8,128)S(1)}, f32[136,128]{1,0:T(8,128)S(1)}) custom-call(s32[4]{0:T(128)S(1)} %pad_add_fusion.sc.sc_ref, bf16[2,2,128,128]{3,2,1,0:T(8,128)(2,1)S(1)} %copy-done.3, bf16[2,256,128]{2,1,0:T(8,128)(2,1)S(1)} %copy-done.4, bf16[2,128,128]{2,1,0:T(8,128)(2,1)S(1)} %copy-done.6, f32[2,2,128]{2,1,0:T(2,128)S(1)} %copy-done.7, ...), custom_call_target="tpu_custom_call" | custom-call | flops 805306368 | bytes 12589072 | tf_op jit(solution)/shard_map/edges0_back/pallas_call | solution.py:731
  103.7 3.3 %collective-permute-start.23 = (f32[256,128]{1,0:T(8,128)S(1)}, f32[256,128]{1,0:T(8,128)S(1)}, u32[]{:S(2)}, u32[]{:S(2)}) collective-permute-start(f32[256,128]{1,0:T(8,128)S(1)} %stack.17.refs_0_), channel_id=1, source_target_pairs={{0,1},{1,0},{2,3},{3,2},{4,5},{5,4},{6,7},{7,6},{8,9},{9,8},{10,11... | collective-permute-start | bytes 393224 | tf_op jit(solution)/shard_map/ppermute | solution.py:814
  107.3 2.2 %collective-permute-start.25 = (f32[256,128]{1,0:T(8,128)S(1)}, f32[256,128]{1,0:T(8,128)S(1)}, u32[]{:S(2)}, u32[]{:S(2)}) collective-permute-start(f32[256,128]{1,0:T(8,128)S(1)} %stack.17.refs_0_), channel_id=1, source_target_pairs={{0,3},{1,2},{2,1},{3,0},{4,7},{5,6},{6,5},{7,4},{8,11},{9,10},{10,... | collective-permute-start | bytes 393224 | tf_op jit(solution)/shard_map/ppermute | solution.py:814
  109.5 2.5 %state_grad.1 = bf16[16,16,16,128]{3,2,1,0:T(8,128)(2,1)} custom-call(s32[4]{0:T(128)S(1)} %pad_add_fusion.sc.sc_ref, bf16[2,2,128,128]{3,2,1,0:T(8,128)(2,1)S(1)} %copy-done.3, bf16[2,256,128]{2,1,0:T(8,128)(2,1)S(1)} %copy-done.4, bf16[16,16,16,128]{3,2,1,0:T(8,128)(2,1)S(1)} %get-tuple-element.188.grad_in, ...), custom_call_target="tpu_custom_call" | custom-call | flops 536870912 | bytes 5505040 | tf_op jit(solution)/shard_map/state_grad/pallas_call | solution.py:731
  112.1 6.8 %collective-permute-done.24.refs_2_ = f32[256,128]{1,0:T(8,128)S(1)} collective-permute-done((f32[256,128]{1,0:T(8,128)S(1)}, f32[256,128]{1,0:T(8,128)S(1)}, u32[]{:S(2)}, u32[]{:S(2)}) %collective-permute-start.24) | collective-permute-done | bytes 131104 | tf_op jit(solution)/shard_map/ppermute | solution.py:814
  119.5 0.9 collective-permute-start.26
  120.4 4.1 %collective-permute-done.26.got = f32[256,128]{1,0:T(8,128)S(1)} collective-permute-done((f32[256,128]{1,0:T(8,128)S(1)}, f32[256,128]{1,0:T(8,128)S(1)}, u32[]{:S(2)}, u32[]{:S(2)}) %collective-permute-start.26) | collective-permute-done | bytes 131104 | tf_op jit(solution)/shard_map/ppermute | solution.py:814
  125.1 5.6 %collective-permute-done.27.got = f32[376,128]{1,0:T(8,128)S(1)} collective-permute-done((f32[376,128]{1,0:T(8,128)S(1)}, f32[376,128]{1,0:T(8,128)S(1)}, u32[]{:S(2)}, u32[]{:S(2)}) %collective-permute-start.27) | collective-permute-done | bytes 192544 | tf_op jit(solution)/shard_map/ppermute | solution.py:814
  131.4 1.6 %collective-permute-done.28.got = f32[616,128]{1,0:T(8,128)S(1)} collective-permute-done((f32[616,128]{1,0:T(8,128)S(1)}, f32[616,128]{1,0:T(8,128)S(1)}, u32[]{:S(2)}, u32[]{:S(2)}) %collective-permute-start.28) | collective-permute-done | bytes 315424 | tf_op jit(solution)/shard_map/ppermute | solution.py:814
  133.0 1.7 %finish.1 = (f32[2,2,128,128]{3,2,1,0:T(8,128)}, f32[2,256,128]{2,1,0:T(8,128)}, f32[2,128,128]{2,1,0:T(8,128)}, f32[2,2,128]{2,1,0:T(2,128)}) custom-call(s32[4]{0:T(128)S(1)} %pad_add_fusion.sc.sc_ref, bf16[2,2,128,128]{3,2,1,0:T(8,128)(2,1)S(1)} %copy-done.3, bf16[2,256,128]{2,1,0:T(8,128)(2,1)S(1)} %copy-done.4, f32[616,128]{1,0:T(8,128)S(1)} %join.3.value, ...), custom_call_target="tpu_custom_call" | custom-call | bytes 1550352 | tf_op jit(solution)/shard_map/finish/pallas_call | solution.py:731
  (55 shorter events, 11.0 us)
Async XLA Ops:
  1.4 1.2 copy-start
  2.6 0.9 copy-start.2
  3.5 0.7 copy-start.7
  5.0 7.0 %collective-permute-start = (f32[16,16,128]{2,1,0:T(8,128)S(1)}, f32[16,16,128]{2,1,0:T(8,128)S(1)}, u32[]{:S(2)}, u32[]{:S(2)}) collective-permute-start(f32[16,16,128]{2,1,0:T(8,128)S(1)} %face0.1), channel_id=1, source_target_pairs={{0,16},{16,0},{1,17},{17,1},{2,18},{18,2},{3,19},{19,3},{4,20},{20... | collective-permute-start | bytes 393224 | tf_op jit(solution)/shard_map/ppermute | solution.py:906
  12.5 1.4 %collective-permute-start.1 = (f32[16,16,128]{2,1,0:T(8,128)S(1)}, f32[16,16,128]{2,1,0:T(8,128)S(1)}, u32[]{:S(2)}, u32[]{:S(2)}) collective-permute-start(f32[16,16,128]{2,1,0:T(8,128)S(1)} %get-tuple-element.104), channel_id=1, source_target_pairs={{0,4},{4,0},{8,12},{12,8},{1,5},{5,1},{9,13},{13,9},{2,6},{6,2},{1... | collective-permute-start | bytes 393224 | tf_op jit(solution)/shard_map/ppermute | solution.py:906
  12.6 1.3 collective-permute-start.2
  14.6 5.1 %copy-start.1 = (bf16[16,16,2,8,128]{4,3,2,1,0:T(8,128)(2,1)S(1)}, bf16[16,16,2,8,128]{4,3,2,1,0:T(8,128)(2,1)}, u32[]{:S(2)}) copy-start(bf16[16,16,2,8,128]{4,3,2,1,0:T(8,128)(2,1)} %param.7) | copy-start | bytes 3145732
  14.7 5.1 %copy-start.3 = (bf16[2,2,128,128]{3,2,1,0:T(8,128)(2,1)S(1)}, bf16[2,2,128,128]{3,2,1,0:T(8,128)(2,1)}, u32[]{:S(2)}) copy-start(bf16[2,2,128,128]{3,2,1,0:T(8,128)(2,1)} %edge_w.21) | copy-start | bytes 393220
  14.7 5.1 %copy-start.4 = (bf16[2,256,128]{2,1,0:T(8,128)(2,1)S(1)}, bf16[2,256,128]{2,1,0:T(8,128)(2,1)}, u32[]{:S(2)}) copy-start(bf16[2,256,128]{2,1,0:T(8,128)(2,1)} %node_in.19) | copy-start | bytes 393220
  14.7 5.1 %copy-start.6 = (bf16[2,128,128]{2,1,0:T(8,128)(2,1)S(1)}, bf16[2,128,128]{2,1,0:T(8,128)(2,1)}, u32[]{:S(2)}) copy-start(bf16[2,128,128]{2,1,0:T(8,128)(2,1)} %node_out.13) | copy-start | bytes 196612
  14.7 5.0 %collective-permute-start.3 = (f32[16,16,128]{2,1,0:T(8,128)S(1)}, f32[16,16,128]{2,1,0:T(8,128)S(1)}, u32[]{:S(2)}, u32[]{:S(2)}) collective-permute-start(f32[16,16,128]{2,1,0:T(8,128)S(1)} %get-tuple-element.111), channel_id=1, source_target_pairs={{0,1},{1,0},{2,3},{3,2},{4,5},{5,4},{6,7},{7,6},{8,9},{9,8},{10,11... | collective-permute-start | bytes 393224 | tf_op jit(solution)/shard_map/ppermute | solution.py:906
  16.3 3.4 %collective-permute-start.4 = (f32[16,16,128]{2,1,0:T(8,128)S(1)}, f32[16,16,128]{2,1,0:T(8,128)S(1)}, u32[]{:S(2)}, u32[]{:S(2)}) collective-permute-start(f32[16,16,128]{2,1,0:T(8,128)S(1)} %get-tuple-element.112), channel_id=1, source_target_pairs={{1,2},{2,1},{0,0},{3,3},{5,6},{6,5},{4,4},{7,7},{9,10},{10,9},{8,8... | collective-permute-start | bytes 393224 | tf_op jit(solution)/shard_map/ppermute | solution.py:906
  21.2 7.8 %collective-permute-start.5 = (f32[16,16,128]{2,1,0:T(8,128)S(1)}, f32[16,16,128]{2,1,0:T(8,128)S(1)}, u32[]{:S(2)}, u32[]{:S(2)}) collective-permute-start(f32[16,16,128]{2,1,0:T(8,128)S(1)} %face1.1), channel_id=1, source_target_pairs={{0,16},{16,0},{1,17},{17,1},{2,18},{18,2},{3,19},{19,3},{4,20},{20... | collective-permute-start | bytes 393224 | tf_op jit(solution)/shard_map/ppermute | solution.py:906
  29.6 6.1 %collective-permute-start.6 = (f32[16,16,128]{2,1,0:T(8,128)S(1)}, f32[16,16,128]{2,1,0:T(8,128)S(1)}, u32[]{:S(2)}, u32[]{:S(2)}) collective-permute-start(f32[16,16,128]{2,1,0:T(8,128)S(1)} %get-tuple-element.120), channel_id=1, source_target_pairs={{0,4},{4,0},{8,12},{12,8},{1,5},{5,1},{9,13},{13,9},{2,6},{6,2},{1... | collective-permute-start | bytes 393224 | tf_op jit(solution)/shard_map/ppermute | solution.py:906
  34.7 1.0 collective-permute-start.7
  36.4 7.5 %copy-start.5 = (bf16[16,16,2,8,128]{4,3,2,1,0:T(8,128)(2,1)S(1)}, bf16[16,16,2,8,128]{4,3,2,1,0:T(8,128)(2,1)}, u32[]{:S(2)}) copy-start(bf16[16,16,2,8,128]{4,3,2,1,0:T(8,128)(2,1)} %param.8) | copy-start | bytes 3145732
  36.4 7.4 %collective-permute-start.8 = (f32[16,16,128]{2,1,0:T(8,128)S(1)}, f32[16,16,128]{2,1,0:T(8,128)S(1)}, u32[]{:S(2)}, u32[]{:S(2)}) collective-permute-start(f32[16,16,128]{2,1,0:T(8,128)S(1)} %get-tuple-element.127), channel_id=1, source_target_pairs={{0,1},{1,0},{2,3},{3,2},{4,5},{5,4},{6,7},{7,6},{8,9},{9,8},{10,11... | collective-permute-start | bytes 393224 | tf_op jit(solution)/shard_map/ppermute | solution.py:906
  40.5 3.3 %collective-permute-start.9 = (f32[16,16,128]{2,1,0:T(8,128)S(1)}, f32[16,16,128]{2,1,0:T(8,128)S(1)}, u32[]{:S(2)}, u32[]{:S(2)}) collective-permute-start(f32[16,16,128]{2,1,0:T(8,128)S(1)} %get-tuple-element.128), channel_id=1, source_target_pairs={{1,2},{2,1},{0,0},{3,3},{5,6},{6,5},{4,4},{7,7},{9,10},{10,9},{8,8... | collective-permute-start | bytes 393224 | tf_op jit(solution)/shard_map/ppermute | solution.py:906
  45.0 5.0 %collective-permute-start.10 = (f32[16,16,128]{2,1,0:T(8,128)S(1)}, f32[16,16,128]{2,1,0:T(8,128)S(1)}, u32[]{:S(2)}, u32[]{:S(2)}) collective-permute-start(f32[16,16,128]{2,1,0:T(8,128)S(1)} %face2.1), channel_id=1, source_target_pairs={{0,16},{16,0},{1,17},{17,1},{2,18},{18,2},{3,19},{19,3},{4,20},{20... | collective-permute-start | bytes 393224 | tf_op jit(solution)/shard_map/ppermute | solution.py:906
  50.6 9.3 %collective-permute-start.11 = (f32[16,16,128]{2,1,0:T(8,128)S(1)}, f32[16,16,128]{2,1,0:T(8,128)S(1)}, u32[]{:S(2)}, u32[]{:S(2)}) collective-permute-start(f32[16,16,128]{2,1,0:T(8,128)S(1)} %get-tuple-element.135), channel_id=1, source_target_pairs={{4,8},{8,4},{0,0},{12,12},{5,9},{9,5},{1,1},{13,13},{6,10},{10,6},... | collective-permute-start | bytes 393224 | tf_op jit(solution)/shard_map/ppermute | solution.py:906
  51.3 9.6 %collective-permute-start.12 = (f32[16,16,128]{2,1,0:T(8,128)S(1)}, f32[16,16,128]{2,1,0:T(8,128)S(1)}, u32[]{:S(2)}, u32[]{:S(2)}) collective-permute-start(f32[16,16,128]{2,1,0:T(8,128)S(1)} %get-tuple-element.136), channel_id=1, source_target_pairs={{0,4},{4,0},{8,12},{12,8},{1,5},{5,1},{9,13},{13,9},{2,6},{6,2},{1... | collective-permute-start | bytes 393224 | tf_op jit(solution)/shard_map/ppermute | solution.py:906
  61.6 7.3 %collective-permute-start.13 = (f32[16,16,128]{2,1,0:T(8,128)S(1)}, f32[16,16,128]{2,1,0:T(8,128)S(1)}, u32[]{:S(2)}, u32[]{:S(2)}) collective-permute-start(f32[16,16,128]{2,1,0:T(8,128)S(1)} %get-tuple-element.144), channel_id=1, source_target_pairs={{0,1},{1,0},{2,3},{3,2},{4,5},{5,4},{6,7},{7,6},{8,9},{9,8},{10,11... | collective-permute-start | bytes 393224 | tf_op jit(solution)/shard_map/ppermute | solution.py:906
  65.4 3.5 %collective-permute-start.14 = (f32[16,16,128]{2,1,0:T(8,128)S(1)}, f32[16,16,128]{2,1,0:T(8,128)S(1)}, u32[]{:S(2)}, u32[]{:S(2)}) collective-permute-start(f32[16,16,128]{2,1,0:T(8,128)S(1)} %get-tuple-element.145), channel_id=1, source_target_pairs={{1,2},{2,1},{0,0},{3,3},{5,6},{6,5},{4,4},{7,7},{9,10},{10,9},{8,8... | collective-permute-start | bytes 393224 | tf_op jit(solution)/shard_map/ppermute | solution.py:906
  70.2 8.1 %collective-permute-start.15 = (f32[16,16,128]{2,1,0:T(8,128)S(1)}, f32[16,16,128]{2,1,0:T(8,128)S(1)}, u32[]{:S(2)}, u32[]{:S(2)}) collective-permute-start(f32[16,16,128]{2,1,0:T(8,128)S(1)} %face3.1), channel_id=1, source_target_pairs={{0,16},{16,0},{1,17},{17,1},{2,18},{18,2},{3,19},{19,3},{4,20},{20... | collective-permute-start | bytes 393224 | tf_op jit(solution)/shard_map/ppermute | solution.py:906
  77.8 3.2 %collective-permute-start.18 = (f32[480,128]{1,0:T(8,128)S(1)}, f32[480,128]{1,0:T(8,128)S(1)}, u32[]{:S(2)}, u32[]{:S(2)}) collective-permute-start(f32[480,128]{1,0:T(8,128)S(1)} %get-tuple-element.172), channel_id=1, source_target_pairs={{0,4},{4,0},{8,12},{12,8},{1,5},{5,1},{9,13},{13,9},{2,6},{6,2},{1... | collective-permute-start | bytes 737288 | tf_op jit(solution)/shard_map/ppermute | solution.py:814
  78.8 1.4 %collective-permute-start.16 = (f32[16,16,128]{2,1,0:T(8,128)S(1)}, f32[16,16,128]{2,1,0:T(8,128)S(1)}, u32[]{:S(2)}, u32[]{:S(2)}) collective-permute-start(f32[16,16,128]{2,1,0:T(8,128)S(1)} %get-tuple-element.165), channel_id=1, source_target_pairs={{0,4},{4,0},{8,12},{12,8},{1,5},{5,1},{9,13},{13,9},{2,6},{6,2},{1... | collective-permute-start | bytes 393224 | tf_op jit(solution)/shard_map/ppermute | solution.py:906
  79.0 1.2 collective-permute-start.17
  80.9 18.2 %collective-permute-start.19 = (f32[16,16,128]{2,1,0:T(8,128)S(1)}, f32[16,16,128]{2,1,0:T(8,128)S(1)}, u32[]{:S(2)}, u32[]{:S(2)}) collective-permute-start(f32[16,16,128]{2,1,0:T(8,128)S(1)} %get-tuple-element.173), channel_id=1, source_target_pairs={{0,1},{1,0},{2,3},{3,2},{4,5},{5,4},{6,7},{7,6},{8,9},{9,8},{10,11... | collective-permute-start | bytes 393224 | tf_op jit(solution)/shard_map/ppermute | solution.py:906
  84.9 14.2 %collective-permute-start.20 = (f32[16,16,128]{2,1,0:T(8,128)S(1)}, f32[16,16,128]{2,1,0:T(8,128)S(1)}, u32[]{:S(2)}, u32[]{:S(2)}) collective-permute-start(f32[16,16,128]{2,1,0:T(8,128)S(1)} %get-tuple-element.174), channel_id=1, source_target_pairs={{1,2},{2,1},{0,0},{3,3},{5,6},{6,5},{4,4},{7,7},{9,10},{10,9},{8,8... | collective-permute-start | bytes 393224 | tf_op jit(solution)/shard_map/ppermute | solution.py:906
  86.2 11.1 %collective-permute-start.21 = (f32[240,128]{1,0:T(8,128)S(1)}, f32[240,128]{1,0:T(8,128)S(1)}, u32[]{:S(2)}, u32[]{:S(2)}) collective-permute-start(f32[240,128]{1,0:T(8,128)S(1)} %get-tuple-element.181), channel_id=1, source_target_pairs={{0,8},{4,12},{8,0},{12,4},{1,9},{5,13},{9,1},{13,5},{2,10},{6,14},... | collective-permute-start | bytes 368648 | tf_op jit(solution)/shard_map/ppermute | solution.py:814
  97.9 5.3 %collective-permute-start.22 = (f32[120,128]{1,0:T(8,128)S(1)}, f32[120,128]{1,0:T(8,128)S(1)}, u32[]{:S(2)}, u32[]{:S(2)}) collective-permute-start(f32[120,128]{1,0:T(8,128)S(1)} %get-tuple-element.183), channel_id=1, source_target_pairs={{0,16},{16,0},{1,17},{17,1},{2,18},{18,2},{3,19},{19,3},{4,20},{20... | collective-permute-start | bytes 184328 | tf_op jit(solution)/shard_map/ppermute | solution.py:814
  103.7 8.3 %collective-permute-start.23 = (f32[256,128]{1,0:T(8,128)S(1)}, f32[256,128]{1,0:T(8,128)S(1)}, u32[]{:S(2)}, u32[]{:S(2)}) collective-permute-start(f32[256,128]{1,0:T(8,128)S(1)} %stack.17.refs_0_), channel_id=1, source_target_pairs={{0,1},{1,0},{2,3},{3,2},{4,5},{5,4},{6,7},{7,6},{8,9},{9,8},{10,11... | collective-permute-start | bytes 393224 | tf_op jit(solution)/shard_map/ppermute | solution.py:814
  107.1 11.8 %collective-permute-start.24 = (f32[256,128]{1,0:T(8,128)S(1)}, f32[256,128]{1,0:T(8,128)S(1)}, u32[]{:S(2)}, u32[]{:S(2)}) collective-permute-start(f32[256,128]{1,0:T(8,128)S(1)} %stack.17.refs_0_), channel_id=1, source_target_pairs={{0,2},{1,3},{2,0},{3,1},{4,6},{5,7},{6,4},{7,5},{8,10},{9,11},{10,... | collective-permute-start | bytes 393224 | tf_op jit(solution)/shard_map/ppermute | solution.py:814
  107.3 11.6 %collective-permute-start.25 = (f32[256,128]{1,0:T(8,128)S(1)}, f32[256,128]{1,0:T(8,128)S(1)}, u32[]{:S(2)}, u32[]{:S(2)}) collective-permute-start(f32[256,128]{1,0:T(8,128)S(1)} %stack.17.refs_0_), channel_id=1, source_target_pairs={{0,3},{1,2},{2,1},{3,0},{4,7},{5,6},{6,5},{7,4},{8,11},{9,10},{10,... | collective-permute-start | bytes 393224 | tf_op jit(solution)/shard_map/ppermute | solution.py:814
  119.5 5.0 %collective-permute-start.26 = (f32[256,128]{1,0:T(8,128)S(1)}, f32[256,128]{1,0:T(8,128)S(1)}, u32[]{:S(2)}, u32[]{:S(2)}) collective-permute-start(f32[256,128]{1,0:T(8,128)S(1)} %add.7.value), channel_id=1, source_target_pairs={{0,16},{16,0},{1,17},{17,1},{2,18},{18,2},{3,19},{19,3},{4,20},{20... | collective-permute-start | bytes 393224 | tf_op jit(solution)/shard_map/ppermute | solution.py:814
  125.1 5.7 %collective-permute-start.27 = (f32[376,128]{1,0:T(8,128)S(1)}, f32[376,128]{1,0:T(8,128)S(1)}, u32[]{:S(2)}, u32[]{:S(2)}) collective-permute-start(f32[376,128]{1,0:T(8,128)S(1)} %join.2.value), channel_id=1, source_target_pairs={{0,8},{4,12},{8,0},{12,4},{1,9},{5,13},{9,1},{13,5},{2,10},{6,14},... | collective-permute-start | bytes 577544 | tf_op jit(solution)/shard_map/ppermute | solution.py:814
  131.3 1.7 %collective-permute-start.28 = (f32[616,128]{1,0:T(8,128)S(1)}, f32[616,128]{1,0:T(8,128)S(1)}, u32[]{:S(2)}, u32[]{:S(2)}) collective-permute-start(f32[616,128]{1,0:T(8,128)S(1)} %join.3.value), channel_id=1, source_target_pairs={{0,4},{4,0},{8,12},{12,8},{1,5},{5,1},{9,13},{13,9},{2,6},{6,2},{1... | collective-permute-start | bytes 946184 | tf_op jit(solution)/shard_map/ppermute | solution.py:814

commit v8 on v6

--- a/solution.py
+++ b/solution.py
@@ -92,8 +92,20 @@
     lax.fori_loop(0, total, step, 0)
 
 
+def edge_dots(parts, weight, weight_both):
+    rows, width = parts[0].shape[1:]
+    if len(parts) == 2:
+        return dot(flat(jnp.concatenate(parts, 0)), weight).reshape(-1, rows, width)
+    both = dot(jnp.concatenate([flat(parts[0]), flat(parts[2])], -1), weight_both)
+    between = dot(flat(parts[1]), weight).reshape(-1, rows, width)
+    first, last = (both[:, k : k + width].reshape(-1, rows, width) for k in (0, width))
+    return jnp.concatenate([first, between, last], 0)
+
+
 def edges_forward(h_ref, w_one, half_bias, filled, sum_ref, half_ref):
     x_len, y_len, rows, width = h_ref.shape
+    blank = jnp.zeros_like(w_one)
+    w_both = jnp.concatenate([jnp.concatenate([w_one, blank], 1), jnp.concatenate([blank, w_one], 1)], 0)
     inner = row_ids() < NODES - 1
 
     def body(x0, y0):
@@ -109,7 +121,7 @@
             parts.append((here[1:] - here[:-1]).astype(bf16))
             cols = node_rows(here)
             parts.append((up(cols) - cols).reshape(here.shape).astype(bf16))
-            half = dot(flat(jnp.concatenate(parts, 0)), w_one).reshape(-1, rows, width) + half_bias
+            half = edge_dots(parts, w_one, w_both) + half_bias
             act = (half + half * jnp.tanh(half)).astype(bf16).astype(f32)
             at = 0
             total = prev
@@ -200,15 +212,9 @@
         faces[ny + kind][...] = end_rows(reader, sc_ref[0], takes_top(sc_ref, kind))
 
 
-def add_halo(sc_ref, from_ref, halo, into_ref, counts):
-    x_len, y_len, rows, width = from_ref.shape
+def add_halo(sc_ref, halo, into_ref, counts):
+    x_len, y_len, rows, width = into_ref.shape
     nx, ny, nz = counts
-
-    def copy(x, carry):
-        into_ref[x] = from_ref[x]
-        return carry
-
-    lax.fori_loop(0, x_len, copy, 0)
     for kind in range(nx):
         into_ref[face_place(sc_ref, 0, kind, x_len - 1)] += halo[kind][...]
     for kind in range(ny):
@@ -530,9 +536,9 @@
     weights = (edge_w, node_in, node_out, biases)
     n = sum(counts)
     halo, refs = refs[:n], refs[n:]
-    scaled_ref, act_ref, slope_ref, next_ref, sums, slopes = refs[:6]
-    faces, (work, inv) = refs[6:-2], refs[-2:]
-    add_halo(sc, sums_in, halo, work, counts)
+    work, scaled_ref, act_ref, slope_ref, next_ref, sums, slopes = refs[:7]
+    faces, inv = refs[7:-1], refs[-1]
+    add_halo(sc, halo, work, counts)
     write_inverse(sc, inv, sizes)
     shape = (chunk_of(h.shape[0]),) + h.shape[1:]
 
@@ -557,9 +563,9 @@
     weights = (edge_w, node_in, node_out, biases)
     n = sum(counts)
     halo, refs = refs[:n], refs[n:]
-    scaled_ref, act_ref, dpn_ref, sums = refs[:4]
-    faces, (work, inv) = refs[4:-2], refs[-2:]
-    add_halo(sc, sums_in, halo, work, counts)
+    work, scaled_ref, act_ref, dpn_ref, sums = refs[:5]
+    faces, inv = refs[5:-1], refs[-1]
+    add_halo(sc, halo, work, counts)
     write_inverse(sc, inv, sizes)
     shape = (chunk_of(h.shape[0]),) + h.shape[1:]
     live = live_rows(sc, h)
@@ -598,17 +604,17 @@
     planes(h.shape[0], body)
 
 
-def edge_parts(counts, sc, weights, layer, sums_in, halo, h, slopes, work, grads, row):
-    add_halo(sc, sums_in, halo, work, counts)
-    shape = (chunk_of(h.shape[0]),) + h.shape[1:]
+def edge_parts(counts, sc, weights, layer, halo, slopes, work, bias):
+    add_halo(sc, halo, work, counts)
+    shape = (chunk_of(work.shape[0]),) + work.shape[1:]
     w_two = twice(weights[0][layer, 1])
 
     def to_q(x):
-        at = pl.ds(x, chunk_of(h.shape[0]))
+        at = pl.ds(x, chunk_of(work.shape[0]))
         work[at] = dot_rt(split_cols(flat(work[at])), w_two).reshape(shape)
 
-    planes(h.shape[0], to_q)
-    edges_backward(work, slopes, work, grads.at[pl.ds(row + 128, NODES)])
+    planes(work.shape[0], to_q)
+    edges_backward(work, slopes, work, bias)
 
 
 def edge_product(h, x, pair, grads, row):
@@ -616,49 +622,58 @@
     grads[pl.ds(row, 128)] += both[:, :128] + both[:, 128:]
 
 
-def join_kernel(
-    counts, sizes, sc, edge_w, node_in, node_out, biases,
-    sums_in, h, base_in, slopes, h0, scaled0, act0, slope0, grads1, *refs
-):
+def join_kernel(counts, sizes, sc, edge_w, node_in, node_out, biases, sums_in, base_in, slopes, slope0, *refs):
     weights = (edge_w, node_in, node_out, biases)
     n = sum(counts)
     halo, refs = refs[:n], refs[n:]
-    grad_ref, dpn_ref, sums, keep, send = refs[:5]
-    faces, (work, inv, grads) = refs[5:-3], refs[-3:]
+    work, grad_ref, dpn_ref, sums, bias = refs[:5]
+    faces, inv = refs[5:-1], refs[-1]
     write_inverse(sc, inv, sizes)
-    grads[...] = jnp.zeros_like(grads)
-    grads[pl.ds(512 + 2 * NODES, grads1.shape[0])] = grads1[...]
-
-    row = 384 + NODES
-    shape = (chunk_of(h.shape[0]),) + h.shape[1:]
-    edge_parts(counts, sc, weights, 1, sums_in, halo, h, slopes, work, grads, row)
+    bias[...] = jnp.zeros_like(bias)
+    edge_parts(counts, sc, weights, 1, halo, slopes, work, bias)
     w_one = twice(edge_w[1, 0])
+    x_len = work.shape[0]
+    shape = (chunk_of(x_len),) + work.shape[1:]
 
     def body(x):
-        at = pl.ds(x, chunk_of(h.shape[0]))
+        at = pl.ds(x, chunk_of(x_len))
         pair = split_cols(flat(work[at]))
-        edge_product(h, x, pair, grads, row)
         grad = (flat(base_in[at]) + dot_rt(pair, w_one)).astype(bf16)
         dpn = node_slopes(grad, flat(slope0[at]), weights, 0)
-        node_products(grad, flat(h0[at]), flat(scaled0[at]), flat(act0[at]), dpn, grads)
         grad_ref[at] = grad.reshape(shape)
         dpn_ref[at] = dpn.reshape(shape)
         node_share(sc, x, inv, sizes[0], dpn, weights, 0, sums)
 
-    planes(h.shape[0], body)
+    planes(x_len, body)
     couple_columns(sums)
     write_faces(sc, sums, faces, counts)
+
+
+def sums_kernel(sizes, sc, h, edges, grad, h0, scaled0, act0, dpn0, grads1, bias, keep, send, grads):
+    grads[...] = jnp.zeros_like(grads)
+    row = 384 + NODES
+    grads[pl.ds(row + 128, NODES)] = bias[...]
+    grads[pl.ds(row + 128 + NODES, grads1.shape[0])] = grads1[...]
+
+    def body(x):
+        at = pl.ds(x, chunk_of(h.shape[0]))
+        edge_product(h, x, split_cols(flat(edges[at])), grads, row)
+        node_products(flat(grad[at]), flat(h0[at]), flat(scaled0[at]), flat(act0[at]), flat(dpn0[at]), grads)
+
+    planes(h.shape[0], body)
     write_halves(sc, halving_steps(sizes)[0], grads, keep, send)
 
 
-def last_kernel(counts, sizes, sc, edge_w, node_in, node_out, biases, sums_in, h, slopes, *refs):
+def last_kernel(counts, sizes, sc, edge_w, node_in, node_out, biases, sums_in, h, slopes, keep, got, *refs):
     n = sum(counts)
     halo, (edges, grads) = refs[:n], refs[n:]
-    grads[...] = jnp.zeros_like(grads)
-    edge_parts(counts, sc, (edge_w,), 0, sums_in, halo, h, slopes, edges, grads, 0)
+    start = 128 + NODES
+    grads[pl.ds(0, start)] = jnp.zeros((start, 128), f32)
+    grads[pl.ds(start, keep.shape[0])] = keep[...] + got[...]
+    edge_parts(counts, sc, (edge_w,), 0, halo, slopes, edges, grads.at[pl.ds(128, NODES)])
 
     def body(x):
-        edge_product(h, x, split_cols(flat(edges[pl.ds(x, chunk_of(edges.shape[0]))])), grads, 0)
+        edge_product(h, x, split_cols(flat(edges[pl.ds(x, chunk_of(h.shape[0]))])), grads, 0)
 
     planes(h.shape[0], body)
 
@@ -743,9 +758,7 @@
 
 
 def whole_steps(sizes):
-    along_z = hops(sizes[2])
-    steps = [(2, along_z[k : k + 2]) for k in range(0, len(along_z), 2)]
-    return steps + [(1, [hop]) for hop in hops(sizes[1])[1:]]
+    return [(2, [hop]) for hop in reversed(hops(sizes[2]))] + [(1, [hop]) for hop in hops(sizes[1])[1:]]
 
 
 def padded_rows(rows, sizes):
@@ -784,12 +797,6 @@
         out[pl.ds(0, start)] = value[pl.ds(0, start)] + got[pl.ds(0, start)]
     out[pl.ds(pl.multiple_of(start + bit * half, NODES), half)] = value[pl.ds(start, half)]
     out[pl.ds(pl.multiple_of(start + (1 - bit) * half, NODES), half)] = got[pl.ds(start, half)]
-
-
-def stack_kernel(sc, first, left, right, out):
-    rows = first.shape[0]
-    out[pl.ds(0, rows)] = first[...]
-    out[pl.ds(rows, left.shape[0])] = left[...] + right[...]
 
 
 def swap(value, step):
@@ -874,14 +881,18 @@
     full = sds(grid)
     full16 = sds(grid, bf16)
     full3 = sds((3,) + grid)
-    work = pltpu.VMEM(grid, f32)
     inv = pltpu.VMEM((y_len, rows, width), f32)
     matmul = 2 * math.prod(grid) * width
     weights = (edge_weights, node_in, node_out, biases)
 
-    def run(kernel, name, inputs, outs, scratch, flops):
+    in_place = {1 + len(weights): 0}
+
+    def run(kernel, name, inputs, outs, scratch, flops, aliases):
         body = functools.partial(kernel, trades, sizes)
-        return call(body, name, (sc, *weights, *inputs), outs, scratch, flops * matmul)
+        return call(body, name, (sc, *weights, *inputs), outs, scratch, flops * matmul, aliases)
+
+    def behind(value, others):
+        return lax.optimization_barrier((value, others))[0]
 
     def trade(faces, axis):
         size = lax.axis_size(axis)
@@ -894,15 +905,21 @@
 
     def first_trade(kernel, name, inputs, scratch, flops):
         faces = call(functools.partial(kernel, trades, sizes), name, (sc, *inputs), [face_x] * nx, scratch, flops)
-        return trade(faces, "gx")
-
-    def exchange(got_x, faces, work=None, held=()):
+        return trade(faces, "gx"), faces
+
+    def exchange(got_x, faces, work=None, held=(), early=None, early_held=()):
         fix = functools.partial(fix_y_kernel, trades)
         faces_y = call(fix, "fix_y", (sc, *got_x, *faces[:ny]), [face_y] * ny)
-        got_y = trade(background.beside(faces_y), "gy")
+        if early is not None:
+            faces_y, early_held = lax.optimization_barrier((faces_y, early_held))
+            keep, send = early(*early_held)
+        got_y = trade(faces_y, "gy")
+        if early is not None:
+            got_y, (keep, send) = lax.optimization_barrier((got_y, (keep, send)))
+            background.add("sums", halve(sc, sizes, keep, send))
         fix = functools.partial(fix_z_kernel, trades)
         faces_z = call(fix, "fix_z", (sc, *got_x, *got_y[::-1], *faces[ny:]), [face_z] * nz)
-        faces_z = background.beside(faces_z)
+        faces_z = background.beside(background.beside(faces_z))
         done = None
         if work is not None:
             faces_z, held = lax.optimization_barrier((faces_z, held))
@@ -919,40 +936,48 @@
             products_kernel, "nodes1_products", (sc, node_in, *held), [full, rows_like(3 * width + NODES)], [], 6 * matmul
         )
 
-    got_x = first_trade(first_face_kernel, "face0", (edge_weights, biases, h0), [], matmul // 8)
+    got_x, faces_x = first_trade(first_face_kernel, "face0", (edge_weights, biases, h0), [], matmul // 8)
     sums, slopes0, *faces = call(
         functools.partial(first_kernel, trades, sizes), "edges0", (sc, edge_weights, biases, h0),
         [full, full3] + face_outs, [], 3 * matmul,
     )
     halo, slopes0 = exchange(got_x, faces, to_slopes, (slopes0,))
     inputs = (*weights, sums, h0, *halo)
-    got_x = first_trade(middle_face_kernel, "face1", inputs, [pair, inv], matmul // 4)
-    scaled0, act0, slope0, h1, sums, slopes1, *faces = run(
-        middle_kernel, "nodes0_edges1", (sums, h0, *halo),
-        [full16, full16, full, full16, full, full3] + face_outs, [work, inv], 8,
+    got_x, faces_x = first_trade(middle_face_kernel, "face1", inputs, [pair, inv], matmul // 4)
+    _, scaled0, act0, slope0, h1, sums, slopes1, *faces = run(
+        middle_kernel, "nodes0_edges1", (behind(sums, faces_x), h0, *halo),
+        [full, full16, full16, full, full16, full, full3] + face_outs, [inv], 8, in_place,
     )
     halo, slopes1 = exchange(got_x, faces, to_slopes, (slopes1,))
     inputs = (*weights, sums, h1, g2, *halo)
-    got_x = first_trade(turn_face_kernel, "face2", inputs, [pair, inv], matmul // 4)
-    scaled1, act1, dpn1, sums, *faces = run(
-        turn_kernel, "nodes1_back", (sums, h1, g2, *halo), [full16] * 3 + [full] + face_outs, [work, inv], 7
+    got_x, faces_x = first_trade(turn_face_kernel, "face2", inputs, [pair, inv], matmul // 4)
+    _, scaled1, act1, dpn1, sums, *faces = run(
+        turn_kernel, "nodes1_back", (behind(sums, faces_x), h1, g2, *halo), [full] + [full16] * 3 + [full] + face_outs,
+        [inv], 7, in_place,
     )
     halo, (base, grads1) = exchange(got_x, faces, products, (h1, g2, scaled1, act1, dpn1))
     inputs = (*weights, sums, base, slopes1, slope0, *halo)
-    got_x = first_trade(join_face_kernel, "face3", inputs, [pair, inv], matmul // 4)
-    grad_rows = padded_rows(7 * width + 3 * NODES, sizes)
-    half = rows_like(grad_rows // 2)
-    grad_in, dpn0, sums, keep, send, *faces = run(
-        join_kernel, "edges1_back_nodes0_back",
-        (sums, h1, base, slopes1, h0, scaled0, act0, slope0, grads1, *halo),
-        [full16, full16, full, half, half] + face_outs, [work, inv, pltpu.VMEM((grad_rows, width), f32)], 12,
+    got_x, faces_x = first_trade(join_face_kernel, "face3", inputs, [pair, inv], matmul // 4)
+    edges1, grad_in, dpn0, sums, bias1, *faces = run(
+        join_kernel, "edges1_back_nodes0_back", (behind(sums, faces_x), base, slopes1, slope0, *halo),
+        [full, full16, full16, full, rows_like(NODES)] + face_outs, [inv], 9, in_place,
     )
-    background.add("sums", halve(sc, sizes, keep, send))
-    halo, _ = exchange(got_x, faces)
+
+    def layer_sums(*held):
+        total = padded_rows(7 * width + 3 * NODES, sizes)
+        return call(
+            functools.partial(sums_kernel, sizes), "gradient_sums", (sc, *held), [rows_like(total // 2)] * 2,
+            [pltpu.VMEM((total, width), f32)], 5 * matmul,
+        )
+
+    held = (h1, edges1, grad_in, h0, scaled0, act0, dpn0, grads1, bias1)
+    halo, _ = exchange(got_x, faces, early=layer_sums, early_held=held)
     tail_rows = width + NODES
-    edges, last = run(last_kernel, "edges0_back", (sums, h0, slopes0, *halo), [full, rows_like(tail_rows)], [], 6)
     keep, got = background.finish("sums")
-    (value,) = call(stack_kernel, "stack", (sc, last, keep, got), [rows_like(tail_rows + keep.shape[0])])
+    edges, value = run(
+        last_kernel, "edges0_back", (sums, h0, slopes0, keep, got, *halo), [full, rows_like(tail_rows + keep.shape[0])],
+        [], 6, in_place,
+    )
     value, grad_in, dpn0, edges = lax.optimization_barrier((value, grad_in, dpn0, edges))
     (grad0,) = call(
         state_kernel, "state_grad", (sc, edge_weights, node_in, grad_in, dpn0, edges), [full16], [], 4 * matmul

time: 134 us -> 134 us (level)
  waiting for transfers between devices: 24.3 us -> 29.6 us
  starting transfers between devices: 55.7 us -> 51.3 us
    ppermute x8 -> x7, waiting for transfers between devices: 19.7 us -> 24.4 us  [swap(): lax.ppermute(value, axis, [(i, i ^ step[1]) for i in range(lax.axis_size(...]
    ppermute x8 -> x7, starting transfers between devices: 16.6 us -> 12.1 us  [swap(): lax.ppermute(value, axis, [(i, i ^ step[1]) for i in range(lax.axis_size(...]
    pallas_call x27 -> x28, Pallas kernels: 48.4 us -> 48.2 us  [call(): pl.pallas_call(kernel, name=name, out_shape=tuple(outs), in_specs=[SM] +...]
  transfers between devices with their start and end apart: 28 -> 27, of which waited for: 13 -> 14; matrix products, arithmetic and copies ran while one was open for 0% -> 0% of each run, Pallas kernels for 27% -> 23%
where the time goes in v8:
time: 134 us
  starting transfers between devices  51.3 us (38%)
  Pallas kernels  48.2 us (36%)
  waiting for transfers between devices  29.6 us (22%)
  local copies, waits for them, and re-layouts  2.84 us (2%)
  between operations  1.65 us (1%)
    pallas_call x28, Pallas kernels, call(): pl.pallas_call(kernel, name=name, out_shape=tuple(outs), in_specs=[SM] +...  48.2 us
    ppermute x20, starting transfers between devices, trade(): lax.ppermute(face, axis, pairs(size, kind))  39.2 us
    ppermute x7, waiting for transfers between devices, swap(): lax.ppermute(value, axis, [(i, i ^ step[1]) for i in range(lax.axis_size(...  24.4 us
    ppermute x7, starting transfers between devices, swap(): lax.ppermute(value, axis, [(i, i ^ step[1]) for i in range(lax.axis_size(...  12.1 us
    ppermute x20, waiting for transfers between devices, trade(): lax.ppermute(face, axis, pairs(size, kind))  5.2 us
    unnamed x16, local copies, waits for them, and re-layouts  2.84 us
  transfers between devices with their start and end apart: 27, of which 14 were waited for; matrix products, arithmetic and copies ran while one was open for 0% of the time, Pallas kernels for 23%

profile of v8, /device:TPU:0, one launch (start us, length us, event | category | flops | bytes accessed | tf_op | source)
XLA Modules:
  0.0 133.6 jit_solution(9463887192985047898)
XLA Ops:
  1.4 1.2 copy-done
  2.6 0.9 copy-done.2
  3.5 0.7 copy-done.7
  4.2 0.8 face0.1
  5.0 3.0 %collective-permute-start = (f32[16,16,128]{2,1,0:T(8,128)S(1)}, f32[16,16,128]{2,1,0:T(8,128)S(1)}, u32[]{:S(2)}, u32[]{:S(2)}) collective-permute-start(f32[16,16,128]{2,1,0:T(8,128)S(1)} %face0.1), channel_id=1, source_target_pairs={{0,16},{16,0},{1,17},{17,1},{2,18},{18,2},{3,19},{19,3},{4,20},{20... | collective-permute-start | bytes 393224 | tf_op jit(solution)/shard_map/ppermute | solution.py:899
  8.0 3.9 %edges0.1 = (f32[16,16,16,128]{3,2,1,0:T(8,128)S(1)}, f32[3,16,16,16,128]{4,3,2,1,0:T(8,128)S(1)}, f32[16,16,128]{2,1,0:T(8,128)S(1)}, f32[16,16,128]{2,1,0:T(8,...) custom-call(s32[4]{0:T(128)S(1)} %pad_add_fusion.sc.sc_ref, bf16[2,2,128,128]{3,2,1,0:T(8,128)(2,1)S(1)} %copy-done.2, ...), custom_call_target="tpu_custom_call" | custom-call | flops 402653184 | bytes 10094608 | tf_op jit(solution)/shard_map/edges0/pallas_call | solution.py:728
  13.9 0.7 fix_z.4
  14.6 1.6 %collective-permute-start.3 = (f32[16,16,128]{2,1,0:T(8,128)S(1)}, f32[16,16,128]{2,1,0:T(8,128)S(1)}, u32[]{:S(2)}, u32[]{:S(2)}) collective-permute-start(f32[16,16,128]{2,1,0:T(8,128)S(1)} %get-tuple-element.133), channel_id=1, source_target_pairs={{0,1},{1,0},{2,3},{3,2},{4,5},{5,4},{6,7},{7,6},{8,9},{9,8},{10,11... | collective-permute-start | bytes 393224 | tf_op jit(solution)/shard_map/ppermute | solution.py:899
  16.9 2.6 %slopes.2 = f32[3,16,16,16,128]{4,3,2,1,0:T(8,128)S(1)} custom-call(s32[4]{0:T(128)S(1)} %pad_add_fusion.sc.sc_ref, f32[3,16,16,16,128]{4,3,2,1,0:T(8,128)S(1)} %get-tuple-element.135.half_in), custom_call_target="tpu_custom_call", output_to_operand_aliasing={{}: (1, {})} | custom-call | flops 134217728 | bytes 12582928 | tf_op jit(solution)/shard_map/slopes/pallas_call | solution.py:728
  19.7 1.4 %face1.1 = f32[16,16,128]{2,1,0:T(8,128)S(1)} custom-call(s32[4]{0:T(128)S(1)} %pad_add_fusion.sc.sc_ref, bf16[2,2,128,128]{3,2,1,0:T(8,128)(2,1)S(1)} %copy-done.3, bf16[2,256,128]{2,1,0:T(8,128)(2,1)S(1)} %copy-done.4, bf16[2,128,128]{2,1,0:T(8,128)(2,1)S(1)} %copy-done.6, f32[2,2,128]{2,1,0:T(2,128)S(1)} %copy-done.7, ...), custom_call_target="tpu_custom_call" | custom-call | flops 33554432 | bytes 4261904 | tf_op jit(solution)/shard_map/face1/pallas_call | solution.py:728
  21.1 1.4 %collective-permute-start.5 = (f32[16,16,128]{2,1,0:T(8,128)S(1)}, f32[16,16,128]{2,1,0:T(8,128)S(1)}, u32[]{:S(2)}, u32[]{:S(2)}) collective-permute-start(f32[16,16,128]{2,1,0:T(8,128)S(1)} %face1.1), channel_id=1, source_target_pairs={{0,16},{16,0},{1,17},{17,1},{2,18},{18,2},{3,19},{19,3},{4,20},{20... | collective-permute-start | bytes 393224 | tf_op jit(solution)/shard_map/ppermute | solution.py:899
  22.5 6.2 %nodes0_edges1.1 = (f32[16,16,16,128]{3,2,1,0:T(8,128)S(1)}, bf16[16,16,16,128]{3,2,1,0:T(8,128)(2,1)S(1)}, bf16[16,16,16,128]{3,2,1,0:T(8,128)(2,1)S(1)}, f32[1...) custom-call(s32[4]{0:T(128)S(1)} %pad_add_fusion.sc.sc_ref, ...), custom_call_target="tpu_custom_call", output_to_operand_aliasing={{0}: (5, {})} | custom-call | flops 1073741824 | bytes 20383760 | tf_op jit(solution)/shard_map/nodes0_edges1/pallas_call | solution.py:728
  29.3 5.1 %collective-permute-start.6 = (f32[16,16,128]{2,1,0:T(8,128)S(1)}, f32[16,16,128]{2,1,0:T(8,128)S(1)}, u32[]{:S(2)}, u32[]{:S(2)}) collective-permute-start(f32[16,16,128]{2,1,0:T(8,128)S(1)} %get-tuple-element.143), channel_id=1, source_target_pairs={{0,4},{4,0},{8,12},{12,8},{1,5},{5,1},{9,13},{13,9},{2,6},{6,2},{1... | collective-permute-start | bytes 393224 | tf_op jit(solution)/shard_map/ppermute | solution.py:899
  35.4 0.7 fix_z.5
  36.1 4.2 %collective-permute-start.8 = (f32[16,16,128]{2,1,0:T(8,128)S(1)}, f32[16,16,128]{2,1,0:T(8,128)S(1)}, u32[]{:S(2)}, u32[]{:S(2)}) collective-permute-start(f32[16,16,128]{2,1,0:T(8,128)S(1)} %get-tuple-element.150), channel_id=1, source_target_pairs={{0,1},{1,0},{2,3},{3,2},{4,5},{5,4},{6,7},{7,6},{8,9},{9,8},{10,11... | collective-permute-start | bytes 393224 | tf_op jit(solution)/shard_map/ppermute | solution.py:899
  40.9 2.6 %slopes.3 = f32[3,16,16,16,128]{4,3,2,1,0:T(8,128)S(1)} custom-call(s32[4]{0:T(128)S(1)} %pad_add_fusion.sc.sc_ref, f32[3,16,16,16,128]{4,3,2,1,0:T(8,128)S(1)} %get-tuple-element.152.half_in), custom_call_target="tpu_custom_call", output_to_operand_aliasing={{}: (1, {})} | custom-call | flops 134217728 | bytes 12582928 | tf_op jit(solution)/shard_map/slopes/pallas_call | solution.py:728
  43.5 1.2 face2.1
  44.7 0.8 collective-permute-start.10
  45.4 3.6 %nodes1_back.1 = (f32[16,16,16,128]{3,2,1,0:T(8,128)S(1)}, bf16[16,16,16,128]{3,2,1,0:T(8,128)(2,1)S(1)}, bf16[16,16,16,128]{3,2,1,0:T(8,128)(2,1)S(1)}, bf16[16...) custom-call(s32[4]{0:T(128)S(1)} %pad_add_fusion.sc.sc_ref, ...), custom_call_target="tpu_custom_call", output_to_operand_aliasing={{0}: (5, {})} | custom-call | flops 939524096 | bytes 13043728 | tf_op jit(solution)/shard_map/nodes1_back/pallas_call | solution.py:728
  50.3 0.7 collective-permute-start.11
  51.0 8.6 %collective-permute-start.12 = (f32[16,16,128]{2,1,0:T(8,128)S(1)}, f32[16,16,128]{2,1,0:T(8,128)S(1)}, u32[]{:S(2)}, u32[]{:S(2)}) collective-permute-start(f32[16,16,128]{2,1,0:T(8,128)S(1)} %get-tuple-element.160), channel_id=1, source_target_pairs={{0,4},{4,0},{8,12},{12,8},{1,5},{5,1},{9,13},{13,9},{2,6},{6,2},{1... | collective-permute-start | bytes 393224 | tf_op jit(solution)/shard_map/ppermute | solution.py:899
  59.6 1.0 collective-permute-done.12.refs_2_.refs_1_
  60.6 0.7 fix_z.6
  61.3 3.8 %collective-permute-start.13 = (f32[16,16,128]{2,1,0:T(8,128)S(1)}, f32[16,16,128]{2,1,0:T(8,128)S(1)}, u32[]{:S(2)}, u32[]{:S(2)}) collective-permute-start(f32[16,16,128]{2,1,0:T(8,128)S(1)} %get-tuple-element.168), channel_id=1, source_target_pairs={{0,1},{1,0},{2,3},{3,2},{4,5},{5,4},{6,7},{7,6},{8,9},{9,8},{10,11... | collective-permute-start | bytes 393224 | tf_op jit(solution)/shard_map/ppermute | solution.py:899
  65.1 0.8 collective-permute-start.14
  65.9 1.6 %nodes1_products.1 = (f32[16,16,16,128]{3,2,1,0:T(8,128)S(1)}, f32[392,128]{1,0:T(8,128)S(1)}) custom-call(s32[4]{0:T(128)S(1)} %pad_add_fusion.sc.sc_ref, bf16[2,256,128]{2,1,0:T(8,128)(2,1)S(1)} %copy-done.4, bf16[16,16,16,128]{3,2,1,0:T(8,128)(2,1)S(1)} %get-tuple-element.198.h, bf16[16,16,16,128]{3,2,1,0:T(8,128)(2,1)S(1)} %bitcast.14, ...), custom_call_target="tpu_custom_call" | custom-call | flops 805306368 | bytes 7671824 | tf_op jit(solution)/shard_map/nodes1_products/pallas_call | solution.py:728
  67.5 1.0 collective-permute-done.13.refs_3_
  68.5 1.3 face3.1
  69.9 0.8 collective-permute-start.15
  70.6 5.3 %edges1_back_nodes0_back.1 = (f32[16,16,16,128]{3,2,1,0:T(8,128)S(1)}, bf16[16,16,16,128]{3,2,1,0:T(8,128)(2,1)S(1)}, bf16[16,16,16,128]{3,2,1,0:T(8,128)(2,1)S(...) custom-call(s32[4]{0:T(128)S(1)} %pad_add_fusion.sc.sc_ref, ...), custom_call_target="tpu_custom_call", output_to_operand_aliasing={{0}: (5, {})} | custom-call | flops 1207959552 | bytes 20387856 | tf_op jit(solution)/shard_map/edges1_back_nodes0_back/pallas_call | solution.py:728
  77.7 1.7 %gradient_sums.1 = (f32[464,128]{1,0:T(8,128)S(1)}, f32[464,128]{1,0:T(8,128)S(1)}) custom-call(s32[4]{0:T(128)S(1)} %pad_add_fusion.sc.sc_ref, bf16[16,16,16,128]{3,2,1,0:T(8,128)(2,1)S(1)} %get-tuple-element.198.h, f32[16,16,16,128]{3,2,1,0:T(8,128)S(1)} %get-tuple-element.199.edges, bf16[16,16,16,128]{3,2,1,0:T(8,128)(2,1)S(1)} %get-tuple-element.228.grad.grad_in, ...), custom_call_target="tpu_custom_call" | custom-call | flops 671088640 | bytes 9068560 | tf_op jit(solution)/shard_map/gradient_sums/pallas_call | solution.py:728
  79.5 4.5 %collective-permute-start.18 = (f32[464,128]{1,0:T(8,128)S(1)}, f32[464,128]{1,0:T(8,128)S(1)}, u32[]{:S(2)}, u32[]{:S(2)}) collective-permute-start(f32[464,128]{1,0:T(8,128)S(1)} %get-tuple-element.216), channel_id=1, source_target_pairs={{0,4},{4,0},{8,12},{12,8},{1,5},{5,1},{9,13},{13,9},{2,6},{6,2},{1... | collective-permute-start | bytes 712712 | tf_op jit(solution)/shard_map/ppermute | solution.py:804
  84.0 0.7 fix_z.7
  85.1 3.9 %collective-permute-start.20 = (f32[16,16,128]{2,1,0:T(8,128)S(1)}, f32[16,16,128]{2,1,0:T(8,128)S(1)}, u32[]{:S(2)}, u32[]{:S(2)}) collective-permute-start(f32[16,16,128]{2,1,0:T(8,128)S(1)} %get-tuple-element.221), channel_id=1, source_target_pairs={{0,1},{1,0},{2,3},{3,2},{4,5},{5,4},{6,7},{7,6},{8,9},{9,8},{10,11... | collective-permute-start | bytes 393224 | tf_op jit(solution)/shard_map/ppermute | solution.py:899
  90.3 1.4 %collective-permute-start.19 = (f32[232,128]{1,0:T(8,128)S(1)}, f32[232,128]{1,0:T(8,128)S(1)}, u32[]{:S(2)}, u32[]{:S(2)}) collective-permute-start(f32[232,128]{1,0:T(8,128)S(1)} %get-tuple-element.220), channel_id=1, source_target_pairs={{0,16},{16,0},{1,17},{17,1},{2,18},{18,2},{3,19},{19,3},{4,20},{20... | collective-permute-start | bytes 356360 | tf_op jit(solution)/shard_map/ppermute | solution.py:804
  91.7 1.4 %collective-permute-done.20.refs_3_ = f32[16,16,128]{2,1,0:T(8,128)S(1)} collective-permute-done((f32[16,16,128]{2,1,0:T(8,128)S(1)}, f32[16,16,128]{2,1,0:T(8,128)S(1)}, u32[]{:S(2)}, u32[]{:S(2)}) %collective-permute-start.20) | collective-permute-done | bytes 131104 | tf_op jit(solution)/shard_map/ppermute | solution.py:899
  93.1 2.5 %collective-permute-done.19.got = f32[232,128]{1,0:T(8,128)S(1)} collective-permute-done((f32[232,128]{1,0:T(8,128)S(1)}, f32[232,128]{1,0:T(8,128)S(1)}, u32[]{:S(2)}, u32[]{:S(2)}) %collective-permute-start.19) | collective-permute-done | bytes 118816 | tf_op jit(solution)/shard_map/ppermute | solution.py:804
  95.6 3.9 %edges0_back.1 = (f32[16,16,16,128]{3,2,1,0:T(8,128)S(1)}, f32[368,128]{1,0:T(8,128)S(1)}) custom-call(s32[4]{0:T(128)S(1)} %pad_add_fusion.sc.sc_ref, bf16[2,2,128,128]{3,2,1,0:T(8,128)(2,1)S(1)} %copy-done.3, bf16[2,256,128]{2,1,0:T(8,128)(2,1)S(1)} %copy-done.4, bf16[2,128,128]{2,1,0:T(8,128)(2,1)S(1)} %copy-done.6, ...), custom_call_target="tpu_custom_call", output_to_operand_aliasing={{0}: (5, {})} | custom-call | flops 805306368 | bytes 12945424 | tf_op jit(solution)/shard_map/edges0_back/pallas_call | solution.py:728
  99.5 3.1 %collective-permute-start.22 = (f32[368,128]{1,0:T(8,128)S(1)}, f32[368,128]{1,0:T(8,128)S(1)}, u32[]{:S(2)}, u32[]{:S(2)}) collective-permute-start(f32[368,128]{1,0:T(8,128)S(1)} %get-tuple-element.227.refs_0_), channel_id=1, source_target_pairs={{0,2},{1,3},{2,0},{3,1},{4,6},{5,7},{6,4},{7,5},{8,10},{9,11},{10,... | collective-permute-start | bytes 565256 | tf_op jit(solution)/shard_map/ppermute | solution.py:804
  102.5 2.5 %state_grad.1 = bf16[16,16,16,128]{3,2,1,0:T(8,128)(2,1)} custom-call(s32[4]{0:T(128)S(1)} %pad_add_fusion.sc.sc_ref, bf16[2,2,128,128]{3,2,1,0:T(8,128)(2,1)S(1)} %copy-done.3, bf16[2,256,128]{2,1,0:T(8,128)(2,1)S(1)} %copy-done.4, bf16[16,16,16,128]{3,2,1,0:T(8,128)(2,1)S(1)} %get-tuple-element.228.grad.grad_in, ...), custom_call_target="tpu_custom_call" | custom-call | flops 536870912 | bytes 5505040 | tf_op jit(solution)/shard_map/state_grad/pallas_call | solution.py:728
  105.1 6.0 %collective-permute-done.22.refs_1_ = f32[368,128]{1,0:T(8,128)S(1)} collective-permute-done((f32[368,128]{1,0:T(8,128)S(1)}, f32[368,128]{1,0:T(8,128)S(1)}, u32[]{:S(2)}, u32[]{:S(2)}) %collective-permute-start.22) | collective-permute-done | bytes 188448 | tf_op jit(solution)/shard_map/ppermute | solution.py:804
  111.7 5.6 %collective-permute-done.23.refs_1_ = f32[368,128]{1,0:T(8,128)S(1)} collective-permute-done((f32[368,128]{1,0:T(8,128)S(1)}, f32[368,128]{1,0:T(8,128)S(1)}, u32[]{:S(2)}, u32[]{:S(2)}) %collective-permute-start.23) | collective-permute-done | bytes 188448 | tf_op jit(solution)/shard_map/ppermute | solution.py:804
  117.8 1.6 %collective-permute-start.24 = (f32[368,128]{1,0:T(8,128)S(1)}, f32[368,128]{1,0:T(8,128)S(1)}, u32[]{:S(2)}, u32[]{:S(2)}) collective-permute-start(f32[368,128]{1,0:T(8,128)S(1)} %add.10.refs_0_), channel_id=1, source_target_pairs={{0,8},{4,12},{8,0},{12,4},{1,9},{5,13},{9,1},{13,5},{2,10},{6,14},... | collective-permute-start | bytes 565256 | tf_op jit(solution)/shard_map/ppermute | solution.py:804
  119.4 4.1 %collective-permute-done.24.refs_1_ = f32[368,128]{1,0:T(8,128)S(1)} collective-permute-done((f32[368,128]{1,0:T(8,128)S(1)}, f32[368,128]{1,0:T(8,128)S(1)}, u32[]{:S(2)}, u32[]{:S(2)}) %collective-permute-start.24) | collective-permute-done | bytes 188448 | tf_op jit(solution)/shard_map/ppermute | solution.py:804
  124.0 1.4 %collective-permute-start.25 = (f32[368,128]{1,0:T(8,128)S(1)}, f32[368,128]{1,0:T(8,128)S(1)}, u32[]{:S(2)}, u32[]{:S(2)}) collective-permute-start(f32[368,128]{1,0:T(8,128)S(1)} %add.11.value), channel_id=1, source_target_pairs={{0,16},{16,0},{1,17},{17,1},{2,18},{18,2},{3,19},{19,3},{4,20},{20... | collective-permute-start | bytes 565256 | tf_op jit(solution)/shard_map/ppermute | solution.py:804
  125.4 4.3 %collective-permute-done.25.got = f32[368,128]{1,0:T(8,128)S(1)} collective-permute-done((f32[368,128]{1,0:T(8,128)S(1)}, f32[368,128]{1,0:T(8,128)S(1)}, u32[]{:S(2)}, u32[]{:S(2)}) %collective-permute-start.25) | collective-permute-done | bytes 188448 | tf_op jit(solution)/shard_map/ppermute | solution.py:804
  130.3 1.6 %collective-permute-done.26.got = f32[600,128]{1,0:T(8,128)S(1)} collective-permute-done((f32[600,128]{1,0:T(8,128)S(1)}, f32[600,128]{1,0:T(8,128)S(1)}, u32[]{:S(2)}, u32[]{:S(2)}) %collective-permute-start.26) | collective-permute-done | bytes 307232 | tf_op jit(solution)/shard_map/ppermute | solution.py:804
  131.9 1.7 %finish.1 = (f32[2,2,128,128]{3,2,1,0:T(8,128)}, f32[2,256,128]{2,1,0:T(8,128)}, f32[2,128,128]{2,1,0:T(8,128)}, f32[2,2,128]{2,1,0:T(2,128)}) custom-call(s32[4]{0:T(128)S(1)} %pad_add_fusion.sc.sc_ref, bf16[2,2,128,128]{3,2,1,0:T(8,128)(2,1)S(1)} %copy-done.3, bf16[2,256,128]{2,1,0:T(8,128)(2,1)S(1)} %copy-done.4, f32[600,128]{1,0:T(8,128)S(1)} %join.1.value, ...), custom_call_target="tpu_custom_call" | custom-call | bytes 1533968 | tf_op jit(solution)/shard_map/finish/pallas_call | solution.py:728
  (51 shorter events, 12.1 us)
Async XLA Ops:
  1.4 1.2 copy-start
  2.6 0.9 copy-start.2
  3.5 0.7 copy-start.7
  5.0 6.9 %collective-permute-start = (f32[16,16,128]{2,1,0:T(8,128)S(1)}, f32[16,16,128]{2,1,0:T(8,128)S(1)}, u32[]{:S(2)}, u32[]{:S(2)}) collective-permute-start(f32[16,16,128]{2,1,0:T(8,128)S(1)} %face0.1), channel_id=1, source_target_pairs={{0,16},{16,0},{1,17},{17,1},{2,18},{18,2},{3,19},{19,3},{4,20},{20... | collective-permute-start | bytes 393224 | tf_op jit(solution)/shard_map/ppermute | solution.py:899
  12.4 1.4 %collective-permute-start.1 = (f32[16,16,128]{2,1,0:T(8,128)S(1)}, f32[16,16,128]{2,1,0:T(8,128)S(1)}, u32[]{:S(2)}, u32[]{:S(2)}) collective-permute-start(f32[16,16,128]{2,1,0:T(8,128)S(1)} %get-tuple-element.126), channel_id=1, source_target_pairs={{0,4},{4,0},{8,12},{12,8},{1,5},{5,1},{9,13},{13,9},{2,6},{6,2},{1... | collective-permute-start | bytes 393224 | tf_op jit(solution)/shard_map/ppermute | solution.py:899
  12.5 1.3 %collective-permute-start.2 = (f32[16,16,128]{2,1,0:T(8,128)S(1)}, f32[16,16,128]{2,1,0:T(8,128)S(1)}, u32[]{:S(2)}, u32[]{:S(2)}) collective-permute-start(f32[16,16,128]{2,1,0:T(8,128)S(1)} %get-tuple-element.127), channel_id=1, source_target_pairs={{4,8},{8,4},{5,9},{9,5},{6,10},{10,6},{7,11},{11,7},{20,24},{24,20... | collective-permute-start | bytes 393224 | tf_op jit(solution)/shard_map/ppermute | solution.py:899
  14.6 5.1 %copy-start.1 = (bf16[16,16,2,8,128]{4,3,2,1,0:T(8,128)(2,1)S(1)}, bf16[16,16,2,8,128]{4,3,2,1,0:T(8,128)(2,1)}, u32[]{:S(2)}) copy-start(bf16[16,16,2,8,128]{4,3,2,1,0:T(8,128)(2,1)} %param.7) | copy-start | bytes 3145732
  14.6 5.1 %copy-start.3 = (bf16[2,2,128,128]{3,2,1,0:T(8,128)(2,1)S(1)}, bf16[2,2,128,128]{3,2,1,0:T(8,128)(2,1)}, u32[]{:S(2)}) copy-start(bf16[2,2,128,128]{3,2,1,0:T(8,128)(2,1)} %edge_w.21) | copy-start | bytes 393220
  14.6 5.1 %copy-start.4 = (bf16[2,256,128]{2,1,0:T(8,128)(2,1)S(1)}, bf16[2,256,128]{2,1,0:T(8,128)(2,1)}, u32[]{:S(2)}) copy-start(bf16[2,256,128]{2,1,0:T(8,128)(2,1)} %node_in.19) | copy-start | bytes 393220
  14.6 5.1 %copy-start.6 = (bf16[2,128,128]{2,1,0:T(8,128)(2,1)S(1)}, bf16[2,128,128]{2,1,0:T(8,128)(2,1)}, u32[]{:S(2)}) copy-start(bf16[2,128,128]{2,1,0:T(8,128)(2,1)} %node_out.13) | copy-start | bytes 196612
  14.6 5.0 %collective-permute-start.3 = (f32[16,16,128]{2,1,0:T(8,128)S(1)}, f32[16,16,128]{2,1,0:T(8,128)S(1)}, u32[]{:S(2)}, u32[]{:S(2)}) collective-permute-start(f32[16,16,128]{2,1,0:T(8,128)S(1)} %get-tuple-element.133), channel_id=1, source_target_pairs={{0,1},{1,0},{2,3},{3,2},{4,5},{5,4},{6,7},{7,6},{8,9},{9,8},{10,11... | collective-permute-start | bytes 393224 | tf_op jit(solution)/shard_map/ppermute | solution.py:899
  16.2 3.4 %collective-permute-start.4 = (f32[16,16,128]{2,1,0:T(8,128)S(1)}, f32[16,16,128]{2,1,0:T(8,128)S(1)}, u32[]{:S(2)}, u32[]{:S(2)}) collective-permute-start(f32[16,16,128]{2,1,0:T(8,128)S(1)} %get-tuple-element.134), channel_id=1, source_target_pairs={{1,2},{2,1},{5,6},{6,5},{9,10},{10,9},{13,14},{14,13},{17,18},{18,... | collective-permute-start | bytes 393224 | tf_op jit(solution)/shard_map/ppermute | solution.py:899
  21.1 7.6 %collective-permute-start.5 = (f32[16,16,128]{2,1,0:T(8,128)S(1)}, f32[16,16,128]{2,1,0:T(8,128)S(1)}, u32[]{:S(2)}, u32[]{:S(2)}) collective-permute-start(f32[16,16,128]{2,1,0:T(8,128)S(1)} %face1.1), channel_id=1, source_target_pairs={{0,16},{16,0},{1,17},{17,1},{2,18},{18,2},{3,19},{19,3},{4,20},{20... | collective-permute-start | bytes 393224 | tf_op jit(solution)/shard_map/ppermute | solution.py:899
  29.3 6.1 %collective-permute-start.6 = (f32[16,16,128]{2,1,0:T(8,128)S(1)}, f32[16,16,128]{2,1,0:T(8,128)S(1)}, u32[]{:S(2)}, u32[]{:S(2)}) collective-permute-start(f32[16,16,128]{2,1,0:T(8,128)S(1)} %get-tuple-element.143), channel_id=1, source_target_pairs={{0,4},{4,0},{8,12},{12,8},{1,5},{5,1},{9,13},{13,9},{2,6},{6,2},{1... | collective-permute-start | bytes 393224 | tf_op jit(solution)/shard_map/ppermute | solution.py:899
  34.4 1.0 collective-permute-start.7
  36.1 7.5 %copy-start.5 = (bf16[16,16,2,8,128]{4,3,2,1,0:T(8,128)(2,1)S(1)}, bf16[16,16,2,8,128]{4,3,2,1,0:T(8,128)(2,1)}, u32[]{:S(2)}) copy-start(bf16[16,16,2,8,128]{4,3,2,1,0:T(8,128)(2,1)} %param.8) | copy-start | bytes 3145732
  36.1 7.4 %collective-permute-start.8 = (f32[16,16,128]{2,1,0:T(8,128)S(1)}, f32[16,16,128]{2,1,0:T(8,128)S(1)}, u32[]{:S(2)}, u32[]{:S(2)}) collective-permute-start(f32[16,16,128]{2,1,0:T(8,128)S(1)} %get-tuple-element.150), channel_id=1, source_target_pairs={{0,1},{1,0},{2,3},{3,2},{4,5},{5,4},{6,7},{7,6},{8,9},{9,8},{10,11... | collective-permute-start | bytes 393224 | tf_op jit(solution)/shard_map/ppermute | solution.py:899
  40.2 3.3 %collective-permute-start.9 = (f32[16,16,128]{2,1,0:T(8,128)S(1)}, f32[16,16,128]{2,1,0:T(8,128)S(1)}, u32[]{:S(2)}, u32[]{:S(2)}) collective-permute-start(f32[16,16,128]{2,1,0:T(8,128)S(1)} %get-tuple-element.151), channel_id=1, source_target_pairs={{1,2},{2,1},{5,6},{6,5},{9,10},{10,9},{13,14},{14,13},{17,18},{18,... | collective-permute-start | bytes 393224 | tf_op jit(solution)/shard_map/ppermute | solution.py:899
  44.7 5.0 %collective-permute-start.10 = (f32[16,16,128]{2,1,0:T(8,128)S(1)}, f32[16,16,128]{2,1,0:T(8,128)S(1)}, u32[]{:S(2)}, u32[]{:S(2)}) collective-permute-start(f32[16,16,128]{2,1,0:T(8,128)S(1)} %face2.1), channel_id=1, source_target_pairs={{0,16},{16,0},{1,17},{17,1},{2,18},{18,2},{3,19},{19,3},{4,20},{20... | collective-permute-start | bytes 393224 | tf_op jit(solution)/shard_map/ppermute | solution.py:899
  50.3 9.3 %collective-permute-start.11 = (f32[16,16,128]{2,1,0:T(8,128)S(1)}, f32[16,16,128]{2,1,0:T(8,128)S(1)}, u32[]{:S(2)}, u32[]{:S(2)}) collective-permute-start(f32[16,16,128]{2,1,0:T(8,128)S(1)} %get-tuple-element.159), channel_id=1, source_target_pairs={{4,8},{8,4},{5,9},{9,5},{6,10},{10,6},{7,11},{11,7},{20,24},{24,20... | collective-permute-start | bytes 393224 | tf_op jit(solution)/shard_map/ppermute | solution.py:899
  51.0 9.6 %collective-permute-start.12 = (f32[16,16,128]{2,1,0:T(8,128)S(1)}, f32[16,16,128]{2,1,0:T(8,128)S(1)}, u32[]{:S(2)}, u32[]{:S(2)}) collective-permute-start(f32[16,16,128]{2,1,0:T(8,128)S(1)} %get-tuple-element.160), channel_id=1, source_target_pairs={{0,4},{4,0},{8,12},{12,8},{1,5},{5,1},{9,13},{13,9},{2,6},{6,2},{1... | collective-permute-start | bytes 393224 | tf_op jit(solution)/shard_map/ppermute | solution.py:899
  61.3 7.3 %collective-permute-start.13 = (f32[16,16,128]{2,1,0:T(8,128)S(1)}, f32[16,16,128]{2,1,0:T(8,128)S(1)}, u32[]{:S(2)}, u32[]{:S(2)}) collective-permute-start(f32[16,16,128]{2,1,0:T(8,128)S(1)} %get-tuple-element.168), channel_id=1, source_target_pairs={{0,1},{1,0},{2,3},{3,2},{4,5},{5,4},{6,7},{7,6},{8,9},{9,8},{10,11... | collective-permute-start | bytes 393224 | tf_op jit(solution)/shard_map/ppermute | solution.py:899
  65.1 3.5 %collective-permute-start.14 = (f32[16,16,128]{2,1,0:T(8,128)S(1)}, f32[16,16,128]{2,1,0:T(8,128)S(1)}, u32[]{:S(2)}, u32[]{:S(2)}) collective-permute-start(f32[16,16,128]{2,1,0:T(8,128)S(1)} %get-tuple-element.169), channel_id=1, source_target_pairs={{1,2},{2,1},{5,6},{6,5},{9,10},{10,9},{13,14},{14,13},{17,18},{18,... | collective-permute-start | bytes 393224 | tf_op jit(solution)/shard_map/ppermute | solution.py:899
  69.9 6.2 %collective-permute-start.15 = (f32[16,16,128]{2,1,0:T(8,128)S(1)}, f32[16,16,128]{2,1,0:T(8,128)S(1)}, u32[]{:S(2)}, u32[]{:S(2)}) collective-permute-start(f32[16,16,128]{2,1,0:T(8,128)S(1)} %face3.1), channel_id=1, source_target_pairs={{0,16},{16,0},{1,17},{17,1},{2,18},{18,2},{3,19},{19,3},{4,20},{20... | collective-permute-start | bytes 393224 | tf_op jit(solution)/shard_map/ppermute | solution.py:899
  76.6 2.8 %collective-permute-start.16 = (f32[16,16,128]{2,1,0:T(8,128)S(1)}, f32[16,16,128]{2,1,0:T(8,128)S(1)}, u32[]{:S(2)}, u32[]{:S(2)}) collective-permute-start(f32[16,16,128]{2,1,0:T(8,128)S(1)} %get-tuple-element.196), channel_id=1, source_target_pairs={{0,4},{4,0},{8,12},{12,8},{1,5},{5,1},{9,13},{13,9},{2,6},{6,2},{1... | collective-permute-start | bytes 393224 | tf_op jit(solution)/shard_map/ppermute | solution.py:899
  77.0 2.4 %collective-permute-start.17 = (f32[16,16,128]{2,1,0:T(8,128)S(1)}, f32[16,16,128]{2,1,0:T(8,128)S(1)}, u32[]{:S(2)}, u32[]{:S(2)}) collective-permute-start(f32[16,16,128]{2,1,0:T(8,128)S(1)} %get-tuple-element.197), channel_id=1, source_target_pairs={{4,8},{8,4},{5,9},{9,5},{6,10},{10,6},{7,11},{11,7},{20,24},{24,20... | collective-permute-start | bytes 393224 | tf_op jit(solution)/shard_map/ppermute | solution.py:899
  79.5 5.7 %collective-permute-start.18 = (f32[464,128]{1,0:T(8,128)S(1)}, f32[464,128]{1,0:T(8,128)S(1)}, u32[]{:S(2)}, u32[]{:S(2)}) collective-permute-start(f32[464,128]{1,0:T(8,128)S(1)} %get-tuple-element.216), channel_id=1, source_target_pairs={{0,4},{4,0},{8,12},{12,8},{1,5},{5,1},{9,13},{13,9},{2,6},{6,2},{1... | collective-permute-start | bytes 712712 | tf_op jit(solution)/shard_map/ppermute | solution.py:804
  85.1 8.0 %collective-permute-start.20 = (f32[16,16,128]{2,1,0:T(8,128)S(1)}, f32[16,16,128]{2,1,0:T(8,128)S(1)}, u32[]{:S(2)}, u32[]{:S(2)}) collective-permute-start(f32[16,16,128]{2,1,0:T(8,128)S(1)} %get-tuple-element.221), channel_id=1, source_target_pairs={{0,1},{1,0},{2,3},{3,2},{4,5},{5,4},{6,7},{7,6},{8,9},{9,8},{10,11... | collective-permute-start | bytes 393224 | tf_op jit(solution)/shard_map/ppermute | solution.py:899
  89.1 4.0 %collective-permute-start.21 = (f32[16,16,128]{2,1,0:T(8,128)S(1)}, f32[16,16,128]{2,1,0:T(8,128)S(1)}, u32[]{:S(2)}, u32[]{:S(2)}) collective-permute-start(f32[16,16,128]{2,1,0:T(8,128)S(1)} %get-tuple-element.222), channel_id=1, source_target_pairs={{1,2},{2,1},{5,6},{6,5},{9,10},{10,9},{13,14},{14,13},{17,18},{18,... | collective-permute-start | bytes 393224 | tf_op jit(solution)/shard_map/ppermute | solution.py:899
  90.3 5.3 %collective-permute-start.19 = (f32[232,128]{1,0:T(8,128)S(1)}, f32[232,128]{1,0:T(8,128)S(1)}, u32[]{:S(2)}, u32[]{:S(2)}) collective-permute-start(f32[232,128]{1,0:T(8,128)S(1)} %get-tuple-element.220), channel_id=1, source_target_pairs={{0,16},{16,0},{1,17},{17,1},{2,18},{18,2},{3,19},{19,3},{4,20},{20... | collective-permute-start | bytes 356360 | tf_op jit(solution)/shard_map/ppermute | solution.py:804
  99.5 11.5 %collective-permute-start.22 = (f32[368,128]{1,0:T(8,128)S(1)}, f32[368,128]{1,0:T(8,128)S(1)}, u32[]{:S(2)}, u32[]{:S(2)}) collective-permute-start(f32[368,128]{1,0:T(8,128)S(1)} %get-tuple-element.227.refs_0_), channel_id=1, source_target_pairs={{0,2},{1,3},{2,0},{3,1},{4,6},{5,7},{6,4},{7,5},{8,10},{9,11},{10,... | collective-permute-start | bytes 565256 | tf_op jit(solution)/shard_map/ppermute | solution.py:804
  111.6 5.6 %collective-permute-start.23 = (f32[368,128]{1,0:T(8,128)S(1)}, f32[368,128]{1,0:T(8,128)S(1)}, u32[]{:S(2)}, u32[]{:S(2)}) collective-permute-start(f32[368,128]{1,0:T(8,128)S(1)} %add.9.refs_0_), channel_id=1, source_target_pairs={{0,1},{1,0},{2,3},{3,2},{4,5},{5,4},{6,7},{7,6},{8,9},{9,8},{10,11... | collective-permute-start | bytes 565256 | tf_op jit(solution)/shard_map/ppermute | solution.py:804
  117.8 5.6 %collective-permute-start.24 = (f32[368,128]{1,0:T(8,128)S(1)}, f32[368,128]{1,0:T(8,128)S(1)}, u32[]{:S(2)}, u32[]{:S(2)}) collective-permute-start(f32[368,128]{1,0:T(8,128)S(1)} %add.10.refs_0_), channel_id=1, source_target_pairs={{0,8},{4,12},{8,0},{12,4},{1,9},{5,13},{9,1},{13,5},{2,10},{6,14},... | collective-permute-start | bytes 565256 | tf_op jit(solution)/shard_map/ppermute | solution.py:804
  124.0 5.6 %collective-permute-start.25 = (f32[368,128]{1,0:T(8,128)S(1)}, f32[368,128]{1,0:T(8,128)S(1)}, u32[]{:S(2)}, u32[]{:S(2)}) collective-permute-start(f32[368,128]{1,0:T(8,128)S(1)} %add.11.value), channel_id=1, source_target_pairs={{0,16},{16,0},{1,17},{17,1},{2,18},{18,2},{3,19},{19,3},{4,20},{20... | collective-permute-start | bytes 565256 | tf_op jit(solution)/shard_map/ppermute | solution.py:804
  130.2 1.7 %collective-permute-start.26 = (f32[600,128]{1,0:T(8,128)S(1)}, f32[600,128]{1,0:T(8,128)S(1)}, u32[]{:S(2)}, u32[]{:S(2)}) collective-permute-start(f32[600,128]{1,0:T(8,128)S(1)} %join.1.value), channel_id=1, source_target_pairs={{0,4},{4,0},{8,12},{12,8},{1,5},{5,1},{9,13},{13,9},{2,6},{6,2},{1... | collective-permute-start | bytes 921608 | tf_op jit(solution)/shard_map/ppermute | solution.py:804

commit v9 on v8

--- a/solution.py
+++ b/solution.py
@@ -233,8 +233,6 @@
     nx, ny, nz = counts
     got, faces, outs = refs[:nx], refs[nx : nx + ny], refs[nx + ny :]
     x_len = faces[0].shape[0]
-    for k in range(ny):
-        outs[k][...] = faces[k][...]
     for kind in range(nx):
         place = face_place(sc_ref, 0, kind, x_len - 1)
         for k in range(ny):
@@ -248,8 +246,6 @@
     got_y, refs = refs[:ny][::-1], refs[ny:]
     faces, outs = refs[:nz], refs[nz:]
     x_len, y_len, width = faces[0].shape
-    for k in range(nz):
-        outs[k][...] = faces[k][...]
     for k in range(nz):
         top = takes_top(sc_ref, k)
         for kind in range(nx):
@@ -664,12 +660,10 @@
     write_halves(sc, halving_steps(sizes)[0], grads, keep, send)
 
 
-def last_kernel(counts, sizes, sc, edge_w, node_in, node_out, biases, sums_in, h, slopes, keep, got, *refs):
+def last_kernel(counts, sizes, sc, edge_w, node_in, node_out, biases, sums_in, h, slopes, *refs):
     n = sum(counts)
     halo, (edges, grads) = refs[:n], refs[n:]
-    start = 128 + NODES
-    grads[pl.ds(0, start)] = jnp.zeros((start, 128), f32)
-    grads[pl.ds(start, keep.shape[0])] = keep[...] + got[...]
+    grads[...] = jnp.zeros_like(grads)
     edge_parts(counts, sc, (edge_w,), 0, halo, slopes, edges, grads.at[pl.ds(128, NODES)])
 
     def body(x):
@@ -758,7 +752,9 @@
 
 
 def whole_steps(sizes):
-    return [(2, [hop]) for hop in reversed(hops(sizes[2]))] + [(1, [hop]) for hop in hops(sizes[1])[1:]]
+    along_z = hops(sizes[2])
+    steps = [(2, along_z[k : k + 2]) for k in range(0, len(along_z), 2)]
+    return steps + [(1, [hop]) for hop in hops(sizes[1])[1:]]
 
 
 def padded_rows(rows, sizes):
@@ -797,6 +793,12 @@
         out[pl.ds(0, start)] = value[pl.ds(0, start)] + got[pl.ds(0, start)]
     out[pl.ds(pl.multiple_of(start + bit * half, NODES), half)] = value[pl.ds(start, half)]
     out[pl.ds(pl.multiple_of(start + (1 - bit) * half, NODES), half)] = got[pl.ds(start, half)]
+
+
+def stack_kernel(sc, first, left, right, out):
+    rows = first.shape[0]
+    out[pl.ds(0, rows)] = first[...]
+    out[pl.ds(rows, left.shape[0])] = left[...] + right[...]
 
 
 def swap(value, step):
@@ -909,7 +911,8 @@
 
     def exchange(got_x, faces, work=None, held=(), early=None, early_held=()):
         fix = functools.partial(fix_y_kernel, trades)
-        faces_y = call(fix, "fix_y", (sc, *got_x, *faces[:ny]), [face_y] * ny)
+        same = {1 + nx + k: k for k in range(ny)}
+        faces_y = call(fix, "fix_y", (sc, *got_x, *faces[:ny]), [face_y] * ny, aliases=same)
         if early is not None:
             faces_y, early_held = lax.optimization_barrier((faces_y, early_held))
             keep, send = early(*early_held)
@@ -917,9 +920,11 @@
         if early is not None:
             got_y, (keep, send) = lax.optimization_barrier((got_y, (keep, send)))
             background.add("sums", halve(sc, sizes, keep, send))
+            background.beside(got_y)
         fix = functools.partial(fix_z_kernel, trades)
-        faces_z = call(fix, "fix_z", (sc, *got_x, *got_y[::-1], *faces[ny:]), [face_z] * nz)
-        faces_z = background.beside(background.beside(faces_z))
+        same = {1 + nx + ny + k: k for k in range(nz)}
+        faces_z = call(fix, "fix_z", (sc, *got_x, *got_y[::-1], *faces[ny:]), [face_z] * nz, aliases=same)
+        background.beside(faces_z)
         done = None
         if work is not None:
             faces_z, held = lax.optimization_barrier((faces_z, held))
@@ -973,11 +978,11 @@
     held = (h1, edges1, grad_in, h0, scaled0, act0, dpn0, grads1, bias1)
     halo, _ = exchange(got_x, faces, early=layer_sums, early_held=held)
     tail_rows = width + NODES
+    edges, last = run(
+        last_kernel, "edges0_back", (sums, h0, slopes0, *halo), [full, rows_like(tail_rows)], [], 6, in_place
+    )
     keep, got = background.finish("sums")
-    edges, value = run(
-        last_kernel, "edges0_back", (sums, h0, slopes0, keep, got, *halo), [full, rows_like(tail_rows + keep.shape[0])],
-        [], 6, in_place,
-    )
+    (value,) = call(stack_kernel, "stack", (sc, last, keep, got), [rows_like(tail_rows + keep.shape[0])])
     value, grad_in, dpn0, edges = lax.optimization_barrier((value, grad_in, dpn0, edges))
     (grad0,) = call(
         state_kernel, "state_grad", (sc, edge_weights, node_in, grad_in, dpn0, edges), [full16], [], 4 * matmul

time: 134 us -> 136 us (1.015)
  starting transfers between devices: 51.3 us -> 55 us
  waiting for transfers between devices: 29.6 us -> 27.9 us
    ppermute x7 -> x8, starting transfers between devices: 12.1 us -> 15.8 us  [swap(): lax.ppermute(value, axis, [(i, i ^ step[1]) for i in range(lax.axis_size(...]
    ppermute x7 -> x8, waiting for transfers between devices: 24.4 us -> 23.1 us  [swap(): lax.ppermute(value, axis, [(i, i ^ step[1]) for i in range(lax.axis_size(...]
  transfers between devices with their start and end apart: 27 -> 28, of which waited for: 14 -> 12; matrix products, arithmetic and copies ran while one was open for 0% -> 0% of each run, Pallas kernels for 23% -> 26%
where the time goes in v9:
time: 136 us
  starting transfers between devices  55 us (40%)
  Pallas kernels  48.1 us (35%)
  waiting for transfers between devices  27.9 us (21%)
  local copies, waits for them, and re-layouts  2.84 us (2%)
  between operations  1.67 us (1%)
    pallas_call x28, Pallas kernels, call(): pl.pallas_call(kernel, name=name, out_shape=tuple(outs), in_specs=[SM] +...  48.1 us
    ppermute x20, starting transfers between devices, trade(): lax.ppermute(face, axis, pairs(size, kind))  39.2 us
    ppermute x8, waiting for transfers between devices, swap(): lax.ppermute(value, axis, [(i, i ^ step[1]) for i in range(lax.axis_size(...  23.1 us
    ppermute x8, starting transfers between devices, swap(): lax.ppermute(value, axis, [(i, i ^ step[1]) for i in range(lax.axis_size(...  15.8 us
    ppermute x20, waiting for transfers between devices, trade(): lax.ppermute(face, axis, pairs(size, kind))  4.81 us
    unnamed x16, local copies, waits for them, and re-layouts  2.84 us
  transfers between devices with their start and end apart: 28, of which 12 were waited for; matrix products, arithmetic and copies ran while one was open for 0% of the time, Pallas kernels for 26%

profile of v9, /device:TPU:0, one launch (start us, length us, event | category | flops | bytes accessed | tf_op | source)
XLA Modules:
  0.0 135.7 jit_solution(1506373556403272177)
XLA Ops:
  1.4 1.2 copy-done
  2.6 0.9 copy-done.2
  3.5 0.7 copy-done.7
  4.2 0.8 face0.1
  5.0 3.0 %collective-permute-start = (f32[16,16,128]{2,1,0:T(8,128)S(1)}, f32[16,16,128]{2,1,0:T(8,128)S(1)}, u32[]{:S(2)}, u32[]{:S(2)}) collective-permute-start(f32[16,16,128]{2,1,0:T(8,128)S(1)} %face0.1), channel_id=1, source_target_pairs={{0,16},{16,0},{1,17},{17,1},{2,18},{18,2},{3,19},{19,3},{4,20},{20... | collective-permute-start | bytes 393224 | tf_op jit(solution)/shard_map/ppermute | solution.py:901
  8.0 3.9 %edges0.1 = (f32[16,16,16,128]{3,2,1,0:T(8,128)S(1)}, f32[3,16,16,16,128]{4,3,2,1,0:T(8,128)S(1)}, f32[16,16,128]{2,1,0:T(8,128)S(1)}, f32[16,16,128]{2,1,0:T(8,...) custom-call(s32[4]{0:T(128)S(1)} %pad_add_fusion.sc.sc_ref, bf16[2,2,128,128]{3,2,1,0:T(8,128)(2,1)S(1)} %copy-done.2, ...), custom_call_target="tpu_custom_call" | custom-call | flops 402653184 | bytes 10094608 | tf_op jit(solution)/shard_map/edges0/pallas_call | solution.py:722
  12.5 0.7 collective-permute-start.2
  13.9 0.7 fix_z.4
  14.6 1.6 %collective-permute-start.3 = (f32[16,16,128]{2,1,0:T(8,128)S(1)}, f32[16,16,128]{2,1,0:T(8,128)S(1)}, u32[]{:S(2)}, u32[]{:S(2)}) collective-permute-start(f32[16,16,128]{2,1,0:T(8,128)S(1)} %get-tuple-element.129), channel_id=1, source_target_pairs={{0,1},{1,0},{2,3},{3,2},{4,5},{5,4},{6,7},{7,6},{8,9},{9,8},{10,11... | collective-permute-start | bytes 393224 | tf_op jit(solution)/shard_map/ppermute | solution.py:901
  16.9 2.6 %slopes.2 = f32[3,16,16,16,128]{4,3,2,1,0:T(8,128)S(1)} custom-call(s32[4]{0:T(128)S(1)} %pad_add_fusion.sc.sc_ref, f32[3,16,16,16,128]{4,3,2,1,0:T(8,128)S(1)} %get-tuple-element.131.half_in), custom_call_target="tpu_custom_call", output_to_operand_aliasing={{}: (1, {})} | custom-call | flops 134217728 | bytes 12582928 | tf_op jit(solution)/shard_map/slopes/pallas_call | solution.py:722
  19.7 1.4 %face1.1 = f32[16,16,128]{2,1,0:T(8,128)S(1)} custom-call(s32[4]{0:T(128)S(1)} %pad_add_fusion.sc.sc_ref, bf16[2,2,128,128]{3,2,1,0:T(8,128)(2,1)S(1)} %copy-done.3, bf16[2,256,128]{2,1,0:T(8,128)(2,1)S(1)} %copy-done.4, bf16[2,128,128]{2,1,0:T(8,128)(2,1)S(1)} %copy-done.6, f32[2,2,128]{2,1,0:T(2,128)S(1)} %copy-done.7, ...), custom_call_target="tpu_custom_call" | custom-call | flops 33554432 | bytes 4261904 | tf_op jit(solution)/shard_map/face1/pallas_call | solution.py:722
  21.1 1.4 %collective-permute-start.5 = (f32[16,16,128]{2,1,0:T(8,128)S(1)}, f32[16,16,128]{2,1,0:T(8,128)S(1)}, u32[]{:S(2)}, u32[]{:S(2)}) collective-permute-start(f32[16,16,128]{2,1,0:T(8,128)S(1)} %face1.1), channel_id=1, source_target_pairs={{0,16},{16,0},{1,17},{17,1},{2,18},{18,2},{3,19},{19,3},{4,20},{20... | collective-permute-start | bytes 393224 | tf_op jit(solution)/shard_map/ppermute | solution.py:901
  22.5 6.2 %nodes0_edges1.1 = (f32[16,16,16,128]{3,2,1,0:T(8,128)S(1)}, bf16[16,16,16,128]{3,2,1,0:T(8,128)(2,1)S(1)}, bf16[16,16,16,128]{3,2,1,0:T(8,128)(2,1)S(1)}, f32[1...) custom-call(s32[4]{0:T(128)S(1)} %pad_add_fusion.sc.sc_ref, ...), custom_call_target="tpu_custom_call", output_to_operand_aliasing={{0}: (5, {})} | custom-call | flops 1073741824 | bytes 20383760 | tf_op jit(solution)/shard_map/nodes0_edges1/pallas_call | solution.py:722
  29.2 5.1 %collective-permute-start.6 = (f32[16,16,128]{2,1,0:T(8,128)S(1)}, f32[16,16,128]{2,1,0:T(8,128)S(1)}, u32[]{:S(2)}, u32[]{:S(2)}) collective-permute-start(f32[16,16,128]{2,1,0:T(8,128)S(1)} %get-tuple-element.139), channel_id=1, source_target_pairs={{0,4},{4,0},{8,12},{12,8},{1,5},{5,1},{9,13},{13,9},{2,6},{6,2},{1... | collective-permute-start | bytes 393224 | tf_op jit(solution)/shard_map/ppermute | solution.py:901
  35.3 0.7 fix_z.5
  36.0 4.2 %collective-permute-start.8 = (f32[16,16,128]{2,1,0:T(8,128)S(1)}, f32[16,16,128]{2,1,0:T(8,128)S(1)}, u32[]{:S(2)}, u32[]{:S(2)}) collective-permute-start(f32[16,16,128]{2,1,0:T(8,128)S(1)} %get-tuple-element.146), channel_id=1, source_target_pairs={{0,1},{1,0},{2,3},{3,2},{4,5},{5,4},{6,7},{7,6},{8,9},{9,8},{10,11... | collective-permute-start | bytes 393224 | tf_op jit(solution)/shard_map/ppermute | solution.py:901
  40.9 2.6 %slopes.3 = f32[3,16,16,16,128]{4,3,2,1,0:T(8,128)S(1)} custom-call(s32[4]{0:T(128)S(1)} %pad_add_fusion.sc.sc_ref, f32[3,16,16,16,128]{4,3,2,1,0:T(8,128)S(1)} %get-tuple-element.148.half_in), custom_call_target="tpu_custom_call", output_to_operand_aliasing={{}: (1, {})} | custom-call | flops 134217728 | bytes 12582928 | tf_op jit(solution)/shard_map/slopes/pallas_call | solution.py:722
  43.5 1.2 face2.1
  44.7 0.7 collective-permute-start.10
  45.4 3.6 %nodes1_back.1 = (f32[16,16,16,128]{3,2,1,0:T(8,128)S(1)}, bf16[16,16,16,128]{3,2,1,0:T(8,128)(2,1)S(1)}, bf16[16,16,16,128]{3,2,1,0:T(8,128)(2,1)S(1)}, bf16[16...) custom-call(s32[4]{0:T(128)S(1)} %pad_add_fusion.sc.sc_ref, ...), custom_call_target="tpu_custom_call", output_to_operand_aliasing={{0}: (5, {})} | custom-call | flops 939524096 | bytes 13043728 | tf_op jit(solution)/shard_map/nodes1_back/pallas_call | solution.py:722
  50.3 0.7 collective-permute-start.11
  50.9 8.6 %collective-permute-start.12 = (f32[16,16,128]{2,1,0:T(8,128)S(1)}, f32[16,16,128]{2,1,0:T(8,128)S(1)}, u32[]{:S(2)}, u32[]{:S(2)}) collective-permute-start(f32[16,16,128]{2,1,0:T(8,128)S(1)} %get-tuple-element.156), channel_id=1, source_target_pairs={{0,4},{4,0},{8,12},{12,8},{1,5},{5,1},{9,13},{13,9},{2,6},{6,2},{1... | collective-permute-start | bytes 393224 | tf_op jit(solution)/shard_map/ppermute | solution.py:901
  59.6 1.0 collective-permute-done.12.refs_2_.refs_1_
  60.5 0.7 fix_z.6
  61.2 3.8 %collective-permute-start.13 = (f32[16,16,128]{2,1,0:T(8,128)S(1)}, f32[16,16,128]{2,1,0:T(8,128)S(1)}, u32[]{:S(2)}, u32[]{:S(2)}) collective-permute-start(f32[16,16,128]{2,1,0:T(8,128)S(1)} %get-tuple-element.164), channel_id=1, source_target_pairs={{0,1},{1,0},{2,3},{3,2},{4,5},{5,4},{6,7},{7,6},{8,9},{9,8},{10,11... | collective-permute-start | bytes 393224 | tf_op jit(solution)/shard_map/ppermute | solution.py:901
  65.0 0.8 collective-permute-start.14
  65.9 1.7 %nodes1_products.1 = (f32[16,16,16,128]{3,2,1,0:T(8,128)S(1)}, f32[392,128]{1,0:T(8,128)S(1)}) custom-call(s32[4]{0:T(128)S(1)} %pad_add_fusion.sc.sc_ref, bf16[2,256,128]{2,1,0:T(8,128)(2,1)S(1)} %copy-done.4, bf16[16,16,16,128]{3,2,1,0:T(8,128)(2,1)S(1)} %get-tuple-element.194.h, bf16[16,16,16,128]{3,2,1,0:T(8,128)(2,1)S(1)} %bitcast.14, ...), custom_call_target="tpu_custom_call" | custom-call | flops 805306368 | bytes 7671824 | tf_op jit(solution)/shard_map/nodes1_products/pallas_call | solution.py:722
  67.5 1.0 collective-permute-done.13.refs_3_
  68.5 1.3 face3.1
  69.8 0.8 collective-permute-start.15
  70.6 5.3 %edges1_back_nodes0_back.1 = (f32[16,16,16,128]{3,2,1,0:T(8,128)S(1)}, bf16[16,16,16,128]{3,2,1,0:T(8,128)(2,1)S(1)}, bf16[16,16,16,128]{3,2,1,0:T(8,128)(2,1)S(...) custom-call(s32[4]{0:T(128)S(1)} %pad_add_fusion.sc.sc_ref, ...), custom_call_target="tpu_custom_call", output_to_operand_aliasing={{0}: (5, {})} | custom-call | flops 1207959552 | bytes 20387856 | tf_op jit(solution)/shard_map/edges1_back_nodes0_back/pallas_call | solution.py:722
  77.6 1.7 %gradient_sums.1 = (f32[464,128]{1,0:T(8,128)S(1)}, f32[464,128]{1,0:T(8,128)S(1)}) custom-call(s32[4]{0:T(128)S(1)} %pad_add_fusion.sc.sc_ref, bf16[16,16,16,128]{3,2,1,0:T(8,128)(2,1)S(1)} %get-tuple-element.194.h, f32[16,16,16,128]{3,2,1,0:T(8,128)S(1)} %get-tuple-element.195.edges, bf16[16,16,16,128]{3,2,1,0:T(8,128)(2,1)S(1)} %get-tuple-element.222.grad.grad_in, ...), custom_call_target="tpu_custom_call" | custom-call | flops 671088640 | bytes 9068560 | tf_op jit(solution)/shard_map/gradient_sums/pallas_call | solution.py:722
  79.4 4.6 %collective-permute-start.20 = (f32[464,128]{1,0:T(8,128)S(1)}, f32[464,128]{1,0:T(8,128)S(1)}, u32[]{:S(2)}, u32[]{:S(2)}) collective-permute-start(f32[464,128]{1,0:T(8,128)S(1)} %get-tuple-element.215), channel_id=1, source_target_pairs={{0,4},{4,0},{8,12},{12,8},{1,5},{5,1},{9,13},{13,9},{2,6},{6,2},{1... | collective-permute-start | bytes 712712 | tf_op jit(solution)/shard_map/ppermute | solution.py:806
  83.9 0.7 fix_z.7
  84.6 4.0 %collective-permute-start.18 = (f32[16,16,128]{2,1,0:T(8,128)S(1)}, f32[16,16,128]{2,1,0:T(8,128)S(1)}, u32[]{:S(2)}, u32[]{:S(2)}) collective-permute-start(f32[16,16,128]{2,1,0:T(8,128)S(1)} %get-tuple-element.209), channel_id=1, source_target_pairs={{0,1},{1,0},{2,3},{3,2},{4,5},{5,4},{6,7},{7,6},{8,9},{9,8},{10,11... | collective-permute-start | bytes 393224 | tf_op jit(solution)/shard_map/ppermute | solution.py:901
  89.9 1.4 %collective-permute-start.21 = (f32[232,128]{1,0:T(8,128)S(1)}, f32[232,128]{1,0:T(8,128)S(1)}, u32[]{:S(2)}, u32[]{:S(2)}) collective-permute-start(f32[232,128]{1,0:T(8,128)S(1)} %get-tuple-element.219), channel_id=1, source_target_pairs={{0,16},{16,0},{1,17},{17,1},{2,18},{18,2},{3,19},{19,3},{4,20},{20... | collective-permute-start | bytes 356360 | tf_op jit(solution)/shard_map/ppermute | solution.py:806
  91.3 1.0 collective-permute-done.18.refs_3_
  92.3 3.9 %edges0_back.1 = (f32[16,16,16,128]{3,2,1,0:T(8,128)S(1)}, f32[136,128]{1,0:T(8,128)S(1)}) custom-call(s32[4]{0:T(128)S(1)} %pad_add_fusion.sc.sc_ref, bf16[2,2,128,128]{3,2,1,0:T(8,128)(2,1)S(1)} %copy-done.3, bf16[2,256,128]{2,1,0:T(8,128)(2,1)S(1)} %copy-done.4, bf16[2,128,128]{2,1,0:T(8,128)(2,1)S(1)} %copy-done.6, ...), custom_call_target="tpu_custom_call", output_to_operand_aliasing={{0}: (5, {})} | custom-call | flops 805306368 | bytes 12589072 | tf_op jit(solution)/shard_map/edges0_back/pallas_call | solution.py:722
  96.7 3.0 %collective-permute-start.24 = (f32[368,128]{1,0:T(8,128)S(1)}, f32[368,128]{1,0:T(8,128)S(1)}, u32[]{:S(2)}, u32[]{:S(2)}) collective-permute-start(f32[368,128]{1,0:T(8,128)S(1)} %stack.17.refs_0_), channel_id=1, source_target_pairs={{0,3},{1,2},{2,1},{3,0},{4,7},{5,6},{6,5},{7,4},{8,11},{9,10},{10,... | collective-permute-start | bytes 565256 | tf_op jit(solution)/shard_map/ppermute | solution.py:806
  99.7 2.5 %collective-permute-start.23 = (f32[368,128]{1,0:T(8,128)S(1)}, f32[368,128]{1,0:T(8,128)S(1)}, u32[]{:S(2)}, u32[]{:S(2)}) collective-permute-start(f32[368,128]{1,0:T(8,128)S(1)} %stack.17.refs_0_), channel_id=1, source_target_pairs={{0,2},{1,3},{2,0},{3,1},{4,6},{5,7},{6,4},{7,5},{8,10},{9,11},{10,... | collective-permute-start | bytes 565256 | tf_op jit(solution)/shard_map/ppermute | solution.py:806
  102.4 2.5 %state_grad.1 = bf16[16,16,16,128]{3,2,1,0:T(8,128)(2,1)} custom-call(s32[4]{0:T(128)S(1)} %pad_add_fusion.sc.sc_ref, bf16[2,2,128,128]{3,2,1,0:T(8,128)(2,1)S(1)} %copy-done.3, bf16[2,256,128]{2,1,0:T(8,128)(2,1)S(1)} %copy-done.4, bf16[16,16,16,128]{3,2,1,0:T(8,128)(2,1)S(1)} %get-tuple-element.222.grad.grad_in, ...), custom_call_target="tpu_custom_call" | custom-call | flops 536870912 | bytes 5505040 | tf_op jit(solution)/shard_map/state_grad/pallas_call | solution.py:722
  105.2 11.6 %collective-permute-done.23.refs_2_ = f32[368,128]{1,0:T(8,128)S(1)} collective-permute-done((f32[368,128]{1,0:T(8,128)S(1)}, f32[368,128]{1,0:T(8,128)S(1)}, u32[]{:S(2)}, u32[]{:S(2)}) %collective-permute-start.23) | collective-permute-done | bytes 188448 | tf_op jit(solution)/shard_map/ppermute | solution.py:806
  117.4 2.7 %collective-permute-start.25 = (f32[368,128]{1,0:T(8,128)S(1)}, f32[368,128]{1,0:T(8,128)S(1)}, u32[]{:S(2)}, u32[]{:S(2)}) collective-permute-start(f32[368,128]{1,0:T(8,128)S(1)} %add.8.refs_0_), channel_id=1, source_target_pairs={{0,8},{4,12},{8,0},{12,4},{1,9},{5,13},{9,1},{13,5},{2,10},{6,14},... | collective-permute-start | bytes 565256 | tf_op jit(solution)/shard_map/ppermute | solution.py:806
  120.0 4.9 %collective-permute-done.25.refs_1_ = f32[368,128]{1,0:T(8,128)S(1)} collective-permute-done((f32[368,128]{1,0:T(8,128)S(1)}, f32[368,128]{1,0:T(8,128)S(1)}, u32[]{:S(2)}, u32[]{:S(2)}) %collective-permute-start.25) | collective-permute-done | bytes 188448 | tf_op jit(solution)/shard_map/ppermute | solution.py:806
  125.5 1.4 %collective-permute-start.26 = (f32[368,128]{1,0:T(8,128)S(1)}, f32[368,128]{1,0:T(8,128)S(1)}, u32[]{:S(2)}, u32[]{:S(2)}) collective-permute-start(f32[368,128]{1,0:T(8,128)S(1)} %add.9.value), channel_id=1, source_target_pairs={{0,16},{16,0},{1,17},{17,1},{2,18},{18,2},{3,19},{19,3},{4,20},{20... | collective-permute-start | bytes 565256 | tf_op jit(solution)/shard_map/ppermute | solution.py:806
  126.9 4.8 %collective-permute-done.26.got = f32[368,128]{1,0:T(8,128)S(1)} collective-permute-done((f32[368,128]{1,0:T(8,128)S(1)}, f32[368,128]{1,0:T(8,128)S(1)}, u32[]{:S(2)}, u32[]{:S(2)}) %collective-permute-start.26) | collective-permute-done | bytes 188448 | tf_op jit(solution)/shard_map/ppermute | solution.py:806
  132.4 1.6 %collective-permute-done.27.got = f32[600,128]{1,0:T(8,128)S(1)} collective-permute-done((f32[600,128]{1,0:T(8,128)S(1)}, f32[600,128]{1,0:T(8,128)S(1)}, u32[]{:S(2)}, u32[]{:S(2)}) %collective-permute-start.27) | collective-permute-done | bytes 307232 | tf_op jit(solution)/shard_map/ppermute | solution.py:806
  133.9 1.7 %finish.1 = (f32[2,2,128,128]{3,2,1,0:T(8,128)}, f32[2,256,128]{2,1,0:T(8,128)}, f32[2,128,128]{2,1,0:T(8,128)}, f32[2,2,128]{2,1,0:T(2,128)}) custom-call(s32[4]{0:T(128)S(1)} %pad_add_fusion.sc.sc_ref, bf16[2,2,128,128]{3,2,1,0:T(8,128)(2,1)S(1)} %copy-done.3, bf16[2,256,128]{2,1,0:T(8,128)(2,1)S(1)} %copy-done.4, f32[600,128]{1,0:T(8,128)S(1)} %join.1.value, ...), custom_call_target="tpu_custom_call" | custom-call | bytes 1533968 | tf_op jit(solution)/shard_map/finish/pallas_call | solution.py:722
  (53 shorter events, 11.5 us)
Async XLA Ops:
  1.4 1.2 copy-start
  2.6 0.9 copy-start.2
  3.5 0.7 copy-start.7
  5.0 6.9 %collective-permute-start = (f32[16,16,128]{2,1,0:T(8,128)S(1)}, f32[16,16,128]{2,1,0:T(8,128)S(1)}, u32[]{:S(2)}, u32[]{:S(2)}) collective-permute-start(f32[16,16,128]{2,1,0:T(8,128)S(1)} %face0.1), channel_id=1, source_target_pairs={{0,16},{16,0},{1,17},{17,1},{2,18},{18,2},{3,19},{19,3},{4,20},{20... | collective-permute-start | bytes 393224 | tf_op jit(solution)/shard_map/ppermute | solution.py:901
  12.4 1.4 %collective-permute-start.1 = (f32[16,16,128]{2,1,0:T(8,128)S(1)}, f32[16,16,128]{2,1,0:T(8,128)S(1)}, u32[]{:S(2)}, u32[]{:S(2)}) collective-permute-start(f32[16,16,128]{2,1,0:T(8,128)S(1)} %get-tuple-element.122), channel_id=1, source_target_pairs={{0,4},{4,0},{8,12},{12,8},{1,5},{5,1},{9,13},{13,9},{2,6},{6,2},{1... | collective-permute-start | bytes 393224 | tf_op jit(solution)/shard_map/ppermute | solution.py:901
  12.5 1.3 collective-permute-start.2
  14.5 5.1 %copy-start.1 = (bf16[16,16,2,8,128]{4,3,2,1,0:T(8,128)(2,1)S(1)}, bf16[16,16,2,8,128]{4,3,2,1,0:T(8,128)(2,1)}, u32[]{:S(2)}) copy-start(bf16[16,16,2,8,128]{4,3,2,1,0:T(8,128)(2,1)} %param.7) | copy-start | bytes 3145732
  14.6 5.1 %copy-start.3 = (bf16[2,2,128,128]{3,2,1,0:T(8,128)(2,1)S(1)}, bf16[2,2,128,128]{3,2,1,0:T(8,128)(2,1)}, u32[]{:S(2)}) copy-start(bf16[2,2,128,128]{3,2,1,0:T(8,128)(2,1)} %edge_w.21) | copy-start | bytes 393220
  14.6 5.1 %copy-start.4 = (bf16[2,256,128]{2,1,0:T(8,128)(2,1)S(1)}, bf16[2,256,128]{2,1,0:T(8,128)(2,1)}, u32[]{:S(2)}) copy-start(bf16[2,256,128]{2,1,0:T(8,128)(2,1)} %node_in.19) | copy-start | bytes 393220
  14.6 5.1 %copy-start.6 = (bf16[2,128,128]{2,1,0:T(8,128)(2,1)S(1)}, bf16[2,128,128]{2,1,0:T(8,128)(2,1)}, u32[]{:S(2)}) copy-start(bf16[2,128,128]{2,1,0:T(8,128)(2,1)} %node_out.13) | copy-start | bytes 196612
  14.6 5.0 %collective-permute-start.3 = (f32[16,16,128]{2,1,0:T(8,128)S(1)}, f32[16,16,128]{2,1,0:T(8,128)S(1)}, u32[]{:S(2)}, u32[]{:S(2)}) collective-permute-start(f32[16,16,128]{2,1,0:T(8,128)S(1)} %get-tuple-element.129), channel_id=1, source_target_pairs={{0,1},{1,0},{2,3},{3,2},{4,5},{5,4},{6,7},{7,6},{8,9},{9,8},{10,11... | collective-permute-start | bytes 393224 | tf_op jit(solution)/shard_map/ppermute | solution.py:901
  16.2 3.4 %collective-permute-start.4 = (f32[16,16,128]{2,1,0:T(8,128)S(1)}, f32[16,16,128]{2,1,0:T(8,128)S(1)}, u32[]{:S(2)}, u32[]{:S(2)}) collective-permute-start(f32[16,16,128]{2,1,0:T(8,128)S(1)} %get-tuple-element.130), channel_id=1, source_target_pairs={{1,2},{2,1},{5,6},{6,5},{9,10},{10,9},{13,14},{14,13},{17,18},{18,... | collective-permute-start | bytes 393224 | tf_op jit(solution)/shard_map/ppermute | solution.py:901
  21.1 7.6 %collective-permute-start.5 = (f32[16,16,128]{2,1,0:T(8,128)S(1)}, f32[16,16,128]{2,1,0:T(8,128)S(1)}, u32[]{:S(2)}, u32[]{:S(2)}) collective-permute-start(f32[16,16,128]{2,1,0:T(8,128)S(1)} %face1.1), channel_id=1, source_target_pairs={{0,16},{16,0},{1,17},{17,1},{2,18},{18,2},{3,19},{19,3},{4,20},{20... | collective-permute-start | bytes 393224 | tf_op jit(solution)/shard_map/ppermute | solution.py:901
  29.2 6.1 %collective-permute-start.6 = (f32[16,16,128]{2,1,0:T(8,128)S(1)}, f32[16,16,128]{2,1,0:T(8,128)S(1)}, u32[]{:S(2)}, u32[]{:S(2)}) collective-permute-start(f32[16,16,128]{2,1,0:T(8,128)S(1)} %get-tuple-element.139), channel_id=1, source_target_pairs={{0,4},{4,0},{8,12},{12,8},{1,5},{5,1},{9,13},{13,9},{2,6},{6,2},{1... | collective-permute-start | bytes 393224 | tf_op jit(solution)/shard_map/ppermute | solution.py:901
  34.4 1.0 collective-permute-start.7
  36.0 7.5 %copy-start.5 = (bf16[16,16,2,8,128]{4,3,2,1,0:T(8,128)(2,1)S(1)}, bf16[16,16,2,8,128]{4,3,2,1,0:T(8,128)(2,1)}, u32[]{:S(2)}) copy-start(bf16[16,16,2,8,128]{4,3,2,1,0:T(8,128)(2,1)} %param.8) | copy-start | bytes 3145732
  36.0 7.4 %collective-permute-start.8 = (f32[16,16,128]{2,1,0:T(8,128)S(1)}, f32[16,16,128]{2,1,0:T(8,128)S(1)}, u32[]{:S(2)}, u32[]{:S(2)}) collective-permute-start(f32[16,16,128]{2,1,0:T(8,128)S(1)} %get-tuple-element.146), channel_id=1, source_target_pairs={{0,1},{1,0},{2,3},{3,2},{4,5},{5,4},{6,7},{7,6},{8,9},{9,8},{10,11... | collective-permute-start | bytes 393224 | tf_op jit(solution)/shard_map/ppermute | solution.py:901
  40.2 3.3 %collective-permute-start.9 = (f32[16,16,128]{2,1,0:T(8,128)S(1)}, f32[16,16,128]{2,1,0:T(8,128)S(1)}, u32[]{:S(2)}, u32[]{:S(2)}) collective-permute-start(f32[16,16,128]{2,1,0:T(8,128)S(1)} %get-tuple-element.147), channel_id=1, source_target_pairs={{1,2},{2,1},{5,6},{6,5},{9,10},{10,9},{13,14},{14,13},{17,18},{18,... | collective-permute-start | bytes 393224 | tf_op jit(solution)/shard_map/ppermute | solution.py:901
  44.7 5.0 %collective-permute-start.10 = (f32[16,16,128]{2,1,0:T(8,128)S(1)}, f32[16,16,128]{2,1,0:T(8,128)S(1)}, u32[]{:S(2)}, u32[]{:S(2)}) collective-permute-start(f32[16,16,128]{2,1,0:T(8,128)S(1)} %face2.1), channel_id=1, source_target_pairs={{0,16},{16,0},{1,17},{17,1},{2,18},{18,2},{3,19},{19,3},{4,20},{20... | collective-permute-start | bytes 393224 | tf_op jit(solution)/shard_map/ppermute | solution.py:901
  50.3 9.3 %collective-permute-start.11 = (f32[16,16,128]{2,1,0:T(8,128)S(1)}, f32[16,16,128]{2,1,0:T(8,128)S(1)}, u32[]{:S(2)}, u32[]{:S(2)}) collective-permute-start(f32[16,16,128]{2,1,0:T(8,128)S(1)} %get-tuple-element.155), channel_id=1, source_target_pairs={{4,8},{8,4},{5,9},{9,5},{6,10},{10,6},{7,11},{11,7},{20,24},{24,20... | collective-permute-start | bytes 393224 | tf_op jit(solution)/shard_map/ppermute | solution.py:901
  50.9 9.6 %collective-permute-start.12 = (f32[16,16,128]{2,1,0:T(8,128)S(1)}, f32[16,16,128]{2,1,0:T(8,128)S(1)}, u32[]{:S(2)}, u32[]{:S(2)}) collective-permute-start(f32[16,16,128]{2,1,0:T(8,128)S(1)} %get-tuple-element.156), channel_id=1, source_target_pairs={{0,4},{4,0},{8,12},{12,8},{1,5},{5,1},{9,13},{13,9},{2,6},{6,2},{1... | collective-permute-start | bytes 393224 | tf_op jit(solution)/shard_map/ppermute | solution.py:901
  61.2 7.3 %collective-permute-start.13 = (f32[16,16,128]{2,1,0:T(8,128)S(1)}, f32[16,16,128]{2,1,0:T(8,128)S(1)}, u32[]{:S(2)}, u32[]{:S(2)}) collective-permute-start(f32[16,16,128]{2,1,0:T(8,128)S(1)} %get-tuple-element.164), channel_id=1, source_target_pairs={{0,1},{1,0},{2,3},{3,2},{4,5},{5,4},{6,7},{7,6},{8,9},{9,8},{10,11... | collective-permute-start | bytes 393224 | tf_op jit(solution)/shard_map/ppermute | solution.py:901
  65.0 3.5 %collective-permute-start.14 = (f32[16,16,128]{2,1,0:T(8,128)S(1)}, f32[16,16,128]{2,1,0:T(8,128)S(1)}, u32[]{:S(2)}, u32[]{:S(2)}) collective-permute-start(f32[16,16,128]{2,1,0:T(8,128)S(1)} %get-tuple-element.165), channel_id=1, source_target_pairs={{1,2},{2,1},{5,6},{6,5},{9,10},{10,9},{13,14},{14,13},{17,18},{18,... | collective-permute-start | bytes 393224 | tf_op jit(solution)/shard_map/ppermute | solution.py:901
  69.8 6.2 %collective-permute-start.15 = (f32[16,16,128]{2,1,0:T(8,128)S(1)}, f32[16,16,128]{2,1,0:T(8,128)S(1)}, u32[]{:S(2)}, u32[]{:S(2)}) collective-permute-start(f32[16,16,128]{2,1,0:T(8,128)S(1)} %face3.1), channel_id=1, source_target_pairs={{0,16},{16,0},{1,17},{17,1},{2,18},{18,2},{3,19},{19,3},{4,20},{20... | collective-permute-start | bytes 393224 | tf_op jit(solution)/shard_map/ppermute | solution.py:901
  76.5 2.8 %collective-permute-start.16 = (f32[16,16,128]{2,1,0:T(8,128)S(1)}, f32[16,16,128]{2,1,0:T(8,128)S(1)}, u32[]{:S(2)}, u32[]{:S(2)}) collective-permute-start(f32[16,16,128]{2,1,0:T(8,128)S(1)} %get-tuple-element.192), channel_id=1, source_target_pairs={{0,4},{4,0},{8,12},{12,8},{1,5},{5,1},{9,13},{13,9},{2,6},{6,2},{1... | collective-permute-start | bytes 393224 | tf_op jit(solution)/shard_map/ppermute | solution.py:901
  77.0 2.4 %collective-permute-start.17 = (f32[16,16,128]{2,1,0:T(8,128)S(1)}, f32[16,16,128]{2,1,0:T(8,128)S(1)}, u32[]{:S(2)}, u32[]{:S(2)}) collective-permute-start(f32[16,16,128]{2,1,0:T(8,128)S(1)} %get-tuple-element.193), channel_id=1, source_target_pairs={{4,8},{8,4},{5,9},{9,5},{6,10},{10,6},{7,11},{11,7},{20,24},{24,20... | collective-permute-start | bytes 393224 | tf_op jit(solution)/shard_map/ppermute | solution.py:901
  79.4 9.9 %collective-permute-start.20 = (f32[464,128]{1,0:T(8,128)S(1)}, f32[464,128]{1,0:T(8,128)S(1)}, u32[]{:S(2)}, u32[]{:S(2)}) collective-permute-start(f32[464,128]{1,0:T(8,128)S(1)} %get-tuple-element.215), channel_id=1, source_target_pairs={{0,4},{4,0},{8,12},{12,8},{1,5},{5,1},{9,13},{13,9},{2,6},{6,2},{1... | collective-permute-start | bytes 712712 | tf_op jit(solution)/shard_map/ppermute | solution.py:806
  84.6 7.7 %collective-permute-start.18 = (f32[16,16,128]{2,1,0:T(8,128)S(1)}, f32[16,16,128]{2,1,0:T(8,128)S(1)}, u32[]{:S(2)}, u32[]{:S(2)}) collective-permute-start(f32[16,16,128]{2,1,0:T(8,128)S(1)} %get-tuple-element.209), channel_id=1, source_target_pairs={{0,1},{1,0},{2,3},{3,2},{4,5},{5,4},{6,7},{7,6},{8,9},{9,8},{10,11... | collective-permute-start | bytes 393224 | tf_op jit(solution)/shard_map/ppermute | solution.py:901
  88.6 3.7 %collective-permute-start.19 = (f32[16,16,128]{2,1,0:T(8,128)S(1)}, f32[16,16,128]{2,1,0:T(8,128)S(1)}, u32[]{:S(2)}, u32[]{:S(2)}) collective-permute-start(f32[16,16,128]{2,1,0:T(8,128)S(1)} %get-tuple-element.210), channel_id=1, source_target_pairs={{1,2},{2,1},{5,6},{6,5},{9,10},{10,9},{13,14},{14,13},{17,18},{18,... | collective-permute-start | bytes 393224 | tf_op jit(solution)/shard_map/ppermute | solution.py:901
  89.9 6.3 %collective-permute-start.21 = (f32[232,128]{1,0:T(8,128)S(1)}, f32[232,128]{1,0:T(8,128)S(1)}, u32[]{:S(2)}, u32[]{:S(2)}) collective-permute-start(f32[232,128]{1,0:T(8,128)S(1)} %get-tuple-element.219), channel_id=1, source_target_pairs={{0,16},{16,0},{1,17},{17,1},{2,18},{18,2},{3,19},{19,3},{4,20},{20... | collective-permute-start | bytes 356360 | tf_op jit(solution)/shard_map/ppermute | solution.py:806
  96.7 8.5 %collective-permute-start.24 = (f32[368,128]{1,0:T(8,128)S(1)}, f32[368,128]{1,0:T(8,128)S(1)}, u32[]{:S(2)}, u32[]{:S(2)}) collective-permute-start(f32[368,128]{1,0:T(8,128)S(1)} %stack.17.refs_0_), channel_id=1, source_target_pairs={{0,3},{1,2},{2,1},{3,0},{4,7},{5,6},{6,5},{7,4},{8,11},{9,10},{10,... | collective-permute-start | bytes 565256 | tf_op jit(solution)/shard_map/ppermute | solution.py:806
  99.7 17.1 %collective-permute-start.23 = (f32[368,128]{1,0:T(8,128)S(1)}, f32[368,128]{1,0:T(8,128)S(1)}, u32[]{:S(2)}, u32[]{:S(2)}) collective-permute-start(f32[368,128]{1,0:T(8,128)S(1)} %stack.17.refs_0_), channel_id=1, source_target_pairs={{0,2},{1,3},{2,0},{3,1},{4,6},{5,7},{6,4},{7,5},{8,10},{9,11},{10,... | collective-permute-start | bytes 565256 | tf_op jit(solution)/shard_map/ppermute | solution.py:806
  102.2 14.6 %collective-permute-start.22 = (f32[368,128]{1,0:T(8,128)S(1)}, f32[368,128]{1,0:T(8,128)S(1)}, u32[]{:S(2)}, u32[]{:S(2)}) collective-permute-start(f32[368,128]{1,0:T(8,128)S(1)} %stack.17.refs_0_), channel_id=1, source_target_pairs={{0,1},{1,0},{2,3},{3,2},{4,5},{5,4},{6,7},{7,6},{8,9},{9,8},{10,11... | collective-permute-start | bytes 565256 | tf_op jit(solution)/shard_map/ppermute | solution.py:806
  117.4 7.6 %collective-permute-start.25 = (f32[368,128]{1,0:T(8,128)S(1)}, f32[368,128]{1,0:T(8,128)S(1)}, u32[]{:S(2)}, u32[]{:S(2)}) collective-permute-start(f32[368,128]{1,0:T(8,128)S(1)} %add.8.refs_0_), channel_id=1, source_target_pairs={{0,8},{4,12},{8,0},{12,4},{1,9},{5,13},{9,1},{13,5},{2,10},{6,14},... | collective-permute-start | bytes 565256 | tf_op jit(solution)/shard_map/ppermute | solution.py:806
  125.5 6.2 %collective-permute-start.26 = (f32[368,128]{1,0:T(8,128)S(1)}, f32[368,128]{1,0:T(8,128)S(1)}, u32[]{:S(2)}, u32[]{:S(2)}) collective-permute-start(f32[368,128]{1,0:T(8,128)S(1)} %add.9.value), channel_id=1, source_target_pairs={{0,16},{16,0},{1,17},{17,1},{2,18},{18,2},{3,19},{19,3},{4,20},{20... | collective-permute-start | bytes 565256 | tf_op jit(solution)/shard_map/ppermute | solution.py:806
  132.3 1.7 %collective-permute-start.27 = (f32[600,128]{1,0:T(8,128)S(1)}, f32[600,128]{1,0:T(8,128)S(1)}, u32[]{:S(2)}, u32[]{:S(2)}) collective-permute-start(f32[600,128]{1,0:T(8,128)S(1)} %join.1.value), channel_id=1, source_target_pairs={{0,4},{4,0},{8,12},{12,8},{1,5},{5,1},{9,13},{13,9},{2,6},{6,2},{1... | collective-permute-start | bytes 921608 | tf_op jit(solution)/shard_map/ppermute | solution.py:806

commit v10 on v9

--- a/solution.py
+++ b/solution.py
@@ -1,5 +1,4 @@
 import functools
-import itertools
 import math
 
 import jax
@@ -748,13 +747,9 @@
 
 
 def halving_steps(sizes):
-    return [(1, hop) for hop in hops(sizes[1])[:1]] + [(0, hop) for hop in hops(sizes[0])]
-
-
-def whole_steps(sizes):
-    along_z = hops(sizes[2])
-    steps = [(2, along_z[k : k + 2]) for k in range(0, len(along_z), 2)]
-    return steps + [(1, [hop]) for hop in hops(sizes[1])[1:]]
+    steps = [(1, hop) for hop in hops(sizes[1])[:1]]
+    steps += [(0, hop) for hop in hops(sizes[0])]
+    return steps + [(1, hop) for hop in hops(sizes[1])[1:]]
 
 
 def padded_rows(rows, sizes):
@@ -779,11 +774,8 @@
     write_halves(sc, step, total, keep, send)
 
 
-def add_kernel(sc, *refs):
-    total = refs[0][...] + refs[1][...]
-    for ref in refs[2:-1]:
-        total = total + ref[...]
-    refs[-1][...] = total
+def add_kernel(sc, left, right, out):
+    out[...] = left[...] + right[...]
 
 
 def join_kernel_of(step, start, sc, value, got, out):
@@ -987,10 +979,8 @@
     (grad0,) = call(
         state_kernel, "state_grad", (sc, edge_weights, node_in, grad_in, dpn0, edges), [full16], [], 4 * matmul
     )
-    for axis, together in whole_steps(sizes):
-        partners = [sum(c) for n in range(1, len(together) + 1) for c in itertools.combinations(together, n)]
-        got = [swap(value, (axis, partner)) for partner in partners]
-        (value,) = call(add_kernel, "add", (sc, value, *got), [rows_like(value.shape[0])])
+    for hop in reversed(hops(sizes[2])):
+        (value,) = call(add_kernel, "add", (sc, value, swap(value, (2, hop))), [rows_like(value.shape[0])])
         value, grad0 = lax.optimization_barrier((value, grad0))
     first, *rest = halving_steps(sizes)
     for step in reversed(rest):

time: 136 us -> 133 us (0.978)
  starting transfers between devices: 55 us -> 52.5 us
  waiting for transfers between devices: 27.9 us -> 26.2 us
    ppermute x8, starting transfers between devices: 15.8 us -> 13.3 us  [swap(): lax.ppermute(value, axis, [(i, i ^ step[1]) for i in range(lax.axis_size(...]
    ppermute x8, waiting for transfers between devices: 23.1 us -> 21.4 us  [swap(): lax.ppermute(value, axis, [(i, i ^ step[1]) for i in range(lax.axis_size(...]
    pallas_call x28 -> x30, Pallas kernels: 48.1 us -> 49.2 us  [call(): pl.pallas_call(kernel, name=name, out_shape=tuple(outs), in_specs=[SM] +...]
  transfers between devices with their start and end apart: 28 -> 28, of which waited for: 12 -> 14; matrix products, arithmetic and copies ran while one was open for 0% -> 0% of each run, Pallas kernels for 26% -> 27%
where the time goes in v10:
time: 133 us
  starting transfers between devices  52.5 us (39%)
  Pallas kernels  49.2 us (37%)
  waiting for transfers between devices  26.2 us (20%)
  local copies, waits for them, and re-layouts  2.84 us (2%)
  between operations  1.71 us (1%)
    pallas_call x30, Pallas kernels, call(): pl.pallas_call(kernel, name=name, out_shape=tuple(outs), in_specs=[SM] +...  49.2 us
    ppermute x20, starting transfers between devices, trade(): lax.ppermute(face, axis, pairs(size, kind))  39.2 us
    ppermute x8, waiting for transfers between devices, swap(): lax.ppermute(value, axis, [(i, i ^ step[1]) for i in range(lax.axis_size(...  21.4 us
    ppermute x8, starting transfers between devices, swap(): lax.ppermute(value, axis, [(i, i ^ step[1]) for i in range(lax.axis_size(...  13.3 us
    ppermute x20, waiting for transfers between devices, trade(): lax.ppermute(face, axis, pairs(size, kind))  4.84 us
    unnamed x16, local copies, waits for them, and re-layouts  2.84 us
  transfers between devices with their start and end apart: 28, of which 14 were waited for; matrix products, arithmetic and copies ran while one was open for 0% of the time, Pallas kernels for 27%

profile of v10, /device:TPU:0, one launch (start us, length us, event | category | flops | bytes accessed | tf_op | source)
XLA Modules:
  0.0 132.5 jit_solution(12325994347630897627)
XLA Ops:
  1.4 1.2 copy-done
  2.6 0.9 copy-done.2
  3.5 0.7 copy-done.7
  4.2 0.8 face0.1
  5.0 3.0 %collective-permute-start = (f32[16,16,128]{2,1,0:T(8,128)S(1)}, f32[16,16,128]{2,1,0:T(8,128)S(1)}, u32[]{:S(2)}, u32[]{:S(2)}) collective-permute-start(f32[16,16,128]{2,1,0:T(8,128)S(1)} %face0.1), channel_id=1, source_target_pairs={{0,16},{16,0},{1,17},{17,1},{2,18},{18,2},{3,19},{19,3},{4,20},{20... | collective-permute-start | bytes 393224 | tf_op jit(solution)/shard_map/ppermute | solution.py:893
  8.0 3.9 %edges0.1 = (f32[16,16,16,128]{3,2,1,0:T(8,128)S(1)}, f32[3,16,16,16,128]{4,3,2,1,0:T(8,128)S(1)}, f32[16,16,128]{2,1,0:T(8,128)S(1)}, f32[16,16,128]{2,1,0:T(8,...) custom-call(s32[4]{0:T(128)S(1)} %pad_add_fusion.sc.sc_ref, bf16[2,2,128,128]{3,2,1,0:T(8,128)(2,1)S(1)} %copy-done.2, ...), custom_call_target="tpu_custom_call" | custom-call | flops 402653184 | bytes 10094608 | tf_op jit(solution)/shard_map/edges0/pallas_call | solution.py:721
  12.5 0.7 collective-permute-start.2
  13.9 0.7 fix_z.4
  14.6 1.6 %collective-permute-start.3 = (f32[16,16,128]{2,1,0:T(8,128)S(1)}, f32[16,16,128]{2,1,0:T(8,128)S(1)}, u32[]{:S(2)}, u32[]{:S(2)}) collective-permute-start(f32[16,16,128]{2,1,0:T(8,128)S(1)} %get-tuple-element.131), channel_id=1, source_target_pairs={{0,1},{1,0},{2,3},{3,2},{4,5},{5,4},{6,7},{7,6},{8,9},{9,8},{10,11... | collective-permute-start | bytes 393224 | tf_op jit(solution)/shard_map/ppermute | solution.py:893
  16.9 2.6 %slopes.2 = f32[3,16,16,16,128]{4,3,2,1,0:T(8,128)S(1)} custom-call(s32[4]{0:T(128)S(1)} %pad_add_fusion.sc.sc_ref, f32[3,16,16,16,128]{4,3,2,1,0:T(8,128)S(1)} %get-tuple-element.133.half_in), custom_call_target="tpu_custom_call", output_to_operand_aliasing={{}: (1, {})} | custom-call | flops 134217728 | bytes 12582928 | tf_op jit(solution)/shard_map/slopes/pallas_call | solution.py:721
  19.7 1.4 %face1.1 = f32[16,16,128]{2,1,0:T(8,128)S(1)} custom-call(s32[4]{0:T(128)S(1)} %pad_add_fusion.sc.sc_ref, bf16[2,2,128,128]{3,2,1,0:T(8,128)(2,1)S(1)} %copy-done.3, bf16[2,256,128]{2,1,0:T(8,128)(2,1)S(1)} %copy-done.4, bf16[2,128,128]{2,1,0:T(8,128)(2,1)S(1)} %copy-done.6, f32[2,2,128]{2,1,0:T(2,128)S(1)} %copy-done.7, ...), custom_call_target="tpu_custom_call" | custom-call | flops 33554432 | bytes 4261904 | tf_op jit(solution)/shard_map/face1/pallas_call | solution.py:721
  21.1 1.4 %collective-permute-start.5 = (f32[16,16,128]{2,1,0:T(8,128)S(1)}, f32[16,16,128]{2,1,0:T(8,128)S(1)}, u32[]{:S(2)}, u32[]{:S(2)}) collective-permute-start(f32[16,16,128]{2,1,0:T(8,128)S(1)} %face1.1), channel_id=1, source_target_pairs={{0,16},{16,0},{1,17},{17,1},{2,18},{18,2},{3,19},{19,3},{4,20},{20... | collective-permute-start | bytes 393224 | tf_op jit(solution)/shard_map/ppermute | solution.py:893
  22.5 6.2 %nodes0_edges1.1 = (f32[16,16,16,128]{3,2,1,0:T(8,128)S(1)}, bf16[16,16,16,128]{3,2,1,0:T(8,128)(2,1)S(1)}, bf16[16,16,16,128]{3,2,1,0:T(8,128)(2,1)S(1)}, f32[1...) custom-call(s32[4]{0:T(128)S(1)} %pad_add_fusion.sc.sc_ref, ...), custom_call_target="tpu_custom_call", output_to_operand_aliasing={{0}: (5, {})} | custom-call | flops 1073741824 | bytes 20383760 | tf_op jit(solution)/shard_map/nodes0_edges1/pallas_call | solution.py:721
  29.2 5.1 %collective-permute-start.6 = (f32[16,16,128]{2,1,0:T(8,128)S(1)}, f32[16,16,128]{2,1,0:T(8,128)S(1)}, u32[]{:S(2)}, u32[]{:S(2)}) collective-permute-start(f32[16,16,128]{2,1,0:T(8,128)S(1)} %get-tuple-element.141), channel_id=1, source_target_pairs={{0,4},{4,0},{8,12},{12,8},{1,5},{5,1},{9,13},{13,9},{2,6},{6,2},{1... | collective-permute-start | bytes 393224 | tf_op jit(solution)/shard_map/ppermute | solution.py:893
  35.3 0.7 fix_z.5
  36.0 4.2 %collective-permute-start.8 = (f32[16,16,128]{2,1,0:T(8,128)S(1)}, f32[16,16,128]{2,1,0:T(8,128)S(1)}, u32[]{:S(2)}, u32[]{:S(2)}) collective-permute-start(f32[16,16,128]{2,1,0:T(8,128)S(1)} %get-tuple-element.148), channel_id=1, source_target_pairs={{0,1},{1,0},{2,3},{3,2},{4,5},{5,4},{6,7},{7,6},{8,9},{9,8},{10,11... | collective-permute-start | bytes 393224 | tf_op jit(solution)/shard_map/ppermute | solution.py:893
  40.9 2.6 %slopes.3 = f32[3,16,16,16,128]{4,3,2,1,0:T(8,128)S(1)} custom-call(s32[4]{0:T(128)S(1)} %pad_add_fusion.sc.sc_ref, f32[3,16,16,16,128]{4,3,2,1,0:T(8,128)S(1)} %get-tuple-element.150.half_in), custom_call_target="tpu_custom_call", output_to_operand_aliasing={{}: (1, {})} | custom-call | flops 134217728 | bytes 12582928 | tf_op jit(solution)/shard_map/slopes/pallas_call | solution.py:721
  43.5 1.2 face2.1
  44.7 0.7 collective-permute-start.10
  45.4 3.6 %nodes1_back.1 = (f32[16,16,16,128]{3,2,1,0:T(8,128)S(1)}, bf16[16,16,16,128]{3,2,1,0:T(8,128)(2,1)S(1)}, bf16[16,16,16,128]{3,2,1,0:T(8,128)(2,1)S(1)}, bf16[16...) custom-call(s32[4]{0:T(128)S(1)} %pad_add_fusion.sc.sc_ref, ...), custom_call_target="tpu_custom_call", output_to_operand_aliasing={{0}: (5, {})} | custom-call | flops 939524096 | bytes 13043728 | tf_op jit(solution)/shard_map/nodes1_back/pallas_call | solution.py:721
  50.3 0.7 collective-permute-start.11
  50.9 8.6 %collective-permute-start.12 = (f32[16,16,128]{2,1,0:T(8,128)S(1)}, f32[16,16,128]{2,1,0:T(8,128)S(1)}, u32[]{:S(2)}, u32[]{:S(2)}) collective-permute-start(f32[16,16,128]{2,1,0:T(8,128)S(1)} %get-tuple-element.158), channel_id=1, source_target_pairs={{0,4},{4,0},{8,12},{12,8},{1,5},{5,1},{9,13},{13,9},{2,6},{6,2},{1... | collective-permute-start | bytes 393224 | tf_op jit(solution)/shard_map/ppermute | solution.py:893
  59.6 1.0 collective-permute-done.12.refs_2_.refs_1_
  61.2 3.8 %collective-permute-start.13 = (f32[16,16,128]{2,1,0:T(8,128)S(1)}, f32[16,16,128]{2,1,0:T(8,128)S(1)}, u32[]{:S(2)}, u32[]{:S(2)}) collective-permute-start(f32[16,16,128]{2,1,0:T(8,128)S(1)} %get-tuple-element.166), channel_id=1, source_target_pairs={{0,1},{1,0},{2,3},{3,2},{4,5},{5,4},{6,7},{7,6},{8,9},{9,8},{10,11... | collective-permute-start | bytes 393224 | tf_op jit(solution)/shard_map/ppermute | solution.py:893
  65.0 0.8 collective-permute-start.14
  65.9 1.6 %nodes1_products.1 = (f32[16,16,16,128]{3,2,1,0:T(8,128)S(1)}, f32[392,128]{1,0:T(8,128)S(1)}) custom-call(s32[4]{0:T(128)S(1)} %pad_add_fusion.sc.sc_ref, bf16[2,256,128]{2,1,0:T(8,128)(2,1)S(1)} %copy-done.4, bf16[16,16,16,128]{3,2,1,0:T(8,128)(2,1)S(1)} %get-tuple-element.196.h, bf16[16,16,16,128]{3,2,1,0:T(8,128)(2,1)S(1)} %bitcast.14, ...), custom_call_target="tpu_custom_call" | custom-call | flops 805306368 | bytes 7671824 | tf_op jit(solution)/shard_map/nodes1_products/pallas_call | solution.py:721
  67.5 1.0 collective-permute-done.13.refs_3_
  68.5 1.3 face3.1
  69.8 0.8 collective-permute-start.15
  70.6 5.3 %edges1_back_nodes0_back.1 = (f32[16,16,16,128]{3,2,1,0:T(8,128)S(1)}, bf16[16,16,16,128]{3,2,1,0:T(8,128)(2,1)S(1)}, bf16[16,16,16,128]{3,2,1,0:T(8,128)(2,1)S(...) custom-call(s32[4]{0:T(128)S(1)} %pad_add_fusion.sc.sc_ref, ...), custom_call_target="tpu_custom_call", output_to_operand_aliasing={{0}: (5, {})} | custom-call | flops 1207959552 | bytes 20387856 | tf_op jit(solution)/shard_map/edges1_back_nodes0_back/pallas_call | solution.py:721
  77.7 1.7 %gradient_sums.1 = (f32[480,128]{1,0:T(8,128)S(1)}, f32[480,128]{1,0:T(8,128)S(1)}) custom-call(s32[4]{0:T(128)S(1)} %pad_add_fusion.sc.sc_ref, bf16[16,16,16,128]{3,2,1,0:T(8,128)(2,1)S(1)} %get-tuple-element.196.h, f32[16,16,16,128]{3,2,1,0:T(8,128)S(1)} %get-tuple-element.197.edges, bf16[16,16,16,128]{3,2,1,0:T(8,128)(2,1)S(1)} %get-tuple-element.226.grad.grad_in, ...), custom_call_target="tpu_custom_call" | custom-call | flops 671088640 | bytes 9084944 | tf_op jit(solution)/shard_map/gradient_sums/pallas_call | solution.py:721
  79.4 4.5 %collective-permute-start.20 = (f32[480,128]{1,0:T(8,128)S(1)}, f32[480,128]{1,0:T(8,128)S(1)}, u32[]{:S(2)}, u32[]{:S(2)}) collective-permute-start(f32[480,128]{1,0:T(8,128)S(1)} %get-tuple-element.217), channel_id=1, source_target_pairs={{0,4},{4,0},{8,12},{12,8},{1,5},{5,1},{9,13},{13,9},{2,6},{6,2},{1... | collective-permute-start | bytes 737288 | tf_op jit(solution)/shard_map/ppermute | solution.py:798
  83.9 0.7 fix_z.7
  84.6 4.0 %collective-permute-start.18 = (f32[16,16,128]{2,1,0:T(8,128)S(1)}, f32[16,16,128]{2,1,0:T(8,128)S(1)}, u32[]{:S(2)}, u32[]{:S(2)}) collective-permute-start(f32[16,16,128]{2,1,0:T(8,128)S(1)} %get-tuple-element.211), channel_id=1, source_target_pairs={{0,1},{1,0},{2,3},{3,2},{4,5},{5,4},{6,7},{7,6},{8,9},{9,8},{10,11... | collective-permute-start | bytes 393224 | tf_op jit(solution)/shard_map/ppermute | solution.py:893
  89.9 1.4 %collective-permute-start.21 = (f32[240,128]{1,0:T(8,128)S(1)}, f32[240,128]{1,0:T(8,128)S(1)}, u32[]{:S(2)}, u32[]{:S(2)}) collective-permute-start(f32[240,128]{1,0:T(8,128)S(1)} %get-tuple-element.221), channel_id=1, source_target_pairs={{0,16},{16,0},{1,17},{17,1},{2,18},{18,2},{3,19},{19,3},{4,20},{20... | collective-permute-start | bytes 368648 | tf_op jit(solution)/shard_map/ppermute | solution.py:798
  91.3 1.0 collective-permute-done.18.refs_3_
  92.3 2.6 %collective-permute-done.21.got = f32[240,128]{1,0:T(8,128)S(1)} collective-permute-done((f32[240,128]{1,0:T(8,128)S(1)}, f32[240,128]{1,0:T(8,128)S(1)}, u32[]{:S(2)}, u32[]{:S(2)}) %collective-permute-start.21) | collective-permute-done | bytes 122912 | tf_op jit(solution)/shard_map/ppermute | solution.py:798
  95.5 2.2 %collective-permute-start.22 = (f32[120,128]{1,0:T(8,128)S(1)}, f32[120,128]{1,0:T(8,128)S(1)}, u32[]{:S(2)}, u32[]{:S(2)}) collective-permute-start(f32[120,128]{1,0:T(8,128)S(1)} %get-tuple-element.223), channel_id=1, source_target_pairs={{0,8},{4,12},{8,0},{12,4},{1,9},{5,13},{9,1},{13,5},{2,10},{6,14},... | collective-permute-start | bytes 184328 | tf_op jit(solution)/shard_map/ppermute | solution.py:798
  97.7 3.9 %edges0_back.1 = (f32[16,16,16,128]{3,2,1,0:T(8,128)S(1)}, f32[136,128]{1,0:T(8,128)S(1)}) custom-call(s32[4]{0:T(128)S(1)} %pad_add_fusion.sc.sc_ref, bf16[2,2,128,128]{3,2,1,0:T(8,128)(2,1)S(1)} %copy-done.3, bf16[2,256,128]{2,1,0:T(8,128)(2,1)S(1)} %copy-done.4, bf16[2,128,128]{2,1,0:T(8,128)(2,1)S(1)} %copy-done.6, ...), custom_call_target="tpu_custom_call", output_to_operand_aliasing={{0}: (5, {})} | custom-call | flops 805306368 | bytes 12589072 | tf_op jit(solution)/shard_map/edges0_back/pallas_call | solution.py:721
  102.1 3.1 %collective-permute-start.23 = (f32[256,128]{1,0:T(8,128)S(1)}, f32[256,128]{1,0:T(8,128)S(1)}, u32[]{:S(2)}, u32[]{:S(2)}) collective-permute-start(f32[256,128]{1,0:T(8,128)S(1)} %stack.17.left), channel_id=1, source_target_pairs={{0,2},{1,3},{2,0},{3,1},{4,6},{5,7},{6,4},{7,5},{8,10},{9,11},{10,... | collective-permute-start | bytes 393224 | tf_op jit(solution)/shard_map/ppermute | solution.py:798
  105.2 2.5 %state_grad.1 = bf16[16,16,16,128]{3,2,1,0:T(8,128)(2,1)} custom-call(s32[4]{0:T(128)S(1)} %pad_add_fusion.sc.sc_ref, bf16[2,2,128,128]{3,2,1,0:T(8,128)(2,1)S(1)} %copy-done.3, bf16[2,256,128]{2,1,0:T(8,128)(2,1)S(1)} %copy-done.4, bf16[16,16,16,128]{3,2,1,0:T(8,128)(2,1)S(1)} %get-tuple-element.226.grad.grad_in, ...), custom_call_target="tpu_custom_call" | custom-call | flops 536870912 | bytes 5505040 | tf_op jit(solution)/shard_map/state_grad/pallas_call | solution.py:721
  107.7 3.4 %collective-permute-done.23.right = f32[256,128]{1,0:T(8,128)S(1)} collective-permute-done((f32[256,128]{1,0:T(8,128)S(1)}, f32[256,128]{1,0:T(8,128)S(1)}, u32[]{:S(2)}, u32[]{:S(2)}) %collective-permute-start.23) | collective-permute-done | bytes 131104 | tf_op jit(solution)/shard_map/ppermute | solution.py:798
  111.9 4.8 %collective-permute-done.24.right = f32[256,128]{1,0:T(8,128)S(1)} collective-permute-done((f32[256,128]{1,0:T(8,128)S(1)}, f32[256,128]{1,0:T(8,128)S(1)}, u32[]{:S(2)}, u32[]{:S(2)}) %collective-permute-start.24) | collective-permute-done | bytes 131104 | tf_op jit(solution)/shard_map/ppermute | solution.py:798
  117.6 4.7 %collective-permute-done.25.got = f32[256,128]{1,0:T(8,128)S(1)} collective-permute-done((f32[256,128]{1,0:T(8,128)S(1)}, f32[256,128]{1,0:T(8,128)S(1)}, u32[]{:S(2)}, u32[]{:S(2)}) %collective-permute-start.25) | collective-permute-done | bytes 131104 | tf_op jit(solution)/shard_map/ppermute | solution.py:798
  122.9 1.4 %collective-permute-start.26 = (f32[376,128]{1,0:T(8,128)S(1)}, f32[376,128]{1,0:T(8,128)S(1)}, u32[]{:S(2)}, u32[]{:S(2)}) collective-permute-start(f32[376,128]{1,0:T(8,128)S(1)} %join.2.value), channel_id=1, source_target_pairs={{0,16},{16,0},{1,17},{17,1},{2,18},{18,2},{3,19},{19,3},{4,20},{20... | collective-permute-start | bytes 577544 | tf_op jit(solution)/shard_map/ppermute | solution.py:798
  124.3 4.3 %collective-permute-done.26.got = f32[376,128]{1,0:T(8,128)S(1)} collective-permute-done((f32[376,128]{1,0:T(8,128)S(1)}, f32[376,128]{1,0:T(8,128)S(1)}, u32[]{:S(2)}, u32[]{:S(2)}) %collective-permute-start.26) | collective-permute-done | bytes 192544 | tf_op jit(solution)/shard_map/ppermute | solution.py:798
  129.2 1.6 %collective-permute-done.27.got = f32[616,128]{1,0:T(8,128)S(1)} collective-permute-done((f32[616,128]{1,0:T(8,128)S(1)}, f32[616,128]{1,0:T(8,128)S(1)}, u32[]{:S(2)}, u32[]{:S(2)}) %collective-permute-start.27) | collective-permute-done | bytes 315424 | tf_op jit(solution)/shard_map/ppermute | solution.py:798
  130.8 1.7 %finish.1 = (f32[2,2,128,128]{3,2,1,0:T(8,128)}, f32[2,256,128]{2,1,0:T(8,128)}, f32[2,128,128]{2,1,0:T(8,128)}, f32[2,2,128]{2,1,0:T(2,128)}) custom-call(s32[4]{0:T(128)S(1)} %pad_add_fusion.sc.sc_ref, bf16[2,2,128,128]{3,2,1,0:T(8,128)(2,1)S(1)} %copy-done.3, bf16[2,256,128]{2,1,0:T(8,128)(2,1)S(1)} %copy-done.4, f32[616,128]{1,0:T(8,128)S(1)} %join.3.value, ...), custom_call_target="tpu_custom_call" | custom-call | bytes 1550352 | tf_op jit(solution)/shard_map/finish/pallas_call | solution.py:721
  (55 shorter events, 13.3 us)
Async XLA Ops:
  1.4 1.2 copy-start
  2.6 0.9 copy-start.2
  3.5 0.7 copy-start.7
  5.0 6.9 %collective-permute-start = (f32[16,16,128]{2,1,0:T(8,128)S(1)}, f32[16,16,128]{2,1,0:T(8,128)S(1)}, u32[]{:S(2)}, u32[]{:S(2)}) collective-permute-start(f32[16,16,128]{2,1,0:T(8,128)S(1)} %face0.1), channel_id=1, source_target_pairs={{0,16},{16,0},{1,17},{17,1},{2,18},{18,2},{3,19},{19,3},{4,20},{20... | collective-permute-start | bytes 393224 | tf_op jit(solution)/shard_map/ppermute | solution.py:893
  12.4 1.4 %collective-permute-start.1 = (f32[16,16,128]{2,1,0:T(8,128)S(1)}, f32[16,16,128]{2,1,0:T(8,128)S(1)}, u32[]{:S(2)}, u32[]{:S(2)}) collective-permute-start(f32[16,16,128]{2,1,0:T(8,128)S(1)} %get-tuple-element.124), channel_id=1, source_target_pairs={{0,4},{4,0},{8,12},{12,8},{1,5},{5,1},{9,13},{13,9},{2,6},{6,2},{1... | collective-permute-start | bytes 393224 | tf_op jit(solution)/shard_map/ppermute | solution.py:893
  12.5 1.3 %collective-permute-start.2 = (f32[16,16,128]{2,1,0:T(8,128)S(1)}, f32[16,16,128]{2,1,0:T(8,128)S(1)}, u32[]{:S(2)}, u32[]{:S(2)}) collective-permute-start(f32[16,16,128]{2,1,0:T(8,128)S(1)} %get-tuple-element.125), channel_id=1, source_target_pairs={{4,8},{8,4},{5,9},{9,5},{6,10},{10,6},{7,11},{11,7},{20,24},{24,20... | collective-permute-start | bytes 393224 | tf_op jit(solution)/shard_map/ppermute | solution.py:893
  14.5 5.1 %copy-start.1 = (bf16[16,16,2,8,128]{4,3,2,1,0:T(8,128)(2,1)S(1)}, bf16[16,16,2,8,128]{4,3,2,1,0:T(8,128)(2,1)}, u32[]{:S(2)}) copy-start(bf16[16,16,2,8,128]{4,3,2,1,0:T(8,128)(2,1)} %param.7) | copy-start | bytes 3145732
  14.6 5.1 %copy-start.3 = (bf16[2,2,128,128]{3,2,1,0:T(8,128)(2,1)S(1)}, bf16[2,2,128,128]{3,2,1,0:T(8,128)(2,1)}, u32[]{:S(2)}) copy-start(bf16[2,2,128,128]{3,2,1,0:T(8,128)(2,1)} %edge_w.21) | copy-start | bytes 393220
  14.6 5.1 %copy-start.4 = (bf16[2,256,128]{2,1,0:T(8,128)(2,1)S(1)}, bf16[2,256,128]{2,1,0:T(8,128)(2,1)}, u32[]{:S(2)}) copy-start(bf16[2,256,128]{2,1,0:T(8,128)(2,1)} %node_in.19) | copy-start | bytes 393220
  14.6 5.1 %copy-start.6 = (bf16[2,128,128]{2,1,0:T(8,128)(2,1)S(1)}, bf16[2,128,128]{2,1,0:T(8,128)(2,1)}, u32[]{:S(2)}) copy-start(bf16[2,128,128]{2,1,0:T(8,128)(2,1)} %node_out.13) | copy-start | bytes 196612
  14.6 5.0 %collective-permute-start.3 = (f32[16,16,128]{2,1,0:T(8,128)S(1)}, f32[16,16,128]{2,1,0:T(8,128)S(1)}, u32[]{:S(2)}, u32[]{:S(2)}) collective-permute-start(f32[16,16,128]{2,1,0:T(8,128)S(1)} %get-tuple-element.131), channel_id=1, source_target_pairs={{0,1},{1,0},{2,3},{3,2},{4,5},{5,4},{6,7},{7,6},{8,9},{9,8},{10,11... | collective-permute-start | bytes 393224 | tf_op jit(solution)/shard_map/ppermute | solution.py:893
  16.2 3.4 %collective-permute-start.4 = (f32[16,16,128]{2,1,0:T(8,128)S(1)}, f32[16,16,128]{2,1,0:T(8,128)S(1)}, u32[]{:S(2)}, u32[]{:S(2)}) collective-permute-start(f32[16,16,128]{2,1,0:T(8,128)S(1)} %get-tuple-element.132), channel_id=1, source_target_pairs={{1,2},{2,1},{5,6},{6,5},{9,10},{10,9},{13,14},{14,13},{17,18},{18,... | collective-permute-start | bytes 393224 | tf_op jit(solution)/shard_map/ppermute | solution.py:893
  21.1 7.6 %collective-permute-start.5 = (f32[16,16,128]{2,1,0:T(8,128)S(1)}, f32[16,16,128]{2,1,0:T(8,128)S(1)}, u32[]{:S(2)}, u32[]{:S(2)}) collective-permute-start(f32[16,16,128]{2,1,0:T(8,128)S(1)} %face1.1), channel_id=1, source_target_pairs={{0,16},{16,0},{1,17},{17,1},{2,18},{18,2},{3,19},{19,3},{4,20},{20... | collective-permute-start | bytes 393224 | tf_op jit(solution)/shard_map/ppermute | solution.py:893
  29.2 6.1 %collective-permute-start.6 = (f32[16,16,128]{2,1,0:T(8,128)S(1)}, f32[16,16,128]{2,1,0:T(8,128)S(1)}, u32[]{:S(2)}, u32[]{:S(2)}) collective-permute-start(f32[16,16,128]{2,1,0:T(8,128)S(1)} %get-tuple-element.141), channel_id=1, source_target_pairs={{0,4},{4,0},{8,12},{12,8},{1,5},{5,1},{9,13},{13,9},{2,6},{6,2},{1... | collective-permute-start | bytes 393224 | tf_op jit(solution)/shard_map/ppermute | solution.py:893
  34.4 1.0 collective-permute-start.7
  36.0 7.5 %copy-start.5 = (bf16[16,16,2,8,128]{4,3,2,1,0:T(8,128)(2,1)S(1)}, bf16[16,16,2,8,128]{4,3,2,1,0:T(8,128)(2,1)}, u32[]{:S(2)}) copy-start(bf16[16,16,2,8,128]{4,3,2,1,0:T(8,128)(2,1)} %param.8) | copy-start | bytes 3145732
  36.0 7.4 %collective-permute-start.8 = (f32[16,16,128]{2,1,0:T(8,128)S(1)}, f32[16,16,128]{2,1,0:T(8,128)S(1)}, u32[]{:S(2)}, u32[]{:S(2)}) collective-permute-start(f32[16,16,128]{2,1,0:T(8,128)S(1)} %get-tuple-element.148), channel_id=1, source_target_pairs={{0,1},{1,0},{2,3},{3,2},{4,5},{5,4},{6,7},{7,6},{8,9},{9,8},{10,11... | collective-permute-start | bytes 393224 | tf_op jit(solution)/shard_map/ppermute | solution.py:893
  40.2 3.3 %collective-permute-start.9 = (f32[16,16,128]{2,1,0:T(8,128)S(1)}, f32[16,16,128]{2,1,0:T(8,128)S(1)}, u32[]{:S(2)}, u32[]{:S(2)}) collective-permute-start(f32[16,16,128]{2,1,0:T(8,128)S(1)} %get-tuple-element.149), channel_id=1, source_target_pairs={{1,2},{2,1},{5,6},{6,5},{9,10},{10,9},{13,14},{14,13},{17,18},{18,... | collective-permute-start | bytes 393224 | tf_op jit(solution)/shard_map/ppermute | solution.py:893
  44.7 5.0 %collective-permute-start.10 = (f32[16,16,128]{2,1,0:T(8,128)S(1)}, f32[16,16,128]{2,1,0:T(8,128)S(1)}, u32[]{:S(2)}, u32[]{:S(2)}) collective-permute-start(f32[16,16,128]{2,1,0:T(8,128)S(1)} %face2.1), channel_id=1, source_target_pairs={{0,16},{16,0},{1,17},{17,1},{2,18},{18,2},{3,19},{19,3},{4,20},{20... | collective-permute-start | bytes 393224 | tf_op jit(solution)/shard_map/ppermute | solution.py:893
  50.3 9.3 %collective-permute-start.11 = (f32[16,16,128]{2,1,0:T(8,128)S(1)}, f32[16,16,128]{2,1,0:T(8,128)S(1)}, u32[]{:S(2)}, u32[]{:S(2)}) collective-permute-start(f32[16,16,128]{2,1,0:T(8,128)S(1)} %get-tuple-element.157), channel_id=1, source_target_pairs={{4,8},{8,4},{5,9},{9,5},{6,10},{10,6},{7,11},{11,7},{20,24},{24,20... | collective-permute-start | bytes 393224 | tf_op jit(solution)/shard_map/ppermute | solution.py:893
  50.9 9.6 %collective-permute-start.12 = (f32[16,16,128]{2,1,0:T(8,128)S(1)}, f32[16,16,128]{2,1,0:T(8,128)S(1)}, u32[]{:S(2)}, u32[]{:S(2)}) collective-permute-start(f32[16,16,128]{2,1,0:T(8,128)S(1)} %get-tuple-element.158), channel_id=1, source_target_pairs={{0,4},{4,0},{8,12},{12,8},{1,5},{5,1},{9,13},{13,9},{2,6},{6,2},{1... | collective-permute-start | bytes 393224 | tf_op jit(solution)/shard_map/ppermute | solution.py:893
  61.2 7.3 %collective-permute-start.13 = (f32[16,16,128]{2,1,0:T(8,128)S(1)}, f32[16,16,128]{2,1,0:T(8,128)S(1)}, u32[]{:S(2)}, u32[]{:S(2)}) collective-permute-start(f32[16,16,128]{2,1,0:T(8,128)S(1)} %get-tuple-element.166), channel_id=1, source_target_pairs={{0,1},{1,0},{2,3},{3,2},{4,5},{5,4},{6,7},{7,6},{8,9},{9,8},{10,11... | collective-permute-start | bytes 393224 | tf_op jit(solution)/shard_map/ppermute | solution.py:893
  65.0 3.5 %collective-permute-start.14 = (f32[16,16,128]{2,1,0:T(8,128)S(1)}, f32[16,16,128]{2,1,0:T(8,128)S(1)}, u32[]{:S(2)}, u32[]{:S(2)}) collective-permute-start(f32[16,16,128]{2,1,0:T(8,128)S(1)} %get-tuple-element.167), channel_id=1, source_target_pairs={{1,2},{2,1},{5,6},{6,5},{9,10},{10,9},{13,14},{14,13},{17,18},{18,... | collective-permute-start | bytes 393224 | tf_op jit(solution)/shard_map/ppermute | solution.py:893
  69.8 6.2 %collective-permute-start.15 = (f32[16,16,128]{2,1,0:T(8,128)S(1)}, f32[16,16,128]{2,1,0:T(8,128)S(1)}, u32[]{:S(2)}, u32[]{:S(2)}) collective-permute-start(f32[16,16,128]{2,1,0:T(8,128)S(1)} %face3.1), channel_id=1, source_target_pairs={{0,16},{16,0},{1,17},{17,1},{2,18},{18,2},{3,19},{19,3},{4,20},{20... | collective-permute-start | bytes 393224 | tf_op jit(solution)/shard_map/ppermute | solution.py:893
  76.5 2.8 %collective-permute-start.16 = (f32[16,16,128]{2,1,0:T(8,128)S(1)}, f32[16,16,128]{2,1,0:T(8,128)S(1)}, u32[]{:S(2)}, u32[]{:S(2)}) collective-permute-start(f32[16,16,128]{2,1,0:T(8,128)S(1)} %get-tuple-element.194), channel_id=1, source_target_pairs={{0,4},{4,0},{8,12},{12,8},{1,5},{5,1},{9,13},{13,9},{2,6},{6,2},{1... | collective-permute-start | bytes 393224 | tf_op jit(solution)/shard_map/ppermute | solution.py:893
  77.0 2.4 %collective-permute-start.17 = (f32[16,16,128]{2,1,0:T(8,128)S(1)}, f32[16,16,128]{2,1,0:T(8,128)S(1)}, u32[]{:S(2)}, u32[]{:S(2)}) collective-permute-start(f32[16,16,128]{2,1,0:T(8,128)S(1)} %get-tuple-element.195), channel_id=1, source_target_pairs={{4,8},{8,4},{5,9},{9,5},{6,10},{10,6},{7,11},{11,7},{20,24},{24,20... | collective-permute-start | bytes 393224 | tf_op jit(solution)/shard_map/ppermute | solution.py:893
  79.4 9.9 %collective-permute-start.20 = (f32[480,128]{1,0:T(8,128)S(1)}, f32[480,128]{1,0:T(8,128)S(1)}, u32[]{:S(2)}, u32[]{:S(2)}) collective-permute-start(f32[480,128]{1,0:T(8,128)S(1)} %get-tuple-element.217), channel_id=1, source_target_pairs={{0,4},{4,0},{8,12},{12,8},{1,5},{5,1},{9,13},{13,9},{2,6},{6,2},{1... | collective-permute-start | bytes 737288 | tf_op jit(solution)/shard_map/ppermute | solution.py:798
  84.6 7.7 %collective-permute-start.18 = (f32[16,16,128]{2,1,0:T(8,128)S(1)}, f32[16,16,128]{2,1,0:T(8,128)S(1)}, u32[]{:S(2)}, u32[]{:S(2)}) collective-permute-start(f32[16,16,128]{2,1,0:T(8,128)S(1)} %get-tuple-element.211), channel_id=1, source_target_pairs={{0,1},{1,0},{2,3},{3,2},{4,5},{5,4},{6,7},{7,6},{8,9},{9,8},{10,11... | collective-permute-start | bytes 393224 | tf_op jit(solution)/shard_map/ppermute | solution.py:893
  88.6 3.7 %collective-permute-start.19 = (f32[16,16,128]{2,1,0:T(8,128)S(1)}, f32[16,16,128]{2,1,0:T(8,128)S(1)}, u32[]{:S(2)}, u32[]{:S(2)}) collective-permute-start(f32[16,16,128]{2,1,0:T(8,128)S(1)} %get-tuple-element.212), channel_id=1, source_target_pairs={{1,2},{2,1},{5,6},{6,5},{9,10},{10,9},{13,14},{14,13},{17,18},{18,... | collective-permute-start | bytes 393224 | tf_op jit(solution)/shard_map/ppermute | solution.py:893
  89.9 5.0 %collective-permute-start.21 = (f32[240,128]{1,0:T(8,128)S(1)}, f32[240,128]{1,0:T(8,128)S(1)}, u32[]{:S(2)}, u32[]{:S(2)}) collective-permute-start(f32[240,128]{1,0:T(8,128)S(1)} %get-tuple-element.221), channel_id=1, source_target_pairs={{0,16},{16,0},{1,17},{17,1},{2,18},{18,2},{3,19},{19,3},{4,20},{20... | collective-permute-start | bytes 368648 | tf_op jit(solution)/shard_map/ppermute | solution.py:798
  95.5 6.1 %collective-permute-start.22 = (f32[120,128]{1,0:T(8,128)S(1)}, f32[120,128]{1,0:T(8,128)S(1)}, u32[]{:S(2)}, u32[]{:S(2)}) collective-permute-start(f32[120,128]{1,0:T(8,128)S(1)} %get-tuple-element.223), channel_id=1, source_target_pairs={{0,8},{4,12},{8,0},{12,4},{1,9},{5,13},{9,1},{13,5},{2,10},{6,14},... | collective-permute-start | bytes 184328 | tf_op jit(solution)/shard_map/ppermute | solution.py:798
  102.1 9.0 %collective-permute-start.23 = (f32[256,128]{1,0:T(8,128)S(1)}, f32[256,128]{1,0:T(8,128)S(1)}, u32[]{:S(2)}, u32[]{:S(2)}) collective-permute-start(f32[256,128]{1,0:T(8,128)S(1)} %stack.17.left), channel_id=1, source_target_pairs={{0,2},{1,3},{2,0},{3,1},{4,6},{5,7},{6,4},{7,5},{8,10},{9,11},{10,... | collective-permute-start | bytes 393224 | tf_op jit(solution)/shard_map/ppermute | solution.py:798
  111.7 5.0 %collective-permute-start.24 = (f32[256,128]{1,0:T(8,128)S(1)}, f32[256,128]{1,0:T(8,128)S(1)}, u32[]{:S(2)}, u32[]{:S(2)}) collective-permute-start(f32[256,128]{1,0:T(8,128)S(1)} %add.8.left), channel_id=1, source_target_pairs={{0,1},{1,0},{2,3},{3,2},{4,5},{5,4},{6,7},{7,6},{8,9},{9,8},{10,11... | collective-permute-start | bytes 393224 | tf_op jit(solution)/shard_map/ppermute | solution.py:798
  117.3 5.0 %collective-permute-start.25 = (f32[256,128]{1,0:T(8,128)S(1)}, f32[256,128]{1,0:T(8,128)S(1)}, u32[]{:S(2)}, u32[]{:S(2)}) collective-permute-start(f32[256,128]{1,0:T(8,128)S(1)} %add.9.value), channel_id=1, source_target_pairs={{0,8},{4,12},{8,0},{12,4},{1,9},{5,13},{9,1},{13,5},{2,10},{6,14},... | collective-permute-start | bytes 393224 | tf_op jit(solution)/shard_map/ppermute | solution.py:798
  122.9 5.7 %collective-permute-start.26 = (f32[376,128]{1,0:T(8,128)S(1)}, f32[376,128]{1,0:T(8,128)S(1)}, u32[]{:S(2)}, u32[]{:S(2)}) collective-permute-start(f32[376,128]{1,0:T(8,128)S(1)} %join.2.value), channel_id=1, source_target_pairs={{0,16},{16,0},{1,17},{17,1},{2,18},{18,2},{3,19},{19,3},{4,20},{20... | collective-permute-start | bytes 577544 | tf_op jit(solution)/shard_map/ppermute | solution.py:798
  129.1 1.7 %collective-permute-start.27 = (f32[616,128]{1,0:T(8,128)S(1)}, f32[616,128]{1,0:T(8,128)S(1)}, u32[]{:S(2)}, u32[]{:S(2)}) collective-permute-start(f32[616,128]{1,0:T(8,128)S(1)} %join.3.value), channel_id=1, source_target_pairs={{0,4},{4,0},{8,12},{12,8},{1,5},{5,1},{9,13},{13,9},{2,6},{6,2},{1... | collective-permute-start | bytes 946184 | tf_op jit(solution)/shard_map/ppermute | solution.py:798

commit v11 on v10

--- a/solution.py
+++ b/solution.py
@@ -88,7 +88,7 @@
         body(x0, y0)
         return carry
 
-    lax.fori_loop(0, total, step, 0)
+    lax.fori_loop(0, total, step, 0, unroll=2 if total % 2 == 0 else 1)
 
 
 def edge_dots(parts, weight, weight_both):
@@ -774,10 +774,6 @@
     write_halves(sc, step, total, keep, send)
 
 
-def add_kernel(sc, left, right, out):
-    out[...] = left[...] + right[...]
-
-
 def join_kernel_of(step, start, sc, value, got, out):
     half = value.shape[0] - start
     bit = bit_of(sc, step)
@@ -980,7 +976,7 @@
         state_kernel, "state_grad", (sc, edge_weights, node_in, grad_in, dpn0, edges), [full16], [], 4 * matmul
     )
     for hop in reversed(hops(sizes[2])):
-        (value,) = call(add_kernel, "add", (sc, value, swap(value, (2, hop))), [rows_like(value.shape[0])])
+        value = value + swap(value, (2, hop))
         value, grad0 = lax.optimization_barrier((value, grad0))
     first, *rest = halving_steps(sizes)
     for step in reversed(rest):

time: 133 us -> 132 us (level)
    pallas_call x30 -> x28, Pallas kernels: 49.2 us -> 48.3 us  [call(): pl.pallas_call(kernel, name=name, out_shape=tuple(outs), in_specs=[SM] +...]
  transfers between devices with their start and end apart: 28 -> 28, of which waited for: 14 -> 13; matrix products, arithmetic and copies ran while one was open for 0% -> 0% of each run, Pallas kernels for 27% -> 27%
where the time goes in v11:
time: 132 us
  starting transfers between devices  52.3 us (40%)
  Pallas kernels  48.3 us (37%)
  waiting for transfers between devices  26.8 us (20%)
  local copies, waits for them, and re-layouts  2.84 us (2%)
  between operations  1.71 us (1%)
    pallas_call x28, Pallas kernels, call(): pl.pallas_call(kernel, name=name, out_shape=tuple(outs), in_specs=[SM] +...  48.3 us
    ppermute x20, starting transfers between devices, trade(): lax.ppermute(face, axis, pairs(size, kind))  39.3 us
    ppermute x8, waiting for transfers between devices, swap(): lax.ppermute(value, axis, [(i, i ^ step[1]) for i in range(lax.axis_size(...  21.7 us
    ppermute x8, starting transfers between devices, swap(): lax.ppermute(value, axis, [(i, i ^ step[1]) for i in range(lax.axis_size(...  13 us
    ppermute x20, waiting for transfers between devices, trade(): lax.ppermute(face, axis, pairs(size, kind))  5.06 us
    unnamed x16, local copies, waits for them, and re-layouts  2.84 us
  transfers between devices with their start and end apart: 28, of which 13 were waited for; matrix products, arithmetic and copies ran while one was open for 0% of the time, Pallas kernels for 27%

profile of v11, /device:TPU:0, one launch (start us, length us, event | category | flops | bytes accessed | tf_op | source)
XLA Modules:
  0.0 132.1 jit_solution(5346871756348965741)
XLA Ops:
  1.4 1.2 copy-done
  2.6 0.9 copy-done.2
  3.5 0.7 copy-done.7
  4.2 0.8 face0.1
  5.0 3.0 %collective-permute-start = (f32[16,16,128]{2,1,0:T(8,128)S(1)}, f32[16,16,128]{2,1,0:T(8,128)S(1)}, u32[]{:S(2)}, u32[]{:S(2)}) collective-permute-start(f32[16,16,128]{2,1,0:T(8,128)S(1)} %face0.1), channel_id=1, source_target_pairs={{0,16},{16,0},{1,17},{17,1},{2,18},{18,2},{3,19},{19,3},{4,20},{20... | collective-permute-start | bytes 393224 | tf_op jit(solution)/shard_map/ppermute | solution.py:889
  8.0 3.8 %edges0.1 = (f32[16,16,16,128]{3,2,1,0:T(8,128)S(1)}, f32[3,16,16,16,128]{4,3,2,1,0:T(8,128)S(1)}, f32[16,16,128]{2,1,0:T(8,128)S(1)}, f32[16,16,128]{2,1,0:T(8,...) custom-call(s32[4]{0:T(128)S(1)} %pad_add_fusion.sc.sc_ref, bf16[2,2,128,128]{3,2,1,0:T(8,128)(2,1)S(1)} %copy-done.2, ...), custom_call_target="tpu_custom_call" | custom-call | flops 402653184 | bytes 10094608 | tf_op jit(solution)/shard_map/edges0/pallas_call | solution.py:721
  12.4 0.7 collective-permute-start.2
  13.8 0.7 fix_z.4
  14.5 1.6 %collective-permute-start.3 = (f32[16,16,128]{2,1,0:T(8,128)S(1)}, f32[16,16,128]{2,1,0:T(8,128)S(1)}, u32[]{:S(2)}, u32[]{:S(2)}) collective-permute-start(f32[16,16,128]{2,1,0:T(8,128)S(1)} %get-tuple-element.131), channel_id=1, source_target_pairs={{0,1},{1,0},{2,3},{3,2},{4,5},{5,4},{6,7},{7,6},{8,9},{9,8},{10,11... | collective-permute-start | bytes 393224 | tf_op jit(solution)/shard_map/ppermute | solution.py:889
  16.8 2.6 %slopes.2 = f32[3,16,16,16,128]{4,3,2,1,0:T(8,128)S(1)} custom-call(s32[4]{0:T(128)S(1)} %pad_add_fusion.sc.sc_ref, f32[3,16,16,16,128]{4,3,2,1,0:T(8,128)S(1)} %get-tuple-element.133.half_in), custom_call_target="tpu_custom_call", output_to_operand_aliasing={{}: (1, {})} | custom-call | flops 134217728 | bytes 12582928 | tf_op jit(solution)/shard_map/slopes/pallas_call | solution.py:721
  19.6 1.4 %face1.1 = f32[16,16,128]{2,1,0:T(8,128)S(1)} custom-call(s32[4]{0:T(128)S(1)} %pad_add_fusion.sc.sc_ref, bf16[2,2,128,128]{3,2,1,0:T(8,128)(2,1)S(1)} %copy-done.3, bf16[2,256,128]{2,1,0:T(8,128)(2,1)S(1)} %copy-done.4, bf16[2,128,128]{2,1,0:T(8,128)(2,1)S(1)} %copy-done.6, f32[2,2,128]{2,1,0:T(2,128)S(1)} %copy-done.7, ...), custom_call_target="tpu_custom_call" | custom-call | flops 33554432 | bytes 4261904 | tf_op jit(solution)/shard_map/face1/pallas_call | solution.py:721
  21.0 1.5 %collective-permute-start.5 = (f32[16,16,128]{2,1,0:T(8,128)S(1)}, f32[16,16,128]{2,1,0:T(8,128)S(1)}, u32[]{:S(2)}, u32[]{:S(2)}) collective-permute-start(f32[16,16,128]{2,1,0:T(8,128)S(1)} %face1.1), channel_id=1, source_target_pairs={{0,16},{16,0},{1,17},{17,1},{2,18},{18,2},{3,19},{19,3},{4,20},{20... | collective-permute-start | bytes 393224 | tf_op jit(solution)/shard_map/ppermute | solution.py:889
  22.5 6.1 %nodes0_edges1.1 = (f32[16,16,16,128]{3,2,1,0:T(8,128)S(1)}, bf16[16,16,16,128]{3,2,1,0:T(8,128)(2,1)S(1)}, bf16[16,16,16,128]{3,2,1,0:T(8,128)(2,1)S(1)}, f32[1...) custom-call(s32[4]{0:T(128)S(1)} %pad_add_fusion.sc.sc_ref, ...), custom_call_target="tpu_custom_call", output_to_operand_aliasing={{0}: (5, {})} | custom-call | flops 1073741824 | bytes 20383760 | tf_op jit(solution)/shard_map/nodes0_edges1/pallas_call | solution.py:721
  29.1 5.1 %collective-permute-start.6 = (f32[16,16,128]{2,1,0:T(8,128)S(1)}, f32[16,16,128]{2,1,0:T(8,128)S(1)}, u32[]{:S(2)}, u32[]{:S(2)}) collective-permute-start(f32[16,16,128]{2,1,0:T(8,128)S(1)} %get-tuple-element.141), channel_id=1, source_target_pairs={{0,4},{4,0},{8,12},{12,8},{1,5},{5,1},{9,13},{13,9},{2,6},{6,2},{1... | collective-permute-start | bytes 393224 | tf_op jit(solution)/shard_map/ppermute | solution.py:889
  35.2 0.7 fix_z.5
  35.9 4.2 %collective-permute-start.8 = (f32[16,16,128]{2,1,0:T(8,128)S(1)}, f32[16,16,128]{2,1,0:T(8,128)S(1)}, u32[]{:S(2)}, u32[]{:S(2)}) collective-permute-start(f32[16,16,128]{2,1,0:T(8,128)S(1)} %get-tuple-element.148), channel_id=1, source_target_pairs={{0,1},{1,0},{2,3},{3,2},{4,5},{5,4},{6,7},{7,6},{8,9},{9,8},{10,11... | collective-permute-start | bytes 393224 | tf_op jit(solution)/shard_map/ppermute | solution.py:889
  40.8 2.6 %slopes.3 = f32[3,16,16,16,128]{4,3,2,1,0:T(8,128)S(1)} custom-call(s32[4]{0:T(128)S(1)} %pad_add_fusion.sc.sc_ref, f32[3,16,16,16,128]{4,3,2,1,0:T(8,128)S(1)} %get-tuple-element.150.half_in), custom_call_target="tpu_custom_call", output_to_operand_aliasing={{}: (1, {})} | custom-call | flops 134217728 | bytes 12582928 | tf_op jit(solution)/shard_map/slopes/pallas_call | solution.py:721
  43.4 1.2 face2.1
  45.2 3.6 %nodes1_back.1 = (f32[16,16,16,128]{3,2,1,0:T(8,128)S(1)}, bf16[16,16,16,128]{3,2,1,0:T(8,128)(2,1)S(1)}, bf16[16,16,16,128]{3,2,1,0:T(8,128)(2,1)S(1)}, bf16[16...) custom-call(s32[4]{0:T(128)S(1)} %pad_add_fusion.sc.sc_ref, ...), custom_call_target="tpu_custom_call", output_to_operand_aliasing={{0}: (5, {})} | custom-call | flops 939524096 | bytes 13043728 | tf_op jit(solution)/shard_map/nodes1_back/pallas_call | solution.py:721
  48.8 0.8 collective-permute-done.10.refs_0_
  50.2 0.8 collective-permute-start.11
  51.0 8.6 %collective-permute-start.12 = (f32[16,16,128]{2,1,0:T(8,128)S(1)}, f32[16,16,128]{2,1,0:T(8,128)S(1)}, u32[]{:S(2)}, u32[]{:S(2)}) collective-permute-start(f32[16,16,128]{2,1,0:T(8,128)S(1)} %get-tuple-element.158), channel_id=1, source_target_pairs={{0,4},{4,0},{8,12},{12,8},{1,5},{5,1},{9,13},{13,9},{2,6},{6,2},{1... | collective-permute-start | bytes 393224 | tf_op jit(solution)/shard_map/ppermute | solution.py:889
  59.6 1.0 collective-permute-done.12.refs_2_.refs_1_
  60.6 0.7 fix_z.6
  61.3 3.8 %collective-permute-start.13 = (f32[16,16,128]{2,1,0:T(8,128)S(1)}, f32[16,16,128]{2,1,0:T(8,128)S(1)}, u32[]{:S(2)}, u32[]{:S(2)}) collective-permute-start(f32[16,16,128]{2,1,0:T(8,128)S(1)} %get-tuple-element.166), channel_id=1, source_target_pairs={{0,1},{1,0},{2,3},{3,2},{4,5},{5,4},{6,7},{7,6},{8,9},{9,8},{10,11... | collective-permute-start | bytes 393224 | tf_op jit(solution)/shard_map/ppermute | solution.py:889
  65.8 1.6 %nodes1_products.1 = (f32[16,16,16,128]{3,2,1,0:T(8,128)S(1)}, f32[392,128]{1,0:T(8,128)S(1)}) custom-call(s32[4]{0:T(128)S(1)} %pad_add_fusion.sc.sc_ref, bf16[2,256,128]{2,1,0:T(8,128)(2,1)S(1)} %copy-done.4, bf16[16,16,16,128]{3,2,1,0:T(8,128)(2,1)S(1)} %get-tuple-element.196.h, bf16[16,16,16,128]{3,2,1,0:T(8,128)(2,1)S(1)} %bitcast.14, ...), custom_call_target="tpu_custom_call" | custom-call | flops 805306368 | bytes 7671824 | tf_op jit(solution)/shard_map/nodes1_products/pallas_call | solution.py:721
  67.4 1.4 %collective-permute-done.13.refs_3_ = f32[16,16,128]{2,1,0:T(8,128)S(1)} collective-permute-done((f32[16,16,128]{2,1,0:T(8,128)S(1)}, f32[16,16,128]{2,1,0:T(8,128)S(1)}, u32[]{:S(2)}, u32[]{:S(2)}) %collective-permute-start.13) | collective-permute-done | bytes 131104 | tf_op jit(solution)/shard_map/ppermute | solution.py:889
  68.8 1.3 face3.1
  70.1 0.8 collective-permute-start.15
  70.8 5.6 %edges1_back_nodes0_back.1 = (f32[16,16,16,128]{3,2,1,0:T(8,128)S(1)}, bf16[16,16,16,128]{3,2,1,0:T(8,128)(2,1)S(1)}, bf16[16,16,16,128]{3,2,1,0:T(8,128)(2,1)S(...) custom-call(s32[4]{0:T(128)S(1)} %pad_add_fusion.sc.sc_ref, ...), custom_call_target="tpu_custom_call", output_to_operand_aliasing={{0}: (5, {})} | custom-call | flops 1207959552 | bytes 20387856 | tf_op jit(solution)/shard_map/edges1_back_nodes0_back/pallas_call | solution.py:721
  78.0 1.7 %gradient_sums.1 = (f32[480,128]{1,0:T(8,128)S(1)}, f32[480,128]{1,0:T(8,128)S(1)}) custom-call(s32[4]{0:T(128)S(1)} %pad_add_fusion.sc.sc_ref, bf16[16,16,16,128]{3,2,1,0:T(8,128)(2,1)S(1)} %get-tuple-element.196.h, f32[16,16,16,128]{3,2,1,0:T(8,128)S(1)} %get-tuple-element.197.edges, bf16[16,16,16,128]{3,2,1,0:T(8,128)(2,1)S(1)} %get-tuple-element.226.grad.grad_in, ...), custom_call_target="tpu_custom_call" | custom-call | flops 671088640 | bytes 9084944 | tf_op jit(solution)/shard_map/gradient_sums/pallas_call | solution.py:721
  79.7 4.4 %collective-permute-start.20 = (f32[480,128]{1,0:T(8,128)S(1)}, f32[480,128]{1,0:T(8,128)S(1)}, u32[]{:S(2)}, u32[]{:S(2)}) collective-permute-start(f32[480,128]{1,0:T(8,128)S(1)} %get-tuple-element.217), channel_id=1, source_target_pairs={{0,4},{4,0},{8,12},{12,8},{1,5},{5,1},{9,13},{13,9},{2,6},{6,2},{1... | collective-permute-start | bytes 737288 | tf_op jit(solution)/shard_map/ppermute | solution.py:794
  84.7 4.0 %collective-permute-start.18 = (f32[16,16,128]{2,1,0:T(8,128)S(1)}, f32[16,16,128]{2,1,0:T(8,128)S(1)}, u32[]{:S(2)}, u32[]{:S(2)}) collective-permute-start(f32[16,16,128]{2,1,0:T(8,128)S(1)} %get-tuple-element.211), channel_id=1, source_target_pairs={{0,1},{1,0},{2,3},{3,2},{4,5},{5,4},{6,7},{7,6},{8,9},{9,8},{10,11... | collective-permute-start | bytes 393224 | tf_op jit(solution)/shard_map/ppermute | solution.py:889
  88.7 0.9 collective-permute-start.19
  90.2 1.4 %collective-permute-start.21 = (f32[240,128]{1,0:T(8,128)S(1)}, f32[240,128]{1,0:T(8,128)S(1)}, u32[]{:S(2)}, u32[]{:S(2)}) collective-permute-start(f32[240,128]{1,0:T(8,128)S(1)} %get-tuple-element.221), channel_id=1, source_target_pairs={{0,16},{16,0},{1,17},{17,1},{2,18},{18,2},{3,19},{19,3},{4,20},{20... | collective-permute-start | bytes 368648 | tf_op jit(solution)/shard_map/ppermute | solution.py:794
  91.6 0.8 collective-permute-done.18.refs_3_
  92.4 2.8 %collective-permute-done.21.got = f32[240,128]{1,0:T(8,128)S(1)} collective-permute-done((f32[240,128]{1,0:T(8,128)S(1)}, f32[240,128]{1,0:T(8,128)S(1)}, u32[]{:S(2)}, u32[]{:S(2)}) %collective-permute-start.21) | collective-permute-done | bytes 122912 | tf_op jit(solution)/shard_map/ppermute | solution.py:794
  95.8 2.2 %collective-permute-start.22 = (f32[120,128]{1,0:T(8,128)S(1)}, f32[120,128]{1,0:T(8,128)S(1)}, u32[]{:S(2)}, u32[]{:S(2)}) collective-permute-start(f32[120,128]{1,0:T(8,128)S(1)} %get-tuple-element.223), channel_id=1, source_target_pairs={{0,8},{4,12},{8,0},{12,4},{1,9},{5,13},{9,1},{13,5},{2,10},{6,14},... | collective-permute-start | bytes 184328 | tf_op jit(solution)/shard_map/ppermute | solution.py:794
  98.0 4.1 %edges0_back.1 = (f32[16,16,16,128]{3,2,1,0:T(8,128)S(1)}, f32[136,128]{1,0:T(8,128)S(1)}) custom-call(s32[4]{0:T(128)S(1)} %pad_add_fusion.sc.sc_ref, bf16[2,2,128,128]{3,2,1,0:T(8,128)(2,1)S(1)} %copy-done.3, bf16[2,256,128]{2,1,0:T(8,128)(2,1)S(1)} %copy-done.4, bf16[2,128,128]{2,1,0:T(8,128)(2,1)S(1)} %copy-done.6, ...), custom_call_target="tpu_custom_call", output_to_operand_aliasing={{0}: (5, {})} | custom-call | flops 805306368 | bytes 12589072 | tf_op jit(solution)/shard_map/edges0_back/pallas_call | solution.py:721
  102.7 3.1 %collective-permute-start.23 = (f32[256,128]{1,0:T(8,128)S(1)}, f32[256,128]{1,0:T(8,128)S(1)}, u32[]{:S(2)}, u32[]{:S(2)}) collective-permute-start(f32[256,128]{1,0:T(8,128)S(1)} %stack.17), channel_id=1, source_target_pairs={{0,2},{1,3},{2,0},{3,1},{4,6},{5,7},{6,4},{7,5},{8,10},{9,11},{10,... | collective-permute-start | bytes 393224 | tf_op jit(solution)/shard_map/ppermute | solution.py:794
  105.7 2.5 %state_grad.1 = bf16[16,16,16,128]{3,2,1,0:T(8,128)(2,1)} custom-call(s32[4]{0:T(128)S(1)} %pad_add_fusion.sc.sc_ref, bf16[2,2,128,128]{3,2,1,0:T(8,128)(2,1)S(1)} %copy-done.3, bf16[2,256,128]{2,1,0:T(8,128)(2,1)S(1)} %copy-done.4, bf16[16,16,16,128]{3,2,1,0:T(8,128)(2,1)S(1)} %get-tuple-element.226.grad.grad_in, ...), custom_call_target="tpu_custom_call" | custom-call | flops 536870912 | bytes 5505040 | tf_op jit(solution)/shard_map/state_grad/pallas_call | solution.py:721
  108.3 3.5 %collective-permute-done.23 = f32[256,128]{1,0:T(8,128)S(1)} collective-permute-done((f32[256,128]{1,0:T(8,128)S(1)}, f32[256,128]{1,0:T(8,128)S(1)}, u32[]{:S(2)}, u32[]{:S(2)}) %collective-permute-start.23) | collective-permute-done | bytes 131104 | tf_op jit(solution)/shard_map/ppermute | solution.py:794
  112.0 4.8 %collective-permute-done.24 = f32[256,128]{1,0:T(8,128)S(1)} collective-permute-done((f32[256,128]{1,0:T(8,128)S(1)}, f32[256,128]{1,0:T(8,128)S(1)}, u32[]{:S(2)}, u32[]{:S(2)}) %collective-permute-start.24) | collective-permute-done | bytes 131104 | tf_op jit(solution)/shard_map/ppermute | solution.py:794
  117.2 4.7 %collective-permute-done.25.got = f32[256,128]{1,0:T(8,128)S(1)} collective-permute-done((f32[256,128]{1,0:T(8,128)S(1)}, f32[256,128]{1,0:T(8,128)S(1)}, u32[]{:S(2)}, u32[]{:S(2)}) %collective-permute-start.25) | collective-permute-done | bytes 131104 | tf_op jit(solution)/shard_map/ppermute | solution.py:794
  122.4 1.4 %collective-permute-start.26 = (f32[376,128]{1,0:T(8,128)S(1)}, f32[376,128]{1,0:T(8,128)S(1)}, u32[]{:S(2)}, u32[]{:S(2)}) collective-permute-start(f32[376,128]{1,0:T(8,128)S(1)} %join.2.value), channel_id=1, source_target_pairs={{0,16},{16,0},{1,17},{17,1},{2,18},{18,2},{3,19},{19,3},{4,20},{20... | collective-permute-start | bytes 577544 | tf_op jit(solution)/shard_map/ppermute | solution.py:794
  123.8 4.3 %collective-permute-done.26.got = f32[376,128]{1,0:T(8,128)S(1)} collective-permute-done((f32[376,128]{1,0:T(8,128)S(1)}, f32[376,128]{1,0:T(8,128)S(1)}, u32[]{:S(2)}, u32[]{:S(2)}) %collective-permute-start.26) | collective-permute-done | bytes 192544 | tf_op jit(solution)/shard_map/ppermute | solution.py:794
  128.8 1.6 %collective-permute-done.27.got = f32[616,128]{1,0:T(8,128)S(1)} collective-permute-done((f32[616,128]{1,0:T(8,128)S(1)}, f32[616,128]{1,0:T(8,128)S(1)}, u32[]{:S(2)}, u32[]{:S(2)}) %collective-permute-start.27) | collective-permute-done | bytes 315424 | tf_op jit(solution)/shard_map/ppermute | solution.py:794
  130.4 1.7 %finish.1 = (f32[2,2,128,128]{3,2,1,0:T(8,128)}, f32[2,256,128]{2,1,0:T(8,128)}, f32[2,128,128]{2,1,0:T(8,128)}, f32[2,2,128]{2,1,0:T(2,128)}) custom-call(s32[4]{0:T(128)S(1)} %pad_add_fusion.sc.sc_ref, bf16[2,2,128,128]{3,2,1,0:T(8,128)(2,1)S(1)} %copy-done.3, bf16[2,256,128]{2,1,0:T(8,128)(2,1)S(1)} %copy-done.4, f32[616,128]{1,0:T(8,128)S(1)} %join.3.value, ...), custom_call_target="tpu_custom_call" | custom-call | bytes 1550352 | tf_op jit(solution)/shard_map/finish/pallas_call | solution.py:721
  (55 shorter events, 12.0 us)
Async XLA Ops:
  1.4 1.2 copy-start
  2.6 0.9 copy-start.2
  3.5 0.7 copy-start.7
  5.0 6.8 %collective-permute-start = (f32[16,16,128]{2,1,0:T(8,128)S(1)}, f32[16,16,128]{2,1,0:T(8,128)S(1)}, u32[]{:S(2)}, u32[]{:S(2)}) collective-permute-start(f32[16,16,128]{2,1,0:T(8,128)S(1)} %face0.1), channel_id=1, source_target_pairs={{0,16},{16,0},{1,17},{17,1},{2,18},{18,2},{3,19},{19,3},{4,20},{20... | collective-permute-start | bytes 393224 | tf_op jit(solution)/shard_map/ppermute | solution.py:889
  12.3 1.4 %collective-permute-start.1 = (f32[16,16,128]{2,1,0:T(8,128)S(1)}, f32[16,16,128]{2,1,0:T(8,128)S(1)}, u32[]{:S(2)}, u32[]{:S(2)}) collective-permute-start(f32[16,16,128]{2,1,0:T(8,128)S(1)} %get-tuple-element.124), channel_id=1, source_target_pairs={{0,4},{4,0},{8,12},{12,8},{1,5},{5,1},{9,13},{13,9},{2,6},{6,2},{1... | collective-permute-start | bytes 393224 | tf_op jit(solution)/shard_map/ppermute | solution.py:889
  12.4 1.3 %collective-permute-start.2 = (f32[16,16,128]{2,1,0:T(8,128)S(1)}, f32[16,16,128]{2,1,0:T(8,128)S(1)}, u32[]{:S(2)}, u32[]{:S(2)}) collective-permute-start(f32[16,16,128]{2,1,0:T(8,128)S(1)} %get-tuple-element.125), channel_id=1, source_target_pairs={{4,8},{8,4},{5,9},{9,5},{6,10},{10,6},{7,11},{11,7},{20,24},{24,20... | collective-permute-start | bytes 393224 | tf_op jit(solution)/shard_map/ppermute | solution.py:889
  14.4 5.1 %copy-start.1 = (bf16[16,16,2,8,128]{4,3,2,1,0:T(8,128)(2,1)S(1)}, bf16[16,16,2,8,128]{4,3,2,1,0:T(8,128)(2,1)}, u32[]{:S(2)}) copy-start(bf16[16,16,2,8,128]{4,3,2,1,0:T(8,128)(2,1)} %param.7) | copy-start | bytes 3145732
  14.5 5.1 %copy-start.3 = (bf16[2,2,128,128]{3,2,1,0:T(8,128)(2,1)S(1)}, bf16[2,2,128,128]{3,2,1,0:T(8,128)(2,1)}, u32[]{:S(2)}) copy-start(bf16[2,2,128,128]{3,2,1,0:T(8,128)(2,1)} %edge_w.21) | copy-start | bytes 393220
  14.5 5.1 %copy-start.4 = (bf16[2,256,128]{2,1,0:T(8,128)(2,1)S(1)}, bf16[2,256,128]{2,1,0:T(8,128)(2,1)}, u32[]{:S(2)}) copy-start(bf16[2,256,128]{2,1,0:T(8,128)(2,1)} %node_in.19) | copy-start | bytes 393220
  14.5 5.1 %copy-start.6 = (bf16[2,128,128]{2,1,0:T(8,128)(2,1)S(1)}, bf16[2,128,128]{2,1,0:T(8,128)(2,1)}, u32[]{:S(2)}) copy-start(bf16[2,128,128]{2,1,0:T(8,128)(2,1)} %node_out.13) | copy-start | bytes 196612
  14.5 5.0 %collective-permute-start.3 = (f32[16,16,128]{2,1,0:T(8,128)S(1)}, f32[16,16,128]{2,1,0:T(8,128)S(1)}, u32[]{:S(2)}, u32[]{:S(2)}) collective-permute-start(f32[16,16,128]{2,1,0:T(8,128)S(1)} %get-tuple-element.131), channel_id=1, source_target_pairs={{0,1},{1,0},{2,3},{3,2},{4,5},{5,4},{6,7},{7,6},{8,9},{9,8},{10,11... | collective-permute-start | bytes 393224 | tf_op jit(solution)/shard_map/ppermute | solution.py:889
  16.1 3.4 %collective-permute-start.4 = (f32[16,16,128]{2,1,0:T(8,128)S(1)}, f32[16,16,128]{2,1,0:T(8,128)S(1)}, u32[]{:S(2)}, u32[]{:S(2)}) collective-permute-start(f32[16,16,128]{2,1,0:T(8,128)S(1)} %get-tuple-element.132), channel_id=1, source_target_pairs={{1,2},{2,1},{5,6},{6,5},{9,10},{10,9},{13,14},{14,13},{17,18},{18,... | collective-permute-start | bytes 393224 | tf_op jit(solution)/shard_map/ppermute | solution.py:889
  21.0 7.6 %collective-permute-start.5 = (f32[16,16,128]{2,1,0:T(8,128)S(1)}, f32[16,16,128]{2,1,0:T(8,128)S(1)}, u32[]{:S(2)}, u32[]{:S(2)}) collective-permute-start(f32[16,16,128]{2,1,0:T(8,128)S(1)} %face1.1), channel_id=1, source_target_pairs={{0,16},{16,0},{1,17},{17,1},{2,18},{18,2},{3,19},{19,3},{4,20},{20... | collective-permute-start | bytes 393224 | tf_op jit(solution)/shard_map/ppermute | solution.py:889
  29.1 6.1 %collective-permute-start.6 = (f32[16,16,128]{2,1,0:T(8,128)S(1)}, f32[16,16,128]{2,1,0:T(8,128)S(1)}, u32[]{:S(2)}, u32[]{:S(2)}) collective-permute-start(f32[16,16,128]{2,1,0:T(8,128)S(1)} %get-tuple-element.141), channel_id=1, source_target_pairs={{0,4},{4,0},{8,12},{12,8},{1,5},{5,1},{9,13},{13,9},{2,6},{6,2},{1... | collective-permute-start | bytes 393224 | tf_op jit(solution)/shard_map/ppermute | solution.py:889
  34.2 1.0 collective-permute-start.7
  35.9 7.5 %copy-start.5 = (bf16[16,16,2,8,128]{4,3,2,1,0:T(8,128)(2,1)S(1)}, bf16[16,16,2,8,128]{4,3,2,1,0:T(8,128)(2,1)}, u32[]{:S(2)}) copy-start(bf16[16,16,2,8,128]{4,3,2,1,0:T(8,128)(2,1)} %param.8) | copy-start | bytes 3145732
  35.9 7.4 %collective-permute-start.8 = (f32[16,16,128]{2,1,0:T(8,128)S(1)}, f32[16,16,128]{2,1,0:T(8,128)S(1)}, u32[]{:S(2)}, u32[]{:S(2)}) collective-permute-start(f32[16,16,128]{2,1,0:T(8,128)S(1)} %get-tuple-element.148), channel_id=1, source_target_pairs={{0,1},{1,0},{2,3},{3,2},{4,5},{5,4},{6,7},{7,6},{8,9},{9,8},{10,11... | collective-permute-start | bytes 393224 | tf_op jit(solution)/shard_map/ppermute | solution.py:889
  40.1 3.3 %collective-permute-start.9 = (f32[16,16,128]{2,1,0:T(8,128)S(1)}, f32[16,16,128]{2,1,0:T(8,128)S(1)}, u32[]{:S(2)}, u32[]{:S(2)}) collective-permute-start(f32[16,16,128]{2,1,0:T(8,128)S(1)} %get-tuple-element.149), channel_id=1, source_target_pairs={{1,2},{2,1},{5,6},{6,5},{9,10},{10,9},{13,14},{14,13},{17,18},{18,... | collective-permute-start | bytes 393224 | tf_op jit(solution)/shard_map/ppermute | solution.py:889
  44.6 5.0 %collective-permute-start.10 = (f32[16,16,128]{2,1,0:T(8,128)S(1)}, f32[16,16,128]{2,1,0:T(8,128)S(1)}, u32[]{:S(2)}, u32[]{:S(2)}) collective-permute-start(f32[16,16,128]{2,1,0:T(8,128)S(1)} %face2.1), channel_id=1, source_target_pairs={{0,16},{16,0},{1,17},{17,1},{2,18},{18,2},{3,19},{19,3},{4,20},{20... | collective-permute-start | bytes 393224 | tf_op jit(solution)/shard_map/ppermute | solution.py:889
  50.2 9.5 %collective-permute-start.11 = (f32[16,16,128]{2,1,0:T(8,128)S(1)}, f32[16,16,128]{2,1,0:T(8,128)S(1)}, u32[]{:S(2)}, u32[]{:S(2)}) collective-permute-start(f32[16,16,128]{2,1,0:T(8,128)S(1)} %get-tuple-element.157), channel_id=1, source_target_pairs={{4,8},{8,4},{5,9},{9,5},{6,10},{10,6},{7,11},{11,7},{20,24},{24,20... | collective-permute-start | bytes 393224 | tf_op jit(solution)/shard_map/ppermute | solution.py:889
  51.0 9.6 %collective-permute-start.12 = (f32[16,16,128]{2,1,0:T(8,128)S(1)}, f32[16,16,128]{2,1,0:T(8,128)S(1)}, u32[]{:S(2)}, u32[]{:S(2)}) collective-permute-start(f32[16,16,128]{2,1,0:T(8,128)S(1)} %get-tuple-element.158), channel_id=1, source_target_pairs={{0,4},{4,0},{8,12},{12,8},{1,5},{5,1},{9,13},{13,9},{2,6},{6,2},{1... | collective-permute-start | bytes 393224 | tf_op jit(solution)/shard_map/ppermute | solution.py:889
  61.3 7.5 %collective-permute-start.13 = (f32[16,16,128]{2,1,0:T(8,128)S(1)}, f32[16,16,128]{2,1,0:T(8,128)S(1)}, u32[]{:S(2)}, u32[]{:S(2)}) collective-permute-start(f32[16,16,128]{2,1,0:T(8,128)S(1)} %get-tuple-element.166), channel_id=1, source_target_pairs={{0,1},{1,0},{2,3},{3,2},{4,5},{5,4},{6,7},{7,6},{8,9},{9,8},{10,11... | collective-permute-start | bytes 393224 | tf_op jit(solution)/shard_map/ppermute | solution.py:889
  65.1 3.7 %collective-permute-start.14 = (f32[16,16,128]{2,1,0:T(8,128)S(1)}, f32[16,16,128]{2,1,0:T(8,128)S(1)}, u32[]{:S(2)}, u32[]{:S(2)}) collective-permute-start(f32[16,16,128]{2,1,0:T(8,128)S(1)} %get-tuple-element.167), channel_id=1, source_target_pairs={{1,2},{2,1},{5,6},{6,5},{9,10},{10,9},{13,14},{14,13},{17,18},{18,... | collective-permute-start | bytes 393224 | tf_op jit(solution)/shard_map/ppermute | solution.py:889
  70.1 6.3 %collective-permute-start.15 = (f32[16,16,128]{2,1,0:T(8,128)S(1)}, f32[16,16,128]{2,1,0:T(8,128)S(1)}, u32[]{:S(2)}, u32[]{:S(2)}) collective-permute-start(f32[16,16,128]{2,1,0:T(8,128)S(1)} %face3.1), channel_id=1, source_target_pairs={{0,16},{16,0},{1,17},{17,1},{2,18},{18,2},{3,19},{19,3},{4,20},{20... | collective-permute-start | bytes 393224 | tf_op jit(solution)/shard_map/ppermute | solution.py:889
  77.0 2.7 %collective-permute-start.16 = (f32[16,16,128]{2,1,0:T(8,128)S(1)}, f32[16,16,128]{2,1,0:T(8,128)S(1)}, u32[]{:S(2)}, u32[]{:S(2)}) collective-permute-start(f32[16,16,128]{2,1,0:T(8,128)S(1)} %get-tuple-element.194), channel_id=1, source_target_pairs={{0,4},{4,0},{8,12},{12,8},{1,5},{5,1},{9,13},{13,9},{2,6},{6,2},{1... | collective-permute-start | bytes 393224 | tf_op jit(solution)/shard_map/ppermute | solution.py:889
  77.3 2.4 %collective-permute-start.17 = (f32[16,16,128]{2,1,0:T(8,128)S(1)}, f32[16,16,128]{2,1,0:T(8,128)S(1)}, u32[]{:S(2)}, u32[]{:S(2)}) collective-permute-start(f32[16,16,128]{2,1,0:T(8,128)S(1)} %get-tuple-element.195), channel_id=1, source_target_pairs={{4,8},{8,4},{5,9},{9,5},{6,10},{10,6},{7,11},{11,7},{20,24},{24,20... | collective-permute-start | bytes 393224 | tf_op jit(solution)/shard_map/ppermute | solution.py:889
  79.7 9.9 %collective-permute-start.20 = (f32[480,128]{1,0:T(8,128)S(1)}, f32[480,128]{1,0:T(8,128)S(1)}, u32[]{:S(2)}, u32[]{:S(2)}) collective-permute-start(f32[480,128]{1,0:T(8,128)S(1)} %get-tuple-element.217), channel_id=1, source_target_pairs={{0,4},{4,0},{8,12},{12,8},{1,5},{5,1},{9,13},{13,9},{2,6},{6,2},{1... | collective-permute-start | bytes 737288 | tf_op jit(solution)/shard_map/ppermute | solution.py:794
  84.7 7.7 %collective-permute-start.18 = (f32[16,16,128]{2,1,0:T(8,128)S(1)}, f32[16,16,128]{2,1,0:T(8,128)S(1)}, u32[]{:S(2)}, u32[]{:S(2)}) collective-permute-start(f32[16,16,128]{2,1,0:T(8,128)S(1)} %get-tuple-element.211), channel_id=1, source_target_pairs={{0,1},{1,0},{2,3},{3,2},{4,5},{5,4},{6,7},{7,6},{8,9},{9,8},{10,11... | collective-permute-start | bytes 393224 | tf_op jit(solution)/shard_map/ppermute | solution.py:889
  88.7 3.7 %collective-permute-start.19 = (f32[16,16,128]{2,1,0:T(8,128)S(1)}, f32[16,16,128]{2,1,0:T(8,128)S(1)}, u32[]{:S(2)}, u32[]{:S(2)}) collective-permute-start(f32[16,16,128]{2,1,0:T(8,128)S(1)} %get-tuple-element.212), channel_id=1, source_target_pairs={{1,2},{2,1},{5,6},{6,5},{9,10},{10,9},{13,14},{14,13},{17,18},{18,... | collective-permute-start | bytes 393224 | tf_op jit(solution)/shard_map/ppermute | solution.py:889
  90.2 5.0 %collective-permute-start.21 = (f32[240,128]{1,0:T(8,128)S(1)}, f32[240,128]{1,0:T(8,128)S(1)}, u32[]{:S(2)}, u32[]{:S(2)}) collective-permute-start(f32[240,128]{1,0:T(8,128)S(1)} %get-tuple-element.221), channel_id=1, source_target_pairs={{0,16},{16,0},{1,17},{17,1},{2,18},{18,2},{3,19},{19,3},{4,20},{20... | collective-permute-start | bytes 368648 | tf_op jit(solution)/shard_map/ppermute | solution.py:794
  95.8 6.3 %collective-permute-start.22 = (f32[120,128]{1,0:T(8,128)S(1)}, f32[120,128]{1,0:T(8,128)S(1)}, u32[]{:S(2)}, u32[]{:S(2)}) collective-permute-start(f32[120,128]{1,0:T(8,128)S(1)} %get-tuple-element.223), channel_id=1, source_target_pairs={{0,8},{4,12},{8,0},{12,4},{1,9},{5,13},{9,1},{13,5},{2,10},{6,14},... | collective-permute-start | bytes 184328 | tf_op jit(solution)/shard_map/ppermute | solution.py:794
  102.7 9.1 %collective-permute-start.23 = (f32[256,128]{1,0:T(8,128)S(1)}, f32[256,128]{1,0:T(8,128)S(1)}, u32[]{:S(2)}, u32[]{:S(2)}) collective-permute-start(f32[256,128]{1,0:T(8,128)S(1)} %stack.17), channel_id=1, source_target_pairs={{0,2},{1,3},{2,0},{3,1},{4,6},{5,7},{6,4},{7,5},{8,10},{9,11},{10,... | collective-permute-start | bytes 393224 | tf_op jit(solution)/shard_map/ppermute | solution.py:794
  111.8 5.0 %collective-permute-start.24 = (f32[256,128]{1,0:T(8,128)S(1)}, f32[256,128]{1,0:T(8,128)S(1)}, u32[]{:S(2)}, u32[]{:S(2)}) collective-permute-start(f32[256,128]{1,0:T(8,128)S(1)} %add.6), channel_id=1, source_target_pairs={{0,1},{1,0},{2,3},{3,2},{4,5},{5,4},{6,7},{7,6},{8,9},{9,8},{10,11... | collective-permute-start | bytes 393224 | tf_op jit(solution)/shard_map/ppermute | solution.py:794
  116.8 5.0 %collective-permute-start.25 = (f32[256,128]{1,0:T(8,128)S(1)}, f32[256,128]{1,0:T(8,128)S(1)}, u32[]{:S(2)}, u32[]{:S(2)}) collective-permute-start(f32[256,128]{1,0:T(8,128)S(1)} %add.7.value), channel_id=1, source_target_pairs={{0,8},{4,12},{8,0},{12,4},{1,9},{5,13},{9,1},{13,5},{2,10},{6,14},... | collective-permute-start | bytes 393224 | tf_op jit(solution)/shard_map/ppermute | solution.py:794
  122.4 5.7 %collective-permute-start.26 = (f32[376,128]{1,0:T(8,128)S(1)}, f32[376,128]{1,0:T(8,128)S(1)}, u32[]{:S(2)}, u32[]{:S(2)}) collective-permute-start(f32[376,128]{1,0:T(8,128)S(1)} %join.2.value), channel_id=1, source_target_pairs={{0,16},{16,0},{1,17},{17,1},{2,18},{18,2},{3,19},{19,3},{4,20},{20... | collective-permute-start | bytes 577544 | tf_op jit(solution)/shard_map/ppermute | solution.py:794
  128.7 1.7 %collective-permute-start.27 = (f32[616,128]{1,0:T(8,128)S(1)}, f32[616,128]{1,0:T(8,128)S(1)}, u32[]{:S(2)}, u32[]{:S(2)}) collective-permute-start(f32[616,128]{1,0:T(8,128)S(1)} %join.3.value), channel_id=1, source_target_pairs={{0,4},{4,0},{8,12},{12,8},{1,5},{5,1},{9,13},{13,9},{2,6},{6,2},{1... | collective-permute-start | bytes 946184 | tf_op jit(solution)/shard_map/ppermute | solution.py:794

commit v12 on v11

--- a/solution.py
+++ b/solution.py
@@ -78,7 +78,7 @@
     return jnp.concatenate(done, 1).reshape(plane.shape)
 
 
-def elements(x_len, y_len, body):
+def elements(x_len, y_len, body, unroll=1):
     ey = y_len // NODES
     total = (x_len // NODES) * ey
 
@@ -88,7 +88,7 @@
         body(x0, y0)
         return carry
 
-    lax.fori_loop(0, total, step, 0, unroll=2 if total % 2 == 0 else 1)
+    lax.fori_loop(0, total, step, 0, unroll=unroll if total % unroll == 0 else 1)
 
 
 def edge_dots(parts, weight, weight_both):
@@ -147,7 +147,7 @@
             sum_ref[x0 + i, ys] = couple_slots(total, filled)
             here = nxt
 
-    elements(x_len, y_len, body)
+    elements(x_len, y_len, body, 2)
 
 
 def slope_kernel(sc, half_in, slope_out):
@@ -661,8 +661,10 @@
 
 def last_kernel(counts, sizes, sc, edge_w, node_in, node_out, biases, sums_in, h, slopes, *refs):
     n = sum(counts)
-    halo, (edges, grads) = refs[:n], refs[n:]
+    halo, (edges, grads, second) = refs[:n], refs[n:]
     grads[...] = jnp.zeros_like(grads)
+    for k, step in enumerate(halving_steps(sizes)):
+        second[k] = jnp.full(second.shape[1:], bit_of(sc, step), jnp.int32)
     edge_parts(counts, sc, (edge_w,), 0, halo, slopes, edges, grads.at[pl.ds(128, NODES)])
 
     def body(x):
@@ -781,12 +783,6 @@
         out[pl.ds(0, start)] = value[pl.ds(0, start)] + got[pl.ds(0, start)]
     out[pl.ds(pl.multiple_of(start + bit * half, NODES), half)] = value[pl.ds(start, half)]
     out[pl.ds(pl.multiple_of(start + (1 - bit) * half, NODES), half)] = got[pl.ds(start, half)]
-
-
-def stack_kernel(sc, first, left, right, out):
-    rows = first.shape[0]
-    out[pl.ds(0, rows)] = first[...]
-    out[pl.ds(rows, left.shape[0])] = left[...] + right[...]
 
 
 def swap(value, step):
@@ -966,11 +962,13 @@
     held = (h1, edges1, grad_in, h0, scaled0, act0, dpn0, grads1, bias1)
     halo, _ = exchange(got_x, faces, early=layer_sums, early_held=held)
     tail_rows = width + NODES
-    edges, last = run(
-        last_kernel, "edges0_back", (sums, h0, slopes0, *halo), [full, rows_like(tail_rows)], [], 6, in_place
+    steps = halving_steps(sizes)
+    edges, last, second = run(
+        last_kernel, "edges0_back", (sums, h0, slopes0, *halo),
+        [full, rows_like(tail_rows), sds((len(steps), NODES, width), jnp.int32)], [], 6, in_place,
     )
     keep, got = background.finish("sums")
-    (value,) = call(stack_kernel, "stack", (sc, last, keep, got), [rows_like(tail_rows + keep.shape[0])])
+    value = jnp.concatenate([last, keep + got], 0)
     value, grad_in, dpn0, edges = lax.optimization_barrier((value, grad_in, dpn0, edges))
     (grad0,) = call(
         state_kernel, "state_grad", (sc, edge_weights, node_in, grad_in, dpn0, edges), [full16], [], 4 * matmul
@@ -978,17 +976,19 @@
     for hop in reversed(hops(sizes[2])):
         value = value + swap(value, (2, hop))
         value, grad0 = lax.optimization_barrier((value, grad0))
-    first, *rest = halving_steps(sizes)
-    for step in reversed(rest):
-        out = rows_like(2 * value.shape[0] - tail_rows)
-        body = functools.partial(join_kernel_of, step, tail_rows)
-        (value,) = call(body, "join", (sc, value, swap(value, step)), [out])
+    for k in reversed(range(1, len(steps))):
+        got = swap(value, steps[k])
+        mine, other = value[tail_rows:], got[tail_rows:]
+        joined = jnp.where(
+            second[k, :1] == 0, jnp.concatenate([mine, other], 0), jnp.concatenate([other, mine], 0)
+        )
+        value = jnp.concatenate([value[:tail_rows] + got[:tail_rows], joined], 0)
     layers_all = 3 * slots * sizes[2] // 4
     nodes_all = x_len * sizes[0] * y_len * sizes[1] * layers_all * nodes
     scale = 1.0 / math.sqrt(nodes_all)
     edge_grads, in_grads, out_grads, bias_grads = call(
-        functools.partial(finish_kernel, scale, tail_rows, first), "finish",
-        (sc, edge_weights, node_in, value, swap(value, first)),
+        functools.partial(finish_kernel, scale, tail_rows, steps[0]), "finish",
+        (sc, edge_weights, node_in, value, swap(value, steps[0])),
         [sds(edge_weights.shape), sds(node_in.shape), sds(node_out.shape), sds(biases.shape)],
         [pltpu.VMEM((2 * value.shape[0] - tail_rows, width), f32)],
     )

time: 132 us -> 130 us (0.985)
  Pallas kernels: 48.3 us -> 46.2 us
    pallas_call x28 -> x25, Pallas kernels: 48.3 us -> 46.2 us  [call(): pl.pallas_call(kernel, name=name, out_shape=tuple(outs), in_specs=[SM] +...]
where the time goes in v12:
time: 130 us
  starting transfers between devices  52.1 us (40%)
  Pallas kernels  46.2 us (36%)
  waiting for transfers between devices  26.8 us (21%)
  local copies, waits for them, and re-layouts  2.86 us (2%)
  between operations  1.75 us (1%)
    pallas_call x25, Pallas kernels, call(): pl.pallas_call(kernel, name=name, out_shape=tuple(outs), in_specs=[SM] +...  46.2 us
    ppermute x20, starting transfers between devices, trade(): lax.ppermute(face, axis, pairs(size, kind))  39.1 us
    ppermute x8, waiting for transfers between devices, swap(): lax.ppermute(value, axis, [(i, i ^ step[1]) for i in range(lax.axis_size(...  21.5 us
    ppermute x8, starting transfers between devices, swap(): lax.ppermute(value, axis, [(i, i ^ step[1]) for i in range(lax.axis_size(...  13 us
    ppermute x20, waiting for transfers between devices, trade(): lax.ppermute(face, axis, pairs(size, kind))  5.28 us
    unnamed x16, local copies, waits for them, and re-layouts  2.84 us
  transfers between devices with their start and end apart: 28, of which 13 were waited for; matrix products, arithmetic and copies ran while one was open for 0% of the time, Pallas kernels for 27%

profile of v12, /device:TPU:0, one launch (start us, length us, event | category | flops | bytes accessed | tf_op | source)
XLA Modules:
  0.0 129.9 jit_solution(14770997283616180527)
XLA Ops:
  1.4 1.2 copy-done
  2.6 0.9 copy-done.2
  3.5 0.7 copy-done.7
  4.2 0.8 face0.1
  5.0 3.0 %collective-permute-start = (f32[16,16,128]{2,1,0:T(8,128)S(1)}, f32[16,16,128]{2,1,0:T(8,128)S(1)}, u32[]{:S(2)}, u32[]{:S(2)}) collective-permute-start(f32[16,16,128]{2,1,0:T(8,128)S(1)} %face0.1), channel_id=1, source_target_pairs={{0,16},{16,0},{1,17},{17,1},{2,18},{18,2},{3,19},{19,3},{4,20},{20... | collective-permute-start | bytes 393224 | tf_op jit(solution)/shard_map/ppermute | solution.py:885
  8.0 3.8 %edges0.1 = (f32[16,16,16,128]{3,2,1,0:T(8,128)S(1)}, f32[3,16,16,16,128]{4,3,2,1,0:T(8,128)S(1)}, f32[16,16,128]{2,1,0:T(8,128)S(1)}, f32[16,16,128]{2,1,0:T(8,...) custom-call(s32[4]{0:T(128)S(1)} %pad_add_fusion.sc.sc_ref, bf16[2,2,128,128]{3,2,1,0:T(8,128)(2,1)S(1)} %copy-done.2, ...), custom_call_target="tpu_custom_call" | custom-call | flops 402653184 | bytes 10094608 | tf_op jit(solution)/shard_map/edges0/pallas_call | solution.py:723
  12.4 0.7 collective-permute-start.2
  13.8 0.7 fix_z.4
  14.5 1.6 %collective-permute-start.3 = (f32[16,16,128]{2,1,0:T(8,128)S(1)}, f32[16,16,128]{2,1,0:T(8,128)S(1)}, u32[]{:S(2)}, u32[]{:S(2)}) collective-permute-start(f32[16,16,128]{2,1,0:T(8,128)S(1)} %get-tuple-element.132), channel_id=1, source_target_pairs={{0,1},{1,0},{2,3},{3,2},{4,5},{5,4},{6,7},{7,6},{8,9},{9,8},{10,11... | collective-permute-start | bytes 393224 | tf_op jit(solution)/shard_map/ppermute | solution.py:885
  16.8 2.6 %slopes.2 = f32[3,16,16,16,128]{4,3,2,1,0:T(8,128)S(1)} custom-call(s32[4]{0:T(128)S(1)} %pad_add_fusion.sc.sc_ref, f32[3,16,16,16,128]{4,3,2,1,0:T(8,128)S(1)} %get-tuple-element.134.half_in), custom_call_target="tpu_custom_call", output_to_operand_aliasing={{}: (1, {})} | custom-call | flops 134217728 | bytes 12582928 | tf_op jit(solution)/shard_map/slopes/pallas_call | solution.py:723
  19.6 1.4 %face1.1 = f32[16,16,128]{2,1,0:T(8,128)S(1)} custom-call(s32[4]{0:T(128)S(1)} %pad_add_fusion.sc.sc_ref, bf16[2,2,128,128]{3,2,1,0:T(8,128)(2,1)S(1)} %copy-done.3, bf16[2,256,128]{2,1,0:T(8,128)(2,1)S(1)} %copy-done.4, bf16[2,128,128]{2,1,0:T(8,128)(2,1)S(1)} %copy-done.6, f32[2,2,128]{2,1,0:T(2,128)S(1)} %copy-done.7, ...), custom_call_target="tpu_custom_call" | custom-call | flops 33554432 | bytes 4261904 | tf_op jit(solution)/shard_map/face1/pallas_call | solution.py:723
  21.0 1.5 %collective-permute-start.5 = (f32[16,16,128]{2,1,0:T(8,128)S(1)}, f32[16,16,128]{2,1,0:T(8,128)S(1)}, u32[]{:S(2)}, u32[]{:S(2)}) collective-permute-start(f32[16,16,128]{2,1,0:T(8,128)S(1)} %face1.1), channel_id=1, source_target_pairs={{0,16},{16,0},{1,17},{17,1},{2,18},{18,2},{3,19},{19,3},{4,20},{20... | collective-permute-start | bytes 393224 | tf_op jit(solution)/shard_map/ppermute | solution.py:885
  22.5 6.1 %nodes0_edges1.1 = (f32[16,16,16,128]{3,2,1,0:T(8,128)S(1)}, bf16[16,16,16,128]{3,2,1,0:T(8,128)(2,1)S(1)}, bf16[16,16,16,128]{3,2,1,0:T(8,128)(2,1)S(1)}, f32[1...) custom-call(s32[4]{0:T(128)S(1)} %pad_add_fusion.sc.sc_ref, ...), custom_call_target="tpu_custom_call", output_to_operand_aliasing={{0}: (5, {})} | custom-call | flops 1073741824 | bytes 20383760 | tf_op jit(solution)/shard_map/nodes0_edges1/pallas_call | solution.py:723
  29.1 5.1 %collective-permute-start.6 = (f32[16,16,128]{2,1,0:T(8,128)S(1)}, f32[16,16,128]{2,1,0:T(8,128)S(1)}, u32[]{:S(2)}, u32[]{:S(2)}) collective-permute-start(f32[16,16,128]{2,1,0:T(8,128)S(1)} %get-tuple-element.142), channel_id=1, source_target_pairs={{0,4},{4,0},{8,12},{12,8},{1,5},{5,1},{9,13},{13,9},{2,6},{6,2},{1... | collective-permute-start | bytes 393224 | tf_op jit(solution)/shard_map/ppermute | solution.py:885
  35.2 0.7 fix_z.5
  35.9 4.2 %collective-permute-start.8 = (f32[16,16,128]{2,1,0:T(8,128)S(1)}, f32[16,16,128]{2,1,0:T(8,128)S(1)}, u32[]{:S(2)}, u32[]{:S(2)}) collective-permute-start(f32[16,16,128]{2,1,0:T(8,128)S(1)} %get-tuple-element.149), channel_id=1, source_target_pairs={{0,1},{1,0},{2,3},{3,2},{4,5},{5,4},{6,7},{7,6},{8,9},{9,8},{10,11... | collective-permute-start | bytes 393224 | tf_op jit(solution)/shard_map/ppermute | solution.py:885
  40.8 2.6 %slopes.3 = f32[3,16,16,16,128]{4,3,2,1,0:T(8,128)S(1)} custom-call(s32[4]{0:T(128)S(1)} %pad_add_fusion.sc.sc_ref, f32[3,16,16,16,128]{4,3,2,1,0:T(8,128)S(1)} %get-tuple-element.151.half_in), custom_call_target="tpu_custom_call", output_to_operand_aliasing={{}: (1, {})} | custom-call | flops 134217728 | bytes 12582928 | tf_op jit(solution)/shard_map/slopes/pallas_call | solution.py:723
  43.4 1.2 face2.1
  45.2 3.6 %nodes1_back.1 = (f32[16,16,16,128]{3,2,1,0:T(8,128)S(1)}, bf16[16,16,16,128]{3,2,1,0:T(8,128)(2,1)S(1)}, bf16[16,16,16,128]{3,2,1,0:T(8,128)(2,1)S(1)}, bf16[16...) custom-call(s32[4]{0:T(128)S(1)} %pad_add_fusion.sc.sc_ref, ...), custom_call_target="tpu_custom_call", output_to_operand_aliasing={{0}: (5, {})} | custom-call | flops 939524096 | bytes 13043728 | tf_op jit(solution)/shard_map/nodes1_back/pallas_call | solution.py:723
  48.8 0.8 collective-permute-done.10.refs_0_
  50.2 0.8 collective-permute-start.11
  51.0 8.6 %collective-permute-start.12 = (f32[16,16,128]{2,1,0:T(8,128)S(1)}, f32[16,16,128]{2,1,0:T(8,128)S(1)}, u32[]{:S(2)}, u32[]{:S(2)}) collective-permute-start(f32[16,16,128]{2,1,0:T(8,128)S(1)} %get-tuple-element.159), channel_id=1, source_target_pairs={{0,4},{4,0},{8,12},{12,8},{1,5},{5,1},{9,13},{13,9},{2,6},{6,2},{1... | collective-permute-start | bytes 393224 | tf_op jit(solution)/shard_map/ppermute | solution.py:885
  59.6 1.0 collective-permute-done.12.refs_2_.refs_1_
  60.6 0.7 fix_z.6
  61.3 3.8 %collective-permute-start.13 = (f32[16,16,128]{2,1,0:T(8,128)S(1)}, f32[16,16,128]{2,1,0:T(8,128)S(1)}, u32[]{:S(2)}, u32[]{:S(2)}) collective-permute-start(f32[16,16,128]{2,1,0:T(8,128)S(1)} %get-tuple-element.167), channel_id=1, source_target_pairs={{0,1},{1,0},{2,3},{3,2},{4,5},{5,4},{6,7},{7,6},{8,9},{9,8},{10,11... | collective-permute-start | bytes 393224 | tf_op jit(solution)/shard_map/ppermute | solution.py:885
  65.8 1.6 %nodes1_products.1 = (f32[16,16,16,128]{3,2,1,0:T(8,128)S(1)}, f32[392,128]{1,0:T(8,128)S(1)}) custom-call(s32[4]{0:T(128)S(1)} %pad_add_fusion.sc.sc_ref, bf16[2,256,128]{2,1,0:T(8,128)(2,1)S(1)} %copy-done.4, bf16[16,16,16,128]{3,2,1,0:T(8,128)(2,1)S(1)} %get-tuple-element.197.h, bf16[16,16,16,128]{3,2,1,0:T(8,128)(2,1)S(1)} %bitcast.18, ...), custom_call_target="tpu_custom_call" | custom-call | flops 805306368 | bytes 7671824 | tf_op jit(solution)/shard_map/nodes1_products/pallas_call | solution.py:723
  67.4 1.4 %collective-permute-done.13.refs_3_ = f32[16,16,128]{2,1,0:T(8,128)S(1)} collective-permute-done((f32[16,16,128]{2,1,0:T(8,128)S(1)}, f32[16,16,128]{2,1,0:T(8,128)S(1)}, u32[]{:S(2)}, u32[]{:S(2)}) %collective-permute-start.13) | collective-permute-done | bytes 131104 | tf_op jit(solution)/shard_map/ppermute | solution.py:885
  68.8 1.3 %face3.1 = f32[16,16,128]{2,1,0:T(8,128)S(1)} custom-call(s32[4]{0:T(128)S(1)} %pad_add_fusion.sc.sc_ref, bf16[2,2,128,128]{3,2,1,0:T(8,128)(2,1)S(1)} %copy-done.3, bf16[2,256,128]{2,1,0:T(8,128)(2,1)S(1)} %copy-done.4, bf16[2,128,128]{2,1,0:T(8,128)(2,1)S(1)} %copy-done.6, f32[2,2,128]{2,1,0:T(2,128)S(1)} %copy-done.7, ...), custom_call_target="tpu_custom_call" | custom-call | flops 33554432 | bytes 13699088 | tf_op jit(solution)/shard_map/face3/pallas_call | solution.py:723
  70.1 0.8 collective-permute-start.15
  70.8 5.3 %edges1_back_nodes0_back.1 = (f32[16,16,16,128]{3,2,1,0:T(8,128)S(1)}, bf16[16,16,16,128]{3,2,1,0:T(8,128)(2,1)S(1)}, bf16[16,16,16,128]{3,2,1,0:T(8,128)(2,1)S(...) custom-call(s32[4]{0:T(128)S(1)} %pad_add_fusion.sc.sc_ref, ...), custom_call_target="tpu_custom_call", output_to_operand_aliasing={{0}: (5, {})} | custom-call | flops 1207959552 | bytes 20387856 | tf_op jit(solution)/shard_map/edges1_back_nodes0_back/pallas_call | solution.py:723
  77.7 1.7 %gradient_sums.1 = (f32[480,128]{1,0:T(8,128)S(1)}, f32[480,128]{1,0:T(8,128)S(1)}) custom-call(s32[4]{0:T(128)S(1)} %pad_add_fusion.sc.sc_ref, bf16[16,16,16,128]{3,2,1,0:T(8,128)(2,1)S(1)} %get-tuple-element.197.h, f32[16,16,16,128]{3,2,1,0:T(8,128)S(1)} %get-tuple-element.198.edges, bf16[16,16,16,128]{3,2,1,0:T(8,128)(2,1)S(1)} %get-tuple-element.227.grad.grad_in, ...), custom_call_target="tpu_custom_call" | custom-call | flops 671088640 | bytes 9084944 | tf_op jit(solution)/shard_map/gradient_sums/pallas_call | solution.py:723
  79.5 4.4 %collective-permute-start.20 = (f32[480,128]{1,0:T(8,128)S(1)}, f32[480,128]{1,0:T(8,128)S(1)}, u32[]{:S(2)}, u32[]{:S(2)}) collective-permute-start(f32[480,128]{1,0:T(8,128)S(1)} %get-tuple-element.218), channel_id=1, source_target_pairs={{0,4},{4,0},{8,12},{12,8},{1,5},{5,1},{9,13},{13,9},{2,6},{6,2},{1... | collective-permute-start | bytes 737288 | tf_op jit(solution)/shard_map/ppermute | solution.py:790
  83.8 0.7 fix_z.7
  84.5 4.0 %collective-permute-start.18 = (f32[16,16,128]{2,1,0:T(8,128)S(1)}, f32[16,16,128]{2,1,0:T(8,128)S(1)}, u32[]{:S(2)}, u32[]{:S(2)}) collective-permute-start(f32[16,16,128]{2,1,0:T(8,128)S(1)} %get-tuple-element.212), channel_id=1, source_target_pairs={{0,1},{1,0},{2,3},{3,2},{4,5},{5,4},{6,7},{7,6},{8,9},{9,8},{10,11... | collective-permute-start | bytes 393224 | tf_op jit(solution)/shard_map/ppermute | solution.py:885
  89.8 1.4 %collective-permute-start.21 = (f32[240,128]{1,0:T(8,128)S(1)}, f32[240,128]{1,0:T(8,128)S(1)}, u32[]{:S(2)}, u32[]{:S(2)}) collective-permute-start(f32[240,128]{1,0:T(8,128)S(1)} %get-tuple-element.222), channel_id=1, source_target_pairs={{0,16},{16,0},{1,17},{17,1},{2,18},{18,2},{3,19},{19,3},{4,20},{20... | collective-permute-start | bytes 368648 | tf_op jit(solution)/shard_map/ppermute | solution.py:790
  91.2 1.0 collective-permute-done.18.refs_3_
  92.2 2.6 %collective-permute-done.21.got = f32[240,128]{1,0:T(8,128)S(1)} collective-permute-done((f32[240,128]{1,0:T(8,128)S(1)}, f32[240,128]{1,0:T(8,128)S(1)}, u32[]{:S(2)}, u32[]{:S(2)}) %collective-permute-start.21) | collective-permute-done | bytes 122912 | tf_op jit(solution)/shard_map/ppermute | solution.py:790
  95.4 2.2 %collective-permute-start.22 = (f32[120,128]{1,0:T(8,128)S(1)}, f32[120,128]{1,0:T(8,128)S(1)}, u32[]{:S(2)}, u32[]{:S(2)}) collective-permute-start(f32[120,128]{1,0:T(8,128)S(1)} %get-tuple-element.224), channel_id=1, source_target_pairs={{0,8},{4,12},{8,0},{12,4},{1,9},{5,13},{9,1},{13,5},{2,10},{6,14},... | collective-permute-start | bytes 184328 | tf_op jit(solution)/shard_map/ppermute | solution.py:790
  97.5 3.9 %edges0_back.1 = (f32[16,16,16,128]{3,2,1,0:T(8,128)S(1)}, f32[136,128]{1,0:T(8,128)S(1)}, s32[3,8,128]{2,1,0:T(8,128)S(1)}) custom-call(s32[4]{0:T(128)S(1)} %pad_add_fusion.sc.sc_ref, bf16[2,2,128,128]{3,2,1,0:T(8,128)(2,1)S(1)} %copy-done.3, bf16[2,256,128]{2,1,0:T(8,128)(2,1)S(1)} %copy-done.4, ...), custom_call_target="tpu_custom_call", output_to_operand_aliasing={{0}: (5, {})} | custom-call | flops 805306368 | bytes 12601360 | tf_op jit(solution)/shard_map/edges0_back/pallas_call | solution.py:723
  101.5 3.1 %collective-permute-start.23 = (f32[256,128]{1,0:T(8,128)S(1)}, f32[256,128]{1,0:T(8,128)S(1)}, u32[]{:S(2)}, u32[]{:S(2)}) collective-permute-start(f32[256,128]{1,0:T(8,128)S(1)} %pad_maximum_fusion.2), channel_id=1, source_target_pairs={{0,2},{1,3},{2,0},{3,1},{4,6},{5,7},{6,4},{7,5},{8,10},{9,11},{10,... | collective-permute-start | bytes 393224 | tf_op jit(solution)/shard_map/ppermute | solution.py:790
  104.6 2.5 %state_grad.1 = bf16[16,16,16,128]{3,2,1,0:T(8,128)(2,1)} custom-call(s32[4]{0:T(128)S(1)} %pad_add_fusion.sc.sc_ref, bf16[2,2,128,128]{3,2,1,0:T(8,128)(2,1)S(1)} %copy-done.3, bf16[2,256,128]{2,1,0:T(8,128)(2,1)S(1)} %copy-done.4, bf16[16,16,16,128]{3,2,1,0:T(8,128)(2,1)S(1)} %get-tuple-element.227.grad.grad_in, ...), custom_call_target="tpu_custom_call" | custom-call | flops 536870912 | bytes 5505040 | tf_op jit(solution)/shard_map/state_grad/pallas_call | solution.py:723
  107.1 3.5 %collective-permute-done.23 = f32[256,128]{1,0:T(8,128)S(1)} collective-permute-done((f32[256,128]{1,0:T(8,128)S(1)}, f32[256,128]{1,0:T(8,128)S(1)}, u32[]{:S(2)}, u32[]{:S(2)}) %collective-permute-start.23) | collective-permute-done | bytes 131104 | tf_op jit(solution)/shard_map/ppermute | solution.py:790
  110.8 4.9 %collective-permute-done.24 = f32[256,128]{1,0:T(8,128)S(1)} collective-permute-done((f32[256,128]{1,0:T(8,128)S(1)}, f32[256,128]{1,0:T(8,128)S(1)}, u32[]{:S(2)}, u32[]{:S(2)}) %collective-permute-start.24) | collective-permute-done | bytes 131104 | tf_op jit(solution)/shard_map/ppermute | solution.py:790
  116.0 4.7 %collective-permute-done.25 = f32[256,128]{1,0:T(8,128)S(1)} collective-permute-done((f32[256,128]{1,0:T(8,128)S(1)}, f32[256,128]{1,0:T(8,128)S(1)}, u32[]{:S(2)}, u32[]{:S(2)}) %collective-permute-start.25) | collective-permute-done | bytes 131104 | tf_op jit(solution)/shard_map/ppermute | solution.py:790
  120.7 1.4 %collective-permute-start.26 = (f32[376,128]{1,0:T(8,128)S(1)}, f32[376,128]{1,0:T(8,128)S(1)}, u32[]{:S(2)}, u32[]{:S(2)}) collective-permute-start(f32[376,128]{1,0:T(8,128)S(1)} %pad_maximum_fusion.1), channel_id=1, source_target_pairs={{0,16},{16,0},{1,17},{17,1},{2,18},{18,2},{3,19},{19,3},{4,20},{20... | collective-permute-start | bytes 577544 | tf_op jit(solution)/shard_map/ppermute | solution.py:790
  122.1 4.3 %collective-permute-done.26 = f32[376,128]{1,0:T(8,128)S(1)} collective-permute-done((f32[376,128]{1,0:T(8,128)S(1)}, f32[376,128]{1,0:T(8,128)S(1)}, u32[]{:S(2)}, u32[]{:S(2)}) %collective-permute-start.26) | collective-permute-done | bytes 192544 | tf_op jit(solution)/shard_map/ppermute | solution.py:790
  126.6 1.6 %collective-permute-done.27.got = f32[616,128]{1,0:T(8,128)S(1)} collective-permute-done((f32[616,128]{1,0:T(8,128)S(1)}, f32[616,128]{1,0:T(8,128)S(1)}, u32[]{:S(2)}, u32[]{:S(2)}) %collective-permute-start.27) | collective-permute-done | bytes 315424 | tf_op jit(solution)/shard_map/ppermute | solution.py:790
  128.2 1.7 %finish.1 = (f32[2,2,128,128]{3,2,1,0:T(8,128)}, f32[2,256,128]{2,1,0:T(8,128)}, f32[2,128,128]{2,1,0:T(8,128)}, f32[2,2,128]{2,1,0:T(2,128)}) custom-call(s32[4]{0:T(128)S(1)} %pad_add_fusion.sc.sc_ref, bf16[2,2,128,128]{3,2,1,0:T(8,128)(2,1)S(1)} %copy-done.3, bf16[2,256,128]{2,1,0:T(8,128)(2,1)S(1)} %copy-done.4, f32[616,128]{1,0:T(8,128)S(1)} %pad_maximum_fusion.value, ...), custom_call_target="tpu_custom_call" | custom-call | bytes 1550352 | tf_op jit(solution)/shard_map/finish/pallas_call | solution.py:723
  (64 shorter events, 10.4 us)
Async XLA Ops:
  1.4 1.2 copy-start
  2.6 0.9 copy-start.2
  3.5 0.7 copy-start.7
  5.0 6.8 %collective-permute-start = (f32[16,16,128]{2,1,0:T(8,128)S(1)}, f32[16,16,128]{2,1,0:T(8,128)S(1)}, u32[]{:S(2)}, u32[]{:S(2)}) collective-permute-start(f32[16,16,128]{2,1,0:T(8,128)S(1)} %face0.1), channel_id=1, source_target_pairs={{0,16},{16,0},{1,17},{17,1},{2,18},{18,2},{3,19},{19,3},{4,20},{20... | collective-permute-start | bytes 393224 | tf_op jit(solution)/shard_map/ppermute | solution.py:885
  12.3 1.4 %collective-permute-start.1 = (f32[16,16,128]{2,1,0:T(8,128)S(1)}, f32[16,16,128]{2,1,0:T(8,128)S(1)}, u32[]{:S(2)}, u32[]{:S(2)}) collective-permute-start(f32[16,16,128]{2,1,0:T(8,128)S(1)} %get-tuple-element.125), channel_id=1, source_target_pairs={{0,4},{4,0},{8,12},{12,8},{1,5},{5,1},{9,13},{13,9},{2,6},{6,2},{1... | collective-permute-start | bytes 393224 | tf_op jit(solution)/shard_map/ppermute | solution.py:885
  12.4 1.3 %collective-permute-start.2 = (f32[16,16,128]{2,1,0:T(8,128)S(1)}, f32[16,16,128]{2,1,0:T(8,128)S(1)}, u32[]{:S(2)}, u32[]{:S(2)}) collective-permute-start(f32[16,16,128]{2,1,0:T(8,128)S(1)} %get-tuple-element.126), channel_id=1, source_target_pairs={{4,8},{8,4},{5,9},{9,5},{6,10},{10,6},{7,11},{11,7},{20,24},{24,20... | collective-permute-start | bytes 393224 | tf_op jit(solution)/shard_map/ppermute | solution.py:885
  14.4 5.1 %copy-start.1 = (bf16[16,16,2,8,128]{4,3,2,1,0:T(8,128)(2,1)S(1)}, bf16[16,16,2,8,128]{4,3,2,1,0:T(8,128)(2,1)}, u32[]{:S(2)}) copy-start(bf16[16,16,2,8,128]{4,3,2,1,0:T(8,128)(2,1)} %param.7) | copy-start | bytes 3145732
  14.5 5.1 %copy-start.3 = (bf16[2,2,128,128]{3,2,1,0:T(8,128)(2,1)S(1)}, bf16[2,2,128,128]{3,2,1,0:T(8,128)(2,1)}, u32[]{:S(2)}) copy-start(bf16[2,2,128,128]{3,2,1,0:T(8,128)(2,1)} %edge_w.21) | copy-start | bytes 393220
  14.5 5.1 %copy-start.4 = (bf16[2,256,128]{2,1,0:T(8,128)(2,1)S(1)}, bf16[2,256,128]{2,1,0:T(8,128)(2,1)}, u32[]{:S(2)}) copy-start(bf16[2,256,128]{2,1,0:T(8,128)(2,1)} %node_in.19) | copy-start | bytes 393220
  14.5 5.1 %copy-start.6 = (bf16[2,128,128]{2,1,0:T(8,128)(2,1)S(1)}, bf16[2,128,128]{2,1,0:T(8,128)(2,1)}, u32[]{:S(2)}) copy-start(bf16[2,128,128]{2,1,0:T(8,128)(2,1)} %node_out.13) | copy-start | bytes 196612
  14.5 5.0 %collective-permute-start.3 = (f32[16,16,128]{2,1,0:T(8,128)S(1)}, f32[16,16,128]{2,1,0:T(8,128)S(1)}, u32[]{:S(2)}, u32[]{:S(2)}) collective-permute-start(f32[16,16,128]{2,1,0:T(8,128)S(1)} %get-tuple-element.132), channel_id=1, source_target_pairs={{0,1},{1,0},{2,3},{3,2},{4,5},{5,4},{6,7},{7,6},{8,9},{9,8},{10,11... | collective-permute-start | bytes 393224 | tf_op jit(solution)/shard_map/ppermute | solution.py:885
  16.1 3.4 %collective-permute-start.4 = (f32[16,16,128]{2,1,0:T(8,128)S(1)}, f32[16,16,128]{2,1,0:T(8,128)S(1)}, u32[]{:S(2)}, u32[]{:S(2)}) collective-permute-start(f32[16,16,128]{2,1,0:T(8,128)S(1)} %get-tuple-element.133), channel_id=1, source_target_pairs={{1,2},{2,1},{5,6},{6,5},{9,10},{10,9},{13,14},{14,13},{17,18},{18,... | collective-permute-start | bytes 393224 | tf_op jit(solution)/shard_map/ppermute | solution.py:885
  21.0 7.6 %collective-permute-start.5 = (f32[16,16,128]{2,1,0:T(8,128)S(1)}, f32[16,16,128]{2,1,0:T(8,128)S(1)}, u32[]{:S(2)}, u32[]{:S(2)}) collective-permute-start(f32[16,16,128]{2,1,0:T(8,128)S(1)} %face1.1), channel_id=1, source_target_pairs={{0,16},{16,0},{1,17},{17,1},{2,18},{18,2},{3,19},{19,3},{4,20},{20... | collective-permute-start | bytes 393224 | tf_op jit(solution)/shard_map/ppermute | solution.py:885
  29.1 6.1 %collective-permute-start.6 = (f32[16,16,128]{2,1,0:T(8,128)S(1)}, f32[16,16,128]{2,1,0:T(8,128)S(1)}, u32[]{:S(2)}, u32[]{:S(2)}) collective-permute-start(f32[16,16,128]{2,1,0:T(8,128)S(1)} %get-tuple-element.142), channel_id=1, source_target_pairs={{0,4},{4,0},{8,12},{12,8},{1,5},{5,1},{9,13},{13,9},{2,6},{6,2},{1... | collective-permute-start | bytes 393224 | tf_op jit(solution)/shard_map/ppermute | solution.py:885
  34.2 1.0 collective-permute-start.7
  35.9 7.5 %copy-start.5 = (bf16[16,16,2,8,128]{4,3,2,1,0:T(8,128)(2,1)S(1)}, bf16[16,16,2,8,128]{4,3,2,1,0:T(8,128)(2,1)}, u32[]{:S(2)}) copy-start(bf16[16,16,2,8,128]{4,3,2,1,0:T(8,128)(2,1)} %param.8) | copy-start | bytes 3145732
  35.9 7.4 %collective-permute-start.8 = (f32[16,16,128]{2,1,0:T(8,128)S(1)}, f32[16,16,128]{2,1,0:T(8,128)S(1)}, u32[]{:S(2)}, u32[]{:S(2)}) collective-permute-start(f32[16,16,128]{2,1,0:T(8,128)S(1)} %get-tuple-element.149), channel_id=1, source_target_pairs={{0,1},{1,0},{2,3},{3,2},{4,5},{5,4},{6,7},{7,6},{8,9},{9,8},{10,11... | collective-permute-start | bytes 393224 | tf_op jit(solution)/shard_map/ppermute | solution.py:885
  40.1 3.3 %collective-permute-start.9 = (f32[16,16,128]{2,1,0:T(8,128)S(1)}, f32[16,16,128]{2,1,0:T(8,128)S(1)}, u32[]{:S(2)}, u32[]{:S(2)}) collective-permute-start(f32[16,16,128]{2,1,0:T(8,128)S(1)} %get-tuple-element.150), channel_id=1, source_target_pairs={{1,2},{2,1},{5,6},{6,5},{9,10},{10,9},{13,14},{14,13},{17,18},{18,... | collective-permute-start | bytes 393224 | tf_op jit(solution)/shard_map/ppermute | solution.py:885
  44.6 5.0 %collective-permute-start.10 = (f32[16,16,128]{2,1,0:T(8,128)S(1)}, f32[16,16,128]{2,1,0:T(8,128)S(1)}, u32[]{:S(2)}, u32[]{:S(2)}) collective-permute-start(f32[16,16,128]{2,1,0:T(8,128)S(1)} %face2.1), channel_id=1, source_target_pairs={{0,16},{16,0},{1,17},{17,1},{2,18},{18,2},{3,19},{19,3},{4,20},{20... | collective-permute-start | bytes 393224 | tf_op jit(solution)/shard_map/ppermute | solution.py:885
  50.2 9.5 %collective-permute-start.11 = (f32[16,16,128]{2,1,0:T(8,128)S(1)}, f32[16,16,128]{2,1,0:T(8,128)S(1)}, u32[]{:S(2)}, u32[]{:S(2)}) collective-permute-start(f32[16,16,128]{2,1,0:T(8,128)S(1)} %get-tuple-element.158), channel_id=1, source_target_pairs={{4,8},{8,4},{5,9},{9,5},{6,10},{10,6},{7,11},{11,7},{20,24},{24,20... | collective-permute-start | bytes 393224 | tf_op jit(solution)/shard_map/ppermute | solution.py:885
  51.0 9.6 %collective-permute-start.12 = (f32[16,16,128]{2,1,0:T(8,128)S(1)}, f32[16,16,128]{2,1,0:T(8,128)S(1)}, u32[]{:S(2)}, u32[]{:S(2)}) collective-permute-start(f32[16,16,128]{2,1,0:T(8,128)S(1)} %get-tuple-element.159), channel_id=1, source_target_pairs={{0,4},{4,0},{8,12},{12,8},{1,5},{5,1},{9,13},{13,9},{2,6},{6,2},{1... | collective-permute-start | bytes 393224 | tf_op jit(solution)/shard_map/ppermute | solution.py:885
  61.3 7.5 %collective-permute-start.13 = (f32[16,16,128]{2,1,0:T(8,128)S(1)}, f32[16,16,128]{2,1,0:T(8,128)S(1)}, u32[]{:S(2)}, u32[]{:S(2)}) collective-permute-start(f32[16,16,128]{2,1,0:T(8,128)S(1)} %get-tuple-element.167), channel_id=1, source_target_pairs={{0,1},{1,0},{2,3},{3,2},{4,5},{5,4},{6,7},{7,6},{8,9},{9,8},{10,11... | collective-permute-start | bytes 393224 | tf_op jit(solution)/shard_map/ppermute | solution.py:885
  65.1 3.7 %collective-permute-start.14 = (f32[16,16,128]{2,1,0:T(8,128)S(1)}, f32[16,16,128]{2,1,0:T(8,128)S(1)}, u32[]{:S(2)}, u32[]{:S(2)}) collective-permute-start(f32[16,16,128]{2,1,0:T(8,128)S(1)} %get-tuple-element.168), channel_id=1, source_target_pairs={{1,2},{2,1},{5,6},{6,5},{9,10},{10,9},{13,14},{14,13},{17,18},{18,... | collective-permute-start | bytes 393224 | tf_op jit(solution)/shard_map/ppermute | solution.py:885
  70.1 6.1 %collective-permute-start.15 = (f32[16,16,128]{2,1,0:T(8,128)S(1)}, f32[16,16,128]{2,1,0:T(8,128)S(1)}, u32[]{:S(2)}, u32[]{:S(2)}) collective-permute-start(f32[16,16,128]{2,1,0:T(8,128)S(1)} %face3.1), channel_id=1, source_target_pairs={{0,16},{16,0},{1,17},{17,1},{2,18},{18,2},{3,19},{19,3},{4,20},{20... | collective-permute-start | bytes 393224 | tf_op jit(solution)/shard_map/ppermute | solution.py:885
  76.8 2.7 %collective-permute-start.16 = (f32[16,16,128]{2,1,0:T(8,128)S(1)}, f32[16,16,128]{2,1,0:T(8,128)S(1)}, u32[]{:S(2)}, u32[]{:S(2)}) collective-permute-start(f32[16,16,128]{2,1,0:T(8,128)S(1)} %get-tuple-element.195), channel_id=1, source_target_pairs={{0,4},{4,0},{8,12},{12,8},{1,5},{5,1},{9,13},{13,9},{2,6},{6,2},{1... | collective-permute-start | bytes 393224 | tf_op jit(solution)/shard_map/ppermute | solution.py:885
  77.1 2.4 %collective-permute-start.17 = (f32[16,16,128]{2,1,0:T(8,128)S(1)}, f32[16,16,128]{2,1,0:T(8,128)S(1)}, u32[]{:S(2)}, u32[]{:S(2)}) collective-permute-start(f32[16,16,128]{2,1,0:T(8,128)S(1)} %get-tuple-element.196), channel_id=1, source_target_pairs={{4,8},{8,4},{5,9},{9,5},{6,10},{10,6},{7,11},{11,7},{20,24},{24,20... | collective-permute-start | bytes 393224 | tf_op jit(solution)/shard_map/ppermute | solution.py:885
  79.5 9.7 %collective-permute-start.20 = (f32[480,128]{1,0:T(8,128)S(1)}, f32[480,128]{1,0:T(8,128)S(1)}, u32[]{:S(2)}, u32[]{:S(2)}) collective-permute-start(f32[480,128]{1,0:T(8,128)S(1)} %get-tuple-element.218), channel_id=1, source_target_pairs={{0,4},{4,0},{8,12},{12,8},{1,5},{5,1},{9,13},{13,9},{2,6},{6,2},{1... | collective-permute-start | bytes 737288 | tf_op jit(solution)/shard_map/ppermute | solution.py:790
  84.5 7.7 %collective-permute-start.18 = (f32[16,16,128]{2,1,0:T(8,128)S(1)}, f32[16,16,128]{2,1,0:T(8,128)S(1)}, u32[]{:S(2)}, u32[]{:S(2)}) collective-permute-start(f32[16,16,128]{2,1,0:T(8,128)S(1)} %get-tuple-element.212), channel_id=1, source_target_pairs={{0,1},{1,0},{2,3},{3,2},{4,5},{5,4},{6,7},{7,6},{8,9},{9,8},{10,11... | collective-permute-start | bytes 393224 | tf_op jit(solution)/shard_map/ppermute | solution.py:885
  88.5 3.7 %collective-permute-start.19 = (f32[16,16,128]{2,1,0:T(8,128)S(1)}, f32[16,16,128]{2,1,0:T(8,128)S(1)}, u32[]{:S(2)}, u32[]{:S(2)}) collective-permute-start(f32[16,16,128]{2,1,0:T(8,128)S(1)} %get-tuple-element.213), channel_id=1, source_target_pairs={{1,2},{2,1},{5,6},{6,5},{9,10},{10,9},{13,14},{14,13},{17,18},{18,... | collective-permute-start | bytes 393224 | tf_op jit(solution)/shard_map/ppermute | solution.py:885
  89.8 5.0 %collective-permute-start.21 = (f32[240,128]{1,0:T(8,128)S(1)}, f32[240,128]{1,0:T(8,128)S(1)}, u32[]{:S(2)}, u32[]{:S(2)}) collective-permute-start(f32[240,128]{1,0:T(8,128)S(1)} %get-tuple-element.222), channel_id=1, source_target_pairs={{0,16},{16,0},{1,17},{17,1},{2,18},{18,2},{3,19},{19,3},{4,20},{20... | collective-permute-start | bytes 368648 | tf_op jit(solution)/shard_map/ppermute | solution.py:790
  95.4 6.1 %collective-permute-start.22 = (f32[120,128]{1,0:T(8,128)S(1)}, f32[120,128]{1,0:T(8,128)S(1)}, u32[]{:S(2)}, u32[]{:S(2)}) collective-permute-start(f32[120,128]{1,0:T(8,128)S(1)} %get-tuple-element.224), channel_id=1, source_target_pairs={{0,8},{4,12},{8,0},{12,4},{1,9},{5,13},{9,1},{13,5},{2,10},{6,14},... | collective-permute-start | bytes 184328 | tf_op jit(solution)/shard_map/ppermute | solution.py:790
  101.5 9.1 %collective-permute-start.23 = (f32[256,128]{1,0:T(8,128)S(1)}, f32[256,128]{1,0:T(8,128)S(1)}, u32[]{:S(2)}, u32[]{:S(2)}) collective-permute-start(f32[256,128]{1,0:T(8,128)S(1)} %pad_maximum_fusion.2), channel_id=1, source_target_pairs={{0,2},{1,3},{2,0},{3,1},{4,6},{5,7},{6,4},{7,5},{8,10},{9,11},{10,... | collective-permute-start | bytes 393224 | tf_op jit(solution)/shard_map/ppermute | solution.py:790
  110.6 5.0 %collective-permute-start.24 = (f32[256,128]{1,0:T(8,128)S(1)}, f32[256,128]{1,0:T(8,128)S(1)}, u32[]{:S(2)}, u32[]{:S(2)}) collective-permute-start(f32[256,128]{1,0:T(8,128)S(1)} %add.16), channel_id=1, source_target_pairs={{0,1},{1,0},{2,3},{3,2},{4,5},{5,4},{6,7},{7,6},{8,9},{9,8},{10,11... | collective-permute-start | bytes 393224 | tf_op jit(solution)/shard_map/ppermute | solution.py:790
  115.6 5.0 %collective-permute-start.25 = (f32[256,128]{1,0:T(8,128)S(1)}, f32[256,128]{1,0:T(8,128)S(1)}, u32[]{:S(2)}, u32[]{:S(2)}) collective-permute-start(f32[256,128]{1,0:T(8,128)S(1)} %add.17), channel_id=1, source_target_pairs={{0,8},{4,12},{8,0},{12,4},{1,9},{5,13},{9,1},{13,5},{2,10},{6,14},... | collective-permute-start | bytes 393224 | tf_op jit(solution)/shard_map/ppermute | solution.py:790
  120.7 5.7 %collective-permute-start.26 = (f32[376,128]{1,0:T(8,128)S(1)}, f32[376,128]{1,0:T(8,128)S(1)}, u32[]{:S(2)}, u32[]{:S(2)}) collective-permute-start(f32[376,128]{1,0:T(8,128)S(1)} %pad_maximum_fusion.1), channel_id=1, source_target_pairs={{0,16},{16,0},{1,17},{17,1},{2,18},{18,2},{3,19},{19,3},{4,20},{20... | collective-permute-start | bytes 577544 | tf_op jit(solution)/shard_map/ppermute | solution.py:790
  126.5 1.7 %collective-permute-start.27 = (f32[616,128]{1,0:T(8,128)S(1)}, f32[616,128]{1,0:T(8,128)S(1)}, u32[]{:S(2)}, u32[]{:S(2)}) collective-permute-start(f32[616,128]{1,0:T(8,128)S(1)} %pad_maximum_fusion.value), channel_id=1, source_target_pairs={{0,4},{4,0},{8,12},{12,8},{1,5},{5,1},{9,13},{13,9},{2,6},{6,2},{1... | collective-permute-start | bytes 946184 | tf_op jit(solution)/shard_map/ppermute | solution.py:790

commit v13 on v12

--- a/solution.py
+++ b/solution.py
@@ -5,6 +5,7 @@
 import jax.numpy as jnp
 from jax import lax
 from jax.experimental import pallas as pl
+from jax.experimental.layout import Layout, with_layout_constraint
 from jax.experimental.pallas import tpu as pltpu
 from jax.sharding import PartitionSpec as P
 
@@ -228,36 +229,42 @@
             into_ref[:, :, s * NODES + NODES - 1] += jnp.where(sc_ref[0] == s + 1, from_above, 0.0)
 
 
-def fix_y_kernel(counts, sc_ref, *refs):
+def add_line(flag, axis, kind, face, line):
+    place = lax.broadcasted_iota(jnp.int32, face.shape, axis)
+    last = face.shape[axis] - 1
+    here = (flag["low", axis, kind] & (place == 0)) | (flag["high", axis, kind] & (place == last))
+    return face + jnp.where(here, jnp.expand_dims(line, axis), 0.0)
+
+
+def corrected_y(counts, flag, got_x, faces):
     nx, ny, nz = counts
-    got, faces, outs = refs[:nx], refs[nx : nx + ny], refs[nx + ny :]
-    x_len = faces[0].shape[0]
-    for kind in range(nx):
-        place = face_place(sc_ref, 0, kind, x_len - 1)
-        for k in range(ny):
-            y_len = got[kind].shape[0]
-            outs[k][place] += got[kind][face_place(sc_ref, 1, k, y_len - 1)]
-
-
-def fix_z_kernel(counts, sc_ref, *refs):
-    nx, ny, nz = counts
-    got_x, refs = refs[:nx], refs[nx:]
-    got_y, refs = refs[:ny][::-1], refs[ny:]
-    faces, outs = refs[:nz], refs[nz:]
-    x_len, y_len, width = faces[0].shape
-    for k in range(nz):
-        top = takes_top(sc_ref, k)
-        for kind in range(nx):
-            ref = got_x[kind]
-            reader = RowReader(ref.shape[1] // NODES, lambda row, ref=ref: ref[:, row])
-            outs[k][face_place(sc_ref, 0, kind, x_len - 1)] += end_rows(reader, sc_ref[0], top)
-        for kind in range(ny):
-            ref = got_y[kind]
-            reader = RowReader(ref.shape[1] // NODES, lambda row, ref=ref: ref[:, row])
-            add = end_rows(reader, sc_ref[0], top)
-            first = face_place(sc_ref, 1, kind, 1) == 0
-            outs[k][:, 0] += jnp.where(first, add, 0.0)
-            outs[k][:, y_len - 1] += jnp.where(first, 0.0, add)
+    done = []
+    for k, face in enumerate(faces):
+        for kind, got in enumerate(got_x):
+            line = jnp.where(flag["high", 1, k], got[-1], got[0])
+            face = add_line(flag, 0, kind, face, line)
+        done.append(face)
+    return done
+
+
+def corrected_z(counts, flag, got_x, got_y, faces):
+    done = []
+    for k, face in enumerate(faces):
+
+        def layer(got):
+            picked = got[:, 0]
+            for s in range(got.shape[1] // NODES):
+                picked = jnp.where(flag["top", k, s], got[:, s * NODES + NODES - 1], picked)
+            return picked
+
+        for kind, got in enumerate(got_x):
+            line = layer(got)
+            face = add_line(flag, 0, kind, face, line)
+        for kind, got in enumerate(got_y):
+            line = layer(got)
+            face = add_line(flag, 1, kind, face, line)
+        done.append(face)
+    return done
 
 
 def write_inverse(sc_ref, inv_ref, sizes):
@@ -457,7 +464,25 @@
     write_faces(sc, sums, faces, counts)
 
 
-def first_face_kernel(counts, sizes, sc, edge_w, biases, h, *faces):
+def flag_values(sc, counts, sizes, slots):
+    found = {}
+    for axis, number in enumerate(counts):
+        for kind in range(number):
+            even = (sc[1 + axis] + kind) % 2 == 0
+            found["high", axis, kind] = even
+            found["low", axis, kind] = jnp.logical_not(even)
+    for kind in range(counts[2]):
+        for s in range(slots):
+            found["top", kind, s] = takes_top(sc, kind) & (sc[0] == s + 1)
+    for step in halving_steps(sizes):
+        found["bit", step] = bit_of(sc, step) == 1
+    return found
+
+
+def first_face_kernel(counts, sizes, sc, edge_w, biases, h, *refs):
+    faces, flags = refs[:-1], refs[-1]
+    for k, value in enumerate(flag_values(sc, counts, sizes, h.shape[2] // NODES).values()):
+        flags[k] = jnp.full(flags.shape[1:], value.astype(jnp.int32), jnp.int32)
     w_one, bias = half_weights((edge_w, None, None, biases), 0)
     for kind, face in enumerate(faces):
         place, start, at_high = face_planes(sc, kind, h.shape[0])
@@ -661,10 +686,8 @@
 
 def last_kernel(counts, sizes, sc, edge_w, node_in, node_out, biases, sums_in, h, slopes, *refs):
     n = sum(counts)
-    halo, (edges, grads, second) = refs[:n], refs[n:]
+    halo, (edges, grads) = refs[:n], refs[n:]
     grads[...] = jnp.zeros_like(grads)
-    for k, step in enumerate(halving_steps(sizes)):
-        second[k] = jnp.full(second.shape[1:], bit_of(sc, step), jnp.int32)
     edge_parts(counts, sc, (edge_w,), 0, halo, slopes, edges, grads.at[pl.ds(128, NODES)])
 
     def body(x):
@@ -771,11 +794,6 @@
     send[...] = from_ref[pl.ds(pl.multiple_of((1 - bit) * half, NODES), half)]
 
 
-def halve_kernel(step, sc, keep_in, got, keep, send, total):
-    total[...] = keep_in[...] + got[...]
-    write_halves(sc, step, total, keep, send)
-
-
 def join_kernel_of(step, start, sc, value, got, out):
     half = value.shape[0] - start
     bit = bit_of(sc, step)
@@ -794,16 +812,16 @@
     return jax.ShapeDtypeStruct((rows, width), f32)
 
 
-def halve(sc, sizes, keep, send):
+def halve(flag, sizes, keep, send):
     steps = halving_steps(sizes)
     got = swap(send, steps[0])
     for step in steps[1:]:
         keep, got = yield keep, got
-        half = rows_like(keep.shape[0] // 2)
-        keep, send = call(
-            functools.partial(halve_kernel, step), "halve", (sc, keep, got), [half, half],
-            [pltpu.VMEM(keep.shape, f32)],
-        )
+        total = keep + got
+        half = total.shape[0] // 2
+        first, second = total[:half], total[half:]
+        keep = jnp.where(flag["bit", step], second, first)
+        send = jnp.where(flag["bit", step], first, second)
         got = swap(send, step)
     keep, got = yield keep, got
     return keep, got
@@ -883,7 +901,7 @@
     def trade(faces, axis):
         size = lax.axis_size(axis)
         got = [lax.ppermute(face, axis, pairs(size, kind)) for kind, face in reversed(list(enumerate(faces)))]
-        return got[::-1]
+        return [with_layout_constraint(value, Layout(major_to_minor=(0, 1, 2))) for value in got[::-1]]
 
     background = Background()
 
@@ -894,20 +912,16 @@
         return trade(faces, "gx"), faces
 
     def exchange(got_x, faces, work=None, held=(), early=None, early_held=()):
-        fix = functools.partial(fix_y_kernel, trades)
-        same = {1 + nx + k: k for k in range(ny)}
-        faces_y = call(fix, "fix_y", (sc, *got_x, *faces[:ny]), [face_y] * ny, aliases=same)
+        faces_y = corrected_y(trades, flag, got_x, faces[:ny])
         if early is not None:
             faces_y, early_held = lax.optimization_barrier((faces_y, early_held))
             keep, send = early(*early_held)
         got_y = trade(faces_y, "gy")
         if early is not None:
             got_y, (keep, send) = lax.optimization_barrier((got_y, (keep, send)))
-            background.add("sums", halve(sc, sizes, keep, send))
+            background.add("sums", halve(flag, sizes, keep, send))
             background.beside(got_y)
-        fix = functools.partial(fix_z_kernel, trades)
-        same = {1 + nx + ny + k: k for k in range(nz)}
-        faces_z = call(fix, "fix_z", (sc, *got_x, *got_y[::-1], *faces[ny:]), [face_z] * nz, aliases=same)
+        faces_z = corrected_z(trades, flag, got_x, got_y, faces[ny:])
         background.beside(faces_z)
         done = None
         if work is not None:
@@ -925,7 +939,13 @@
             products_kernel, "nodes1_products", (sc, node_in, *held), [full, rows_like(3 * width + NODES)], [], 6 * matmul
         )
 
-    got_x, faces_x = first_trade(first_face_kernel, "face0", (edge_weights, biases, h0), [], matmul // 8)
+    names = list(flag_values([jnp.int32(0)] * 4, trades, sizes, slots))
+    *faces_x, flag_rows = call(
+        functools.partial(first_face_kernel, trades, sizes), "face0", (sc, edge_weights, biases, h0),
+        [face_x] * nx + [sds((len(names), NODES, width), jnp.int32)], [], matmul // 8,
+    )
+    flag = {name: flag_rows[k, 0] == 1 for k, name in enumerate(names)}
+    got_x = trade(faces_x, "gx")
     sums, slopes0, *faces = call(
         functools.partial(first_kernel, trades, sizes), "edges0", (sc, edge_weights, biases, h0),
         [full, full3] + face_outs, [], 3 * matmul,
@@ -963,9 +983,8 @@
     halo, _ = exchange(got_x, faces, early=layer_sums, early_held=held)
     tail_rows = width + NODES
     steps = halving_steps(sizes)
-    edges, last, second = run(
-        last_kernel, "edges0_back", (sums, h0, slopes0, *halo),
-        [full, rows_like(tail_rows), sds((len(steps), NODES, width), jnp.int32)], [], 6, in_place,
+    edges, last = run(
+        last_kernel, "edges0_back", (sums, h0, slopes0, *halo), [full, rows_like(tail_rows)], [], 6, in_place
     )
     keep, got = background.finish("sums")
     value = jnp.concatenate([last, keep + got], 0)
@@ -980,7 +999,7 @@
         got = swap(value, steps[k])
         mine, other = value[tail_rows:], got[tail_rows:]
         joined = jnp.where(
-            second[k, :1] == 0, jnp.concatenate([mine, other], 0), jnp.concatenate([other, mine], 0)
+            flag["bit", steps[k]], jnp.concatenate([other, mine], 0), jnp.concatenate([mine, other], 0)
         )
         value = jnp.concatenate([value[:tail_rows] + got[:tail_rows], joined], 0)
     layers_all = 3 * slots * sizes[2] // 4

time: 130 us -> 128 us (0.985)
  Pallas kernels: 46.2 us -> 40.1 us
  waiting for transfers between devices: 26.8 us -> 30.3 us
  starting transfers between devices: 52.1 us -> 50.5 us
  other arithmetic: 0.23 us -> 1.59 us
    pallas_call x25 -> x15, Pallas kernels: 46.2 us -> 40.1 us  [call(): pl.pallas_call(kernel, name=name, out_shape=tuple(outs), in_specs=[SM] +...]
    ppermute x8, starting transfers between devices: 13 us -> 9.93 us  [swap(): lax.ppermute(value, axis, [(i, i ^ step[1]) for i in range(lax.axis_size(...]
    ppermute x20, waiting for transfers between devices: 5.28 us -> 7.82 us  [trade(): lax.ppermute(face, axis, pairs(size, kind))]
    ppermute x20, starting transfers between devices: 39.1 us -> 40.5 us  [trade(): lax.ppermute(face, axis, pairs(size, kind))]
  transfers between devices with their start and end apart: 28 -> 28, of which waited for: 13 -> 13; matrix products, arithmetic and copies ran while one was open for 0% -> 0% of each run, Pallas kernels for 27% -> 26%
where the time goes in v13:
time: 128 us; the launch traced here: 127 us
  starting transfers between devices  50.5 us (39%)
  Pallas kernels  40.1 us (31%)
  waiting for transfers between devices  30.3 us (24%)
  local copies, waits for them, and re-layouts  2.94 us (2%)
  between operations  1.83 us (1%)
  other arithmetic  1.59 us (1%)
    ppermute x20, starting transfers between devices, trade(): lax.ppermute(face, axis, pairs(size, kind))  40.5 us
    pallas_call x15, Pallas kernels, call(): pl.pallas_call(kernel, name=name, out_shape=tuple(outs), in_specs=[SM] +...  40.1 us
    ppermute x8, waiting for transfers between devices, swap(): lax.ppermute(value, axis, [(i, i ^ step[1]) for i in range(lax.axis_size(...  22.5 us
    ppermute x8, starting transfers between devices, swap(): lax.ppermute(value, axis, [(i, i ^ step[1]) for i in range(lax.axis_size(...  9.93 us
    ppermute x20, waiting for transfers between devices, trade(): lax.ppermute(face, axis, pairs(size, kind))  7.82 us
    unnamed x16, local copies, waits for them, and re-layouts  2.84 us
  transfers between devices with their start and end apart: 28, of which 13 were waited for; matrix products, arithmetic and copies ran while one was open for 0% of the time, Pallas kernels for 26%

profile of v13, /device:TPU:0, one launch (start us, length us, event | category | flops | bytes accessed | tf_op | source)
XLA Modules:
  0.0 127.2 jit_solution(5213537617117843693)
XLA Ops:
  1.4 1.2 copy-done
  2.6 0.9 copy-done.2
  3.5 0.7 copy-done.7
  4.2 0.8 face0.1
  5.0 3.0 %collective-permute-start = (f32[16,16,128]{2,1,0:T(8,128)S(1)}, f32[16,16,128]{2,1,0:T(8,128)S(1)}, u32[]{:S(2)}, u32[]{:S(2)}) collective-permute-start(f32[16,16,128]{2,1,0:T(8,128)S(1)} %get-tuple-element.104), channel_id=1, source_target_pairs={{0,16},{16,0},{1,17},{17,1},{2,18},{18,2},{3,19},{19,3},{4,20},{20... | collective-permute-start | bytes 393224 | tf_op jit(solution)/shard_map/ppermute | solution.py:903
  8.0 3.8 %edges0.1 = (f32[16,16,16,128]{3,2,1,0:T(8,128)S(1)}, f32[3,16,16,16,128]{4,3,2,1,0:T(8,128)S(1)}, f32[16,16,128]{2,1,0:T(8,128)S(1)}, f32[16,16,128]{2,1,0:T(8,...) custom-call(s32[4]{0:T(128)S(1)} %pad_add_fusion.sc, bf16[2,2,128,128]{3,2,1,0:T(8,128)(2,1)S(1)} %copy-done.2, ...), custom_call_target="tpu_custom_call" | custom-call | flops 402653184 | bytes 10094608 | tf_op jit(solution)/shard_map/edges0/pallas_call | solution.py:746
  12.0 0.7 collective-permute-start.2
  12.6 2.9 %collective-permute-start.1 = (f32[16,16,128]{2,1,0:T(8,128)S(1)}, f32[16,16,128]{2,1,0:T(8,128)S(1)}, u32[]{:S(2)}, u32[]{:S(2)}) collective-permute-start(f32[16,16,128]{2,1,0:T(8,128)S(1)} %get-tuple-element.280), channel_id=1, source_target_pairs={{0,4},{4,0},{8,12},{12,8},{1,5},{5,1},{9,13},{13,9},{2,6},{6,2},{1... | collective-permute-start | bytes 393224 | tf_op jit(solution)/shard_map/ppermute | solution.py:903
  15.6 0.9 collective-permute-done.1.refs_1_
  16.8 1.6 %collective-permute-start.3 = (f32[16,16,128]{2,1,0:T(8,128)S(1)}, f32[16,16,128]{2,1,0:T(8,128)S(1)}, u32[]{:S(2)}, u32[]{:S(2)}) collective-permute-start(f32[16,16,128]{2,1,0:T(8,128)S(1)} %get-tuple-element.111), channel_id=1, source_target_pairs={{0,1},{1,0},{2,3},{3,2},{4,5},{5,4},{6,7},{7,6},{8,9},{9,8},{10,11... | collective-permute-start | bytes 393224 | tf_op jit(solution)/shard_map/ppermute | solution.py:903
  19.1 2.6 %slopes.2 = f32[3,16,16,16,128]{4,3,2,1,0:T(8,128)S(1)} custom-call(s32[4]{0:T(128)S(1)} %pad_add_fusion.sc, f32[3,16,16,16,128]{4,3,2,1,0:T(8,128)S(1)} %get-tuple-element.113.half_in), custom_call_target="tpu_custom_call", output_to_operand_aliasing={{}: (1, {})} | custom-call | flops 134217728 | bytes 12582928 | tf_op jit(solution)/shard_map/slopes/pallas_call | solution.py:746
  21.7 1.0 collective-permute-done.3.refs_3_
  22.7 1.4 %face1.1 = f32[16,16,128]{2,1,0:T(8,128)S(1)} custom-call(s32[4]{0:T(128)S(1)} %pad_add_fusion.sc, bf16[2,2,128,128]{3,2,1,0:T(8,128)(2,1)S(1)} %copy-done.3, bf16[2,256,128]{2,1,0:T(8,128)(2,1)S(1)} %copy-done.4, bf16[2,128,128]{2,1,0:T(8,128)(2,1)S(1)} %copy-done.6, f32[2,2,128]{2,1,0:T(2,128)S(1)} %copy-done.7, ...), custom_call_target="tpu_custom_call" | custom-call | flops 33554432 | bytes 4261904 | tf_op jit(solution)/shard_map/face1/pallas_call | solution.py:746
  24.1 1.5 %collective-permute-start.5 = (f32[16,16,128]{2,1,0:T(8,128)S(1)}, f32[16,16,128]{2,1,0:T(8,128)S(1)}, u32[]{:S(2)}, u32[]{:S(2)}) collective-permute-start(f32[16,16,128]{2,1,0:T(8,128)S(1)} %face1.1), channel_id=1, source_target_pairs={{0,16},{16,0},{1,17},{17,1},{2,18},{18,2},{3,19},{19,3},{4,20},{20... | collective-permute-start | bytes 393224 | tf_op jit(solution)/shard_map/ppermute | solution.py:903
  25.6 6.1 %nodes0_edges1.1 = (f32[16,16,16,128]{3,2,1,0:T(8,128)S(1)}, bf16[16,16,16,128]{3,2,1,0:T(8,128)(2,1)S(1)}, bf16[16,16,16,128]{3,2,1,0:T(8,128)(2,1)S(1)}, f32[1...) custom-call(s32[4]{0:T(128)S(1)} %pad_add_fusion.sc, ...), custom_call_target="tpu_custom_call", output_to_operand_aliasing={{0}: (5, {})} | custom-call | flops 1073741824 | bytes 20383760 | tf_op jit(solution)/shard_map/nodes0_edges1/pallas_call | solution.py:746
  31.9 0.7 collective-permute-start.7
  32.5 3.8 %collective-permute-start.6 = (f32[16,16,128]{2,1,0:T(8,128)S(1)}, f32[16,16,128]{2,1,0:T(8,128)S(1)}, u32[]{:S(2)}, u32[]{:S(2)}) collective-permute-start(f32[16,16,128]{2,1,0:T(8,128)S(1)} %get-tuple-element.278), channel_id=1, source_target_pairs={{0,4},{4,0},{8,12},{12,8},{1,5},{5,1},{9,13},{13,9},{2,6},{6,2},{1... | collective-permute-start | bytes 393224 | tf_op jit(solution)/shard_map/ppermute | solution.py:903
  36.3 0.9 collective-permute-done.6.refs_1_
  37.5 4.7 %collective-permute-start.8 = (f32[16,16,128]{2,1,0:T(8,128)S(1)}, f32[16,16,128]{2,1,0:T(8,128)S(1)}, u32[]{:S(2)}, u32[]{:S(2)}) collective-permute-start(f32[16,16,128]{2,1,0:T(8,128)S(1)} %get-tuple-element.124), channel_id=1, source_target_pairs={{0,1},{1,0},{2,3},{3,2},{4,5},{5,4},{6,7},{7,6},{8,9},{9,8},{10,11... | collective-permute-start | bytes 393224 | tf_op jit(solution)/shard_map/ppermute | solution.py:903
  42.2 0.8 collective-permute-start.9
  43.0 2.6 %slopes.3 = f32[3,16,16,16,128]{4,3,2,1,0:T(8,128)S(1)} custom-call(s32[4]{0:T(128)S(1)} %pad_add_fusion.sc, f32[3,16,16,16,128]{4,3,2,1,0:T(8,128)S(1)} %get-tuple-element.126.half_in), custom_call_target="tpu_custom_call", output_to_operand_aliasing={{}: (1, {})} | custom-call | flops 134217728 | bytes 12582928 | tf_op jit(solution)/shard_map/slopes/pallas_call | solution.py:746
  45.6 1.2 face2.1
  46.8 0.7 collective-permute-start.10
  47.5 3.6 %nodes1_back.1 = (f32[16,16,16,128]{3,2,1,0:T(8,128)S(1)}, bf16[16,16,16,128]{3,2,1,0:T(8,128)(2,1)S(1)}, bf16[16,16,16,128]{3,2,1,0:T(8,128)(2,1)S(1)}, bf16[16...) custom-call(s32[4]{0:T(128)S(1)} %pad_add_fusion.sc, ...), custom_call_target="tpu_custom_call", output_to_operand_aliasing={{0}: (5, {})} | custom-call | flops 939524096 | bytes 13043728 | tf_op jit(solution)/shard_map/nodes1_back/pallas_call | solution.py:746
  51.1 1.8 %collective-permute-done.10.refs_0_ = f32[16,16,128]{2,1,0:T(8,128)S(1)} collective-permute-done((f32[16,16,128]{2,1,0:T(8,128)S(1)}, f32[16,16,128]{2,1,0:T(8,128)S(1)}, u32[]{:S(2)}, u32[]{:S(2)}) %collective-permute-start.10) | collective-permute-done | bytes 131104 | tf_op jit(solution)/shard_map/ppermute | solution.py:903
  54.7 4.2 %collective-permute-start.13 = (f32[16,16,128]{2,1,0:T(8,128)S(1)}, f32[16,16,128]{2,1,0:T(8,128)S(1)}, u32[]{:S(2)}, u32[]{:S(2)}) collective-permute-start(f32[16,16,128]{2,1,0:T(8,128)S(1)} %get-tuple-element.138), channel_id=1, source_target_pairs={{0,1},{1,0},{2,3},{3,2},{4,5},{5,4},{6,7},{7,6},{8,9},{9,8},{10,11... | collective-permute-start | bytes 393224 | tf_op jit(solution)/shard_map/ppermute | solution.py:903
  59.5 1.6 %nodes1_products.1 = (f32[16,16,16,128]{3,2,1,0:T(8,128)S(1)}, f32[392,128]{1,0:T(8,128)S(1)}) custom-call(s32[4]{0:T(128)S(1)} %pad_add_fusion.sc, bf16[2,256,128]{2,1,0:T(8,128)(2,1)S(1)} %copy-done.4, bf16[16,16,16,128]{3,2,1,0:T(8,128)(2,1)S(1)} %get-tuple-element.166.h, bf16[16,16,16,128]{3,2,1,0:T(8,128)(2,1)S(1)} %bitcast.104, ...), custom_call_target="tpu_custom_call" | custom-call | flops 805306368 | bytes 7671824 | tf_op jit(solution)/shard_map/nodes1_products/pallas_call | solution.py:746
  61.8 1.3 %face3.1 = f32[16,16,128]{2,1,0:T(8,128)S(1)} custom-call(s32[4]{0:T(128)S(1)} %pad_add_fusion.sc, bf16[2,2,128,128]{3,2,1,0:T(8,128)(2,1)S(1)} %copy-done.3, bf16[2,256,128]{2,1,0:T(8,128)(2,1)S(1)} %copy-done.4, bf16[2,128,128]{2,1,0:T(8,128)(2,1)S(1)} %copy-done.6, f32[2,2,128]{2,1,0:T(2,128)S(1)} %copy-done.7, ...), custom_call_target="tpu_custom_call" | custom-call | flops 33554432 | bytes 13699088 | tf_op jit(solution)/shard_map/face3/pallas_call | solution.py:746
  63.1 0.7 collective-permute-start.15
  63.8 5.3 %edges1_back_nodes0_back.1 = (f32[16,16,16,128]{3,2,1,0:T(8,128)S(1)}, bf16[16,16,16,128]{3,2,1,0:T(8,128)(2,1)S(1)}, bf16[16,16,16,128]{3,2,1,0:T(8,128)(2,1)S(...) custom-call(s32[4]{0:T(128)S(1)} %pad_add_fusion.sc, ...), custom_call_target="tpu_custom_call", output_to_operand_aliasing={{0}: (5, {})} | custom-call | flops 1207959552 | bytes 20387856 | tf_op jit(solution)/shard_map/edges1_back_nodes0_back/pallas_call | solution.py:746
  69.3 4.3 %collective-permute-start.16 = (f32[16,16,128]{2,1,0:T(8,128)S(1)}, f32[16,16,128]{2,1,0:T(8,128)S(1)}, u32[]{:S(2)}, u32[]{:S(2)}) collective-permute-start(f32[16,16,128]{2,1,0:T(8,128)S(1)} %get-tuple-element.164), channel_id=1, source_target_pairs={{0,4},{4,0},{8,12},{12,8},{1,5},{5,1},{9,13},{13,9},{2,6},{6,2},{1... | collective-permute-start | bytes 393224 | tf_op jit(solution)/shard_map/ppermute | solution.py:903
  74.3 1.7 %gradient_sums.1 = (f32[480,128]{1,0:T(8,128)S(1)}, f32[480,128]{1,0:T(8,128)S(1)}) custom-call(s32[4]{0:T(128)S(1)} %pad_add_fusion.sc, bf16[16,16,16,128]{3,2,1,0:T(8,128)(2,1)S(1)} %get-tuple-element.166.h, f32[16,16,16,128]{3,2,1,0:T(8,128)S(1)} %get-tuple-element.167.edges, bf16[16,16,16,128]{3,2,1,0:T(8,128)(2,1)S(1)} %get-tuple-element.190.grad.grad_in, ...), custom_call_target="tpu_custom_call" | custom-call | flops 671088640 | bytes 9084944 | tf_op jit(solution)/shard_map/gradient_sums/pallas_call | solution.py:746
  76.1 4.5 %collective-permute-start.20 = (f32[480,128]{1,0:T(8,128)S(1)}, f32[480,128]{1,0:T(8,128)S(1)}, u32[]{:S(2)}, u32[]{:S(2)}) collective-permute-start(f32[480,128]{1,0:T(8,128)S(1)} %get-tuple-element.185), channel_id=1, source_target_pairs={{0,4},{4,0},{8,12},{12,8},{1,5},{5,1},{9,13},{13,9},{2,6},{6,2},{1... | collective-permute-start | bytes 737288 | tf_op jit(solution)/shard_map/ppermute | solution.py:808
  80.8 0.9 collective-permute-start.19
  81.7 7.2 %collective-permute-start.18 = (f32[16,16,128]{2,1,0:T(8,128)S(1)}, f32[16,16,128]{2,1,0:T(8,128)S(1)}, u32[]{:S(2)}, u32[]{:S(2)}) collective-permute-start(f32[16,16,128]{2,1,0:T(8,128)S(1)} %get-tuple-element.258), channel_id=1, source_target_pairs={{0,1},{1,0},{2,3},{3,2},{4,5},{5,4},{6,7},{7,6},{8,9},{9,8},{10,11... | collective-permute-start | bytes 393224 | tf_op jit(solution)/shard_map/ppermute | solution.py:903
  89.0 1.4 %collective-permute-start.21 = (f32[240,128]{1,0:T(8,128)S(1)}, f32[240,128]{1,0:T(8,128)S(1)}, u32[]{:S(2)}, u32[]{:S(2)}) collective-permute-start(f32[240,128]{1,0:T(8,128)S(1)} %slice_select_fusion), channel_id=1, source_target_pairs={{0,16},{16,0},{1,17},{17,1},{2,18},{18,2},{3,19},{19,3},{4,20},{20... | collective-permute-start | bytes 368648 | tf_op jit(solution)/shard_map/ppermute | solution.py:808
  90.4 1.9 %collective-permute-done.18.refs_3_ = f32[16,16,128]{2,1,0:T(8,128)S(1)} collective-permute-done((f32[16,16,128]{2,1,0:T(8,128)S(1)}, f32[16,16,128]{2,1,0:T(8,128)S(1)}, u32[]{:S(2)}, u32[]{:S(2)}) %collective-permute-start.18) | collective-permute-done | bytes 131104 | tf_op jit(solution)/shard_map/ppermute | solution.py:903
  92.3 1.6 %collective-permute-done.21 = f32[240,128]{1,0:T(8,128)S(1)} collective-permute-done((f32[240,128]{1,0:T(8,128)S(1)}, f32[240,128]{1,0:T(8,128)S(1)}, u32[]{:S(2)}, u32[]{:S(2)}) %collective-permute-start.21) | collective-permute-done | bytes 122912 | tf_op jit(solution)/shard_map/ppermute | solution.py:808
  94.0 2.0 %collective-permute-start.22 = (f32[120,128]{1,0:T(8,128)S(1)}, f32[120,128]{1,0:T(8,128)S(1)}, u32[]{:S(2)}, u32[]{:S(2)}) collective-permute-start(f32[120,128]{1,0:T(8,128)S(1)} %slice_select_fusion.1), channel_id=1, source_target_pairs={{0,8},{4,12},{8,0},{12,4},{1,9},{5,13},{9,1},{13,5},{2,10},{6,14},... | collective-permute-start | bytes 184328 | tf_op jit(solution)/shard_map/ppermute | solution.py:808
  96.0 3.9 %edges0_back.1 = (f32[16,16,16,128]{3,2,1,0:T(8,128)S(1)}, f32[136,128]{1,0:T(8,128)S(1)}) custom-call(s32[4]{0:T(128)S(1)} %pad_add_fusion.sc, bf16[2,2,128,128]{3,2,1,0:T(8,128)(2,1)S(1)} %copy-done.3, bf16[2,256,128]{2,1,0:T(8,128)(2,1)S(1)} %copy-done.4, bf16[2,128,128]{2,1,0:T(8,128)(2,1)S(1)} %copy-done.6, ...), custom_call_target="tpu_custom_call", output_to_operand_aliasing={{0}: (5, {})} | custom-call | flops 805306368 | bytes 12589072 | tf_op jit(solution)/shard_map/edges0_back/pallas_call | solution.py:746
  100.0 2.5 %state_grad.1 = bf16[16,16,16,128]{3,2,1,0:T(8,128)(2,1)} custom-call(s32[4]{0:T(128)S(1)} %pad_add_fusion.sc, bf16[2,2,128,128]{3,2,1,0:T(8,128)(2,1)S(1)} %copy-done.3, bf16[2,256,128]{2,1,0:T(8,128)(2,1)S(1)} %copy-done.4, bf16[16,16,16,128]{3,2,1,0:T(8,128)(2,1)S(1)} %get-tuple-element.190.grad.grad_in, ...), custom_call_target="tpu_custom_call" | custom-call | flops 536870912 | bytes 5505040 | tf_op jit(solution)/shard_map/state_grad/pallas_call | solution.py:746
  102.5 5.3 %collective-permute-done.23 = f32[256,128]{1,0:T(8,128)S(1)} collective-permute-done((f32[256,128]{1,0:T(8,128)S(1)}, f32[256,128]{1,0:T(8,128)S(1)}, u32[]{:S(2)}, u32[]{:S(2)}) %collective-permute-start.23) | collective-permute-done | bytes 131104 | tf_op jit(solution)/shard_map/ppermute | solution.py:808
  108.0 5.0 %collective-permute-done.24 = f32[256,128]{1,0:T(8,128)S(1)} collective-permute-done((f32[256,128]{1,0:T(8,128)S(1)}, f32[256,128]{1,0:T(8,128)S(1)}, u32[]{:S(2)}, u32[]{:S(2)}) %collective-permute-start.24) | collective-permute-done | bytes 131104 | tf_op jit(solution)/shard_map/ppermute | solution.py:808
  113.3 4.7 %collective-permute-done.25 = f32[256,128]{1,0:T(8,128)S(1)} collective-permute-done((f32[256,128]{1,0:T(8,128)S(1)}, f32[256,128]{1,0:T(8,128)S(1)}, u32[]{:S(2)}, u32[]{:S(2)}) %collective-permute-start.25) | collective-permute-done | bytes 131104 | tf_op jit(solution)/shard_map/ppermute | solution.py:808
  118.0 1.4 %collective-permute-start.26 = (f32[376,128]{1,0:T(8,128)S(1)}, f32[376,128]{1,0:T(8,128)S(1)}, u32[]{:S(2)}, u32[]{:S(2)}) collective-permute-start(f32[376,128]{1,0:T(8,128)S(1)} %pad_maximum_fusion.1), channel_id=1, source_target_pairs={{0,16},{16,0},{1,17},{17,1},{2,18},{18,2},{3,19},{19,3},{4,20},{20... | collective-permute-start | bytes 577544 | tf_op jit(solution)/shard_map/ppermute | solution.py:808
  119.4 4.3 %collective-permute-done.26 = f32[376,128]{1,0:T(8,128)S(1)} collective-permute-done((f32[376,128]{1,0:T(8,128)S(1)}, f32[376,128]{1,0:T(8,128)S(1)}, u32[]{:S(2)}, u32[]{:S(2)}) %collective-permute-start.26) | collective-permute-done | bytes 192544 | tf_op jit(solution)/shard_map/ppermute | solution.py:808
  123.9 1.6 %collective-permute-done.27.got = f32[616,128]{1,0:T(8,128)S(1)} collective-permute-done((f32[616,128]{1,0:T(8,128)S(1)}, f32[616,128]{1,0:T(8,128)S(1)}, u32[]{:S(2)}, u32[]{:S(2)}) %collective-permute-start.27) | collective-permute-done | bytes 315424 | tf_op jit(solution)/shard_map/ppermute | solution.py:808
  125.5 1.7 %finish.1 = (f32[2,2,128,128]{3,2,1,0:T(8,128)}, f32[2,256,128]{2,1,0:T(8,128)}, f32[2,128,128]{2,1,0:T(8,128)}, f32[2,2,128]{2,1,0:T(2,128)}) custom-call(s32[4]{0:T(128)S(1)} %pad_add_fusion.sc, bf16[2,2,128,128]{3,2,1,0:T(8,128)(2,1)S(1)} %copy-done.3, bf16[2,256,128]{2,1,0:T(8,128)(2,1)S(1)} %copy-done.4, f32[616,128]{1,0:T(8,128)S(1)} %pad_maximum_fusion.value, ...), custom_call_target="tpu_custom_call" | custom-call | bytes 1550352 | tf_op jit(solution)/shard_map/finish/pallas_call | solution.py:746
  (83 shorter events, 6.4 us)
Async XLA Ops:
  1.4 1.2 copy-start
  2.6 0.9 copy-start.2
  3.5 0.7 copy-start.7
  5.0 6.8 %collective-permute-start = (f32[16,16,128]{2,1,0:T(8,128)S(1)}, f32[16,16,128]{2,1,0:T(8,128)S(1)}, u32[]{:S(2)}, u32[]{:S(2)}) collective-permute-start(f32[16,16,128]{2,1,0:T(8,128)S(1)} %get-tuple-element.104), channel_id=1, source_target_pairs={{0,16},{16,0},{1,17},{17,1},{2,18},{18,2},{3,19},{19,3},{4,20},{20... | collective-permute-start | bytes 393224 | tf_op jit(solution)/shard_map/ppermute | solution.py:903
  12.0 3.7 %collective-permute-start.2 = (f32[16,16,128]{2,1,0:T(8,128)S(1)}, f32[16,16,128]{2,1,0:T(8,128)S(1)}, u32[]{:S(2)}, u32[]{:S(2)}) collective-permute-start(f32[16,16,128]{2,1,0:T(8,128)S(1)} %get-tuple-element.279), channel_id=1, source_target_pairs={{4,8},{8,4},{5,9},{9,5},{6,10},{10,6},{7,11},{11,7},{20,24},{24,20... | collective-permute-start | bytes 393224 | tf_op jit(solution)/shard_map/ppermute | solution.py:903
  12.6 3.9 %collective-permute-start.1 = (f32[16,16,128]{2,1,0:T(8,128)S(1)}, f32[16,16,128]{2,1,0:T(8,128)S(1)}, u32[]{:S(2)}, u32[]{:S(2)}) collective-permute-start(f32[16,16,128]{2,1,0:T(8,128)S(1)} %get-tuple-element.280), channel_id=1, source_target_pairs={{0,4},{4,0},{8,12},{12,8},{1,5},{5,1},{9,13},{13,9},{2,6},{6,2},{1... | collective-permute-start | bytes 393224 | tf_op jit(solution)/shard_map/ppermute | solution.py:903
  16.8 5.9 %copy-start.1 = (bf16[16,16,2,8,128]{4,3,2,1,0:T(8,128)(2,1)S(1)}, bf16[16,16,2,8,128]{4,3,2,1,0:T(8,128)(2,1)}, u32[]{:S(2)}) copy-start(bf16[16,16,2,8,128]{4,3,2,1,0:T(8,128)(2,1)} %param.7) | copy-start | bytes 3145732
  16.8 5.9 %copy-start.3 = (bf16[2,2,128,128]{3,2,1,0:T(8,128)(2,1)S(1)}, bf16[2,2,128,128]{3,2,1,0:T(8,128)(2,1)}, u32[]{:S(2)}) copy-start(bf16[2,2,128,128]{3,2,1,0:T(8,128)(2,1)} %edge_w.21) | copy-start | bytes 393220
  16.8 5.9 %copy-start.4 = (bf16[2,256,128]{2,1,0:T(8,128)(2,1)S(1)}, bf16[2,256,128]{2,1,0:T(8,128)(2,1)}, u32[]{:S(2)}) copy-start(bf16[2,256,128]{2,1,0:T(8,128)(2,1)} %node_in.19) | copy-start | bytes 393220
  16.8 5.9 %copy-start.6 = (bf16[2,128,128]{2,1,0:T(8,128)(2,1)S(1)}, bf16[2,128,128]{2,1,0:T(8,128)(2,1)}, u32[]{:S(2)}) copy-start(bf16[2,128,128]{2,1,0:T(8,128)(2,1)} %node_out.13) | copy-start | bytes 196612
  16.8 5.9 %collective-permute-start.3 = (f32[16,16,128]{2,1,0:T(8,128)S(1)}, f32[16,16,128]{2,1,0:T(8,128)S(1)}, u32[]{:S(2)}, u32[]{:S(2)}) collective-permute-start(f32[16,16,128]{2,1,0:T(8,128)S(1)} %get-tuple-element.111), channel_id=1, source_target_pairs={{0,1},{1,0},{2,3},{3,2},{4,5},{5,4},{6,7},{7,6},{8,9},{9,8},{10,11... | collective-permute-start | bytes 393224 | tf_op jit(solution)/shard_map/ppermute | solution.py:903
  18.5 4.2 %collective-permute-start.4 = (f32[16,16,128]{2,1,0:T(8,128)S(1)}, f32[16,16,128]{2,1,0:T(8,128)S(1)}, u32[]{:S(2)}, u32[]{:S(2)}) collective-permute-start(f32[16,16,128]{2,1,0:T(8,128)S(1)} %get-tuple-element.112), channel_id=1, source_target_pairs={{1,2},{2,1},{5,6},{6,5},{9,10},{10,9},{13,14},{14,13},{17,18},{18,... | collective-permute-start | bytes 393224 | tf_op jit(solution)/shard_map/ppermute | solution.py:903
  24.1 7.6 %collective-permute-start.5 = (f32[16,16,128]{2,1,0:T(8,128)S(1)}, f32[16,16,128]{2,1,0:T(8,128)S(1)}, u32[]{:S(2)}, u32[]{:S(2)}) collective-permute-start(f32[16,16,128]{2,1,0:T(8,128)S(1)} %face1.1), channel_id=1, source_target_pairs={{0,16},{16,0},{1,17},{17,1},{2,18},{18,2},{3,19},{19,3},{4,20},{20... | collective-permute-start | bytes 393224 | tf_op jit(solution)/shard_map/ppermute | solution.py:903
  31.9 4.5 %collective-permute-start.7 = (f32[16,16,128]{2,1,0:T(8,128)S(1)}, f32[16,16,128]{2,1,0:T(8,128)S(1)}, u32[]{:S(2)}, u32[]{:S(2)}) collective-permute-start(f32[16,16,128]{2,1,0:T(8,128)S(1)} %get-tuple-element.277), channel_id=1, source_target_pairs={{4,8},{8,4},{5,9},{9,5},{6,10},{10,6},{7,11},{11,7},{20,24},{24,20... | collective-permute-start | bytes 393224 | tf_op jit(solution)/shard_map/ppermute | solution.py:903
  32.5 4.8 %collective-permute-start.6 = (f32[16,16,128]{2,1,0:T(8,128)S(1)}, f32[16,16,128]{2,1,0:T(8,128)S(1)}, u32[]{:S(2)}, u32[]{:S(2)}) collective-permute-start(f32[16,16,128]{2,1,0:T(8,128)S(1)} %get-tuple-element.278), channel_id=1, source_target_pairs={{0,4},{4,0},{8,12},{12,8},{1,5},{5,1},{9,13},{13,9},{2,6},{6,2},{1... | collective-permute-start | bytes 393224 | tf_op jit(solution)/shard_map/ppermute | solution.py:903
  37.5 8.1 %copy-start.5 = (bf16[16,16,2,8,128]{4,3,2,1,0:T(8,128)(2,1)S(1)}, bf16[16,16,2,8,128]{4,3,2,1,0:T(8,128)(2,1)}, u32[]{:S(2)}) copy-start(bf16[16,16,2,8,128]{4,3,2,1,0:T(8,128)(2,1)} %param.8) | copy-start | bytes 3145732
  37.5 8.1 %collective-permute-start.8 = (f32[16,16,128]{2,1,0:T(8,128)S(1)}, f32[16,16,128]{2,1,0:T(8,128)S(1)}, u32[]{:S(2)}, u32[]{:S(2)}) collective-permute-start(f32[16,16,128]{2,1,0:T(8,128)S(1)} %get-tuple-element.124), channel_id=1, source_target_pairs={{0,1},{1,0},{2,3},{3,2},{4,5},{5,4},{6,7},{7,6},{8,9},{9,8},{10,11... | collective-permute-start | bytes 393224 | tf_op jit(solution)/shard_map/ppermute | solution.py:903
  42.2 3.5 %collective-permute-start.9 = (f32[16,16,128]{2,1,0:T(8,128)S(1)}, f32[16,16,128]{2,1,0:T(8,128)S(1)}, u32[]{:S(2)}, u32[]{:S(2)}) collective-permute-start(f32[16,16,128]{2,1,0:T(8,128)S(1)} %get-tuple-element.125), channel_id=1, source_target_pairs={{1,2},{2,1},{5,6},{6,5},{9,10},{10,9},{13,14},{14,13},{17,18},{18,... | collective-permute-start | bytes 393224 | tf_op jit(solution)/shard_map/ppermute | solution.py:903
  46.8 6.1 %collective-permute-start.10 = (f32[16,16,128]{2,1,0:T(8,128)S(1)}, f32[16,16,128]{2,1,0:T(8,128)S(1)}, u32[]{:S(2)}, u32[]{:S(2)}) collective-permute-start(f32[16,16,128]{2,1,0:T(8,128)S(1)} %face2.1), channel_id=1, source_target_pairs={{0,16},{16,0},{1,17},{17,1},{2,18},{18,2},{3,19},{19,3},{4,20},{20... | collective-permute-start | bytes 393224 | tf_op jit(solution)/shard_map/ppermute | solution.py:903
  53.0 1.4 %collective-permute-start.11 = (f32[16,16,128]{2,1,0:T(8,128)S(1)}, f32[16,16,128]{2,1,0:T(8,128)S(1)}, u32[]{:S(2)}, u32[]{:S(2)}) collective-permute-start(f32[16,16,128]{2,1,0:T(8,128)S(1)} %get-tuple-element.275), channel_id=1, source_target_pairs={{0,4},{4,0},{8,12},{12,8},{1,5},{5,1},{9,13},{13,9},{2,6},{6,2},{1... | collective-permute-start | bytes 393224 | tf_op jit(solution)/shard_map/ppermute | solution.py:903
  53.2 1.2 collective-permute-start.12
  54.7 7.1 %collective-permute-start.13 = (f32[16,16,128]{2,1,0:T(8,128)S(1)}, f32[16,16,128]{2,1,0:T(8,128)S(1)}, u32[]{:S(2)}, u32[]{:S(2)}) collective-permute-start(f32[16,16,128]{2,1,0:T(8,128)S(1)} %get-tuple-element.138), channel_id=1, source_target_pairs={{0,1},{1,0},{2,3},{3,2},{4,5},{5,4},{6,7},{7,6},{8,9},{9,8},{10,11... | collective-permute-start | bytes 393224 | tf_op jit(solution)/shard_map/ppermute | solution.py:903
  58.8 3.0 %collective-permute-start.14 = (f32[16,16,128]{2,1,0:T(8,128)S(1)}, f32[16,16,128]{2,1,0:T(8,128)S(1)}, u32[]{:S(2)}, u32[]{:S(2)}) collective-permute-start(f32[16,16,128]{2,1,0:T(8,128)S(1)} %get-tuple-element.139), channel_id=1, source_target_pairs={{1,2},{2,1},{5,6},{6,5},{9,10},{10,9},{13,14},{14,13},{17,18},{18,... | collective-permute-start | bytes 393224 | tf_op jit(solution)/shard_map/ppermute | solution.py:903
  63.1 6.0 %collective-permute-start.15 = (f32[16,16,128]{2,1,0:T(8,128)S(1)}, f32[16,16,128]{2,1,0:T(8,128)S(1)}, u32[]{:S(2)}, u32[]{:S(2)}) collective-permute-start(f32[16,16,128]{2,1,0:T(8,128)S(1)} %face3.1), channel_id=1, source_target_pairs={{0,16},{16,0},{1,17},{17,1},{2,18},{18,2},{3,19},{19,3},{4,20},{20... | collective-permute-start | bytes 393224 | tf_op jit(solution)/shard_map/ppermute | solution.py:903
  69.3 6.8 %collective-permute-start.16 = (f32[16,16,128]{2,1,0:T(8,128)S(1)}, f32[16,16,128]{2,1,0:T(8,128)S(1)}, u32[]{:S(2)}, u32[]{:S(2)}) collective-permute-start(f32[16,16,128]{2,1,0:T(8,128)S(1)} %get-tuple-element.164), channel_id=1, source_target_pairs={{0,4},{4,0},{8,12},{12,8},{1,5},{5,1},{9,13},{13,9},{2,6},{6,2},{1... | collective-permute-start | bytes 393224 | tf_op jit(solution)/shard_map/ppermute | solution.py:903
  73.6 2.5 %collective-permute-start.17 = (f32[16,16,128]{2,1,0:T(8,128)S(1)}, f32[16,16,128]{2,1,0:T(8,128)S(1)}, u32[]{:S(2)}, u32[]{:S(2)}) collective-permute-start(f32[16,16,128]{2,1,0:T(8,128)S(1)} %get-tuple-element.165), channel_id=1, source_target_pairs={{4,8},{8,4},{5,9},{9,5},{6,10},{10,6},{7,11},{11,7},{20,24},{24,20... | collective-permute-start | bytes 393224 | tf_op jit(solution)/shard_map/ppermute | solution.py:903
  76.1 12.9 %collective-permute-start.20 = (f32[480,128]{1,0:T(8,128)S(1)}, f32[480,128]{1,0:T(8,128)S(1)}, u32[]{:S(2)}, u32[]{:S(2)}) collective-permute-start(f32[480,128]{1,0:T(8,128)S(1)} %get-tuple-element.185), channel_id=1, source_target_pairs={{0,4},{4,0},{8,12},{12,8},{1,5},{5,1},{9,13},{13,9},{2,6},{6,2},{1... | collective-permute-start | bytes 737288 | tf_op jit(solution)/shard_map/ppermute | solution.py:808
  80.8 9.6 %collective-permute-start.19 = (f32[16,16,128]{2,1,0:T(8,128)S(1)}, f32[16,16,128]{2,1,0:T(8,128)S(1)}, u32[]{:S(2)}, u32[]{:S(2)}) collective-permute-start(f32[16,16,128]{2,1,0:T(8,128)S(1)} %get-tuple-element.257), channel_id=1, source_target_pairs={{1,2},{2,1},{5,6},{6,5},{9,10},{10,9},{13,14},{14,13},{17,18},{18,... | collective-permute-start | bytes 393224 | tf_op jit(solution)/shard_map/ppermute | solution.py:903
  81.7 10.6 %collective-permute-start.18 = (f32[16,16,128]{2,1,0:T(8,128)S(1)}, f32[16,16,128]{2,1,0:T(8,128)S(1)}, u32[]{:S(2)}, u32[]{:S(2)}) collective-permute-start(f32[16,16,128]{2,1,0:T(8,128)S(1)} %get-tuple-element.258), channel_id=1, source_target_pairs={{0,1},{1,0},{2,3},{3,2},{4,5},{5,4},{6,7},{7,6},{8,9},{9,8},{10,11... | collective-permute-start | bytes 393224 | tf_op jit(solution)/shard_map/ppermute | solution.py:903
  89.0 4.9 %collective-permute-start.21 = (f32[240,128]{1,0:T(8,128)S(1)}, f32[240,128]{1,0:T(8,128)S(1)}, u32[]{:S(2)}, u32[]{:S(2)}) collective-permute-start(f32[240,128]{1,0:T(8,128)S(1)} %slice_select_fusion), channel_id=1, source_target_pairs={{0,16},{16,0},{1,17},{17,1},{2,18},{18,2},{3,19},{19,3},{4,20},{20... | collective-permute-start | bytes 368648 | tf_op jit(solution)/shard_map/ppermute | solution.py:808
  94.0 5.9 %collective-permute-start.22 = (f32[120,128]{1,0:T(8,128)S(1)}, f32[120,128]{1,0:T(8,128)S(1)}, u32[]{:S(2)}, u32[]{:S(2)}) collective-permute-start(f32[120,128]{1,0:T(8,128)S(1)} %slice_select_fusion.1), channel_id=1, source_target_pairs={{0,8},{4,12},{8,0},{12,4},{1,9},{5,13},{9,1},{13,5},{2,10},{6,14},... | collective-permute-start | bytes 184328 | tf_op jit(solution)/shard_map/ppermute | solution.py:808
  99.9 8.0 %collective-permute-start.23 = (f32[256,128]{1,0:T(8,128)S(1)}, f32[256,128]{1,0:T(8,128)S(1)}, u32[]{:S(2)}, u32[]{:S(2)}) collective-permute-start(f32[256,128]{1,0:T(8,128)S(1)} %pad_maximum_fusion.2), channel_id=1, source_target_pairs={{0,2},{1,3},{2,0},{3,1},{4,6},{5,7},{6,4},{7,5},{8,10},{9,11},{10,... | collective-permute-start | bytes 393224 | tf_op jit(solution)/shard_map/ppermute | solution.py:808
  107.9 5.0 %collective-permute-start.24 = (f32[256,128]{1,0:T(8,128)S(1)}, f32[256,128]{1,0:T(8,128)S(1)}, u32[]{:S(2)}, u32[]{:S(2)}) collective-permute-start(f32[256,128]{1,0:T(8,128)S(1)} %add.152), channel_id=1, source_target_pairs={{0,1},{1,0},{2,3},{3,2},{4,5},{5,4},{6,7},{7,6},{8,9},{9,8},{10,11... | collective-permute-start | bytes 393224 | tf_op jit(solution)/shard_map/ppermute | solution.py:808
  112.9 5.0 %collective-permute-start.25 = (f32[256,128]{1,0:T(8,128)S(1)}, f32[256,128]{1,0:T(8,128)S(1)}, u32[]{:S(2)}, u32[]{:S(2)}) collective-permute-start(f32[256,128]{1,0:T(8,128)S(1)} %add.153), channel_id=1, source_target_pairs={{0,8},{4,12},{8,0},{12,4},{1,9},{5,13},{9,1},{13,5},{2,10},{6,14},... | collective-permute-start | bytes 393224 | tf_op jit(solution)/shard_map/ppermute | solution.py:808
  118.0 5.7 %collective-permute-start.26 = (f32[376,128]{1,0:T(8,128)S(1)}, f32[376,128]{1,0:T(8,128)S(1)}, u32[]{:S(2)}, u32[]{:S(2)}) collective-permute-start(f32[376,128]{1,0:T(8,128)S(1)} %pad_maximum_fusion.1), channel_id=1, source_target_pairs={{0,16},{16,0},{1,17},{17,1},{2,18},{18,2},{3,19},{19,3},{4,20},{20... | collective-permute-start | bytes 577544 | tf_op jit(solution)/shard_map/ppermute | solution.py:808
  123.8 1.7 %collective-permute-start.27 = (f32[616,128]{1,0:T(8,128)S(1)}, f32[616,128]{1,0:T(8,128)S(1)}, u32[]{:S(2)}, u32[]{:S(2)}) collective-permute-start(f32[616,128]{1,0:T(8,128)S(1)} %pad_maximum_fusion.value), channel_id=1, source_target_pairs={{0,4},{4,0},{8,12},{12,8},{1,5},{5,1},{9,13},{13,9},{2,6},{6,2},{1... | collective-permute-start | bytes 946184 | tf_op jit(solution)/shard_map/ppermute | solution.py:808
